TPU v7x, 256 devices: a whole 4x4x8 slice. The times are simulated.
256 devices in a mesh: ctx: 8 (over x, core), dp: 32 (over y, z).
Axes of the slice: x: 4, y: 4, z: 8, core: 2. Of those that a mesh axis runs over, the one named last changes fastest.
Arguments:
- tokens: bfloat16 [32, 1024, 1536], P('dp', 'ctx')
- grad_heads: bfloat16 [32, 1024, 1536], P('dp', 'ctx'), may hold values from -6 to 6
- tile_mask: int32 [32, 8, 8], P('dp', 'ctx'), may hold values from 0 to 1
- segments: int32 [32, 1024], P('dp'), may hold values from 0 to 3, never falling along the last dimension, each value on 1 to 512 neighbouring positions
- w_query: bfloat16 [1536, 1536], replicated
- w_key: bfloat16 [1536, 256], replicated
- w_value: bfloat16 [1536, 256], replicated, may hold values from -0.15625 to 0.15625
Outputs:
- grad_tokens: bfloat16 [32, 1024, 1536], P('dp', 'ctx')
- grad_projection: float32 [1536, 2048], P('dp', 'ctx')
Inputs may be any that keep to these rules, and one draw needn't show every extreme that they name: `segments`: segment numbers never fall along a sequence.
All inputs are finite; a program needn't handle non-finite values.
Results may differ from a plain program's by a relative error of at most 0.029.
Values may be sent and summed in bfloat16 or wider, within the bound.
No kernel may reach another device: no remote copies, remote signals or barrier semaphores. Data moves between devices by JAX's collectives and lax.ppermute only.
A program may use at most 128 MiB of HBM per device.

v0:
```python
import math

import jax
import jax.numpy as jnp
from jax import lax
from jax.sharding import PartitionSpec as P

QH = 12
KVH = 2
HD = 128
TILE = 128


def shards(tokens, grad_heads, tile_mask, segments, w_query, w_key, w_value):
    softmax_scale = 1.0 / math.sqrt(HD)
    inputs = tokens[0]
    upstream = grad_heads[0]
    local_rows = inputs.shape[0]
    queries = jnp.dot(inputs, w_query, preferred_element_type=jnp.float32).astype(jnp.bfloat16)
    keys = jnp.dot(inputs, w_key, preferred_element_type=jnp.float32).astype(jnp.bfloat16)
    values = jnp.dot(inputs, w_value, preferred_element_type=jnp.float32).astype(jnp.bfloat16)
    all_keys, all_values = (
        lax.all_gather(keys, "ctx", axis=0, tiled=True),
        lax.all_gather(values, "ctx", axis=0, tiled=True),
    )
    first_row = lax.axis_index("ctx") * local_rows
    passages = segments[0]
    own_passages = lax.dynamic_slice_in_dim(passages, first_row, local_rows)
    spread = jnp.repeat(jnp.repeat(tile_mask[0], TILE, axis=0), TILE, axis=1)
    allowed = (spread == 1) | (own_passages[:, None] == passages[None, :])
    group = QH // KVH
    query_parts = []
    key_parts = []
    value_parts = []
    for kv_head in range(KVH):
        key_head = all_keys[:, kv_head * HD : (kv_head + 1) * HD]
        value_head = all_values[:, kv_head * HD : (kv_head + 1) * HD]
        query_group = queries[:, kv_head * group * HD : (kv_head + 1) * group * HD].reshape(
            local_rows, group, HD
        )
        upstream_group = upstream[:, kv_head * group * HD : (kv_head + 1) * group * HD].reshape(
            local_rows, group, HD
        )
        scores = (
            jnp.einsum("thd,kd->htk", query_group, key_head, preferred_element_type=jnp.float32)
            * softmax_scale
        )
        scores = jnp.where(allowed[None], scores, -jnp.inf)
        probs = jax.nn.softmax(scores, axis=-1)
        probs_low = probs.astype(jnp.bfloat16)
        attended = jnp.einsum(
            "htk,kd->htd", probs_low, value_head, preferred_element_type=jnp.float32
        )
        delta = jnp.einsum("thd,htd->ht", upstream_group.astype(jnp.float32), attended)[:, :, None]
        grad_probs = jnp.einsum(
            "thd,kd->htk", upstream_group, value_head, preferred_element_type=jnp.float32
        )
        grad_scores = (probs * (grad_probs - delta)).astype(jnp.bfloat16)
        query_grad = (
            jnp.einsum("htk,kd->thd", grad_scores, key_head, preferred_element_type=jnp.float32)
            * softmax_scale
        )
        query_parts.append(query_grad.astype(jnp.bfloat16).reshape(local_rows, group * HD))
        key_parts.append(
            jnp.einsum("htk,thd->kd", grad_scores, query_group, preferred_element_type=jnp.float32)
            * softmax_scale
        )
        value_parts.append(
            jnp.einsum("htk,thd->kd", probs_low, upstream_group, preferred_element_type=jnp.float32)
        )
    grad_query = jnp.concatenate(query_parts, axis=1)
    key_terms = jnp.concatenate(key_parts, axis=1)
    value_terms = jnp.concatenate(value_parts, axis=1)
    key_sum, value_sum = (
        lax.psum_scatter(
            key_terms.astype(jnp.bfloat16), "ctx", scatter_dimension=0, tiled=True
        ).astype(jnp.float32),
        lax.psum_scatter(
            value_terms.astype(jnp.bfloat16), "ctx", scatter_dimension=0, tiled=True
        ).astype(jnp.float32),
    )
    grad_key = key_sum.astype(jnp.bfloat16)
    grad_value = value_sum.astype(jnp.bfloat16)
    grad_inputs = jnp.dot(grad_query, w_query.T, preferred_element_type=jnp.float32)
    grad_inputs = grad_inputs + jnp.dot(grad_key, w_key.T, preferred_element_type=jnp.float32)
    grad_inputs = grad_inputs + jnp.dot(grad_value, w_value.T, preferred_element_type=jnp.float32)
    stacked = jnp.concatenate([grad_query, grad_key, grad_value], axis=1)
    row_block = lax.psum_scatter(
        lax.dot_general(
            inputs, stacked, (((0,), (0,)), ((), ())), preferred_element_type=jnp.float32
        ).astype(jnp.bfloat16),
        "dp",
        scatter_dimension=0,
        tiled=True,
    )
    weight_grad = lax.psum_scatter(row_block, "ctx", scatter_dimension=1, tiled=True).astype(
        jnp.float32
    )
    return (grad_inputs.astype(jnp.bfloat16)[None], weight_grad)


def solution(mesh):
    return jax.shard_map(
        shards,
        mesh=mesh,
        in_specs=(
            P("dp", "ctx", None),
            P("dp", "ctx", None),
            P("dp", "ctx", None),
            P("dp", None),
            P(),
            P(),
            P(),
        ),
        out_specs=(P("dp", "ctx", None), P("dp", "ctx")),
        check_vma=False,
    )
```

profile of v0, /device:TPU:8, one launch (start us, length us, event | category | flops | bytes accessed | tf_op | source)
XLA Modules:
  0.0 413.8 jit_solution(1361583993193071649)
XLA Ops:
  7.2 0.0 copy-start
  7.2 0.0 copy-start.1
  7.2 0.0 reduce-scatter.13.cloned.1.call-start
  7.2 0.7 compare_bitcast_fusion
  8.0 0.1 broadcast_bitcast_fusion
  8.1 0.3 copy-done
  8.3 1.3 convolution_convert_fusion.3
  9.6 1.5 convolution_convert_fusion.2
  11.1 1.2 copy.42
  12.4 0.7 fusion.57
  13.1 3.2 convolution_convert_fusion.1
  16.3 0.8 copy.40
  17.1 0.2 copy.47
  17.3 13.5 %all_gather.7 = bf16[1024,256]{1,0:T(8,128)(2,1)S(1)} all-gather(bf16[128,256]{1,0:T(8,128)(2,1)S(1)} %convolution_convert_fusion.2), channel_id=1, replica_groups=mesh['ctx'=8,'dp'=32] {'ctx'}, dimensions={0}, use_global_device_ids=true | all-gather | bytes 589824 | tf_op jit(solution)/shard_map/all_gather | solution.py:24
  30.8 13.1 %all_gather.6 = bf16[1024,256]{1,0:T(8,128)(2,1)S(1)} all-gather(bf16[128,256]{1,0:T(8,128)(2,1)S(1)} %convolution_convert_fusion.3), channel_id=1, replica_groups=mesh['ctx'=8,'dp'=32] {'ctx'}, dimensions={0}, use_global_device_ids=true | all-gather | bytes 589824 | tf_op jit(solution)/shard_map/all_gather | solution.py:23
  43.9 0.3 compare_or_fusion
  44.2 0.0 copy-start.18
  44.2 2.7 fusion.58
  46.9 0.0 copy-done.10
  46.9 2.3 fusion.18
  49.2 0.4 fusion.28
  49.7 0.0 copy-done.13
  49.7 0.1 copy-done.7
  49.8 1.6 fusion.4
  51.4 0.6 fusion.22
  52.0 0.0 copy-done.8
  52.0 3.7 fusion.59
  55.7 2.3 fusion.17
  58.0 0.0 copy-start.4
  58.0 0.0 copy-done.12
  58.1 0.0 copy-done.15
  58.1 0.4 fusion.27
  58.5 0.3 copy-done.6
  58.8 0.6 fusion.6
  59.5 1.1 copy-done.2
  60.6 0.6 fusion.21
  61.3 1.0 copy.84
  62.3 0.0 reduce-scatter.13.cloned.1.call-update
  62.4 0.0 reduce-scatter.15.cloned.1.call-start
  62.4 2.1 fusion.24
  64.5 2.1 fusion.23
  66.6 1.0 copy.86
  67.6 0.0 reduce-scatter.15.cloned.1.call-update
  67.6 0.2 reduce-scatter.17.cloned.1.call-start
  67.8 1.4 fusion.26
  69.2 1.9 fusion.25
  71.1 27.2 %reduce-scatter.13.cloned.1.call-done = bf16[128,256]{1,0:T(8,128)(2,1)} async-done(((bf16[1024,256]{1,0:T(8,128)(2,1)}), bf16[128,256]{1,0:T(8,128)(2,1)}) %reduce-scatter.13.cloned.1.call-update) | async-done | bytes 65552
  98.3 0.9 copy.85
  99.2 34.1 %reduce-scatter.15.cloned.1.call-done = bf16[128,256]{1,0:T(8,128)(2,1)} async-done(((bf16[1024,256]{1,0:T(8,128)(2,1)}), bf16[128,256]{1,0:T(8,128)(2,1)}) %reduce-scatter.15.cloned.1.call-update) | async-done | bytes 65552
  133.3 0.9 copy.87
  134.3 4.4 %fusion.2 = bf16[1536,2048]{0,1:T(8,128)(2,1)} fusion(bf16[128,256]{0,1:T(8,128)(2,1)S(1)} %copy.87, bf16[128,256]{0,1:T(8,128)(2,1)S(1)} %copy.85, bf16[128,768]{0,1:T(8,128)(2,1)S(1)} %bitcast.154, bf16[128,768]{0,1:T(8,128)(2,1)S(1)} %bitcast.156, bf16[1,128,1536]{2,1,0:T(8,128)(2,1)S(1)} %copy-done.1), kind=kOutput, calls=%fused_computation.3 | convolution fusion | flops 810549248 | bytes 7208960 | tf_op jit(solution)/shard_map/dot_general | solution.py:89
  138.7 8.7 %copy.88 = bf16[1536,2048]{1,0:T(8,128)(2,1)} copy(bf16[1536,2048]{0,1:T(8,128)(2,1)} %fusion.2) | data formatting | bytes 12582912
  147.5 0.0 reduce-scatter.17.cloned.1.call-update
  147.5 0.0 copy-start.16
  147.5 0.0 reduce-scatter.11.cloned.1.call-start
  147.5 4.0 fusion.36
  151.6 0.0 copy-start.5
  151.6 219.0 %reduce-scatter.17.cloned.1.call-done = bf16[48,2048]{1,0:T(8,128)(2,1)} async-done(((bf16[1536,2048]{1,0:T(8,128)(2,1)}), bf16[48,2048]{1,0:T(8,128)(2,1)}) %reduce-scatter.17.cloned.1.call-update) | async-done | bytes 196624
  370.6 1.9 copy.89
  372.5 0.0 reduce-scatter.11.cloned.1.call-update
  372.5 0.4 convolution_add_fusion.1
  372.9 1.1 fusion.10
  374.1 31.6 %reduce-scatter.11.cloned.1.call-done = bf16[48,256]{0,1:T(8,128)(2,1)} async-done(((bf16[48,2048]{0,1:T(8,128)(2,1)}), bf16[48,256]{0,1:T(8,128)(2,1)}) %reduce-scatter.11.cloned.1.call-update) | async-done | bytes 24592 | tf_op jit(solution)/shard_map/reduce_scatter | solution.py:96
  405.7 1.5 copy.57
  (29 shorter events, 0.1 us)
Async XLA Ops:
  7.2 1.2 copy-start
  7.2 5.9 %copy-start.1 = (bf16[1,128,1536]{2,1,0:T(8,128)(2,1)S(1)}, bf16[1,128,1536]{2,1,0:T(8,128)(2,1)}, u32[]{:S(2)}) copy-start(bf16[1,128,1536]{2,1,0:T(8,128)(2,1)} %param.7) | copy-start | bytes 1179652
  7.2 91.1 %reduce-scatter.13.cloned.1.call-start = ((), (), s32[]{:S(2)}) async-start(), calls=%async_computation.5 | async-start | bytes 589824
  13.1 36.6 %copy-start.13 = (bf16[128,768]{0,1:T(8,128)(2,1)}, bf16[128,768]{0,1:T(8,128)(2,1)S(1)}, u32[]{:S(2)}) copy-start(bf16[128,768]{0,1:T(8,128)(2,1)S(1)} %get-tuple-element.11) | copy-start | bytes 589828
  13.1 30.8 %copy-start.19 = (s32[1,1024]{1,0:T(1,128)S(1)}, s32[1,1024]{1,0:T(1,128)}, u32[]{:S(2)}) copy-start(s32[1,1024]{1,0:T(1,128)} %param.10) | copy-start | bytes 12292
  17.3 29.6 %copy-start.10 = (bf16[128,768]{0,1:T(8,128)(2,1)}, bf16[128,768]{0,1:T(8,128)(2,1)S(1)}, u32[]{:S(2)}) copy-start(bf16[128,768]{0,1:T(8,128)(2,1)S(1)} %copy.47) | copy-start | bytes 589828
  30.8 18.5 %copy-start.14 = (bf16[1024,256]{1,0:T(8,128)(2,1)}, bf16[1024,256]{1,0:T(8,128)(2,1)S(1)}, u32[]{:S(2)}) copy-start(bf16[1024,256]{1,0:T(8,128)(2,1)S(1)} %all_gather.7) | copy-start | bytes 1572868
  43.9 8.2 %copy-start.8 = (bf16[1024,256]{1,0:T(8,128)(2,1)}, bf16[1024,256]{1,0:T(8,128)(2,1)S(1)}, u32[]{:S(2)}) copy-start(bf16[1024,256]{1,0:T(8,128)(2,1)S(1)} %all_gather.6) | copy-start | bytes 1572868
  44.2 5.0 %copy-start.18 = (pred[128,1024]{0,1:T(8,128)(4,1)}, pred[128,1024]{0,1:T(8,128)(4,1)S(1)}, u32[]{:S(2)}) copy-start(pred[128,1024]{0,1:T(8,128)(4,1)S(1)} %compare_or_fusion) | copy-start | bytes 393220
  46.9 2.8 copy-start.7
  49.2 2.1 copy-start.3
  49.8 1.6 copy-start.11
  55.7 2.3 copy-start.12
  55.7 2.3 copy-start.15
  55.7 3.1 copy-start.6
  58.0 1.4 copy-start.4
  58.8 1.8 copy-start.9
  59.5 1.2 copy-start.2
  62.4 71.0 %reduce-scatter.15.cloned.1.call-start = ((), (), s32[]{:S(2)}) async-start(), calls=%async_computation.6 | async-start | bytes 589824
  67.6 303.0 %reduce-scatter.17.cloned.1.call-start = ((), (), s32[]{:S(2)}) async-start(), calls=%async_computation.7 | async-start | bytes 6488064
  147.5 225.0 %copy-start.16 = (bf16[128,256]{1,0:T(8,128)(2,1)S(1)}, bf16[128,256]{1,0:T(8,128)(2,1)}, u32[]{:S(2)}) copy-start(bf16[128,256]{1,0:T(8,128)(2,1)} %reduce-scatter.13.cloned.1.call-done) | copy-start | bytes 196612
  147.5 258.2 %reduce-scatter.11.cloned.1.call-start = ((), (), s32[]{:S(2)}) async-start(), calls=%async_computation.4 | async-start | bytes 589824 | tf_op jit(solution)/shard_map/reduce_scatter | solution.py:96
  151.6 221.4 %copy-start.5 = (bf16[1536,256]{1,0:T(8,128)(2,1)S(1)}, bf16[1536,256]{1,0:T(8,128)(2,1)}, u32[]{:S(2)}) copy-start(bf16[1536,256]{1,0:T(8,128)(2,1)} %param.13) | copy-start | bytes 2359300
  151.6 221.4 %copy-start.17 = (bf16[128,256]{1,0:T(8,128)(2,1)S(1)}, bf16[128,256]{1,0:T(8,128)(2,1)}, u32[]{:S(2)}) copy-start(bf16[128,256]{1,0:T(8,128)(2,1)} %reduce-scatter.15.cloned.1.call-done) | copy-start | bytes 196612
Sparse Core Ops, SparseCore 0:
  62.5 35.7 reduce-scatter.12
  101.0 32.3 reduce-scatter.14
  147.6 222.9 reduce-scatter.16
  373.1 32.5 reduce-scatter.10
where the time goes:
time: 415 us; the launch traced here: 414 us
  waiting for transfers between devices  312 us (75%)
  matrix products  34.1 us (8%)
  blocking collectives  26.5 us (6%)
  local copies, waits for them, and re-layouts  21 us (5%)
  between operations  14.1 us (3%)
  other arithmetic  5.73 us (1%)
    unnamed x7, waiting for transfers between devices  280 us
    reduce_scatter x1, waiting for transfers between devices, shards(): lax.psum_scatter(row_block, 'ctx', scatter_dimension=1, tiled=True)  31.6 us
    unnamed x48, local copies, waits for them, and re-layouts  19.2 us
    all_gather x1, blocking collectives, shards(): lax.all_gather(values, 'ctx', axis=0, tiled=True)  13.5 us
    all_gather x1, blocking collectives, shards(): lax.all_gather(keys, 'ctx', axis=0, tiled=True)  13.1 us
  transfers between devices with their start and end apart: 4, of which 4 were waited for; matrix products, arithmetic and copies ran while one was open for 4% of the time, Pallas kernels for 0%

commit v1 on v0

v1 whole, which is shorter than its diff:
```python
import functools
import math

import jax
import jax.numpy as jnp
from jax import lax
from jax.experimental import pallas as pl
from jax.experimental.pallas import tpu as pltpu
from jax.sharding import PartitionSpec as P

QH = 12
KVH = 2
HD = 128
TILE = 128
D = 1536
KEYS = 1024
CHIPS = 4
GROUP = QH // KVH
GF = GROUP * HD
YS = 4
ZS = 8
SCALE = 1.0 / math.sqrt(HD)
LOG2_SCALE = SCALE * math.log2(math.e)
BF = jnp.bfloat16
F32 = jnp.float32
VMEM_LIMIT = 48 * 1024 * 1024

CORE = [(i, i ^ 1) for i in range(8)]
NT = (((1,), (1,)), ((), ()))


def chip_shift(d):
    return [(i, ((i // 2 + d) % CHIPS) * 2 + i % 2) for i in range(8)]


def y_shift(d):
    return [(i, ((i // ZS + d) % YS) * ZS + i % ZS) for i in range(32)]


Z_GROUPS = [[y * ZS + z for z in range(ZS)] for y in range(YS)]


def dot(a, b):
    return jnp.dot(a, b, preferred_element_type=F32)


def dot_nt(a, b):
    return lax.dot_general(a, b, NT, preferred_element_type=F32)


def cost(flops, bytes_accessed, transcendentals=0):
    return pl.CostEstimate(
        flops=flops, bytes_accessed=bytes_accessed, transcendentals=transcendentals
    )


PARAMS = pltpu.CompilerParams(vmem_limit_bytes=VMEM_LIMIT)
WHOLE = pl.BlockSpec(memory_space=pltpu.VMEM)


def kv_kernel(place, own, other, w_key, w_value, out):
    weights = jnp.concatenate([w_key[...], w_value[...]], axis=1)
    out[:TILE] = dot(own[...], weights).astype(BF)
    out[TILE:] = dot(other[...], weights).astype(BF)


def project_kv(place, own, other, w_key, w_value):
    return pl.pallas_call(
        kv_kernel,
        grid_spec=pltpu.PrefetchScalarGridSpec(
            num_scalar_prefetch=1,
            grid=(1,),
            in_specs=[
                pl.BlockSpec((TILE, D), lambda i, p: (0, 0)),
                pl.BlockSpec((TILE, D), lambda i, p: (0, 0)),
                pl.BlockSpec((D, HD), lambda i, p: (0, p[1])),
                pl.BlockSpec((D, HD), lambda i, p: (0, p[1])),
            ],
            out_specs=pl.BlockSpec((2 * TILE, 2 * HD), lambda i, p: (0, 0)),
        ),
        out_shape=jax.ShapeDtypeStruct((2 * TILE, 2 * HD), BF),
        compiler_params=PARAMS,
        cost_estimate=cost(2 * 256 * D * 256, 2 * (256 * D + D * 256)),
        name="project_kv",
    )(place, own, other, w_key, w_value)


def query_kernel(place, own, other, w_query, segments, mask_own, mask_other, out, bias):
    out[:TILE] = dot(own[...], w_query[...]).astype(BF)
    out[TILE:] = dot(other[...], w_query[...]).astype(BF)

    @pl.when(pl.program_id(0) == 0)
    def _():
        chip, core = place[0], place[1]
        passages = segments[...]
        ends = [jnp.sum((passages <= s).astype(jnp.int32)) for s in range(3)]
        for slot in range(2):
            masks = mask_own if slot == 0 else mask_other
            tile = 2 * chip + (core if slot == 0 else 1 - core)
            mine = segments[:, pl.ds(pl.multiple_of(tile * TILE, TILE), TILE)]
            low = jnp.where(
                mine == 0, 0, jnp.where(mine == 1, ends[0], jnp.where(mine == 2, ends[1], ends[2]))
            )
            high = jnp.where(
                mine == 0,
                ends[0],
                jnp.where(mine == 1, ends[1], jnp.where(mine == 2, ends[2], KEYS)),
            )
            for d in range(CHIPS):
                for key_slot in range(2):
                    key_tile = 2 * lax.rem(chip + CHIPS - d, CHIPS) + (
                        core if key_slot == 0 else 1 - core
                    )
                    seen = masks[0, key_tile] == 1
                    position = key_tile * TILE + lax.broadcasted_iota(
                        jnp.int32, (TILE, TILE), 0
                    )
                    first = jnp.where(seen, 0, low)
                    last = jnp.where(seen, KEYS, high)
                    allowed = (position >= first) & (position < last)
                    row = d * 2 * TILE + key_slot * TILE
                    bias[row : row + TILE, slot * TILE : (slot + 1) * TILE] = jnp.where(
                        allowed, 0.0, -jnp.inf
                    )


def project_query(place, own, other, w_query, segments, mask_own, mask_other):
    blocks = GF // 256
    return pl.pallas_call(
        query_kernel,
        grid_spec=pltpu.PrefetchScalarGridSpec(
            num_scalar_prefetch=1,
            grid=(blocks,),
            in_specs=[
                pl.BlockSpec((TILE, D), lambda i, p: (0, 0)),
                pl.BlockSpec((TILE, D), lambda i, p: (0, 0)),
                pl.BlockSpec((D, 256), lambda i, p: (0, p[1] * blocks + i)),
                pl.BlockSpec((1, KEYS), lambda i, p: (0, 0)),
                pl.BlockSpec(memory_space=pltpu.SMEM),
                pl.BlockSpec(memory_space=pltpu.SMEM),
            ],
            out_specs=[
                pl.BlockSpec((2 * TILE, 256), lambda i, p: (0, i)),
                pl.BlockSpec((KEYS, 2 * TILE), lambda i, p: (0, 0)),
            ],
        ),
        out_shape=[
            jax.ShapeDtypeStruct((2 * TILE, GF), BF),
            jax.ShapeDtypeStruct((KEYS, 2 * TILE), F32),
        ],
        compiler_params=PARAMS,
        cost_estimate=cost(2 * 256 * D * GF, 2 * (256 * D + D * GF + 256 * GF)),
        name="project_query",
    )(place, own, other, w_query, segments, mask_own, mask_other)


def attention_kernel(
    place, query, up_own, up_other, kv0, kv1, kv2, kv3, bias,
    grad_query, out0, out1, out2, out3,
    keys, values, keys_t, grad_key, grad_value,
):
    step = pl.program_id(0)

    @pl.when(step == 0)
    def _():
        for d, kv in enumerate((kv0, kv1, kv2, kv3)):
            keys[d * 256 : (d + 1) * 256] = kv[:, :HD]
            values[d * 256 : (d + 1) * 256] = kv[:, HD:]
            keys_t[:, d * 256 : (d + 1) * 256] = kv[:, :HD].T
        grad_key[...] = jnp.zeros_like(grad_key)
        grad_value[...] = jnp.zeros_like(grad_value)

    for member in range(2):
        columns = slice(member * HD, (member + 1) * HD)
        q = query[:, columns]
        up = jnp.concatenate([up_own[:, columns], up_other[:, columns]], axis=0)
        scores = dot_nt(keys[...], q) * LOG2_SCALE + bias[...]
        top = jnp.max(scores, axis=0, keepdims=True)
        powers = jnp.exp2(scores - top)
        probs = powers * (1.0 / jnp.sum(powers, axis=0, keepdims=True))
        probs_low = probs.astype(BF)
        grad_probs = dot_nt(values[...], up)
        delta = jnp.sum(probs_low.astype(F32) * grad_probs, axis=0, keepdims=True)
        grad_scores = (probs * (grad_probs - delta)).astype(BF)
        grad_value[...] += dot(probs_low, up)
        grad_key[...] += dot(grad_scores, q)
        grad_query[:, columns] = (dot(keys_t[...], grad_scores) * SCALE).T.astype(BF)

    @pl.when(step == pl.num_programs(0) - 1)
    def _():
        for d, out in enumerate((out0, out1, out2, out3)):
            rows = slice(d * 256, (d + 1) * 256)
            out[:, :HD] = (grad_key[rows] * SCALE).astype(out.dtype)
            out[:, HD:] = grad_value[rows].astype(out.dtype)


def attention(place, query, up_own, up_other, kvs, bias):
    blocks = GF // 256
    fixed = pl.BlockSpec((256, 256), lambda i, p: (0, 0))
    return pl.pallas_call(
        attention_kernel,
        grid_spec=pltpu.PrefetchScalarGridSpec(
            num_scalar_prefetch=1,
            grid=(blocks,),
            in_specs=[
                pl.BlockSpec((256, 256), lambda i, p: (0, i)),
                pl.BlockSpec((TILE, 256), lambda i, p: (0, p[1] * blocks + i)),
                pl.BlockSpec((TILE, 256), lambda i, p: (0, p[1] * blocks + i)),
                fixed, fixed, fixed, fixed,
                pl.BlockSpec((KEYS, 256), lambda i, p: (0, 0)),
            ],
            out_specs=[pl.BlockSpec((256, 256), lambda i, p: (0, i)), fixed, fixed, fixed, fixed],
            scratch_shapes=[
                pltpu.VMEM((KEYS, HD), BF),
                pltpu.VMEM((KEYS, HD), BF),
                pltpu.VMEM((HD, KEYS), BF),
                pltpu.VMEM((KEYS, HD), F32),
                pltpu.VMEM((KEYS, HD), F32),
            ],
        ),
        out_shape=[
            jax.ShapeDtypeStruct((256, GF), BF),
            jax.ShapeDtypeStruct((256, 256), F32),
            jax.ShapeDtypeStruct((256, 256), BF),
            jax.ShapeDtypeStruct((256, 256), BF),
            jax.ShapeDtypeStruct((256, 256), BF),
        ],
        compiler_params=PARAMS,
        cost_estimate=cost(10 * GROUP * 256 * KEYS * HD * 2, 4 << 20, GROUP * 256 * KEYS),
        name="attention",
    )(place, query, up_own, up_other, *kvs, bias)


def sum_kernel(a, b, c, d, out):
    total = (a[...] + b[...].astype(F32)) + (c[...].astype(F32) + d[...].astype(F32))
    out[...] = total.astype(out.dtype)


def sum_four(a, b, c, d):
    return pl.pallas_call(
        sum_kernel,
        in_specs=[WHOLE] * 4,
        out_specs=WHOLE,
        out_shape=jax.ShapeDtypeStruct(a.shape, BF),
        compiler_params=PARAMS,
        cost_estimate=cost(4 * a.size, 12 * a.size),
        name="sum_four",
    )(a, b, c, d)


def pack_kernel(place, dq, dq_other, dkv, dkv_other, out0, out1, out2, out3, blocks):
    core = place[1]

    def swapped(ref, columns):
        return jnp.concatenate([ref[TILE:, columns], ref[:TILE, columns]], axis=0)

    middle = slice(256, 512)

    @pl.when(core == 0)
    def _():
        blocks[0] = dq[:, 0:256]
        blocks[1] = dq[:, 512:768]
        blocks[2] = swapped(dq_other, middle)
        blocks[3, :, :HD] = dkv[:, :HD]
        blocks[3, :, HD:] = swapped(dkv_other, slice(0, HD))

    @pl.when(core == 1)
    def _():
        blocks[0] = swapped(dq_other, middle)
        blocks[1] = dq[:, 0:256]
        blocks[2] = dq[:, 512:768]
        blocks[3, :, :HD] = swapped(dkv_other, slice(HD, 2 * HD))
        blocks[3, :, HD:] = dkv[:, HD:]

    for d, out in enumerate((out0, out1, out2, out3)):
        out[...] = blocks[lax.rem(place[0] + d, CHIPS)]


def pack(place, dq, dq_other, dkv, dkv_other):
    return pl.pallas_call(
        pack_kernel,
        in_specs=[pl.BlockSpec(memory_space=pltpu.SMEM)] + [WHOLE] * 4,
        out_specs=[WHOLE] * 4,
        out_shape=[jax.ShapeDtypeStruct((256, 256), BF)] * 4,
        scratch_shapes=[pltpu.VMEM((4, 256, 256), BF)],
        compiler_params=PARAMS,
        cost_estimate=cost(0, 4 << 19),
        name="pack",
    )(place, dq, dq_other, dkv, dkv_other)


def transpose_kernel(*refs):
    out = refs[-1]
    for i, ref in enumerate(refs[:-1]):
        out[:, i * TILE : (i + 1) * TILE] = ref[...].T


def transpose(parts):
    return pl.pallas_call(
        transpose_kernel,
        in_specs=[WHOLE] * 8,
        out_specs=WHOLE,
        out_shape=jax.ShapeDtypeStruct((D, KEYS), BF),
        compiler_params=PARAMS,
        cost_estimate=cost(0, 4 * D * KEYS),
        name="transpose_tokens",
    )(*parts)


def weight_kernel(place, tokens_t, a, b, c, d, out0, out1, out2, out3):
    right = jnp.concatenate([a[...], b[...], c[...], d[...]], axis=0)
    for shift, out in enumerate((out0, out1, out2, out3)):
        row = pl.multiple_of(lax.rem(place[2] + shift, YS) * (D // YS), 128)
        out[...] = dot(tokens_t[pl.ds(row, D // YS)], right).astype(out.dtype)


def weight_grad(place, tokens_t, parts):
    shape = (D // YS, 256)
    return pl.pallas_call(
        weight_kernel,
        in_specs=[pl.BlockSpec(memory_space=pltpu.SMEM)] + [WHOLE] * 5,
        out_specs=[WHOLE] * 4,
        out_shape=[jax.ShapeDtypeStruct(shape, F32)] + [jax.ShapeDtypeStruct(shape, BF)] * 3,
        compiler_params=PARAMS,
        cost_estimate=cost(2 * D * KEYS * 256, 2 * D * KEYS + 3 * D * 256),
        name="weight_grad",
    )(place, tokens_t, *parts)


def input_kernel(place, dq, dq_other, dkv, dkv_other, w_query, w_key, w_value, out, left):
    core = place[1]

    @pl.when(pl.program_id(0) == 0)
    def _():
        mine = pl.ds(pl.multiple_of(core * GF, 128), GF)
        theirs = pl.ds(pl.multiple_of((1 - core) * GF, 128), GF)
        left[:, mine] = dq[:TILE]
        left[:, theirs] = dq_other[TILE:]
        for part in range(2):
            columns = slice(part * HD, (part + 1) * HD)
            base = D + part * KVH * HD
            left[:, pl.ds(pl.multiple_of(base + core * HD, 128), HD)] = dkv[:TILE, columns]
            left[:, pl.ds(pl.multiple_of(base + (1 - core) * HD, 128), HD)] = dkv_other[
                TILE:, columns
            ]

    total = dot_nt(left[:, :D], w_query[...])
    total += dot_nt(left[:, D : D + 256], w_key[...])
    total += dot_nt(left[:, D + 256 :], w_value[...])
    out[...] = total.astype(BF)


def input_grad(place, dq, dq_other, dkv, dkv_other, w_query, w_key, w_value):
    width = 256
    return pl.pallas_call(
        input_kernel,
        grid_spec=pltpu.PrefetchScalarGridSpec(
            num_scalar_prefetch=1,
            grid=(D // width,),
            in_specs=[
                pl.BlockSpec((256, GF), lambda i, p: (0, 0)),
                pl.BlockSpec((256, GF), lambda i, p: (0, 0)),
                pl.BlockSpec((256, 256), lambda i, p: (0, 0)),
                pl.BlockSpec((256, 256), lambda i, p: (0, 0)),
                pl.BlockSpec((width, D), lambda i, p: (i, 0)),
                pl.BlockSpec((width, 256), lambda i, p: (i, 0)),
                pl.BlockSpec((width, 256), lambda i, p: (i, 0)),
            ],
            out_specs=pl.BlockSpec((TILE, width), lambda i, p: (0, i)),
            scratch_shapes=[pltpu.VMEM((TILE, D + 512), BF)],
        ),
        out_shape=jax.ShapeDtypeStruct((TILE, D), BF),
        compiler_params=PARAMS,
        cost_estimate=cost(2 * TILE * D * 2048, 2 * D * 2048),
        name="input_grad",
    )(place, dq, dq_other, dkv, dkv_other, w_query, w_key, w_value)


def final_kernel(parts, out):
    total = parts[0:48].astype(F32)
    for z in range(1, ZS):
        total += parts[z * 48 : (z + 1) * 48].astype(F32)
    out[...] = total


def final_sum(parts):
    return pl.pallas_call(
        final_kernel,
        in_specs=[WHOLE],
        out_specs=WHOLE,
        out_shape=jax.ShapeDtypeStruct((48, 256), F32),
        compiler_params=PARAMS,
        cost_estimate=cost(parts.size, 2 * parts.size),
        name="final_sum",
    )(parts)


def shards(tokens, grad_heads, tile_mask, segments, w_query, w_key, w_value):
    ctx = lax.axis_index("ctx")
    dp = lax.axis_index("dp")
    place = jnp.stack([ctx // 2, ctx % 2, dp // ZS, dp % ZS]).astype(jnp.int32)
    own, up = tokens[0], grad_heads[0]
    other = lax.ppermute(own, "ctx", CORE)
    up_other = lax.ppermute(up, "ctx", CORE)
    mask_other = lax.ppermute(tile_mask[0], "ctx", CORE)

    kv = project_kv(place, own, other, w_key, w_value)
    kvs = [kv] + [lax.ppermute(kv, "ctx", chip_shift(d)) for d in (1, 2, 3)]
    query, bias = project_query(
        place, own, other, w_query, segments, tile_mask[0], mask_other
    )
    kvs, late_own = lax.optimization_barrier((kvs, own))
    far = [lax.ppermute(late_own, "ctx", chip_shift(d)) for d in (1, 2, 3)]

    dq, g0, g1, g2, g3 = attention(place, query, up, up_other, kvs, bias)
    dq_other = lax.ppermute(dq, "ctx", CORE)
    back = [
        lax.ppermute(g, "ctx", chip_shift(CHIPS - d)) for d, g in ((1, g1), (2, g2), (3, g3))
    ]
    dkv = sum_four(g0, *back)
    dkv_other = lax.ppermute(dkv, "ctx", CORE)

    far_other = [lax.ppermute(part, "ctx", CORE) for part in far]
    tokens_t = transpose(
        [own, other] + [part for pair in zip(far, far_other) for part in pair]
    )

    packed = pack(place, dq, dq_other, dkv, dkv_other)
    columns = [packed[0]] + [
        lax.ppermute(packed[d], "ctx", chip_shift(d)) for d in (1, 2, 3)
    ]
    terms = weight_grad(place, tokens_t, columns)
    y_parts = [terms[0]] + [lax.ppermute(terms[d], "dp", y_shift(d)) for d in (1, 2, 3)]
    y_sum = sum_four(*y_parts)
    z_parts = lax.all_to_all(y_sum, "dp", 0, 0, tiled=True, axis_index_groups=Z_GROUPS)
    grad_projection = final_sum(z_parts)

    grad_tokens = input_grad(
        place, dq, dq_other, dkv, dkv_other, w_query, w_key, w_value
    )
    return grad_tokens[None], grad_projection


def solution(mesh):
    return jax.shard_map(
        shards,
        mesh=mesh,
        in_specs=(
            P("dp", "ctx", None),
            P("dp", "ctx", None),
            P("dp", "ctx", None),
            P("dp", None),
            P(),
            P(),
            P(),
        ),
        out_specs=(P("dp", "ctx", None), P("dp", "ctx")),
        check_vma=False,
    )
```

time: 415 us -> 100 us (0.24)
  waiting for transfers between devices: 312 us -> 30.5 us
  matrix products: 34.1 us -> 0 us
  starting transfers between devices: 0.34 us -> 32.2 us
  Pallas kernels: 0 us -> 29.5 us
  blocking collectives: 26.5 us -> 0 us
  local copies, waits for them, and re-layouts: 21 us -> 5.51 us
  between operations: 14.1 us -> 0.75 us
  other arithmetic: 5.73 us -> 0.08 us
    unnamed x7 -> x0, waiting for transfers between devices: 280 us -> none
    reduce_scatter x1 -> x0, waiting for transfers between devices: 31.6 us -> none  [shards(): lax.psum_scatter(row_block, 'ctx', scatter_dimension=1, tiled=True)]
    pallas_call x0 -> x10, Pallas kernels: none -> 29.5 us  [the longest x1 9.32 us: attention(): pl.pallas_call(attention_kernel, grid_spec=pltpu.PrefetchScalarGridSpec(n...]
    ppermute x0 -> x23, waiting for transfers between devices: none -> 27.5 us  [the longest x3 12.6 us: shards(): lax.ppermute(g, 'ctx', chip_shift(CHIPS - d))]
    dot_general x15 -> x0, matrix products: 26.8 us -> none  [the longest x1 4.43 us: shards(): lax.dot_general(inputs, stacked, (((0,), (0,)), ((), ())), preferred_elem...]
    all_gather x2 -> x0, blocking collectives: 26.5 us -> none  [the longest x1 13.5 us: shards(): lax.all_gather(values, 'ctx', axis=0, tiled=True)]
    ppermute x0 -> x23, starting transfers between devices: none -> 23.7 us  [the longest x3 5.6 us: shards(): lax.ppermute(g, 'ctx', chip_shift(CHIPS - d))]
    unnamed x48 -> x16, local copies, waits for them, and re-layouts: 19.2 us -> 5.51 us
  transfers between devices with their start and end apart: 4 -> 24, of which waited for: 4 -> 13; matrix products, arithmetic and copies ran while one was open for 4% -> 0% of each run, Pallas kernels for 0% -> 27%
where the time goes in v1:
time: 100 us; the launch traced here: 98.4 us
  starting transfers between devices  32.2 us (32%)
  waiting for transfers between devices  30.5 us (30%)
  Pallas kernels  29.5 us (30%)
  local copies, waits for them, and re-layouts  5.51 us (6%)
    ppermute x3, waiting for transfers between devices, shards(): lax.ppermute(g, 'ctx', chip_shift(CHIPS - d))  12.6 us
    pallas_call x1, Pallas kernels, attention(): pl.pallas_call(attention_kernel, grid_spec=pltpu.PrefetchScalarGridSpec(n...  9.32 us
    all_to_all x1, starting transfers between devices, shards(): lax.all_to_all(y_sum, 'dp', 0, 0, tiled=True, axis_index_groups=Z_GROUPS)  8.47 us
    ppermute x3, waiting for transfers between devices, shards(): lax.ppermute(terms[d], 'dp', y_shift(d))  7.21 us
    pallas_call x1, Pallas kernels, input_grad(): pl.pallas_call(input_kernel, grid_spec=pltpu.PrefetchScalarGridSpec(num_s...  6.86 us
    ppermute x3, starting transfers between devices, shards(): lax.ppermute(g, 'ctx', chip_shift(CHIPS - d))  5.6 us
    unnamed x16, local copies, waits for them, and re-layouts  5.51 us
    ppermute x3, starting transfers between devices, shards(): lax.ppermute(terms[d], 'dp', y_shift(d))  5.01 us
  transfers between devices with their start and end apart: 24, of which 13 were waited for; matrix products, arithmetic and copies ran while one was open for 0% of the time, Pallas kernels for 27%

profile of v1, /device:TPU:8, one launch (start us, length us, event | category | flops | bytes accessed | tf_op | source)
XLA Modules:
  0.0 98.4 jit_solution(16341377211266898171)
XLA Ops:
  0.6 0.1 collective-permute-start
  0.7 0.5 collective-permute-start.2
  1.2 0.1 pad_add_fusion.place
  1.3 1.3 %collective-permute-done.other.refs_1_ = bf16[128,1536]{1,0:T(8,128)(2,1)S(1)} collective-permute-done((bf16[128,1536]{1,0:T(8,128)(2,1)}, bf16[128,1536]{1,0:T(8,128)(2,1)S(1)}, u32[]{:S(2)}, u32[]{:S(2)}) %collective-permute-start) | collective-permute-done | bytes 393248 | tf_op jit(solution)/shard_map/ppermute | solution.py:403
  2.7 1.1 %copy-done.1 = bf16[1536,256]{1,0:T(8,128)(2,1)S(1)} copy-done((bf16[1536,256]{1,0:T(8,128)(2,1)S(1)}, bf16[1536,256]{1,0:T(8,128)(2,1)}, u32[]{:S(2)}) %copy-start.1) | copy-done | bytes 786456
  3.8 1.1 %copy-done.3 = bf16[1536,256]{1,0:T(8,128)(2,1)S(1)} copy-done((bf16[1536,256]{1,0:T(8,128)(2,1)S(1)}, bf16[1536,256]{1,0:T(8,128)(2,1)}, u32[]{:S(2)}) %copy-start.3) | copy-done | bytes 786456
  4.9 1.9 %project_kv.1.kv0 = bf16[256,256]{1,0:T(8,128)(2,1)S(1)} custom-call(s32[4]{0:T(128)S(1)} %pad_add_fusion.place, bf16[128,1536]{1,0:T(8,128)(2,1)} %bitcast.4.own.refs_0_, bf16[128,1536]{1,0:T(8,128)(2,1)S(1)} %collective-permute-done.other.refs_1_, bf16[1536,256]{1,0:T(8,128)(2,1)S(1)} %copy-done.1, bf16[1536,256]{1,0:T(8,128)(2,1)S(1)} %copy-done.3), custom_call_target="tpu_custom_call" | custom-call | flops 201326592 | bytes 1572864 | tf_op jit(solution)/shard_map/project_kv/pallas_call | solution.py:68
  6.8 2.8 %collective-permute-start.5 = (bf16[256,256]{1,0:T(8,128)(2,1)S(1)}, bf16[256,256]{1,0:T(8,128)(2,1)S(1)}, u32[]{:S(2)}, u32[]{:S(2)}) collective-permute-start(bf16[256,256]{1,0:T(8,128)(2,1)S(1)} %project_kv.1.kv0), channel_id=1, source_target_pairs={{0,192},{32,224},{64,0},{96,32},{128,64},{160,96},{192,128},{224,1... | collective-permute-start | bytes 393224 | tf_op jit(solution)/shard_map/ppermute | solution.py:408
  9.7 0.8 collective-permute-start.4
  10.5 0.9 collective-permute-start.3
  11.4 0.0 collective-permute-start.1
  11.4 1.3 %collective-permute-done.1.mask_other = s32[1,8]{1,0:T(1,128)S(1)} collective-permute-done((s32[1,8]{1,0:T(1,128)}, s32[1,8]{1,0:T(1,128)S(1)}, u32[]{:S(2)}, u32[]{:S(2)}) %collective-permute-start.1) | collective-permute-done | bytes 64 | tf_op jit(solution)/shard_map/ppermute | solution.py:405
  12.6 0.7 copy-done.5
  13.3 0.7 copy-done.6
  14.0 4.1 %project_query.1 = (bf16[256,768]{1,0:T(8,128)(2,1)S(1)}, f32[1024,256]{1,0:T(8,128)S(1)}) custom-call(s32[4]{0:T(128)S(1)} %pad_add_fusion.place, bf16[128,1536]{1,0:T(8,128)(2,1)} %bitcast.4.own.refs_0_, bf16[128,1536]{1,0:T(8,128)(2,1)S(1)} %collective-permute-done.other.refs_1_, bf16[1536,1536]{1,0:T(8,128)(2,1)} %w_query.3, s32[1,1024]{1,0:T(1,128)S(1)} %copy-done.5, ...), custom_call_target="tpu_custom_call" | custom-call | flops 603979776 | bytes 3538944 | tf_op jit(solution)/shard_map/project_query/pallas_call | solution.py:129
  18.1 0.0 collective-permute-done.5.kv3
  18.1 0.0 collective-permute-done.4.kv2
  18.1 1.2 %collective-permute-done.3.kv1 = bf16[256,256]{1,0:T(8,128)(2,1)S(1)} collective-permute-done((bf16[256,256]{1,0:T(8,128)(2,1)S(1)}, bf16[256,256]{1,0:T(8,128)(2,1)S(1)}, u32[]{:S(2)}, u32[]{:S(2)}) %collective-permute-start.3) | collective-permute-done | bytes 131104 | tf_op jit(solution)/shard_map/ppermute | solution.py:408
  19.2 1.3 %collective-permute-start.15 = (bf16[128,1536]{1,0:T(8,128)(2,1)}, bf16[128,1536]{1,0:T(8,128)(2,1)S(1)}, u32[]{:S(2)}, u32[]{:S(2)}) collective-permute-start(bf16[128,1536]{1,0:T(8,128)(2,1)} %bitcast.4.own.refs_0_), channel_id=1, source_target_pairs={{0,192},{32,224},{64,0},{96,32},{128,64},{160,96},{192,128},{224,1... | collective-permute-start | bytes 1179656 | tf_op jit(solution)/shard_map/ppermute | solution.py:413
  20.5 1.6 %collective-permute-start.13 = (bf16[128,1536]{1,0:T(8,128)(2,1)}, bf16[128,1536]{1,0:T(8,128)(2,1)S(1)}, u32[]{:S(2)}, u32[]{:S(2)}) collective-permute-start(bf16[128,1536]{1,0:T(8,128)(2,1)} %bitcast.4.own.refs_0_), channel_id=1, source_target_pairs={{0,128},{32,160},{64,192},{96,224},{128,0},{160,32},{192,64},{224,... | collective-permute-start | bytes 1179656 | tf_op jit(solution)/shard_map/ppermute | solution.py:413
  22.1 0.0 collective-permute-start.11
  22.1 0.0 collective-permute-done.2.up_other
  22.1 9.3 %attention.1 = (bf16[256,768]{1,0:T(8,128)(2,1)S(1)}, f32[256,256]{1,0:T(8,128)S(1)}, bf16[256,256]{1,0:T(8,128)(2,1)S(1)}, bf16[256,256]{1,0:T(8,128)(2,1)S(1)}, bf16[256,256]{1,0:T(8,128)(2,1)S(1)}) custom-call(s32[4]{0:T(128)S(1)} %pad_add_fusion.place, bf16[256,768]{1,0:T(8,128)(2,1)S(1)} %get-tuple-element.22.query, bf16[128,1536]{1,0:T(8,128)(2,1)S(1)} %bitcast.14, ...), custom_call_target="tpu_custom_call" | custom-call | flops 4026531840 | bytes 4194304 | tf_op jit(solution)/shard_map/attention/pallas_call | solution.py:200
  31.4 3.3 %collective-permute-start.7 = (bf16[256,256]{1,0:T(8,128)(2,1)S(1)}, bf16[256,256]{1,0:T(8,128)(2,1)S(1)}, u32[]{:S(2)}, u32[]{:S(2)}) collective-permute-start(bf16[256,256]{1,0:T(8,128)(2,1)S(1)} %get-tuple-element.30), channel_id=1, source_target_pairs={{0,192},{32,224},{64,0},{96,32},{128,64},{160,96},{192,128},{224,1... | collective-permute-start | bytes 393224 | tf_op jit(solution)/shard_map/ppermute | solution.py:418
  34.7 0.8 collective-permute-start.8
  35.5 7.2 %collective-permute-done.7.b = bf16[256,256]{1,0:T(8,128)(2,1)S(1)} collective-permute-done((bf16[256,256]{1,0:T(8,128)(2,1)S(1)}, bf16[256,256]{1,0:T(8,128)(2,1)S(1)}, u32[]{:S(2)}, u32[]{:S(2)}) %collective-permute-start.7) | collective-permute-done | bytes 131104 | tf_op jit(solution)/shard_map/ppermute | solution.py:418
  42.7 0.0 collective-permute-start.6
  42.7 0.0 collective-permute-done.15.refs_6_
  42.7 0.5 collective-permute-start.16
  43.2 1.2 %collective-permute-done.8.c = bf16[256,256]{1,0:T(8,128)(2,1)S(1)} collective-permute-done((bf16[256,256]{1,0:T(8,128)(2,1)S(1)}, bf16[256,256]{1,0:T(8,128)(2,1)S(1)}, u32[]{:S(2)}, u32[]{:S(2)}) %collective-permute-start.8) | collective-permute-done | bytes 131104 | tf_op jit(solution)/shard_map/ppermute | solution.py:418
  44.5 1.5 %collective-permute-start.9 = (bf16[256,256]{1,0:T(8,128)(2,1)S(1)}, bf16[256,256]{1,0:T(8,128)(2,1)S(1)}, u32[]{:S(2)}, u32[]{:S(2)}) collective-permute-start(bf16[256,256]{1,0:T(8,128)(2,1)S(1)} %get-tuple-element.32), channel_id=1, source_target_pairs={{0,64},{32,96},{64,128},{96,160},{128,192},{160,224},{192,0},{224,... | collective-permute-start | bytes 393224 | tf_op jit(solution)/shard_map/ppermute | solution.py:418
  46.0 0.0 collective-permute-done.13.refs_4_
  46.0 0.0 collective-permute-start.14
  46.0 0.0 collective-permute-done.11.refs_2_
  46.0 0.5 collective-permute-start.12
  46.5 4.1 %collective-permute-done.9.d = bf16[256,256]{1,0:T(8,128)(2,1)S(1)} collective-permute-done((bf16[256,256]{1,0:T(8,128)(2,1)S(1)}, bf16[256,256]{1,0:T(8,128)(2,1)S(1)}, u32[]{:S(2)}, u32[]{:S(2)}) %collective-permute-start.9) | collective-permute-done | bytes 131104 | tf_op jit(solution)/shard_map/ppermute | solution.py:418
  50.6 0.1 sum_four.2.dkv
  50.7 0.1 collective-permute-start.10
  50.8 1.3 %collective-permute-done.10.dkv_other = bf16[256,256]{1,0:T(8,128)(2,1)S(1)} collective-permute-done((bf16[256,256]{1,0:T(8,128)(2,1)S(1)}, bf16[256,256]{1,0:T(8,128)(2,1)S(1)}, u32[]{:S(2)}, u32[]{:S(2)}) %collective-permute-start.10) | collective-permute-done | bytes 131104 | tf_op jit(solution)/shard_map/ppermute | solution.py:421
  52.1 0.0 collective-permute-done.6.dq_other
  52.1 0.6 pack.1
  52.8 1.1 %collective-permute-start.17 = (bf16[256,256]{1,0:T(8,128)(2,1)S(1)}, bf16[256,256]{1,0:T(8,128)(2,1)S(1)}, u32[]{:S(2)}, u32[]{:S(2)}) collective-permute-start(bf16[256,256]{1,0:T(8,128)(2,1)S(1)} %get-tuple-element.35), channel_id=1, source_target_pairs={{0,64},{32,96},{64,128},{96,160},{128,192},{160,224},{192,0},{224,... | collective-permute-start | bytes 393224 | tf_op jit(solution)/shard_map/ppermute | solution.py:430
  53.9 2.0 %collective-permute-start.18 = (bf16[256,256]{1,0:T(8,128)(2,1)S(1)}, bf16[256,256]{1,0:T(8,128)(2,1)S(1)}, u32[]{:S(2)}, u32[]{:S(2)}) collective-permute-start(bf16[256,256]{1,0:T(8,128)(2,1)S(1)} %get-tuple-element.36), channel_id=1, source_target_pairs={{0,128},{32,160},{64,192},{96,224},{128,0},{160,32},{192,64},{224,... | collective-permute-start | bytes 393224 | tf_op jit(solution)/shard_map/ppermute | solution.py:430
  55.9 0.0 collective-permute-done.16.refs_7_
  55.9 0.9 collective-permute-start.19
  56.8 0.0 collective-permute-done.14.refs_5_
  56.9 0.0 collective-permute-done.12.refs_3_
  56.9 3.6 %transpose_tokens.1.tokens_t = bf16[1536,1024]{1,0:T(8,128)(2,1)} custom-call(bf16[128,1536]{1,0:T(8,128)(2,1)} %bitcast.4.own.refs_0_, bf16[128,1536]{1,0:T(8,128)(2,1)S(1)} %collective-permute-done.other.refs_1_, bf16[128,1536]{1,0:T(8,128)(2,1)S(1)} %collective-permute-done.11.refs_2_, bf16[128,1536]{1,0:T(8,128)(2,1)S(1)} %collective-permute-done.12.refs_3_, ...), custom_call_target="tpu_custom_call" | custom-call | bytes 6291456 | tf_op jit(solution)/shard_map/transpose_tokens/pallas_call | solution.py:299
  60.5 2.0 %collective-permute-done.17.b = bf16[256,256]{1,0:T(8,128)(2,1)S(1)} collective-permute-done((bf16[256,256]{1,0:T(8,128)(2,1)S(1)}, bf16[256,256]{1,0:T(8,128)(2,1)S(1)}, u32[]{:S(2)}, u32[]{:S(2)}) %collective-permute-start.17) | collective-permute-done | bytes 131104 | tf_op jit(solution)/shard_map/ppermute | solution.py:430
  62.4 0.0 collective-permute-done.18.c
  62.4 0.6 collective-permute-done.19.d
  63.0 1.9 %copy-done = bf16[1536,1024]{1,0:T(8,128)(2,1)S(1)} copy-done((bf16[1536,1024]{1,0:T(8,128)(2,1)S(1)}, bf16[1536,1024]{1,0:T(8,128)(2,1)}, u32[]{:S(2)}) %copy-start) | copy-done | bytes 3145752
  64.9 1.5 %weight_grad.1 = (f32[384,256]{1,0:T(8,128)S(1)}, bf16[384,256]{1,0:T(8,128)(2,1)S(1)}, bf16[384,256]{1,0:T(8,128)(2,1)S(1)}, bf16[384,256]{1,0:T(8,128)(2,1)S(1)}) custom-call(s32[4]{0:T(128)S(1)} %pad_add_fusion.place, bf16[1536,1024]{1,0:T(8,128)(2,1)S(1)} %copy-done, bf16[256,256]{1,0:T(8,128)(2,1)S(1)} %get-tuple-element.34.a, ...), custom_call_target="tpu_custom_call" | custom-call | flops 805306368 | bytes 4325376 | tf_op jit(solution)/shard_map/weight_grad/pallas_call | solution.py:319
  66.4 1.7 %collective-permute-start.20 = (bf16[384,256]{1,0:T(8,128)(2,1)S(1)}, bf16[384,256]{1,0:T(8,128)(2,1)S(1)}, u32[]{:S(2)}, u32[]{:S(2)}) collective-permute-start(bf16[384,256]{1,0:T(8,128)(2,1)S(1)} %get-tuple-element.39), channel_id=1, source_target_pairs={{0,8},{1,9},{2,10},{3,11},{4,12},{5,13},{6,14},{7,15},{8,16},{9,17... | collective-permute-start | bytes 589832 | tf_op jit(solution)/shard_map/ppermute | solution.py:433
  68.1 0.9 collective-permute-start.21
  69.0 2.4 %collective-permute-start.22 = (bf16[384,256]{1,0:T(8,128)(2,1)S(1)}, bf16[384,256]{1,0:T(8,128)(2,1)S(1)}, u32[]{:S(2)}, u32[]{:S(2)}) collective-permute-start(bf16[384,256]{1,0:T(8,128)(2,1)S(1)} %get-tuple-element.41), channel_id=1, source_target_pairs={{0,24},{1,25},{2,26},{3,27},{4,28},{5,29},{6,30},{7,31},{8,0},{9,1... | collective-permute-start | bytes 589832 | tf_op jit(solution)/shard_map/ppermute | solution.py:433
  71.4 2.5 %collective-permute-done.20.b = bf16[384,256]{1,0:T(8,128)(2,1)S(1)} collective-permute-done((bf16[384,256]{1,0:T(8,128)(2,1)S(1)}, bf16[384,256]{1,0:T(8,128)(2,1)S(1)}, u32[]{:S(2)}, u32[]{:S(2)}) %collective-permute-start.20) | collective-permute-done | bytes 196640 | tf_op jit(solution)/shard_map/ppermute | solution.py:433
  73.9 3.3 %collective-permute-done.21.c = bf16[384,256]{1,0:T(8,128)(2,1)S(1)} collective-permute-done((bf16[384,256]{1,0:T(8,128)(2,1)S(1)}, bf16[384,256]{1,0:T(8,128)(2,1)S(1)}, u32[]{:S(2)}, u32[]{:S(2)}) %collective-permute-start.21) | collective-permute-done | bytes 196640 | tf_op jit(solution)/shard_map/ppermute | solution.py:433
  77.3 1.4 %collective-permute-done.22.d = bf16[384,256]{1,0:T(8,128)(2,1)S(1)} collective-permute-done((bf16[384,256]{1,0:T(8,128)(2,1)S(1)}, bf16[384,256]{1,0:T(8,128)(2,1)S(1)}, u32[]{:S(2)}, u32[]{:S(2)}) %collective-permute-start.22) | collective-permute-done | bytes 196640 | tf_op jit(solution)/shard_map/ppermute | solution.py:433
  78.7 0.8 sum_four.3
  79.4 8.5 %all-to-all-start = ((bf16[8,48,256]{2,1,0:T(8,128)(2,1)}), bf16[8,48,256]{2,1,0:T(8,128)(2,1)S(1)}, u32[]{:S(2)}, u32[]{:S(2)}) async-start(bf16[8,48,256]{2,1,0:T(8,128)(2,1)} %bitcast.8), calls=%async_computation | async-start | bytes 393216 | tf_op jit(solution)/shard_map/all_to_all | solution.py:435
  87.9 6.9 %input_grad.1 = bf16[128,1536]{1,0:T(8,128)(2,1)} custom-call(s32[4]{0:T(128)S(1)} %pad_add_fusion.place, bf16[256,768]{1,0:T(8,128)(2,1)S(1)} %get-tuple-element.28.dq, bf16[256,768]{1,0:T(8,128)(2,1)S(1)} %collective-permute-done.6.dq_other, bf16[256,256]{1,0:T(8,128)(2,1)S(1)} %sum_four.2.dkv, bf16[256,256]{1,0:T(8,128)(2,1)S(1)} %collective-permute-done.10.dkv_other, ...), custom_call_target="tpu_custom_call" | custom-call | flops 805306368 | bytes 6291456 | tf_op jit(solution)/shard_map/input_grad/pallas_call | solution.py:355
  94.8 3.0 %all-to-all-done = bf16[8,48,256]{2,1,0:T(8,128)(2,1)S(1)} async-done(((bf16[8,48,256]{2,1,0:T(8,128)(2,1)}), bf16[8,48,256]{2,1,0:T(8,128)(2,1)S(1)}, u32[]{:S(2)}, u32[]{:S(2)}) %all-to-all-start) | async-done | bytes 196640 | tf_op jit(solution)/shard_map/all_to_all | solution.py:435
  97.8 0.6 final_sum.1
  (11 shorter events, 0.0 us)
Async XLA Ops:
  0.6 2.0 %collective-permute-start = (bf16[128,1536]{1,0:T(8,128)(2,1)}, bf16[128,1536]{1,0:T(8,128)(2,1)S(1)}, u32[]{:S(2)}, u32[]{:S(2)}) collective-permute-start(bf16[128,1536]{1,0:T(8,128)(2,1)} %bitcast.4.own.refs_0_), channel_id=1, source_target_pairs={{0,32},{32,0},{64,96},{96,64},{128,160},{160,128},{192,224},{224,1... | collective-permute-start | bytes 1179656 | tf_op jit(solution)/shard_map/ppermute | solution.py:403
  0.7 21.3 %collective-permute-start.2 = (bf16[128,1536]{1,0:T(8,128)(2,1)}, bf16[128,1536]{1,0:T(8,128)(2,1)S(1)}, u32[]{:S(2)}, u32[]{:S(2)}) collective-permute-start(bf16[128,1536]{1,0:T(8,128)(2,1)} %bitcast.13), channel_id=1, source_target_pairs={{0,32},{32,0},{64,96},{96,64},{128,160},{160,128},{192,224},{224,1... | collective-permute-start | bytes 1179656 | tf_op jit(solution)/shard_map/ppermute | solution.py:404
  2.6 1.1 %copy-start.1 = (bf16[1536,256]{1,0:T(8,128)(2,1)S(1)}, bf16[1536,256]{1,0:T(8,128)(2,1)}, u32[]{:S(2)}) copy-start(bf16[1536,256]{1,0:T(8,128)(2,1)} %w_key.3) | copy-start | bytes 2359300
  3.8 1.1 %copy-start.3 = (bf16[1536,256]{1,0:T(8,128)(2,1)S(1)}, bf16[1536,256]{1,0:T(8,128)(2,1)}, u32[]{:S(2)}) copy-start(bf16[1536,256]{1,0:T(8,128)(2,1)} %w_value.3) | copy-start | bytes 2359300
  4.9 17.2 %copy-start.7 = (bf16[1,128,1536]{2,1,0:T(8,128)(2,1)S(1)}, bf16[1,128,1536]{2,1,0:T(8,128)(2,1)}, u32[]{:S(2)}) copy-start(bf16[1,128,1536]{2,1,0:T(8,128)(2,1)} %param.8) | copy-start | bytes 1179652
  6.8 11.2 %collective-permute-start.5 = (bf16[256,256]{1,0:T(8,128)(2,1)S(1)}, bf16[256,256]{1,0:T(8,128)(2,1)S(1)}, u32[]{:S(2)}, u32[]{:S(2)}) collective-permute-start(bf16[256,256]{1,0:T(8,128)(2,1)S(1)} %project_kv.1.kv0), channel_id=1, source_target_pairs={{0,192},{32,224},{64,0},{96,32},{128,64},{160,96},{192,128},{224,1... | collective-permute-start | bytes 393224 | tf_op jit(solution)/shard_map/ppermute | solution.py:408
  9.7 8.4 %collective-permute-start.4 = (bf16[256,256]{1,0:T(8,128)(2,1)S(1)}, bf16[256,256]{1,0:T(8,128)(2,1)S(1)}, u32[]{:S(2)}, u32[]{:S(2)}) collective-permute-start(bf16[256,256]{1,0:T(8,128)(2,1)S(1)} %project_kv.1.kv0), channel_id=1, source_target_pairs={{0,128},{32,160},{64,192},{96,224},{128,0},{160,32},{192,64},{224,... | collective-permute-start | bytes 393224 | tf_op jit(solution)/shard_map/ppermute | solution.py:408
  10.5 8.8 %collective-permute-start.3 = (bf16[256,256]{1,0:T(8,128)(2,1)S(1)}, bf16[256,256]{1,0:T(8,128)(2,1)S(1)}, u32[]{:S(2)}, u32[]{:S(2)}) collective-permute-start(bf16[256,256]{1,0:T(8,128)(2,1)S(1)} %project_kv.1.kv0), channel_id=1, source_target_pairs={{0,64},{32,96},{64,128},{96,160},{128,192},{160,224},{192,0},{224,... | collective-permute-start | bytes 393224 | tf_op jit(solution)/shard_map/ppermute | solution.py:408
  11.4 1.3 %collective-permute-start.1 = (s32[1,8]{1,0:T(1,128)}, s32[1,8]{1,0:T(1,128)S(1)}, u32[]{:S(2)}, u32[]{:S(2)}) collective-permute-start(s32[1,8]{1,0:T(1,128)} %bitcast.11), channel_id=1, source_target_pairs={{0,32},{32,0},{64,96},{96,64},{128,160},{160,128},{192,224},{224,1... | collective-permute-start | bytes 104 | tf_op jit(solution)/shard_map/ppermute | solution.py:405
  12.6 0.7 copy-start.5
  13.3 0.7 copy-start.6
  19.2 23.5 %collective-permute-start.15 = (bf16[128,1536]{1,0:T(8,128)(2,1)}, bf16[128,1536]{1,0:T(8,128)(2,1)S(1)}, u32[]{:S(2)}, u32[]{:S(2)}) collective-permute-start(bf16[128,1536]{1,0:T(8,128)(2,1)} %bitcast.4.own.refs_0_), channel_id=1, source_target_pairs={{0,192},{32,224},{64,0},{96,32},{128,64},{160,96},{192,128},{224,1... | collective-permute-start | bytes 1179656 | tf_op jit(solution)/shard_map/ppermute | solution.py:413
  20.5 25.5 %collective-permute-start.13 = (bf16[128,1536]{1,0:T(8,128)(2,1)}, bf16[128,1536]{1,0:T(8,128)(2,1)S(1)}, u32[]{:S(2)}, u32[]{:S(2)}) collective-permute-start(bf16[128,1536]{1,0:T(8,128)(2,1)} %bitcast.4.own.refs_0_), channel_id=1, source_target_pairs={{0,128},{32,160},{64,192},{96,224},{128,0},{160,32},{192,64},{224,... | collective-permute-start | bytes 1179656 | tf_op jit(solution)/shard_map/ppermute | solution.py:413
  22.1 23.9 %collective-permute-start.11 = (bf16[128,1536]{1,0:T(8,128)(2,1)}, bf16[128,1536]{1,0:T(8,128)(2,1)S(1)}, u32[]{:S(2)}, u32[]{:S(2)}) collective-permute-start(bf16[128,1536]{1,0:T(8,128)(2,1)} %bitcast.4.own.refs_0_), channel_id=1, source_target_pairs={{0,64},{32,96},{64,128},{96,160},{128,192},{160,224},{192,0},{224,... | collective-permute-start | bytes 1179656 | tf_op jit(solution)/shard_map/ppermute | solution.py:413
  31.4 11.3 %collective-permute-start.7 = (bf16[256,256]{1,0:T(8,128)(2,1)S(1)}, bf16[256,256]{1,0:T(8,128)(2,1)S(1)}, u32[]{:S(2)}, u32[]{:S(2)}) collective-permute-start(bf16[256,256]{1,0:T(8,128)(2,1)S(1)} %get-tuple-element.30), channel_id=1, source_target_pairs={{0,192},{32,224},{64,0},{96,32},{128,64},{160,96},{192,128},{224,1... | collective-permute-start | bytes 393224 | tf_op jit(solution)/shard_map/ppermute | solution.py:418
  34.7 9.8 %collective-permute-start.8 = (bf16[256,256]{1,0:T(8,128)(2,1)S(1)}, bf16[256,256]{1,0:T(8,128)(2,1)S(1)}, u32[]{:S(2)}, u32[]{:S(2)}) collective-permute-start(bf16[256,256]{1,0:T(8,128)(2,1)S(1)} %get-tuple-element.31), channel_id=1, source_target_pairs={{0,128},{32,160},{64,192},{96,224},{128,0},{160,32},{192,64},{224,... | collective-permute-start | bytes 393224 | tf_op jit(solution)/shard_map/ppermute | solution.py:418
  42.7 9.4 %collective-permute-start.6 = (bf16[256,768]{1,0:T(8,128)(2,1)S(1)}, bf16[256,768]{1,0:T(8,128)(2,1)S(1)}, u32[]{:S(2)}, u32[]{:S(2)}) collective-permute-start(bf16[256,768]{1,0:T(8,128)(2,1)S(1)} %get-tuple-element.28.dq), channel_id=1, source_target_pairs={{0,32},{32,0},{64,96},{96,64},{128,160},{160,128},{192,224},{224,1... | collective-permute-start | bytes 1179656 | tf_op jit(solution)/shard_map/ppermute | solution.py:416
  42.7 13.2 %collective-permute-start.16 = (bf16[128,1536]{1,0:T(8,128)(2,1)S(1)}, bf16[128,1536]{1,0:T(8,128)(2,1)S(1)}, u32[]{:S(2)}, u32[]{:S(2)}) collective-permute-start(bf16[128,1536]{1,0:T(8,128)(2,1)S(1)} %collective-permute-done.15.refs_6_), channel_id=1, source_target_pairs={{0,32},{32,0},{64,96},{96,64},{128,160},{160,128},{192,224},{224,1... | collective-permute-start | bytes 1179656 | tf_op jit(solution)/shard_map/ppermute | solution.py:423
  44.5 6.2 %collective-permute-start.9 = (bf16[256,256]{1,0:T(8,128)(2,1)S(1)}, bf16[256,256]{1,0:T(8,128)(2,1)S(1)}, u32[]{:S(2)}, u32[]{:S(2)}) collective-permute-start(bf16[256,256]{1,0:T(8,128)(2,1)S(1)} %get-tuple-element.32), channel_id=1, source_target_pairs={{0,64},{32,96},{64,128},{96,160},{128,192},{160,224},{192,0},{224,... | collective-permute-start | bytes 393224 | tf_op jit(solution)/shard_map/ppermute | solution.py:418
  46.0 10.9 %collective-permute-start.14 = (bf16[128,1536]{1,0:T(8,128)(2,1)S(1)}, bf16[128,1536]{1,0:T(8,128)(2,1)S(1)}, u32[]{:S(2)}, u32[]{:S(2)}) collective-permute-start(bf16[128,1536]{1,0:T(8,128)(2,1)S(1)} %collective-permute-done.13.refs_4_), channel_id=1, source_target_pairs={{0,32},{32,0},{64,96},{96,64},{128,160},{160,128},{192,224},{224,1... | collective-permute-start | bytes 1179656 | tf_op jit(solution)/shard_map/ppermute | solution.py:423
  46.0 10.9 %collective-permute-start.12 = (bf16[128,1536]{1,0:T(8,128)(2,1)S(1)}, bf16[128,1536]{1,0:T(8,128)(2,1)S(1)}, u32[]{:S(2)}, u32[]{:S(2)}) collective-permute-start(bf16[128,1536]{1,0:T(8,128)(2,1)S(1)} %collective-permute-done.11.refs_2_), channel_id=1, source_target_pairs={{0,32},{32,0},{64,96},{96,64},{128,160},{160,128},{192,224},{224,1... | collective-permute-start | bytes 1179656 | tf_op jit(solution)/shard_map/ppermute | solution.py:423
  50.7 1.4 %collective-permute-start.10 = (bf16[256,256]{1,0:T(8,128)(2,1)S(1)}, bf16[256,256]{1,0:T(8,128)(2,1)S(1)}, u32[]{:S(2)}, u32[]{:S(2)}) collective-permute-start(bf16[256,256]{1,0:T(8,128)(2,1)S(1)} %sum_four.2.dkv), channel_id=1, source_target_pairs={{0,32},{32,0},{64,96},{96,64},{128,160},{160,128},{192,224},{224,1... | collective-permute-start | bytes 393224 | tf_op jit(solution)/shard_map/ppermute | solution.py:421
  52.8 9.6 %collective-permute-start.17 = (bf16[256,256]{1,0:T(8,128)(2,1)S(1)}, bf16[256,256]{1,0:T(8,128)(2,1)S(1)}, u32[]{:S(2)}, u32[]{:S(2)}) collective-permute-start(bf16[256,256]{1,0:T(8,128)(2,1)S(1)} %get-tuple-element.35), channel_id=1, source_target_pairs={{0,64},{32,96},{64,128},{96,160},{128,192},{160,224},{192,0},{224,... | collective-permute-start | bytes 393224 | tf_op jit(solution)/shard_map/ppermute | solution.py:430
  53.9 8.6 %collective-permute-start.18 = (bf16[256,256]{1,0:T(8,128)(2,1)S(1)}, bf16[256,256]{1,0:T(8,128)(2,1)S(1)}, u32[]{:S(2)}, u32[]{:S(2)}) collective-permute-start(bf16[256,256]{1,0:T(8,128)(2,1)S(1)} %get-tuple-element.36), channel_id=1, source_target_pairs={{0,128},{32,160},{64,192},{96,224},{128,0},{160,32},{192,64},{224,... | collective-permute-start | bytes 393224 | tf_op jit(solution)/shard_map/ppermute | solution.py:430
  55.9 32.0 %copy-start.2 = (bf16[1536,256]{1,0:T(8,128)(2,1)S(1)}, bf16[1536,256]{1,0:T(8,128)(2,1)}, u32[]{:S(2)}) copy-start(bf16[1536,256]{1,0:T(8,128)(2,1)} %w_key.3) | copy-start | bytes 2359300
  55.9 32.0 %copy-start.4 = (bf16[1536,256]{1,0:T(8,128)(2,1)S(1)}, bf16[1536,256]{1,0:T(8,128)(2,1)}, u32[]{:S(2)}) copy-start(bf16[1536,256]{1,0:T(8,128)(2,1)} %w_value.3) | copy-start | bytes 2359300
  55.9 7.1 %collective-permute-start.19 = (bf16[256,256]{1,0:T(8,128)(2,1)S(1)}, bf16[256,256]{1,0:T(8,128)(2,1)S(1)}, u32[]{:S(2)}, u32[]{:S(2)}) collective-permute-start(bf16[256,256]{1,0:T(8,128)(2,1)S(1)} %get-tuple-element.37), channel_id=1, source_target_pairs={{0,192},{32,224},{64,0},{96,32},{128,64},{160,96},{192,128},{224,1... | collective-permute-start | bytes 393224 | tf_op jit(solution)/shard_map/ppermute | solution.py:430
  63.0 1.9 %copy-start = (bf16[1536,1024]{1,0:T(8,128)(2,1)S(1)}, bf16[1536,1024]{1,0:T(8,128)(2,1)}, u32[]{:S(2)}) copy-start(bf16[1536,1024]{1,0:T(8,128)(2,1)} %transpose_tokens.1.tokens_t) | copy-start | bytes 9437188
  66.4 7.5 %collective-permute-start.20 = (bf16[384,256]{1,0:T(8,128)(2,1)S(1)}, bf16[384,256]{1,0:T(8,128)(2,1)S(1)}, u32[]{:S(2)}, u32[]{:S(2)}) collective-permute-start(bf16[384,256]{1,0:T(8,128)(2,1)S(1)} %get-tuple-element.39), channel_id=1, source_target_pairs={{0,8},{1,9},{2,10},{3,11},{4,12},{5,13},{6,14},{7,15},{8,16},{9,17... | collective-permute-start | bytes 589832 | tf_op jit(solution)/shard_map/ppermute | solution.py:433
  68.1 9.2 %collective-permute-start.21 = (bf16[384,256]{1,0:T(8,128)(2,1)S(1)}, bf16[384,256]{1,0:T(8,128)(2,1)S(1)}, u32[]{:S(2)}, u32[]{:S(2)}) collective-permute-start(bf16[384,256]{1,0:T(8,128)(2,1)S(1)} %get-tuple-element.40), channel_id=1, source_target_pairs={{0,16},{1,17},{2,18},{3,19},{4,20},{5,21},{6,22},{7,23},{8,24},{9,... | collective-permute-start | bytes 589832 | tf_op jit(solution)/shard_map/ppermute | solution.py:433
  69.0 9.6 %collective-permute-start.22 = (bf16[384,256]{1,0:T(8,128)(2,1)S(1)}, bf16[384,256]{1,0:T(8,128)(2,1)S(1)}, u32[]{:S(2)}, u32[]{:S(2)}) collective-permute-start(bf16[384,256]{1,0:T(8,128)(2,1)S(1)} %get-tuple-element.41), channel_id=1, source_target_pairs={{0,24},{1,25},{2,26},{3,27},{4,28},{5,29},{6,30},{7,31},{8,0},{9,1... | collective-permute-start | bytes 589832 | tf_op jit(solution)/shard_map/ppermute | solution.py:433
  79.4 18.4 %all-to-all-start = ((bf16[8,48,256]{2,1,0:T(8,128)(2,1)}), bf16[8,48,256]{2,1,0:T(8,128)(2,1)S(1)}, u32[]{:S(2)}, u32[]{:S(2)}) async-start(bf16[8,48,256]{2,1,0:T(8,128)(2,1)} %bitcast.8), calls=%async_computation | async-start | bytes 393216 | tf_op jit(solution)/shard_map/all_to_all | solution.py:435

commit v2 on v1

--- a/solution.py
+++ b/solution.py
@@ -23,7 +23,10 @@
 LOG2_SCALE = SCALE * math.log2(math.e)
 BF = jnp.bfloat16
 F32 = jnp.float32
-VMEM_LIMIT = 48 * 1024 * 1024
+VMEM_LIMIT = 24 * 1024 * 1024
+W_CHUNKS = 4
+Q_CHUNKS = 6
+IN_CHUNKS = 6
 
 CORE = [(i, i ^ 1) for i in range(8)]
 NT = (((1,), (1,)), ((), ()))
@@ -46,6 +49,10 @@
 
 def dot_nt(a, b):
     return lax.dot_general(a, b, NT, preferred_element_type=F32)
+
+
+def in_hbm(array):
+    return pltpu.with_memory_space_constraint(array, pltpu.HBM)
 
 
 def cost(flops, bytes_accessed, transcendentals=0):
@@ -56,98 +63,126 @@
 
 PARAMS = pltpu.CompilerParams(vmem_limit_bytes=VMEM_LIMIT)
 WHOLE = pl.BlockSpec(memory_space=pltpu.VMEM)
-
-
-def kv_kernel(place, own, other, w_key, w_value, out):
-    weights = jnp.concatenate([w_key[...], w_value[...]], axis=1)
-    out[:TILE] = dot(own[...], weights).astype(BF)
-    out[TILE:] = dot(other[...], weights).astype(BF)
-
-
-def project_kv(place, own, other, w_key, w_value):
+SCALARS = pl.BlockSpec(memory_space=pltpu.SMEM)
+STAY = pl.BlockSpec(memory_space=pltpu.HBM)
+
+
+def kv_own_kernel(place, own, w_key, w_value, weights, out, rows, sems):
+    columns = pl.ds(pl.multiple_of(place[1] * HD, HD), HD)
+    copies = []
+    for chunk in range(W_CHUNKS):
+        part = pl.ds(chunk * (TILE // W_CHUNKS), TILE // W_CHUNKS)
+        copies.append(pltpu.make_async_copy(own.at[part], rows.at[part], sems.at[chunk, 2]))
+        part = pl.ds(chunk * (D // W_CHUNKS), D // W_CHUNKS)
+        for side, source in enumerate((w_key, w_value)):
+            copies.append(
+                pltpu.make_async_copy(
+                    source.at[part, columns],
+                    weights.at[part, pl.ds(side * HD, HD)],
+                    sems.at[chunk, side],
+                )
+            )
+    for copy in copies:
+        copy.start()
+    for copy in copies:
+        copy.wait()
+    out[...] = dot(rows[...], weights[...]).astype(BF)
+
+
+def project_kv_own(place, own, w_key, w_value):
+    return pl.pallas_call(
+        kv_own_kernel,
+        in_specs=[SCALARS, STAY, STAY, STAY],
+        out_specs=[WHOLE, WHOLE],
+        out_shape=[
+            jax.ShapeDtypeStruct((D, 2 * HD), BF),
+            jax.ShapeDtypeStruct((TILE, 2 * HD), BF),
+        ],
+        scratch_shapes=[pltpu.VMEM((TILE, D), BF), pltpu.SemaphoreType.DMA((W_CHUNKS, 3))],
+        compiler_params=PARAMS,
+        cost_estimate=cost(2 * TILE * D * 256, 2 * (TILE * D + D * 256)),
+        name="project_kv_own",
+    )(place, own, w_key, w_value)
+
+
+def kv_kernel(other, weights, kv_own, out):
+    out[:TILE] = kv_own[...]
+    out[TILE:] = dot(other[...], weights[...]).astype(BF)
+
+
+def project_kv(other, weights, kv_own):
     return pl.pallas_call(
         kv_kernel,
-        grid_spec=pltpu.PrefetchScalarGridSpec(
-            num_scalar_prefetch=1,
-            grid=(1,),
-            in_specs=[
-                pl.BlockSpec((TILE, D), lambda i, p: (0, 0)),
-                pl.BlockSpec((TILE, D), lambda i, p: (0, 0)),
-                pl.BlockSpec((D, HD), lambda i, p: (0, p[1])),
-                pl.BlockSpec((D, HD), lambda i, p: (0, p[1])),
-            ],
-            out_specs=pl.BlockSpec((2 * TILE, 2 * HD), lambda i, p: (0, 0)),
-        ),
+        in_specs=[WHOLE] * 3,
+        out_specs=WHOLE,
         out_shape=jax.ShapeDtypeStruct((2 * TILE, 2 * HD), BF),
         compiler_params=PARAMS,
-        cost_estimate=cost(2 * 256 * D * 256, 2 * (256 * D + D * 256)),
+        cost_estimate=cost(2 * TILE * D * 256, 2 * (TILE * D + D * 256)),
         name="project_kv",
-    )(place, own, other, w_key, w_value)
-
-
-def query_kernel(place, own, other, w_query, segments, mask_own, mask_other, out, bias):
-    out[:TILE] = dot(own[...], w_query[...]).astype(BF)
-    out[TILE:] = dot(other[...], w_query[...]).astype(BF)
-
-    @pl.when(pl.program_id(0) == 0)
-    def _():
-        chip, core = place[0], place[1]
-        passages = segments[...]
-        ends = [jnp.sum((passages <= s).astype(jnp.int32)) for s in range(3)]
-        for slot in range(2):
-            masks = mask_own if slot == 0 else mask_other
-            tile = 2 * chip + (core if slot == 0 else 1 - core)
-            mine = segments[:, pl.ds(pl.multiple_of(tile * TILE, TILE), TILE)]
-            low = jnp.where(
-                mine == 0, 0, jnp.where(mine == 1, ends[0], jnp.where(mine == 2, ends[1], ends[2]))
-            )
-            high = jnp.where(
-                mine == 0,
-                ends[0],
-                jnp.where(mine == 1, ends[1], jnp.where(mine == 2, ends[2], KEYS)),
-            )
-            for d in range(CHIPS):
-                for key_slot in range(2):
-                    key_tile = 2 * lax.rem(chip + CHIPS - d, CHIPS) + (
-                        core if key_slot == 0 else 1 - core
-                    )
-                    seen = masks[0, key_tile] == 1
-                    position = key_tile * TILE + lax.broadcasted_iota(
-                        jnp.int32, (TILE, TILE), 0
-                    )
-                    first = jnp.where(seen, 0, low)
-                    last = jnp.where(seen, KEYS, high)
-                    allowed = (position >= first) & (position < last)
-                    row = d * 2 * TILE + key_slot * TILE
-                    bias[row : row + TILE, slot * TILE : (slot + 1) * TILE] = jnp.where(
-                        allowed, 0.0, -jnp.inf
-                    )
+    )(other, weights, kv_own)
+
+
+def query_kernel(
+    place, own, other, w_query, segments, mask_own, mask_other, out, bias, weights, sems
+):
+    columns = pl.ds(pl.multiple_of(place[1] * GF, HD), GF)
+    copies = []
+    for chunk in range(Q_CHUNKS):
+        part = pl.ds(chunk * (D // Q_CHUNKS), D // Q_CHUNKS)
+        copies.append(
+            pltpu.make_async_copy(w_query.at[part, columns], weights.at[part], sems.at[chunk])
+        )
+    for copy in copies:
+        copy.start()
+
+    chip, core = place[0], place[1]
+    passages = segments[...]
+    ends = [jnp.sum((passages <= s).astype(jnp.int32)) for s in range(3)]
+    for slot in range(2):
+        masks = mask_own if slot == 0 else mask_other
+        tile = 2 * chip + (core if slot == 0 else 1 - core)
+        mine = segments[:, pl.ds(pl.multiple_of(tile * TILE, TILE), TILE)]
+        low = jnp.where(
+            mine == 0, 0, jnp.where(mine == 1, ends[0], jnp.where(mine == 2, ends[1], ends[2]))
+        )
+        high = jnp.where(
+            mine == 0,
+            ends[0],
+            jnp.where(mine == 1, ends[1], jnp.where(mine == 2, ends[2], KEYS)),
+        )
+        for d in range(CHIPS):
+            for key_slot in range(2):
+                key_tile = 2 * lax.rem(chip + CHIPS - d, CHIPS) + (
+                    core if key_slot == 0 else 1 - core
+                )
+                seen = masks[0, key_tile] == 1
+                position = key_tile * TILE + lax.broadcasted_iota(
+                    jnp.int32, (TILE, TILE), 0
+                )
+                first = jnp.where(seen, 0, low)
+                last = jnp.where(seen, KEYS, high)
+                allowed = (position >= first) & (position < last)
+                row = d * 2 * TILE + key_slot * TILE
+                bias[row : row + TILE, slot * TILE : (slot + 1) * TILE] = jnp.where(
+                    allowed, 0.0, -jnp.inf
+                )
+
+    for copy in copies:
+        copy.wait()
+    out[:TILE] = dot(own[...], weights[...]).astype(BF)
+    out[TILE:] = dot(other[...], weights[...]).astype(BF)
 
 
 def project_query(place, own, other, w_query, segments, mask_own, mask_other):
-    blocks = GF // 256
     return pl.pallas_call(
         query_kernel,
-        grid_spec=pltpu.PrefetchScalarGridSpec(
-            num_scalar_prefetch=1,
-            grid=(blocks,),
-            in_specs=[
-                pl.BlockSpec((TILE, D), lambda i, p: (0, 0)),
-                pl.BlockSpec((TILE, D), lambda i, p: (0, 0)),
-                pl.BlockSpec((D, 256), lambda i, p: (0, p[1] * blocks + i)),
-                pl.BlockSpec((1, KEYS), lambda i, p: (0, 0)),
-                pl.BlockSpec(memory_space=pltpu.SMEM),
-                pl.BlockSpec(memory_space=pltpu.SMEM),
-            ],
-            out_specs=[
-                pl.BlockSpec((2 * TILE, 256), lambda i, p: (0, i)),
-                pl.BlockSpec((KEYS, 2 * TILE), lambda i, p: (0, 0)),
-            ],
-        ),
+        in_specs=[SCALARS, WHOLE, WHOLE, STAY, WHOLE, SCALARS, SCALARS],
+        out_specs=[WHOLE, WHOLE],
         out_shape=[
             jax.ShapeDtypeStruct((2 * TILE, GF), BF),
             jax.ShapeDtypeStruct((KEYS, 2 * TILE), F32),
         ],
+        scratch_shapes=[pltpu.VMEM((D, GF), BF), pltpu.SemaphoreType.DMA((Q_CHUNKS,))],
         compiler_params=PARAMS,
         cost_estimate=cost(2 * 256 * D * GF, 2 * (256 * D + D * GF + 256 * GF)),
         name="project_query",
@@ -279,7 +314,7 @@
 def pack(place, dq, dq_other, dkv, dkv_other):
     return pl.pallas_call(
         pack_kernel,
-        in_specs=[pl.BlockSpec(memory_space=pltpu.SMEM)] + [WHOLE] * 4,
+        in_specs=[SCALARS] + [WHOLE] * 4,
         out_specs=[WHOLE] * 4,
         out_shape=[jax.ShapeDtypeStruct((256, 256), BF)] * 4,
         scratch_shapes=[pltpu.VMEM((4, 256, 256), BF)],
@@ -289,87 +324,114 @@
     )(place, dq, dq_other, dkv, dkv_other)
 
 
-def transpose_kernel(*refs):
-    out = refs[-1]
-    for i, ref in enumerate(refs[:-1]):
-        out[:, i * TILE : (i + 1) * TILE] = ref[...].T
-
-
-def transpose(parts):
+def transpose_kernel(tokens, out, rows, sems):
+    copies = []
+    for chunk in range(KEYS // TILE):
+        part = pl.ds(chunk * TILE, TILE)
+        copies.append(pltpu.make_async_copy(tokens.at[part], rows.at[part], sems.at[chunk]))
+    for copy in copies:
+        copy.start()
+    for chunk, copy in enumerate(copies):
+        copy.wait()
+        part = slice(chunk * TILE, (chunk + 1) * TILE)
+        out[:, part] = rows[part].T
+
+
+def transpose(tokens):
     return pl.pallas_call(
         transpose_kernel,
-        in_specs=[WHOLE] * 8,
+        in_specs=[STAY],
         out_specs=WHOLE,
         out_shape=jax.ShapeDtypeStruct((D, KEYS), BF),
+        scratch_shapes=[
+            pltpu.VMEM((KEYS, D), BF),
+            pltpu.SemaphoreType.DMA((KEYS // TILE,)),
+        ],
         compiler_params=PARAMS,
         cost_estimate=cost(0, 4 * D * KEYS),
         name="transpose_tokens",
-    )(*parts)
-
-
-def weight_kernel(place, tokens_t, a, b, c, d, out0, out1, out2, out3):
-    right = jnp.concatenate([a[...], b[...], c[...], d[...]], axis=0)
+    )(tokens)
+
+
+def weight_kernel(place, tokens_t, a, b, c, d, out0, out1, out2, out3, right):
+    for shift, part in enumerate((a, b, c, d)):
+        chip = lax.rem(place[0] + CHIPS - shift, CHIPS)
+        for slot in range(2):
+            tile = 2 * chip + (place[1] if slot == 0 else 1 - place[1])
+            right[pl.ds(pl.multiple_of(tile * TILE, TILE), TILE)] = part[
+                slot * TILE : (slot + 1) * TILE
+            ]
     for shift, out in enumerate((out0, out1, out2, out3)):
         row = pl.multiple_of(lax.rem(place[2] + shift, YS) * (D // YS), 128)
-        out[...] = dot(tokens_t[pl.ds(row, D // YS)], right).astype(out.dtype)
+        out[...] = dot(tokens_t[pl.ds(row, D // YS)], right[...]).astype(out.dtype)
 
 
 def weight_grad(place, tokens_t, parts):
     shape = (D // YS, 256)
     return pl.pallas_call(
         weight_kernel,
-        in_specs=[pl.BlockSpec(memory_space=pltpu.SMEM)] + [WHOLE] * 5,
+        in_specs=[SCALARS] + [WHOLE] * 5,
         out_specs=[WHOLE] * 4,
         out_shape=[jax.ShapeDtypeStruct(shape, F32)] + [jax.ShapeDtypeStruct(shape, BF)] * 3,
+        scratch_shapes=[pltpu.VMEM((KEYS, 256), BF)],
         compiler_params=PARAMS,
         cost_estimate=cost(2 * D * KEYS * 256, 2 * D * KEYS + 3 * D * 256),
         name="weight_grad",
     )(place, tokens_t, *parts)
 
 
-def input_kernel(place, dq, dq_other, dkv, dkv_other, w_query, w_key, w_value, out, left):
+def input_kernel(
+    place, dq, dq_other, dkv, dkv_other, w_query, w_key, w_value, out, left, right, sems
+):
     core = place[1]
-
-    @pl.when(pl.program_id(0) == 0)
-    def _():
-        mine = pl.ds(pl.multiple_of(core * GF, 128), GF)
-        theirs = pl.ds(pl.multiple_of((1 - core) * GF, 128), GF)
-        left[:, mine] = dq[:TILE]
-        left[:, theirs] = dq_other[TILE:]
-        for part in range(2):
-            columns = slice(part * HD, (part + 1) * HD)
-            base = D + part * KVH * HD
-            left[:, pl.ds(pl.multiple_of(base + core * HD, 128), HD)] = dkv[:TILE, columns]
-            left[:, pl.ds(pl.multiple_of(base + (1 - core) * HD, 128), HD)] = dkv_other[
-                TILE:, columns
+    width = D // IN_CHUNKS
+    copies = []
+    for chunk in range(IN_CHUNKS):
+        part = pl.ds(chunk * width, width)
+        copies.append(
+            [
+                pltpu.make_async_copy(
+                    source.at[part],
+                    right.at[part, pl.ds(start, size)],
+                    sems.at[chunk, side],
+                )
+                for side, (source, start, size) in enumerate(
+                    ((w_query, 0, D), (w_key, D, 256), (w_value, D + 256, 256))
+                )
             ]
-
-    total = dot_nt(left[:, :D], w_query[...])
-    total += dot_nt(left[:, D : D + 256], w_key[...])
-    total += dot_nt(left[:, D + 256 :], w_value[...])
-    out[...] = total.astype(BF)
+        )
+    for group in copies:
+        for copy in group:
+            copy.start()
+    mine = pl.ds(pl.multiple_of(core * GF, 128), GF)
+    theirs = pl.ds(pl.multiple_of((1 - core) * GF, 128), GF)
+    left[:, mine] = dq[:TILE]
+    left[:, theirs] = dq_other[TILE:]
+    for part in range(2):
+        columns = slice(part * HD, (part + 1) * HD)
+        base = D + part * KVH * HD
+        left[:, pl.ds(pl.multiple_of(base + core * HD, 128), HD)] = dkv[:TILE, columns]
+        left[:, pl.ds(pl.multiple_of(base + (1 - core) * HD, 128), HD)] = dkv_other[
+            TILE:, columns
+        ]
+    for chunk, group in enumerate(copies):
+        for copy in group:
+            copy.wait()
+        part = slice(chunk * width, (chunk + 1) * width)
+        out[:, part] = dot_nt(left[...], right[part]).astype(BF)
 
 
 def input_grad(place, dq, dq_other, dkv, dkv_other, w_query, w_key, w_value):
-    width = 256
     return pl.pallas_call(
         input_kernel,
-        grid_spec=pltpu.PrefetchScalarGridSpec(
-            num_scalar_prefetch=1,
-            grid=(D // width,),
-            in_specs=[
-                pl.BlockSpec((256, GF), lambda i, p: (0, 0)),
-                pl.BlockSpec((256, GF), lambda i, p: (0, 0)),
-                pl.BlockSpec((256, 256), lambda i, p: (0, 0)),
-                pl.BlockSpec((256, 256), lambda i, p: (0, 0)),
-                pl.BlockSpec((width, D), lambda i, p: (i, 0)),
-                pl.BlockSpec((width, 256), lambda i, p: (i, 0)),
-                pl.BlockSpec((width, 256), lambda i, p: (i, 0)),
-            ],
-            out_specs=pl.BlockSpec((TILE, width), lambda i, p: (0, i)),
-            scratch_shapes=[pltpu.VMEM((TILE, D + 512), BF)],
-        ),
+        in_specs=[SCALARS] + [WHOLE] * 4 + [STAY] * 3,
+        out_specs=WHOLE,
         out_shape=jax.ShapeDtypeStruct((TILE, D), BF),
+        scratch_shapes=[
+            pltpu.VMEM((TILE, D + 512), BF),
+            pltpu.VMEM((D, D + 512), BF),
+            pltpu.SemaphoreType.DMA((IN_CHUNKS, 3)),
+        ],
         compiler_params=PARAMS,
         cost_estimate=cost(2 * TILE * D * 2048, 2 * D * 2048),
         name="input_grad",
@@ -403,14 +465,15 @@
     other = lax.ppermute(own, "ctx", CORE)
     up_other = lax.ppermute(up, "ctx", CORE)
     mask_other = lax.ppermute(tile_mask[0], "ctx", CORE)
-
-    kv = project_kv(place, own, other, w_key, w_value)
+    gathered = lax.all_gather(own, "ctx", axis=0, tiled=True)
+
+    w_query, w_key, w_value = (in_hbm(w) for w in (w_query, w_key, w_value))
+    weights, kv_own = project_kv_own(place, in_hbm(own), w_key, w_value)
+    kv = project_kv(other, weights, kv_own)
     kvs = [kv] + [lax.ppermute(kv, "ctx", chip_shift(d)) for d in (1, 2, 3)]
     query, bias = project_query(
         place, own, other, w_query, segments, tile_mask[0], mask_other
     )
-    kvs, late_own = lax.optimization_barrier((kvs, own))
-    far = [lax.ppermute(late_own, "ctx", chip_shift(d)) for d in (1, 2, 3)]
 
     dq, g0, g1, g2, g3 = attention(place, query, up, up_other, kvs, bias)
     dq_other = lax.ppermute(dq, "ctx", CORE)
@@ -420,24 +483,22 @@
     dkv = sum_four(g0, *back)
     dkv_other = lax.ppermute(dkv, "ctx", CORE)
 
-    far_other = [lax.ppermute(part, "ctx", CORE) for part in far]
-    tokens_t = transpose(
-        [own, other] + [part for pair in zip(far, far_other) for part in pair]
-    )
-
-    packed = pack(place, dq, dq_other, dkv, dkv_other)
+    gathered, dkv_late = lax.optimization_barrier((gathered, dkv_other))
+    tokens_t = transpose(in_hbm(gathered))
+
+    packed = pack(place, dq, dq_other, dkv, dkv_late)
     columns = [packed[0]] + [
         lax.ppermute(packed[d], "ctx", chip_shift(d)) for d in (1, 2, 3)
     ]
     terms = weight_grad(place, tokens_t, columns)
     y_parts = [terms[0]] + [lax.ppermute(terms[d], "dp", y_shift(d)) for d in (1, 2, 3)]
+    grad_tokens = input_grad(
+        place, dq, dq_other, dkv, dkv_late, w_query, w_key, w_value
+    )
+    y_parts, grad_tokens = lax.optimization_barrier((y_parts, grad_tokens))
     y_sum = sum_four(*y_parts)
     z_parts = lax.all_to_all(y_sum, "dp", 0, 0, tiled=True, axis_index_groups=Z_GROUPS)
     grad_projection = final_sum(z_parts)
-
-    grad_tokens = input_grad(
-        place, dq, dq_other, dkv, dkv_other, w_query, w_key, w_value
-    )
     return grad_tokens[None], grad_projection
 
 

time: 100 us -> 98.9 us (0.989)
  blocking collectives: 0 us -> 16.4 us
  starting transfers between devices: 32.2 us -> 17 us
  between operations: 0.75 us -> 14.2 us
  waiting for transfers between devices: 30.5 us -> 22.8 us
  local copies, waits for them, and re-layouts: 5.51 us -> 0.02 us
  Pallas kernels: 29.5 us -> 27.2 us
    all_to_all x0 -> x1, blocking collectives: none -> 16.4 us  [shards(): lax.all_to_all(y_sum, 'dp', 0, 0, tiled=True, axis_index_groups=Z_GROUPS)]
    all_to_all x1 -> x0, starting transfers between devices: 8.47 us -> none  [shards(): lax.all_to_all(y_sum, 'dp', 0, 0, tiled=True, axis_index_groups=Z_GROUPS)]
    ppermute x3, waiting for transfers between devices: 7.21 us -> 0.53 us  [shards(): lax.ppermute(terms[d], 'dp', y_shift(d))]
    unnamed x16 -> x8, local copies, waits for them, and re-layouts: 5.51 us -> 0.02 us
    ppermute x6 -> x0, starting transfers between devices: 3.83 us -> none  [the longest x3 2.82 us: shards(): far = [lax.ppermute(late_own, 'ctx', chip_shift(d)) for d in (1, 2, 3)]]
    ppermute x3, starting transfers between devices: 5.6 us -> 2.29 us  [shards(): lax.ppermute(g, 'ctx', chip_shift(CHIPS - d))]
    all_to_all x1 -> x0, waiting for transfers between devices: 3.03 us -> none  [shards(): lax.all_to_all(y_sum, 'dp', 0, 0, tiled=True, axis_index_groups=Z_GROUPS)]
    ppermute x3, waiting for transfers between devices: 1.17 us -> 3.72 us  [shards(): kvs = [kv] + [lax.ppermute(kv, 'ctx', chip_shift(d)) for d in (1, 2, 3)]]
  transfers between devices with their start and end apart: 24 -> 18, of which waited for: 13 -> 11; matrix products, arithmetic and copies ran while one was open for 0% -> 0% of each run, Pallas kernels for 27% -> 25%
where the time goes in v2:
time: 98.9 us; the launch traced here: 97.7 us
  Pallas kernels  27.2 us (28%)
  waiting for transfers between devices  22.8 us (23%)
  starting transfers between devices  17 us (17%)
  blocking collectives  16.4 us (17%)
  between operations  14.2 us (14%)
    all_to_all x1, blocking collectives, shards(): lax.all_to_all(y_sum, 'dp', 0, 0, tiled=True, axis_index_groups=Z_GROUPS)  16.4 us
    ppermute x3, waiting for transfers between devices, shards(): lax.ppermute(g, 'ctx', chip_shift(CHIPS - d))  11.6 us
    pallas_call x1, Pallas kernels, attention(): pl.pallas_call(attention_kernel, grid_spec=pltpu.PrefetchScalarGridSpec(n...  9.38 us
    pallas_call x1, Pallas kernels, input_grad(): pl.pallas_call(input_kernel, in_specs=[SCALARS] + [WHOLE] * 4 + [STAY] *...  6.88 us
    ppermute x3, starting transfers between devices, shards(): lax.ppermute(terms[d], 'dp', y_shift(d))  4.82 us
    ppermute x3, starting transfers between devices, shards(): kvs = [kv] + [lax.ppermute(kv, 'ctx', chip_shift(d)) for d in (1, 2, 3)]  4.52 us
    ppermute x3, starting transfers between devices, shards(): lax.ppermute(packed[d], 'ctx', chip_shift(d))  4.49 us
    ppermute x3, waiting for transfers between devices, shards(): kvs = [kv] + [lax.ppermute(kv, 'ctx', chip_shift(d)) for d in (1, 2, 3)]  3.72 us
  transfers between devices with their start and end apart: 18, of which 11 were waited for; matrix products, arithmetic and copies ran while one was open for 0% of the time, Pallas kernels for 25%

profile of v2, /device:TPU:8, one launch (start us, length us, event | category | flops | bytes accessed | tf_op | source)
XLA Modules:
  0.0 97.7 jit_solution(15735904370498077845)
XLA Ops:
  7.2 0.0 copy-start
  7.2 0.0 copy-start.2
  7.2 0.0 copy-start.1
  7.2 0.0 all-gather.3.cloned.1.call-start
  7.2 0.7 all-gather.3.cloned.1.call-update
  7.9 0.1 collective-permute-start
  8.0 0.5 collective-permute-start.2
  8.5 0.1 pad_add_fusion.place
  8.6 2.3 %project_kv_own.1 = (bf16[1536,256]{1,0:T(8,128)(2,1)S(1)}, bf16[128,256]{1,0:T(8,128)(2,1)S(1)}) custom-call(s32[4]{0:T(128)S(1)} %pad_add_fusion.place, bf16[128,1536]{1,0:T(8,128)(2,1)} %bitcast.12, bf16[1536,256]{1,0:T(8,128)(2,1)} %w_key.3, bf16[1536,256]{1,0:T(8,128)(2,1)} %w_value.3), custom_call_target="tpu_custom_call" | custom-call | flops 100663296 | bytes 1179648 | tf_op jit(solution)/shard_map/project_kv_own/pallas_call | solution.py:93
  10.9 0.0 collective-permute-done.other
  10.9 0.0 copy-start.3
  10.9 0.3 project_kv.1.kv0
  11.2 2.8 %collective-permute-start.5 = (bf16[256,256]{1,0:T(8,128)(2,1)S(1)}, bf16[256,256]{1,0:T(8,128)(2,1)S(1)}, u32[]{:S(2)}, u32[]{:S(2)}) collective-permute-start(bf16[256,256]{1,0:T(8,128)(2,1)S(1)} %project_kv.1.kv0), channel_id=1, source_target_pairs={{0,192},{32,224},{64,0},{96,32},{128,64},{160,96},{192,128},{224,1... | collective-permute-start | bytes 393224 | tf_op jit(solution)/shard_map/ppermute | solution.py:473
  14.0 0.8 collective-permute-start.4
  14.8 0.9 collective-permute-start.3
  15.7 0.0 copy-done.2
  15.7 0.0 collective-permute-start.1
  15.7 1.1 %collective-permute-done.1.mask_other = s32[1,8]{1,0:T(1,128)S(1)} collective-permute-done((s32[1,8]{1,0:T(1,128)S(1)}, s32[1,8]{1,0:T(1,128)S(1)}, u32[]{:S(2)}, u32[]{:S(2)}) %collective-permute-start.1) | collective-permute-done | bytes 64 | tf_op jit(solution)/shard_map/ppermute | solution.py:467
  16.8 0.0 copy-done
  16.8 0.0 copy-done.1
  16.8 3.0 %project_query.1 = (bf16[256,768]{1,0:T(8,128)(2,1)S(1)}, f32[1024,256]{1,0:T(8,128)S(1)}) custom-call(s32[4]{0:T(128)S(1)} %pad_add_fusion.place, bf16[128,1536]{1,0:T(8,128)(2,1)S(1)} %bitcast.13, bf16[128,1536]{1,0:T(8,128)(2,1)S(1)} %collective-permute-done.other, bf16[1536,1536]{1,0:T(8,128)(2,1)} %w_query.3, s32[1,1024]{1,0:T(1,128)S(1)} %copy-done.1, ...), custom_call_target="tpu_custom_call" | custom-call | flops 603979776 | bytes 3538944 | tf_op jit(solution)/shard_map/project_query/pallas_call | solution.py:177
  19.8 0.0 collective-permute-done.2.up_other
  19.8 0.0 collective-permute-done.5.kv3
  19.9 2.0 %collective-permute-done.4.kv2 = bf16[256,256]{1,0:T(8,128)(2,1)S(1)} collective-permute-done((bf16[256,256]{1,0:T(8,128)(2,1)S(1)}, bf16[256,256]{1,0:T(8,128)(2,1)S(1)}, u32[]{:S(2)}, u32[]{:S(2)}) %collective-permute-start.4) | collective-permute-done | bytes 131104 | tf_op jit(solution)/shard_map/ppermute | solution.py:473
  21.9 1.7 %collective-permute-done.3.kv1 = bf16[256,256]{1,0:T(8,128)(2,1)S(1)} collective-permute-done((bf16[256,256]{1,0:T(8,128)(2,1)S(1)}, bf16[256,256]{1,0:T(8,128)(2,1)S(1)}, u32[]{:S(2)}, u32[]{:S(2)}) %collective-permute-start.3) | collective-permute-done | bytes 131104 | tf_op jit(solution)/shard_map/ppermute | solution.py:473
  23.5 0.0 copy-done.3
  23.5 9.4 %attention.1 = (bf16[256,768]{1,0:T(8,128)(2,1)S(1)}, f32[256,256]{1,0:T(8,128)S(1)}, bf16[256,256]{1,0:T(8,128)(2,1)S(1)}, bf16[256,256]{1,0:T(8,128)(2,1)S(1)}, bf16[256,256]{1,0:T(8,128)(2,1)S(1)}) custom-call(s32[4]{0:T(128)S(1)} %pad_add_fusion.place, bf16[256,768]{1,0:T(8,128)(2,1)S(1)} %get-tuple-element.26.query, bf16[128,1536]{1,0:T(8,128)(2,1)S(1)} %bitcast.19, ...), custom_call_target="tpu_custom_call" | custom-call | flops 4026531840 | bytes 4194304 | tf_op jit(solution)/shard_map/attention/pallas_call | solution.py:235
  32.9 0.1 collective-permute-start.10
  33.0 0.6 collective-permute-start.6
  33.7 0.8 collective-permute-start.7
  34.5 0.9 collective-permute-start.8
  35.3 6.7 %collective-permute-done.6.b = bf16[256,256]{1,0:T(8,128)(2,1)S(1)} collective-permute-done((bf16[256,256]{1,0:T(8,128)(2,1)S(1)}, bf16[256,256]{1,0:T(8,128)(2,1)S(1)}, u32[]{:S(2)}, u32[]{:S(2)}) %collective-permute-start.6) | collective-permute-done | bytes 131104 | tf_op jit(solution)/shard_map/ppermute | solution.py:481
  42.0 2.3 %collective-permute-done.7.c = bf16[256,256]{1,0:T(8,128)(2,1)S(1)} collective-permute-done((bf16[256,256]{1,0:T(8,128)(2,1)S(1)}, bf16[256,256]{1,0:T(8,128)(2,1)S(1)}, u32[]{:S(2)}, u32[]{:S(2)}) %collective-permute-start.7) | collective-permute-done | bytes 131104 | tf_op jit(solution)/shard_map/ppermute | solution.py:481
  44.3 2.6 %collective-permute-done.8.d = bf16[256,256]{1,0:T(8,128)(2,1)S(1)} collective-permute-done((bf16[256,256]{1,0:T(8,128)(2,1)S(1)}, bf16[256,256]{1,0:T(8,128)(2,1)S(1)}, u32[]{:S(2)}, u32[]{:S(2)}) %collective-permute-start.8) | collective-permute-done | bytes 131104 | tf_op jit(solution)/shard_map/ppermute | solution.py:481
  46.9 0.1 sum_four.2.dkv
  47.0 0.1 collective-permute-start.9
  47.1 1.3 %collective-permute-done.9.dkv_other = bf16[256,256]{1,0:T(8,128)(2,1)S(1)} collective-permute-done((bf16[256,256]{1,0:T(8,128)(2,1)S(1)}, bf16[256,256]{1,0:T(8,128)(2,1)S(1)}, u32[]{:S(2)}, u32[]{:S(2)}) %collective-permute-start.9) | collective-permute-done | bytes 131104 | tf_op jit(solution)/shard_map/ppermute | solution.py:484
  48.4 0.2 all-gather.3.cloned.1.call-done
  48.7 0.0 collective-permute-done.10.dq_other
  48.7 0.6 pack.1
  49.3 1.0 %collective-permute-start.11 = (bf16[256,256]{1,0:T(8,128)(2,1)S(1)}, bf16[256,256]{1,0:T(8,128)(2,1)S(1)}, u32[]{:S(2)}, u32[]{:S(2)}) collective-permute-start(bf16[256,256]{1,0:T(8,128)(2,1)S(1)} %get-tuple-element.38), channel_id=1, source_target_pairs={{0,64},{32,96},{64,128},{96,160},{128,192},{160,224},{192,0},{224,... | collective-permute-start | bytes 393224 | tf_op jit(solution)/shard_map/ppermute | solution.py:491
  50.3 2.3 %collective-permute-start.12 = (bf16[256,256]{1,0:T(8,128)(2,1)S(1)}, bf16[256,256]{1,0:T(8,128)(2,1)S(1)}, u32[]{:S(2)}, u32[]{:S(2)}) collective-permute-start(bf16[256,256]{1,0:T(8,128)(2,1)S(1)} %get-tuple-element.39), channel_id=1, source_target_pairs={{0,128},{32,160},{64,192},{96,224},{128,0},{160,32},{192,64},{224,... | collective-permute-start | bytes 393224 | tf_op jit(solution)/shard_map/ppermute | solution.py:491
  52.6 1.2 %collective-permute-start.13 = (bf16[256,256]{1,0:T(8,128)(2,1)S(1)}, bf16[256,256]{1,0:T(8,128)(2,1)S(1)}, u32[]{:S(2)}, u32[]{:S(2)}) collective-permute-start(bf16[256,256]{1,0:T(8,128)(2,1)S(1)} %get-tuple-element.40), channel_id=1, source_target_pairs={{0,192},{32,224},{64,0},{96,32},{128,64},{160,96},{192,128},{224,1... | collective-permute-start | bytes 393224 | tf_op jit(solution)/shard_map/ppermute | solution.py:491
  53.8 2.5 %transpose_tokens.1.tokens_t = bf16[1536,1024]{1,0:T(8,128)(2,1)S(1)} custom-call(bf16[1024,1536]{1,0:T(8,128)(2,1)} %bitcast.20), custom_call_target="tpu_custom_call" | custom-call | bytes 6291456 | tf_op jit(solution)/shard_map/transpose_tokens/pallas_call | solution.py:341
  56.3 3.0 %collective-permute-done.11.b = bf16[256,256]{1,0:T(8,128)(2,1)S(1)} collective-permute-done((bf16[256,256]{1,0:T(8,128)(2,1)S(1)}, bf16[256,256]{1,0:T(8,128)(2,1)S(1)}, u32[]{:S(2)}, u32[]{:S(2)}) %collective-permute-start.11) | collective-permute-done | bytes 131104 | tf_op jit(solution)/shard_map/ppermute | solution.py:491
  59.3 0.0 collective-permute-done.12.c
  59.3 0.6 collective-permute-done.13.d
  59.8 1.6 %weight_grad.1 = (f32[384,256]{1,0:T(8,128)S(1)}, bf16[384,256]{1,0:T(8,128)(2,1)S(1)}, bf16[384,256]{1,0:T(8,128)(2,1)S(1)}, bf16[384,256]{1,0:T(8,128)(2,1)S(1)}) custom-call(s32[4]{0:T(128)S(1)} %pad_add_fusion.place, bf16[1536,1024]{1,0:T(8,128)(2,1)S(1)} %transpose_tokens.1.tokens_t, bf16[256,256]{1,0:T(8,128)(2,1)S(1)} %get-tuple-element.37.a, ...), custom_call_target="tpu_custom_call" | custom-call | flops 805306368 | bytes 4325376 | tf_op jit(solution)/shard_map/weight_grad/pallas_call | solution.py:371
  61.4 1.6 %collective-permute-start.14 = (bf16[384,256]{1,0:T(8,128)(2,1)S(1)}, bf16[384,256]{1,0:T(8,128)(2,1)S(1)}, u32[]{:S(2)}, u32[]{:S(2)}) collective-permute-start(bf16[384,256]{1,0:T(8,128)(2,1)S(1)} %get-tuple-element.42), channel_id=1, source_target_pairs={{0,8},{1,9},{2,10},{3,11},{4,12},{5,13},{6,14},{7,15},{8,16},{9,17... | collective-permute-start | bytes 589832 | tf_op jit(solution)/shard_map/ppermute | solution.py:494
  63.0 1.1 %collective-permute-start.15 = (bf16[384,256]{1,0:T(8,128)(2,1)S(1)}, bf16[384,256]{1,0:T(8,128)(2,1)S(1)}, u32[]{:S(2)}, u32[]{:S(2)}) collective-permute-start(bf16[384,256]{1,0:T(8,128)(2,1)S(1)} %get-tuple-element.43), channel_id=1, source_target_pairs={{0,16},{1,17},{2,18},{3,19},{4,20},{5,21},{6,22},{7,23},{8,24},{9,... | collective-permute-start | bytes 589832 | tf_op jit(solution)/shard_map/ppermute | solution.py:494
  64.1 2.1 %collective-permute-start.16 = (bf16[384,256]{1,0:T(8,128)(2,1)S(1)}, bf16[384,256]{1,0:T(8,128)(2,1)S(1)}, u32[]{:S(2)}, u32[]{:S(2)}) collective-permute-start(bf16[384,256]{1,0:T(8,128)(2,1)S(1)} %get-tuple-element.44), channel_id=1, source_target_pairs={{0,24},{1,25},{2,26},{3,27},{4,28},{5,29},{6,30},{7,31},{8,0},{9,1... | collective-permute-start | bytes 589832 | tf_op jit(solution)/shard_map/ppermute | solution.py:494
  66.2 6.9 %input_grad.1 = bf16[128,1536]{1,0:T(8,128)(2,1)} custom-call(s32[4]{0:T(128)S(1)} %pad_add_fusion.place, bf16[256,768]{1,0:T(8,128)(2,1)S(1)} %get-tuple-element.35.dq, bf16[256,768]{1,0:T(8,128)(2,1)S(1)} %collective-permute-done.10.dq_other, bf16[256,256]{1,0:T(8,128)(2,1)S(1)} %sum_four.2.dkv, bf16[256,256]{1,0:T(8,128)(2,1)S(1)} %collective-permute-done.9.dkv_other, ...), custom_call_target="tpu_custom_call" | custom-call | flops 805306368 | bytes 6291456 | tf_op jit(solution)/shard_map/input_grad/pallas_call | solution.py:425
  73.1 0.0 collective-permute-done.14.b
  73.1 0.0 collective-permute-done.15.c
  73.1 0.5 collective-permute-done.16.d
  73.7 0.1 sum_four.3
  73.8 16.4 %all_to_all.11 = bf16[8,48,256]{2,1,0:T(8,128)(2,1)S(1)} all-to-all(bf16[8,48,256]{2,1,0:T(8,128)(2,1)S(1)} %bitcast.14), channel_id=1, replica_groups={{0,1,2,3,4,5,6,7},{8,9,10,11,12,13,14,15},{16,17,18,19,20,21,22,23},{24..., dimensions={0} | all-to-all | bytes 393216 | tf_op jit(solution)/shard_map/all_to_all | solution.py:500
  90.2 0.6 final_sum.1
Async XLA Ops:
  7.2 9.7 %copy-start = (bf16[1,128,1536]{2,1,0:T(8,128)(2,1)S(1)}, bf16[1,128,1536]{2,1,0:T(8,128)(2,1)}, u32[]{:S(2)}) copy-start(bf16[1,128,1536]{2,1,0:T(8,128)(2,1)} %param.7) | copy-start | bytes 1179652
  7.2 8.5 %copy-start.2 = (s32[1,1,8]{2,1,0:T(1,128)S(1)}, s32[1,1,8]{2,1,0:T(1,128)}, u32[]{:S(2)}) copy-start(s32[1,1,8]{2,1,0:T(1,128)} %param.9) | copy-start | bytes 100
  7.2 9.6 %copy-start.1 = (s32[1,1024]{1,0:T(1,128)S(1)}, s32[1,1024]{1,0:T(1,128)}, u32[]{:S(2)}) copy-start(s32[1,1024]{1,0:T(1,128)} %segments.1) | copy-start | bytes 12292
  7.2 41.5 %all-gather.3.cloned.1.call-start = ((), (), s32[]{:S(2)}) async-start(), calls=%async_computation.1 | async-start | bytes 3538944 | tf_op jit(solution)/shard_map/all_gather | solution.py:468
  7.9 2.9 %collective-permute-start = (bf16[128,1536]{1,0:T(8,128)(2,1)}, bf16[128,1536]{1,0:T(8,128)(2,1)S(1)}, u32[]{:S(2)}, u32[]{:S(2)}) collective-permute-start(bf16[128,1536]{1,0:T(8,128)(2,1)} %bitcast.11), channel_id=1, source_target_pairs={{0,32},{32,0},{64,96},{96,64},{128,160},{160,128},{192,224},{224,1... | collective-permute-start | bytes 1179656 | tf_op jit(solution)/shard_map/ppermute | solution.py:465
  8.0 11.8 %collective-permute-start.2 = (bf16[128,1536]{1,0:T(8,128)(2,1)}, bf16[128,1536]{1,0:T(8,128)(2,1)S(1)}, u32[]{:S(2)}, u32[]{:S(2)}) collective-permute-start(bf16[128,1536]{1,0:T(8,128)(2,1)} %bitcast.18), channel_id=1, source_target_pairs={{0,32},{32,0},{64,96},{96,64},{128,160},{160,128},{192,224},{224,1... | collective-permute-start | bytes 1179656 | tf_op jit(solution)/shard_map/ppermute | solution.py:466
  10.9 12.7 %copy-start.3 = (bf16[1,128,1536]{2,1,0:T(8,128)(2,1)S(1)}, bf16[1,128,1536]{2,1,0:T(8,128)(2,1)}, u32[]{:S(2)}) copy-start(bf16[1,128,1536]{2,1,0:T(8,128)(2,1)} %param.8) | copy-start | bytes 1179652
  11.2 8.7 %collective-permute-start.5 = (bf16[256,256]{1,0:T(8,128)(2,1)S(1)}, bf16[256,256]{1,0:T(8,128)(2,1)S(1)}, u32[]{:S(2)}, u32[]{:S(2)}) collective-permute-start(bf16[256,256]{1,0:T(8,128)(2,1)S(1)} %project_kv.1.kv0), channel_id=1, source_target_pairs={{0,192},{32,224},{64,0},{96,32},{128,64},{160,96},{192,128},{224,1... | collective-permute-start | bytes 393224 | tf_op jit(solution)/shard_map/ppermute | solution.py:473
  14.0 7.9 %collective-permute-start.4 = (bf16[256,256]{1,0:T(8,128)(2,1)S(1)}, bf16[256,256]{1,0:T(8,128)(2,1)S(1)}, u32[]{:S(2)}, u32[]{:S(2)}) collective-permute-start(bf16[256,256]{1,0:T(8,128)(2,1)S(1)} %project_kv.1.kv0), channel_id=1, source_target_pairs={{0,128},{32,160},{64,192},{96,224},{128,0},{160,32},{192,64},{224,... | collective-permute-start | bytes 393224 | tf_op jit(solution)/shard_map/ppermute | solution.py:473
  14.8 8.7 %collective-permute-start.3 = (bf16[256,256]{1,0:T(8,128)(2,1)S(1)}, bf16[256,256]{1,0:T(8,128)(2,1)S(1)}, u32[]{:S(2)}, u32[]{:S(2)}) collective-permute-start(bf16[256,256]{1,0:T(8,128)(2,1)S(1)} %project_kv.1.kv0), channel_id=1, source_target_pairs={{0,64},{32,96},{64,128},{96,160},{128,192},{160,224},{192,0},{224,... | collective-permute-start | bytes 393224 | tf_op jit(solution)/shard_map/ppermute | solution.py:473
  15.7 1.1 %collective-permute-start.1 = (s32[1,8]{1,0:T(1,128)S(1)}, s32[1,8]{1,0:T(1,128)S(1)}, u32[]{:S(2)}, u32[]{:S(2)}) collective-permute-start(s32[1,8]{1,0:T(1,128)S(1)} %bitcast.16), channel_id=1, source_target_pairs={{0,32},{32,0},{64,96},{96,64},{128,160},{160,128},{192,224},{224,1... | collective-permute-start | bytes 104 | tf_op jit(solution)/shard_map/ppermute | solution.py:467
  32.9 15.7 %collective-permute-start.10 = (bf16[256,768]{1,0:T(8,128)(2,1)S(1)}, bf16[256,768]{1,0:T(8,128)(2,1)S(1)}, u32[]{:S(2)}, u32[]{:S(2)}) collective-permute-start(bf16[256,768]{1,0:T(8,128)(2,1)S(1)} %get-tuple-element.35.dq), channel_id=1, source_target_pairs={{0,32},{32,0},{64,96},{96,64},{128,160},{160,128},{192,224},{224,1... | collective-permute-start | bytes 1179656 | tf_op jit(solution)/shard_map/ppermute | solution.py:479
  33.0 9.0 %collective-permute-start.6 = (bf16[256,256]{1,0:T(8,128)(2,1)S(1)}, bf16[256,256]{1,0:T(8,128)(2,1)S(1)}, u32[]{:S(2)}, u32[]{:S(2)}) collective-permute-start(bf16[256,256]{1,0:T(8,128)(2,1)S(1)} %get-tuple-element.31), channel_id=1, source_target_pairs={{0,192},{32,224},{64,0},{96,32},{128,64},{160,96},{192,128},{224,1... | collective-permute-start | bytes 393224 | tf_op jit(solution)/shard_map/ppermute | solution.py:481
  33.7 10.7 %collective-permute-start.7 = (bf16[256,256]{1,0:T(8,128)(2,1)S(1)}, bf16[256,256]{1,0:T(8,128)(2,1)S(1)}, u32[]{:S(2)}, u32[]{:S(2)}) collective-permute-start(bf16[256,256]{1,0:T(8,128)(2,1)S(1)} %get-tuple-element.32), channel_id=1, source_target_pairs={{0,128},{32,160},{64,192},{96,224},{128,0},{160,32},{192,64},{224,... | collective-permute-start | bytes 393224 | tf_op jit(solution)/shard_map/ppermute | solution.py:481
  34.5 12.4 %collective-permute-start.8 = (bf16[256,256]{1,0:T(8,128)(2,1)S(1)}, bf16[256,256]{1,0:T(8,128)(2,1)S(1)}, u32[]{:S(2)}, u32[]{:S(2)}) collective-permute-start(bf16[256,256]{1,0:T(8,128)(2,1)S(1)} %get-tuple-element.33), channel_id=1, source_target_pairs={{0,64},{32,96},{64,128},{96,160},{128,192},{160,224},{192,0},{224,... | collective-permute-start | bytes 393224 | tf_op jit(solution)/shard_map/ppermute | solution.py:481
  47.0 1.4 %collective-permute-start.9 = (bf16[256,256]{1,0:T(8,128)(2,1)S(1)}, bf16[256,256]{1,0:T(8,128)(2,1)S(1)}, u32[]{:S(2)}, u32[]{:S(2)}) collective-permute-start(bf16[256,256]{1,0:T(8,128)(2,1)S(1)} %sum_four.2.dkv), channel_id=1, source_target_pairs={{0,32},{32,0},{64,96},{96,64},{128,160},{160,128},{192,224},{224,1... | collective-permute-start | bytes 393224 | tf_op jit(solution)/shard_map/ppermute | solution.py:484
  49.3 9.9 %collective-permute-start.11 = (bf16[256,256]{1,0:T(8,128)(2,1)S(1)}, bf16[256,256]{1,0:T(8,128)(2,1)S(1)}, u32[]{:S(2)}, u32[]{:S(2)}) collective-permute-start(bf16[256,256]{1,0:T(8,128)(2,1)S(1)} %get-tuple-element.38), channel_id=1, source_target_pairs={{0,64},{32,96},{64,128},{96,160},{128,192},{160,224},{192,0},{224,... | collective-permute-start | bytes 393224 | tf_op jit(solution)/shard_map/ppermute | solution.py:491
  50.3 9.0 %collective-permute-start.12 = (bf16[256,256]{1,0:T(8,128)(2,1)S(1)}, bf16[256,256]{1,0:T(8,128)(2,1)S(1)}, u32[]{:S(2)}, u32[]{:S(2)}) collective-permute-start(bf16[256,256]{1,0:T(8,128)(2,1)S(1)} %get-tuple-element.39), channel_id=1, source_target_pairs={{0,128},{32,160},{64,192},{96,224},{128,0},{160,32},{192,64},{224,... | collective-permute-start | bytes 393224 | tf_op jit(solution)/shard_map/ppermute | solution.py:491
  52.6 7.2 %collective-permute-start.13 = (bf16[256,256]{1,0:T(8,128)(2,1)S(1)}, bf16[256,256]{1,0:T(8,128)(2,1)S(1)}, u32[]{:S(2)}, u32[]{:S(2)}) collective-permute-start(bf16[256,256]{1,0:T(8,128)(2,1)S(1)} %get-tuple-element.40), channel_id=1, source_target_pairs={{0,192},{32,224},{64,0},{96,32},{128,64},{160,96},{192,128},{224,1... | collective-permute-start | bytes 393224 | tf_op jit(solution)/shard_map/ppermute | solution.py:491
  61.4 11.7 %collective-permute-start.14 = (bf16[384,256]{1,0:T(8,128)(2,1)S(1)}, bf16[384,256]{1,0:T(8,128)(2,1)S(1)}, u32[]{:S(2)}, u32[]{:S(2)}) collective-permute-start(bf16[384,256]{1,0:T(8,128)(2,1)S(1)} %get-tuple-element.42), channel_id=1, source_target_pairs={{0,8},{1,9},{2,10},{3,11},{4,12},{5,13},{6,14},{7,15},{8,16},{9,17... | collective-permute-start | bytes 589832 | tf_op jit(solution)/shard_map/ppermute | solution.py:494
  63.0 10.2 %collective-permute-start.15 = (bf16[384,256]{1,0:T(8,128)(2,1)S(1)}, bf16[384,256]{1,0:T(8,128)(2,1)S(1)}, u32[]{:S(2)}, u32[]{:S(2)}) collective-permute-start(bf16[384,256]{1,0:T(8,128)(2,1)S(1)} %get-tuple-element.43), channel_id=1, source_target_pairs={{0,16},{1,17},{2,18},{3,19},{4,20},{5,21},{6,22},{7,23},{8,24},{9,... | collective-permute-start | bytes 589832 | tf_op jit(solution)/shard_map/ppermute | solution.py:494
  64.1 9.6 %collective-permute-start.16 = (bf16[384,256]{1,0:T(8,128)(2,1)S(1)}, bf16[384,256]{1,0:T(8,128)(2,1)S(1)}, u32[]{:S(2)}, u32[]{:S(2)}) collective-permute-start(bf16[384,256]{1,0:T(8,128)(2,1)S(1)} %get-tuple-element.44), channel_id=1, source_target_pairs={{0,24},{1,25},{2,26},{3,27},{4,28},{5,29},{6,30},{7,31},{8,0},{9,1... | collective-permute-start | bytes 589832 | tf_op jit(solution)/shard_map/ppermute | solution.py:494
Sparse Core Ops, SparseCore 0:
  9.9 38.7 all-gather.2

commit v3 on v2

--- a/solution.py
+++ b/solution.py
@@ -103,6 +103,23 @@
         cost_estimate=cost(2 * TILE * D * 256, 2 * (TILE * D + D * 256)),
         name="project_kv_own",
     )(place, own, w_key, w_value)
+
+
+def kv_pair_kernel(own, other, weights, out):
+    out[:TILE] = dot(own[...], weights[...]).astype(BF)
+    out[TILE:] = dot(other[...], weights[...]).astype(BF)
+
+
+def project_kv_pair(own, other, weights):
+    return pl.pallas_call(
+        kv_pair_kernel,
+        in_specs=[WHOLE] * 3,
+        out_specs=WHOLE,
+        out_shape=jax.ShapeDtypeStruct((2 * TILE, 2 * HD), BF),
+        compiler_params=PARAMS,
+        cost_estimate=cost(4 * TILE * D * 256, 2 * (2 * TILE * D + D * 256)),
+        name="project_kv_pair",
+    )(own, other, weights)
 
 
 def kv_kernel(other, weights, kv_own, out):
@@ -324,46 +341,29 @@
     )(place, dq, dq_other, dkv, dkv_other)
 
 
-def transpose_kernel(tokens, out, rows, sems):
-    copies = []
-    for chunk in range(KEYS // TILE):
-        part = pl.ds(chunk * TILE, TILE)
-        copies.append(pltpu.make_async_copy(tokens.at[part], rows.at[part], sems.at[chunk]))
-    for copy in copies:
-        copy.start()
-    for chunk, copy in enumerate(copies):
-        copy.wait()
-        part = slice(chunk * TILE, (chunk + 1) * TILE)
-        out[:, part] = rows[part].T
-
-
-def transpose(tokens):
+def transpose_kernel(*refs):
+    out = refs[-1]
+    for i, ref in enumerate(refs[:-1]):
+        out[:, i * TILE : (i + 1) * TILE] = ref[...].T
+
+
+def transpose(parts):
     return pl.pallas_call(
         transpose_kernel,
-        in_specs=[STAY],
+        in_specs=[WHOLE] * 8,
         out_specs=WHOLE,
         out_shape=jax.ShapeDtypeStruct((D, KEYS), BF),
-        scratch_shapes=[
-            pltpu.VMEM((KEYS, D), BF),
-            pltpu.SemaphoreType.DMA((KEYS // TILE,)),
-        ],
         compiler_params=PARAMS,
         cost_estimate=cost(0, 4 * D * KEYS),
         name="transpose_tokens",
-    )(tokens)
-
-
-def weight_kernel(place, tokens_t, a, b, c, d, out0, out1, out2, out3, right):
-    for shift, part in enumerate((a, b, c, d)):
-        chip = lax.rem(place[0] + CHIPS - shift, CHIPS)
-        for slot in range(2):
-            tile = 2 * chip + (place[1] if slot == 0 else 1 - place[1])
-            right[pl.ds(pl.multiple_of(tile * TILE, TILE), TILE)] = part[
-                slot * TILE : (slot + 1) * TILE
-            ]
+    )(*parts)
+
+
+def weight_kernel(place, tokens_t, a, b, c, d, out0, out1, out2, out3):
+    right = jnp.concatenate([a[...], b[...], c[...], d[...]], axis=0)
     for shift, out in enumerate((out0, out1, out2, out3)):
         row = pl.multiple_of(lax.rem(place[2] + shift, YS) * (D // YS), 128)
-        out[...] = dot(tokens_t[pl.ds(row, D // YS)], right[...]).astype(out.dtype)
+        out[...] = dot(tokens_t[pl.ds(row, D // YS)], right).astype(out.dtype)
 
 
 def weight_grad(place, tokens_t, parts):
@@ -373,7 +373,6 @@
         in_specs=[SCALARS] + [WHOLE] * 5,
         out_specs=[WHOLE] * 4,
         out_shape=[jax.ShapeDtypeStruct(shape, F32)] + [jax.ShapeDtypeStruct(shape, BF)] * 3,
-        scratch_shapes=[pltpu.VMEM((KEYS, 256), BF)],
         compiler_params=PARAMS,
         cost_estimate=cost(2 * D * KEYS * 256, 2 * D * KEYS + 3 * D * 256),
         name="weight_grad",
@@ -462,18 +461,20 @@
     dp = lax.axis_index("dp")
     place = jnp.stack([ctx // 2, ctx % 2, dp // ZS, dp % ZS]).astype(jnp.int32)
     own, up = tokens[0], grad_heads[0]
+    far = {d: lax.ppermute(own, "ctx", chip_shift(d)) for d in (1, 3, 2)}
     other = lax.ppermute(own, "ctx", CORE)
     up_other = lax.ppermute(up, "ctx", CORE)
     mask_other = lax.ppermute(tile_mask[0], "ctx", CORE)
-    gathered = lax.all_gather(own, "ctx", axis=0, tiled=True)
 
     w_query, w_key, w_value = (in_hbm(w) for w in (w_query, w_key, w_value))
     weights, kv_own = project_kv_own(place, in_hbm(own), w_key, w_value)
     kv = project_kv(other, weights, kv_own)
-    kvs = [kv] + [lax.ppermute(kv, "ctx", chip_shift(d)) for d in (1, 2, 3)]
     query, bias = project_query(
         place, own, other, w_query, segments, tile_mask[0], mask_other
     )
+    far, query, kv = lax.optimization_barrier((far, query, kv))
+    far_other = {d: lax.ppermute(far[d], "ctx", CORE) for d in (1, 3, 2)}
+    kvs = [kv] + [project_kv_pair(far[d], far_other[d], weights) for d in (1, 2, 3)]
 
     dq, g0, g1, g2, g3 = attention(place, query, up, up_other, kvs, bias)
     dq_other = lax.ppermute(dq, "ctx", CORE)
@@ -483,17 +484,17 @@
     dkv = sum_four(g0, *back)
     dkv_other = lax.ppermute(dkv, "ctx", CORE)
 
-    gathered, dkv_late = lax.optimization_barrier((gathered, dkv_other))
-    tokens_t = transpose(in_hbm(gathered))
-
-    packed = pack(place, dq, dq_other, dkv, dkv_late)
+    tokens_t = transpose(
+        [own, other] + [part for d in (1, 2, 3) for part in (far[d], far_other[d])]
+    )
+    packed = pack(place, dq, dq_other, dkv, dkv_other)
     columns = [packed[0]] + [
         lax.ppermute(packed[d], "ctx", chip_shift(d)) for d in (1, 2, 3)
     ]
     terms = weight_grad(place, tokens_t, columns)
     y_parts = [terms[0]] + [lax.ppermute(terms[d], "dp", y_shift(d)) for d in (1, 2, 3)]
     grad_tokens = input_grad(
-        place, dq, dq_other, dkv, dkv_late, w_query, w_key, w_value
+        place, dq, dq_other, dkv, dkv_other, w_query, w_key, w_value
     )
     y_parts, grad_tokens = lax.optimization_barrier((y_parts, grad_tokens))
     y_sum = sum_four(*y_parts)

time: 98.9 us -> 94.2 us (0.952)
  between operations: 14.2 us -> 0.81 us
  waiting for transfers between devices: 22.8 us -> 28.5 us
  local copies, waits for them, and re-layouts: 0.02 us -> 2.34 us
  blocking collectives: 16.4 us -> 18.2 us
    ppermute x3 -> x6, waiting for transfers between devices: 3.72 us -> 12.7 us  [the longest x3 11.7 us: shards(): far = {d: lax.ppermute(own, 'ctx', chip_shift(d)) for d in (1, 3, 2)}]
    ppermute x3, waiting for transfers between devices: 11.6 us -> 8.18 us  [shards(): lax.ppermute(g, 'ctx', chip_shift(CHIPS - d))]
    unnamed x8 -> x10, local copies, waits for them, and re-layouts: 0.02 us -> 2.34 us
    ppermute x3, waiting for transfers between devices: 3.55 us -> 5.76 us  [shards(): lax.ppermute(packed[d], 'ctx', chip_shift(d))]
    all_to_all x1, blocking collectives: 16.4 us -> 18.2 us  [shards(): lax.all_to_all(y_sum, 'dp', 0, 0, tiled=True, axis_index_groups=Z_GROUPS)]
    ppermute x1, waiting for transfers between devices: 1.12 us -> 0.01 us  [shards(): mask_other = lax.ppermute(tile_mask[0], 'ctx', CORE)]
    ppermute x3, starting transfers between devices: 4.49 us -> 3.5 us  [shards(): lax.ppermute(packed[d], 'ctx', chip_shift(d))]
    ppermute x3 -> x6, starting transfers between devices: 4.52 us -> 5.05 us  [the longest x3 4.52 us: shards(): far = {d: lax.ppermute(own, 'ctx', chip_shift(d)) for d in (1, 3, 2)}]
  transfers between devices with their start and end apart: 18 -> 20, of which waited for: 11 -> 13; matrix products, arithmetic and copies ran while one was open for 0% -> 0% of each run, Pallas kernels for 25% -> 16%
where the time goes in v3:
time: 94.2 us; the launch traced here: 93.4 us
  waiting for transfers between devices  28.5 us (30%)
  Pallas kernels  26.8 us (28%)
  blocking collectives  18.2 us (19%)
  starting transfers between devices  16.7 us (18%)
  local copies, waits for them, and re-layouts  2.34 us (2%)
    all_to_all x1, blocking collectives, shards(): lax.all_to_all(y_sum, 'dp', 0, 0, tiled=True, axis_index_groups=Z_GROUPS)  18.2 us
    ppermute x3, waiting for transfers between devices, shards(): far = {d: lax.ppermute(own, 'ctx', chip_shift(d)) for d in (1, 3, 2)}  11.7 us
    pallas_call x1, Pallas kernels, attention(): pl.pallas_call(attention_kernel, grid_spec=pltpu.PrefetchScalarGridSpec(n...  9.38 us
    ppermute x3, waiting for transfers between devices, shards(): lax.ppermute(g, 'ctx', chip_shift(CHIPS - d))  8.18 us
    pallas_call x1, Pallas kernels, input_grad(): pl.pallas_call(input_kernel, in_specs=[SCALARS] + [WHOLE] * 4 + [STAY] *...  6.88 us
    ppermute x3, waiting for transfers between devices, shards(): lax.ppermute(packed[d], 'ctx', chip_shift(d))  5.76 us
    ppermute x3, starting transfers between devices, shards(): lax.ppermute(terms[d], 'dp', y_shift(d))  5 us
    ppermute x3, starting transfers between devices, shards(): far = {d: lax.ppermute(own, 'ctx', chip_shift(d)) for d in (1, 3, 2)}  4.52 us
  transfers between devices with their start and end apart: 20, of which 13 were waited for; matrix products, arithmetic and copies ran while one was open for 0% of the time, Pallas kernels for 16%

profile of v3, /device:TPU:8, one launch (start us, length us, event | category | flops | bytes accessed | tf_op | source)
XLA Modules:
  0.0 93.4 jit_solution(17661809146163974077)
XLA Ops:
  0.6 0.0 copy-start.4
  0.6 0.1 collective-permute-start
  0.7 2.8 %collective-permute-start.3 = (bf16[128,1536]{1,0:T(8,128)(2,1)}, bf16[128,1536]{1,0:T(8,128)(2,1)S(1)}, u32[]{:S(2)}, u32[]{:S(2)}) collective-permute-start(bf16[128,1536]{1,0:T(8,128)(2,1)} %bitcast.11), channel_id=1, source_target_pairs={{0,192},{32,224},{64,0},{96,32},{128,64},{160,96},{192,128},{224,1... | collective-permute-start | bytes 1179656 | tf_op jit(solution)/shard_map/ppermute | solution.py:464
  3.6 0.8 collective-permute-start.2
  4.4 0.9 collective-permute-start.1
  5.3 0.0 collective-permute-start.4
  5.3 0.1 pad_add_fusion.place
  5.3 2.3 %project_kv_own.1 = (bf16[1536,256]{1,0:T(8,128)(2,1)S(1)}, bf16[128,256]{1,0:T(8,128)(2,1)S(1)}) custom-call(s32[4]{0:T(128)S(1)} %pad_add_fusion.place, bf16[128,1536]{1,0:T(8,128)(2,1)} %bitcast.14, bf16[1536,256]{1,0:T(8,128)(2,1)} %w_key.3, bf16[1536,256]{1,0:T(8,128)(2,1)} %w_value.3), custom_call_target="tpu_custom_call" | custom-call | flops 100663296 | bytes 1179648 | tf_op jit(solution)/shard_map/project_kv_own/pallas_call | solution.py:93
  7.6 0.0 collective-permute-done.other.refs_1_
  7.6 0.3 project_kv.1.kv0
  7.9 0.0 collective-permute-done.4.mask_other
  7.9 0.0 copy-start
  7.9 1.0 %copy-done = bf16[1,128,1536]{2,1,0:T(8,128)(2,1)S(1)} copy-done((bf16[1,128,1536]{2,1,0:T(8,128)(2,1)S(1)}, bf16[1,128,1536]{2,1,0:T(8,128)(2,1)}, u32[]{:S(2)}) %copy-start) | copy-done | bytes 393240
  8.9 0.0 copy-start.2
  8.9 0.7 copy-done.2
  9.6 0.7 copy-done.3
  10.2 3.0 %project_query.1 = (bf16[256,768]{1,0:T(8,128)(2,1)S(1)}, f32[1024,256]{1,0:T(8,128)S(1)}) custom-call(s32[4]{0:T(128)S(1)} %pad_add_fusion.place, bf16[128,1536]{1,0:T(8,128)(2,1)S(1)} %bitcast.15, bf16[128,1536]{1,0:T(8,128)(2,1)S(1)} %collective-permute-done.other.refs_1_, bf16[1536,1536]{1,0:T(8,128)(2,1)} %w_query.3, s32[1,1024]{1,0:T(1,128)S(1)} %copy-done.2, ...), custom_call_target="tpu_custom_call" | custom-call | flops 603979776 | bytes 3538944 | tf_op jit(solution)/shard_map/project_query/pallas_call | solution.py:194
  13.2 8.1 %collective-permute-done.3.refs_6_.own = bf16[128,1536]{1,0:T(8,128)(2,1)S(1)} collective-permute-done((bf16[128,1536]{1,0:T(8,128)(2,1)}, bf16[128,1536]{1,0:T(8,128)(2,1)S(1)}, u32[]{:S(2)}, u32[]{:S(2)}) %collective-permute-start.3) | collective-permute-done | bytes 393248 | tf_op jit(solution)/shard_map/ppermute | solution.py:464
  21.3 0.0 collective-permute-done.2.refs_4_.own
  21.3 3.6 %collective-permute-done.1.refs_2_.own = bf16[128,1536]{1,0:T(8,128)(2,1)S(1)} collective-permute-done((bf16[128,1536]{1,0:T(8,128)(2,1)}, bf16[128,1536]{1,0:T(8,128)(2,1)S(1)}, u32[]{:S(2)}, u32[]{:S(2)}) %collective-permute-start.1) | collective-permute-done | bytes 393248 | tf_op jit(solution)/shard_map/ppermute | solution.py:464
  24.9 0.0 collective-permute-start.5
  24.9 0.5 collective-permute-start.6
  25.4 0.0 collective-permute-start.7
  25.4 0.0 copy-done.4
  25.4 0.5 collective-permute-start.8
  25.9 0.7 collective-permute-done.5.refs_3_.other
  26.6 0.4 project_kv_pair.3.kv1
  27.0 0.2 collective-permute-done.6.refs_5_.other
  27.2 0.4 project_kv_pair.4.kv2
  27.6 0.2 collective-permute-done.7.refs_7_.other
  27.7 0.4 project_kv_pair.5.kv3
  28.1 0.2 collective-permute-done.8.up_other
  28.3 9.4 %attention.1 = (bf16[256,768]{1,0:T(8,128)(2,1)S(1)}, f32[256,256]{1,0:T(8,128)S(1)}, bf16[256,256]{1,0:T(8,128)(2,1)S(1)}, bf16[256,256]{1,0:T(8,128)(2,1)S(1)}, bf16[256,256]{1,0:T(8,128)(2,1)S(1)}) custom-call(s32[4]{0:T(128)S(1)} %pad_add_fusion.place, bf16[256,768]{1,0:T(8,128)(2,1)S(1)} %get-tuple-element.35.query, bf16[128,1536]{1,0:T(8,128)(2,1)S(1)} %bitcast.22, ...), custom_call_target="tpu_custom_call" | custom-call | flops 4026531840 | bytes 4194304 | tf_op jit(solution)/shard_map/attention/pallas_call | solution.py:252
  37.7 0.2 collective-permute-start.9
  37.9 0.6 collective-permute-start.10
  38.5 0.8 collective-permute-start.11
  39.3 0.8 collective-permute-start.12
  40.2 4.1 %collective-permute-done.10.b = bf16[256,256]{1,0:T(8,128)(2,1)S(1)} collective-permute-done((bf16[256,256]{1,0:T(8,128)(2,1)S(1)}, bf16[256,256]{1,0:T(8,128)(2,1)S(1)}, u32[]{:S(2)}, u32[]{:S(2)}) %collective-permute-start.10) | collective-permute-done | bytes 131104 | tf_op jit(solution)/shard_map/ppermute | solution.py:482
  44.2 2.2 %collective-permute-done.11.c = bf16[256,256]{1,0:T(8,128)(2,1)S(1)} collective-permute-done((bf16[256,256]{1,0:T(8,128)(2,1)S(1)}, bf16[256,256]{1,0:T(8,128)(2,1)S(1)}, u32[]{:S(2)}, u32[]{:S(2)}) %collective-permute-start.11) | collective-permute-done | bytes 131104 | tf_op jit(solution)/shard_map/ppermute | solution.py:482
  46.4 1.9 %collective-permute-done.12.d = bf16[256,256]{1,0:T(8,128)(2,1)S(1)} collective-permute-done((bf16[256,256]{1,0:T(8,128)(2,1)S(1)}, bf16[256,256]{1,0:T(8,128)(2,1)S(1)}, u32[]{:S(2)}, u32[]{:S(2)}) %collective-permute-start.12) | collective-permute-done | bytes 131104 | tf_op jit(solution)/shard_map/ppermute | solution.py:482
  48.3 0.1 sum_four.2.dkv
  48.4 0.1 collective-permute-start.13
  48.5 1.3 %collective-permute-done.13.dkv_other = bf16[256,256]{1,0:T(8,128)(2,1)S(1)} collective-permute-done((bf16[256,256]{1,0:T(8,128)(2,1)S(1)}, bf16[256,256]{1,0:T(8,128)(2,1)S(1)}, u32[]{:S(2)}, u32[]{:S(2)}) %collective-permute-start.13) | collective-permute-done | bytes 131104 | tf_op jit(solution)/shard_map/ppermute | solution.py:485
  49.8 0.0 collective-permute-done.9.dq_other
  49.8 0.6 pack.1
  50.5 0.1 collective-permute-start.14
  50.6 2.3 %collective-permute-start.15 = (bf16[256,256]{1,0:T(8,128)(2,1)S(1)}, bf16[256,256]{1,0:T(8,128)(2,1)S(1)}, u32[]{:S(2)}, u32[]{:S(2)}) collective-permute-start(bf16[256,256]{1,0:T(8,128)(2,1)S(1)} %get-tuple-element.45), channel_id=1, source_target_pairs={{0,128},{32,160},{64,192},{96,224},{128,0},{160,32},{192,64},{224,... | collective-permute-start | bytes 393224 | tf_op jit(solution)/shard_map/ppermute | solution.py:492
  52.9 1.1 %collective-permute-start.16 = (bf16[256,256]{1,0:T(8,128)(2,1)S(1)}, bf16[256,256]{1,0:T(8,128)(2,1)S(1)}, u32[]{:S(2)}, u32[]{:S(2)}) collective-permute-start(bf16[256,256]{1,0:T(8,128)(2,1)S(1)} %get-tuple-element.46), channel_id=1, source_target_pairs={{0,192},{32,224},{64,0},{96,32},{128,64},{160,96},{192,128},{224,1... | collective-permute-start | bytes 393224 | tf_op jit(solution)/shard_map/ppermute | solution.py:492
  54.0 0.0 copy-done.1
  54.0 1.0 %transpose_tokens.1.tokens_t = bf16[1536,1024]{1,0:T(8,128)(2,1)S(1)} custom-call(bf16[128,1536]{1,0:T(8,128)(2,1)S(1)} %bitcast.16, bf16[128,1536]{1,0:T(8,128)(2,1)S(1)} %collective-permute-done.other.refs_1_, bf16[128,1536]{1,0:T(8,128)(2,1)S(1)} %collective-permute-done.1.refs_2_.own, bf16[128,1536]{1,0:T(8,128)(2,1)S(1)} %collective-permute-done.5.refs_3_.other, ...), custom_call_target="tpu_custom_call" | custom-call | bytes 6291456 | tf_op jit(solution)/shard_map/transpose_tokens/pallas_call | solution.py:351
  55.0 5.1 %collective-permute-done.14.b = bf16[256,256]{1,0:T(8,128)(2,1)S(1)} collective-permute-done((bf16[256,256]{1,0:T(8,128)(2,1)S(1)}, bf16[256,256]{1,0:T(8,128)(2,1)S(1)}, u32[]{:S(2)}, u32[]{:S(2)}) %collective-permute-start.14) | collective-permute-done | bytes 131104 | tf_op jit(solution)/shard_map/ppermute | solution.py:492
  60.1 0.0 collective-permute-done.15.c
  60.1 0.6 collective-permute-done.16.d
  60.8 1.5 %weight_grad.1 = (f32[384,256]{1,0:T(8,128)S(1)}, bf16[384,256]{1,0:T(8,128)(2,1)S(1)}, bf16[384,256]{1,0:T(8,128)(2,1)S(1)}, bf16[384,256]{1,0:T(8,128)(2,1)S(1)}) custom-call(s32[4]{0:T(128)S(1)} %pad_add_fusion.place, bf16[1536,1024]{1,0:T(8,128)(2,1)S(1)} %transpose_tokens.1.tokens_t, bf16[256,256]{1,0:T(8,128)(2,1)S(1)} %get-tuple-element.43.a, ...), custom_call_target="tpu_custom_call" | custom-call | flops 805306368 | bytes 4325376 | tf_op jit(solution)/shard_map/weight_grad/pallas_call | solution.py:371
  62.3 1.7 %collective-permute-start.17 = (bf16[384,256]{1,0:T(8,128)(2,1)S(1)}, bf16[384,256]{1,0:T(8,128)(2,1)S(1)}, u32[]{:S(2)}, u32[]{:S(2)}) collective-permute-start(bf16[384,256]{1,0:T(8,128)(2,1)S(1)} %get-tuple-element.48), channel_id=1, source_target_pairs={{0,8},{1,9},{2,10},{3,11},{4,12},{5,13},{6,14},{7,15},{8,16},{9,17... | collective-permute-start | bytes 589832 | tf_op jit(solution)/shard_map/ppermute | solution.py:495
  63.9 0.9 %collective-permute-start.18 = (bf16[384,256]{1,0:T(8,128)(2,1)S(1)}, bf16[384,256]{1,0:T(8,128)(2,1)S(1)}, u32[]{:S(2)}, u32[]{:S(2)}) collective-permute-start(bf16[384,256]{1,0:T(8,128)(2,1)S(1)} %get-tuple-element.49), channel_id=1, source_target_pairs={{0,16},{1,17},{2,18},{3,19},{4,20},{5,21},{6,22},{7,23},{8,24},{9,... | collective-permute-start | bytes 589832 | tf_op jit(solution)/shard_map/ppermute | solution.py:495
  64.9 2.4 %collective-permute-start.19 = (bf16[384,256]{1,0:T(8,128)(2,1)S(1)}, bf16[384,256]{1,0:T(8,128)(2,1)S(1)}, u32[]{:S(2)}, u32[]{:S(2)}) collective-permute-start(bf16[384,256]{1,0:T(8,128)(2,1)S(1)} %get-tuple-element.50), channel_id=1, source_target_pairs={{0,24},{1,25},{2,26},{3,27},{4,28},{5,29},{6,30},{7,31},{8,0},{9,1... | collective-permute-start | bytes 589832 | tf_op jit(solution)/shard_map/ppermute | solution.py:495
  67.3 6.9 %input_grad.1 = bf16[128,1536]{1,0:T(8,128)(2,1)} custom-call(s32[4]{0:T(128)S(1)} %pad_add_fusion.place, bf16[256,768]{1,0:T(8,128)(2,1)S(1)} %get-tuple-element.38.dq, bf16[256,768]{1,0:T(8,128)(2,1)S(1)} %collective-permute-done.9.dq_other, bf16[256,256]{1,0:T(8,128)(2,1)S(1)} %sum_four.2.dkv, bf16[256,256]{1,0:T(8,128)(2,1)S(1)} %collective-permute-done.13.dkv_other, ...), custom_call_target="tpu_custom_call" | custom-call | flops 805306368 | bytes 6291456 | tf_op jit(solution)/shard_map/input_grad/pallas_call | solution.py:424
  74.2 0.0 collective-permute-done.17.b
  74.2 0.0 collective-permute-done.18.c
  74.2 0.3 collective-permute-done.19.d
  74.5 0.1 sum_four.3
  74.6 18.2 %all_to_all.11 = bf16[8,48,256]{2,1,0:T(8,128)(2,1)S(1)} all-to-all(bf16[8,48,256]{2,1,0:T(8,128)(2,1)S(1)} %bitcast.17), channel_id=1, replica_groups={{0,1,2,3,4,5,6,7},{8,9,10,11,12,13,14,15},{16,17,18,19,20,21,22,23},{24..., dimensions={0} | all-to-all | bytes 393216 | tf_op jit(solution)/shard_map/all_to_all | solution.py:501
  92.8 0.6 final_sum.1
  (2 shorter events, 0.0 us)
Async XLA Ops:
  0.6 24.8 %copy-start.4 = (bf16[1,128,1536]{2,1,0:T(8,128)(2,1)S(1)}, bf16[1,128,1536]{2,1,0:T(8,128)(2,1)}, u32[]{:S(2)}) copy-start(bf16[1,128,1536]{2,1,0:T(8,128)(2,1)} %param.8) | copy-start | bytes 1179652
  0.6 7.0 %collective-permute-start = (bf16[128,1536]{1,0:T(8,128)(2,1)}, bf16[128,1536]{1,0:T(8,128)(2,1)S(1)}, u32[]{:S(2)}, u32[]{:S(2)}) collective-permute-start(bf16[128,1536]{1,0:T(8,128)(2,1)} %bitcast.10), channel_id=1, source_target_pairs={{0,32},{32,0},{64,96},{96,64},{128,160},{160,128},{192,224},{224,1... | collective-permute-start | bytes 1179656 | tf_op jit(solution)/shard_map/ppermute | solution.py:465
  0.7 20.6 %collective-permute-start.3 = (bf16[128,1536]{1,0:T(8,128)(2,1)}, bf16[128,1536]{1,0:T(8,128)(2,1)S(1)}, u32[]{:S(2)}, u32[]{:S(2)}) collective-permute-start(bf16[128,1536]{1,0:T(8,128)(2,1)} %bitcast.11), channel_id=1, source_target_pairs={{0,192},{32,224},{64,0},{96,32},{128,64},{160,96},{192,128},{224,1... | collective-permute-start | bytes 1179656 | tf_op jit(solution)/shard_map/ppermute | solution.py:464
  3.6 17.7 %collective-permute-start.2 = (bf16[128,1536]{1,0:T(8,128)(2,1)}, bf16[128,1536]{1,0:T(8,128)(2,1)S(1)}, u32[]{:S(2)}, u32[]{:S(2)}) collective-permute-start(bf16[128,1536]{1,0:T(8,128)(2,1)} %bitcast.12), channel_id=1, source_target_pairs={{0,128},{32,160},{64,192},{96,224},{128,0},{160,32},{192,64},{224,... | collective-permute-start | bytes 1179656 | tf_op jit(solution)/shard_map/ppermute | solution.py:464
  4.4 20.5 %collective-permute-start.1 = (bf16[128,1536]{1,0:T(8,128)(2,1)}, bf16[128,1536]{1,0:T(8,128)(2,1)S(1)}, u32[]{:S(2)}, u32[]{:S(2)}) collective-permute-start(bf16[128,1536]{1,0:T(8,128)(2,1)} %bitcast.13), channel_id=1, source_target_pairs={{0,64},{32,96},{64,128},{96,160},{128,192},{160,224},{192,0},{224,... | collective-permute-start | bytes 1179656 | tf_op jit(solution)/shard_map/ppermute | solution.py:464
  5.3 2.6 %collective-permute-start.4 = (s32[1,8]{1,0:T(1,128)}, s32[1,8]{1,0:T(1,128)S(1)}, u32[]{:S(2)}, u32[]{:S(2)}) collective-permute-start(s32[1,8]{1,0:T(1,128)} %bitcast.19), channel_id=1, source_target_pairs={{0,32},{32,0},{64,96},{96,64},{128,160},{160,128},{192,224},{224,1... | collective-permute-start | bytes 104 | tf_op jit(solution)/shard_map/ppermute | solution.py:467
  7.9 1.0 %copy-start = (bf16[1,128,1536]{2,1,0:T(8,128)(2,1)S(1)}, bf16[1,128,1536]{2,1,0:T(8,128)(2,1)}, u32[]{:S(2)}) copy-start(bf16[1,128,1536]{2,1,0:T(8,128)(2,1)} %param.7) | copy-start | bytes 1179652
  8.9 0.7 copy-start.2
  9.6 0.7 copy-start.3
  24.9 1.7 %collective-permute-start.5 = (bf16[128,1536]{1,0:T(8,128)(2,1)S(1)}, bf16[128,1536]{1,0:T(8,128)(2,1)S(1)}, u32[]{:S(2)}, u32[]{:S(2)}) collective-permute-start(bf16[128,1536]{1,0:T(8,128)(2,1)S(1)} %collective-permute-done.1.refs_2_.own), channel_id=1, source_target_pairs={{0,32},{32,0},{64,96},{96,64},{128,160},{160,128},{192,224},{224,1... | collective-permute-start | bytes 1179656 | tf_op jit(solution)/shard_map/ppermute | solution.py:476
  24.9 2.3 %collective-permute-start.6 = (bf16[128,1536]{1,0:T(8,128)(2,1)S(1)}, bf16[128,1536]{1,0:T(8,128)(2,1)S(1)}, u32[]{:S(2)}, u32[]{:S(2)}) collective-permute-start(bf16[128,1536]{1,0:T(8,128)(2,1)S(1)} %collective-permute-done.2.refs_4_.own), channel_id=1, source_target_pairs={{0,32},{32,0},{64,96},{96,64},{128,160},{160,128},{192,224},{224,1... | collective-permute-start | bytes 1179656 | tf_op jit(solution)/shard_map/ppermute | solution.py:476
  25.4 2.3 %collective-permute-start.7 = (bf16[128,1536]{1,0:T(8,128)(2,1)S(1)}, bf16[128,1536]{1,0:T(8,128)(2,1)S(1)}, u32[]{:S(2)}, u32[]{:S(2)}) collective-permute-start(bf16[128,1536]{1,0:T(8,128)(2,1)S(1)} %collective-permute-done.3.refs_6_.own), channel_id=1, source_target_pairs={{0,32},{32,0},{64,96},{96,64},{128,160},{160,128},{192,224},{224,1... | collective-permute-start | bytes 1179656 | tf_op jit(solution)/shard_map/ppermute | solution.py:476
  25.4 2.9 %collective-permute-start.8 = (bf16[128,1536]{1,0:T(8,128)(2,1)S(1)}, bf16[128,1536]{1,0:T(8,128)(2,1)S(1)}, u32[]{:S(2)}, u32[]{:S(2)}) collective-permute-start(bf16[128,1536]{1,0:T(8,128)(2,1)S(1)} %bitcast.21), channel_id=1, source_target_pairs={{0,32},{32,0},{64,96},{96,64},{128,160},{160,128},{192,224},{224,1... | collective-permute-start | bytes 1179656 | tf_op jit(solution)/shard_map/ppermute | solution.py:466
  28.3 25.7 %copy-start.1 = (bf16[1,128,1536]{2,1,0:T(8,128)(2,1)S(1)}, bf16[1,128,1536]{2,1,0:T(8,128)(2,1)}, u32[]{:S(2)}) copy-start(bf16[1,128,1536]{2,1,0:T(8,128)(2,1)} %param.7) | copy-start | bytes 1179652
  37.7 12.1 %collective-permute-start.9 = (bf16[256,768]{1,0:T(8,128)(2,1)S(1)}, bf16[256,768]{1,0:T(8,128)(2,1)S(1)}, u32[]{:S(2)}, u32[]{:S(2)}) collective-permute-start(bf16[256,768]{1,0:T(8,128)(2,1)S(1)} %get-tuple-element.38.dq), channel_id=1, source_target_pairs={{0,32},{32,0},{64,96},{96,64},{128,160},{160,128},{192,224},{224,1... | collective-permute-start | bytes 1179656 | tf_op jit(solution)/shard_map/ppermute | solution.py:480
  37.9 6.3 %collective-permute-start.10 = (bf16[256,256]{1,0:T(8,128)(2,1)S(1)}, bf16[256,256]{1,0:T(8,128)(2,1)S(1)}, u32[]{:S(2)}, u32[]{:S(2)}) collective-permute-start(bf16[256,256]{1,0:T(8,128)(2,1)S(1)} %get-tuple-element.40), channel_id=1, source_target_pairs={{0,192},{32,224},{64,0},{96,32},{128,64},{160,96},{192,128},{224,1... | collective-permute-start | bytes 393224 | tf_op jit(solution)/shard_map/ppermute | solution.py:482
  38.5 7.9 %collective-permute-start.11 = (bf16[256,256]{1,0:T(8,128)(2,1)S(1)}, bf16[256,256]{1,0:T(8,128)(2,1)S(1)}, u32[]{:S(2)}, u32[]{:S(2)}) collective-permute-start(bf16[256,256]{1,0:T(8,128)(2,1)S(1)} %get-tuple-element.41), channel_id=1, source_target_pairs={{0,128},{32,160},{64,192},{96,224},{128,0},{160,32},{192,64},{224,... | collective-permute-start | bytes 393224 | tf_op jit(solution)/shard_map/ppermute | solution.py:482
  39.3 9.0 %collective-permute-start.12 = (bf16[256,256]{1,0:T(8,128)(2,1)S(1)}, bf16[256,256]{1,0:T(8,128)(2,1)S(1)}, u32[]{:S(2)}, u32[]{:S(2)}) collective-permute-start(bf16[256,256]{1,0:T(8,128)(2,1)S(1)} %get-tuple-element.42), channel_id=1, source_target_pairs={{0,64},{32,96},{64,128},{96,160},{128,192},{160,224},{192,0},{224,... | collective-permute-start | bytes 393224 | tf_op jit(solution)/shard_map/ppermute | solution.py:482
  48.4 1.4 %collective-permute-start.13 = (bf16[256,256]{1,0:T(8,128)(2,1)S(1)}, bf16[256,256]{1,0:T(8,128)(2,1)S(1)}, u32[]{:S(2)}, u32[]{:S(2)}) collective-permute-start(bf16[256,256]{1,0:T(8,128)(2,1)S(1)} %sum_four.2.dkv), channel_id=1, source_target_pairs={{0,32},{32,0},{64,96},{96,64},{128,160},{160,128},{192,224},{224,1... | collective-permute-start | bytes 393224 | tf_op jit(solution)/shard_map/ppermute | solution.py:485
  50.5 9.6 %collective-permute-start.14 = (bf16[256,256]{1,0:T(8,128)(2,1)S(1)}, bf16[256,256]{1,0:T(8,128)(2,1)S(1)}, u32[]{:S(2)}, u32[]{:S(2)}) collective-permute-start(bf16[256,256]{1,0:T(8,128)(2,1)S(1)} %get-tuple-element.44), channel_id=1, source_target_pairs={{0,64},{32,96},{64,128},{96,160},{128,192},{160,224},{192,0},{224,... | collective-permute-start | bytes 393224 | tf_op jit(solution)/shard_map/ppermute | solution.py:492
  50.6 9.6 %collective-permute-start.15 = (bf16[256,256]{1,0:T(8,128)(2,1)S(1)}, bf16[256,256]{1,0:T(8,128)(2,1)S(1)}, u32[]{:S(2)}, u32[]{:S(2)}) collective-permute-start(bf16[256,256]{1,0:T(8,128)(2,1)S(1)} %get-tuple-element.45), channel_id=1, source_target_pairs={{0,128},{32,160},{64,192},{96,224},{128,0},{160,32},{192,64},{224,... | collective-permute-start | bytes 393224 | tf_op jit(solution)/shard_map/ppermute | solution.py:492
  52.9 7.9 %collective-permute-start.16 = (bf16[256,256]{1,0:T(8,128)(2,1)S(1)}, bf16[256,256]{1,0:T(8,128)(2,1)S(1)}, u32[]{:S(2)}, u32[]{:S(2)}) collective-permute-start(bf16[256,256]{1,0:T(8,128)(2,1)S(1)} %get-tuple-element.46), channel_id=1, source_target_pairs={{0,192},{32,224},{64,0},{96,32},{128,64},{160,96},{192,128},{224,1... | collective-permute-start | bytes 393224 | tf_op jit(solution)/shard_map/ppermute | solution.py:492
  62.3 11.9 %collective-permute-start.17 = (bf16[384,256]{1,0:T(8,128)(2,1)S(1)}, bf16[384,256]{1,0:T(8,128)(2,1)S(1)}, u32[]{:S(2)}, u32[]{:S(2)}) collective-permute-start(bf16[384,256]{1,0:T(8,128)(2,1)S(1)} %get-tuple-element.48), channel_id=1, source_target_pairs={{0,8},{1,9},{2,10},{3,11},{4,12},{5,13},{6,14},{7,15},{8,16},{9,17... | collective-permute-start | bytes 589832 | tf_op jit(solution)/shard_map/ppermute | solution.py:495
  63.9 10.3 %collective-permute-start.18 = (bf16[384,256]{1,0:T(8,128)(2,1)S(1)}, bf16[384,256]{1,0:T(8,128)(2,1)S(1)}, u32[]{:S(2)}, u32[]{:S(2)}) collective-permute-start(bf16[384,256]{1,0:T(8,128)(2,1)S(1)} %get-tuple-element.49), channel_id=1, source_target_pairs={{0,16},{1,17},{2,18},{3,19},{4,20},{5,21},{6,22},{7,23},{8,24},{9,... | collective-permute-start | bytes 589832 | tf_op jit(solution)/shard_map/ppermute | solution.py:495
  64.9 9.7 %collective-permute-start.19 = (bf16[384,256]{1,0:T(8,128)(2,1)S(1)}, bf16[384,256]{1,0:T(8,128)(2,1)S(1)}, u32[]{:S(2)}, u32[]{:S(2)}) collective-permute-start(bf16[384,256]{1,0:T(8,128)(2,1)S(1)} %get-tuple-element.50), channel_id=1, source_target_pairs={{0,24},{1,25},{2,26},{3,27},{4,28},{5,29},{6,30},{7,31},{8,0},{9,1... | collective-permute-start | bytes 589832 | tf_op jit(solution)/shard_map/ppermute | solution.py:495

commit v4 on v3

--- a/solution.py
+++ b/solution.py
@@ -105,23 +105,6 @@
     )(place, own, w_key, w_value)
 
 
-def kv_pair_kernel(own, other, weights, out):
-    out[:TILE] = dot(own[...], weights[...]).astype(BF)
-    out[TILE:] = dot(other[...], weights[...]).astype(BF)
-
-
-def project_kv_pair(own, other, weights):
-    return pl.pallas_call(
-        kv_pair_kernel,
-        in_specs=[WHOLE] * 3,
-        out_specs=WHOLE,
-        out_shape=jax.ShapeDtypeStruct((2 * TILE, 2 * HD), BF),
-        compiler_params=PARAMS,
-        cost_estimate=cost(4 * TILE * D * 256, 2 * (2 * TILE * D + D * 256)),
-        name="project_kv_pair",
-    )(own, other, weights)
-
-
 def kv_kernel(other, weights, kv_own, out):
     out[:TILE] = kv_own[...]
     out[TILE:] = dot(other[...], weights[...]).astype(BF)
@@ -140,8 +123,15 @@
 
 
 def query_kernel(
-    place, own, other, w_query, segments, mask_own, mask_other, out, bias, weights, sems
+    place, own, other, w_query, segments_far, mask_far, mask_other, out, bias,
+    weights, segments, mask_own, sems, small_sems,
 ):
+    small = [
+        pltpu.make_async_copy(segments_far, segments, small_sems.at[0]),
+        pltpu.make_async_copy(mask_far, mask_own, small_sems.at[1]),
+    ]
+    for copy in small:
+        copy.start()
     columns = pl.ds(pl.multiple_of(place[1] * GF, HD), GF)
     copies = []
     for chunk in range(Q_CHUNKS):
@@ -151,6 +141,8 @@
         )
     for copy in copies:
         copy.start()
+    for copy in small:
+        copy.wait()
 
     chip, core = place[0], place[1]
     passages = segments[...]
@@ -193,13 +185,19 @@
 def project_query(place, own, other, w_query, segments, mask_own, mask_other):
     return pl.pallas_call(
         query_kernel,
-        in_specs=[SCALARS, WHOLE, WHOLE, STAY, WHOLE, SCALARS, SCALARS],
+        in_specs=[SCALARS, WHOLE, WHOLE, STAY, STAY, STAY, SCALARS],
         out_specs=[WHOLE, WHOLE],
         out_shape=[
             jax.ShapeDtypeStruct((2 * TILE, GF), BF),
             jax.ShapeDtypeStruct((KEYS, 2 * TILE), F32),
         ],
-        scratch_shapes=[pltpu.VMEM((D, GF), BF), pltpu.SemaphoreType.DMA((Q_CHUNKS,))],
+        scratch_shapes=[
+            pltpu.VMEM((D, GF), BF),
+            pltpu.VMEM((1, KEYS), jnp.int32),
+            pltpu.SMEM((1, KEYS // TILE), jnp.int32),
+            pltpu.SemaphoreType.DMA((Q_CHUNKS,)),
+            pltpu.SemaphoreType.DMA((2,)),
+        ],
         compiler_params=PARAMS,
         cost_estimate=cost(2 * 256 * D * GF, 2 * (256 * D + D * GF + 256 * GF)),
         name="project_query",
@@ -461,7 +459,6 @@
     dp = lax.axis_index("dp")
     place = jnp.stack([ctx // 2, ctx % 2, dp // ZS, dp % ZS]).astype(jnp.int32)
     own, up = tokens[0], grad_heads[0]
-    far = {d: lax.ppermute(own, "ctx", chip_shift(d)) for d in (1, 3, 2)}
     other = lax.ppermute(own, "ctx", CORE)
     up_other = lax.ppermute(up, "ctx", CORE)
     mask_other = lax.ppermute(tile_mask[0], "ctx", CORE)
@@ -469,21 +466,29 @@
     w_query, w_key, w_value = (in_hbm(w) for w in (w_query, w_key, w_value))
     weights, kv_own = project_kv_own(place, in_hbm(own), w_key, w_value)
     kv = project_kv(other, weights, kv_own)
+    kvs = [kv] + [lax.ppermute(kv, "ctx", chip_shift(d)) for d in (1, 2, 3)]
     query, bias = project_query(
-        place, own, other, w_query, segments, tile_mask[0], mask_other
+        place, own, other, w_query, in_hbm(segments), in_hbm(tile_mask[0]), mask_other
     )
-    far, query, kv = lax.optimization_barrier((far, query, kv))
-    far_other = {d: lax.ppermute(far[d], "ctx", CORE) for d in (1, 3, 2)}
-    kvs = [kv] + [project_kv_pair(far[d], far_other[d], weights) for d in (1, 2, 3)]
-
-    dq, g0, g1, g2, g3 = attention(place, query, up, up_other, kvs, bias)
+    far = {2: lax.ppermute(own, "ctx", chip_shift(2))}
+    kvs, query, far, late_own = lax.optimization_barrier((kvs, query, far, own))
+    near = {d: lax.ppermute(late_own, "ctx", chip_shift(d)) for d in (1, 3)}
+
+    far_other = {2: lax.ppermute(far[2], "ctx", CORE)}
+    grads = attention(place, query, up, up_other, kvs, bias)
+    near, far_other, (dq, g0, g1, g2, g3) = lax.optimization_barrier((near, far_other, grads))
     dq_other = lax.ppermute(dq, "ctx", CORE)
     back = [
         lax.ppermute(g, "ctx", chip_shift(CHIPS - d)) for d, g in ((1, g1), (2, g2), (3, g3))
     ]
+    back, dq_other = lax.optimization_barrier((back, dq_other))
     dkv = sum_four(g0, *back)
     dkv_other = lax.ppermute(dkv, "ctx", CORE)
 
+    near, dkv_other = lax.optimization_barrier((near, dkv_other))
+    for d in (1, 3):
+        far[d] = near[d]
+        far_other[d] = lax.ppermute(near[d], "ctx", CORE)
     tokens_t = transpose(
         [own, other] + [part for d in (1, 2, 3) for part in (far[d], far_other[d])]
     )

time: 94.2 us -> 91.6 us (0.972)
  waiting for transfers between devices: 28.5 us -> 24 us
  starting transfers between devices: 16.7 us -> 20.5 us
  local copies, waits for them, and re-layouts: 2.34 us -> 0.01 us
    ppermute x6 -> x9, starting transfers between devices: 5.05 us -> 9.17 us  [the longest x1 3.11 us: shards(): far = {2: lax.ppermute(own, 'ctx', chip_shift(2))}]
    ppermute x6 -> x9, waiting for transfers between devices: 12.7 us -> 8.78 us  [the longest x3 5.05 us: shards(): kvs = [kv] + [lax.ppermute(kv, 'ctx', chip_shift(d)) for d in (1, 2, 3)]]
    unnamed x10 -> x2, local copies, waits for them, and re-layouts: 2.34 us -> 0.01 us
    pallas_call x1, Pallas kernels: 0.99 us -> 1.99 us  [transpose(): pl.pallas_call(transpose_kernel, in_specs=[WHOLE] * 8, out_specs=WHOLE, o...]
    pallas_call x4 -> x1, Pallas kernels: 4.1 us -> 3.47 us  [project_query(): pl.pallas_call(query_kernel, in_specs=[SCALARS, WHOLE, WHOLE, STAY, STAY,...]
  transfers between devices with their start and end apart: 20 -> 23, of which waited for: 13 -> 11; matrix products, arithmetic and copies ran while one was open for 0% -> 0% of each run, Pallas kernels for 16% -> 27%
where the time goes in v4:
time: 91.6 us; the launch traced here: 90.8 us
  Pallas kernels  27.2 us (30%)
  waiting for transfers between devices  24 us (26%)
  starting transfers between devices  20.5 us (22%)
  blocking collectives  18.2 us (20%)
    all_to_all x1, blocking collectives, shards(): lax.all_to_all(y_sum, 'dp', 0, 0, tiled=True, axis_index_groups=Z_GROUPS)  18.2 us
    pallas_call x1, Pallas kernels, attention(): pl.pallas_call(attention_kernel, grid_spec=pltpu.PrefetchScalarGridSpec(n...  9.39 us
    ppermute x3, waiting for transfers between devices, shards(): lax.ppermute(g, 'ctx', chip_shift(CHIPS - d))  8.65 us
    pallas_call x1, Pallas kernels, input_grad(): pl.pallas_call(input_kernel, in_specs=[SCALARS] + [WHOLE] * 4 + [STAY] *...  6.88 us
    ppermute x3, waiting for transfers between devices, shards(): kvs = [kv] + [lax.ppermute(kv, 'ctx', chip_shift(d)) for d in (1, 2, 3)]  5.05 us
    ppermute x3, starting transfers between devices, shards(): lax.ppermute(terms[d], 'dp', y_shift(d))  5 us
    ppermute x3, waiting for transfers between devices, shards(): lax.ppermute(packed[d], 'ctx', chip_shift(d))  4.95 us
    pallas_call x1, Pallas kernels, project_query(): pl.pallas_call(query_kernel, in_specs=[SCALARS, WHOLE, WHOLE, STAY, STAY,...  3.47 us
  transfers between devices with their start and end apart: 23, of which 11 were waited for; matrix products, arithmetic and copies ran while one was open for 0% of the time, Pallas kernels for 27%

profile of v4, /device:TPU:8, one launch (start us, length us, event | category | flops | bytes accessed | tf_op | source)
XLA Modules:
  0.0 90.8 jit_solution(17497377253891160208)
XLA Ops:
  0.6 0.0 copy-start
  0.6 0.1 collective-permute-start
  0.7 3.1 %collective-permute-start.5 = (bf16[128,1536]{1,0:T(8,128)(2,1)}, bf16[128,1536]{1,0:T(8,128)(2,1)S(1)}, u32[]{:S(2)}, u32[]{:S(2)}) collective-permute-start(bf16[128,1536]{1,0:T(8,128)(2,1)} %bitcast.4.own.refs_0_), channel_id=1, source_target_pairs={{0,128},{32,160},{64,192},{96,224},{128,0},{160,32},{192,64},{224,... | collective-permute-start | bytes 1179656 | tf_op jit(solution)/shard_map/ppermute | solution.py:473
  3.9 0.1 collective-permute-start.9
  4.0 0.4 collective-permute-start.4
  4.4 0.1 pad_add_fusion.place
  4.4 2.3 %project_kv_own.1 = (bf16[1536,256]{1,0:T(8,128)(2,1)S(1)}, bf16[128,256]{1,0:T(8,128)(2,1)S(1)}) custom-call(s32[4]{0:T(128)S(1)} %pad_add_fusion.place, bf16[128,1536]{1,0:T(8,128)(2,1)} %bitcast.4.own.refs_0_, bf16[1536,256]{1,0:T(8,128)(2,1)} %w_key.3, bf16[1536,256]{1,0:T(8,128)(2,1)} %w_value.3), custom_call_target="tpu_custom_call" | custom-call | flops 100663296 | bytes 1179648 | tf_op jit(solution)/shard_map/project_kv_own/pallas_call | solution.py:93
  6.7 0.0 collective-permute-done.other.refs_1_
  6.7 0.3 project_kv.1.kv0
  7.0 1.2 %collective-permute-start.3 = (bf16[256,256]{1,0:T(8,128)(2,1)S(1)}, bf16[256,256]{1,0:T(8,128)(2,1)S(1)}, u32[]{:S(2)}, u32[]{:S(2)}) collective-permute-start(bf16[256,256]{1,0:T(8,128)(2,1)S(1)} %project_kv.1.kv0), channel_id=1, source_target_pairs={{0,192},{32,224},{64,0},{96,32},{128,64},{160,96},{192,128},{224,1... | collective-permute-start | bytes 393224 | tf_op jit(solution)/shard_map/ppermute | solution.py:469
  8.2 1.5 %collective-permute-start.2 = (bf16[256,256]{1,0:T(8,128)(2,1)S(1)}, bf16[256,256]{1,0:T(8,128)(2,1)S(1)}, u32[]{:S(2)}, u32[]{:S(2)}) collective-permute-start(bf16[256,256]{1,0:T(8,128)(2,1)S(1)} %project_kv.1.kv0), channel_id=1, source_target_pairs={{0,128},{32,160},{64,192},{96,224},{128,0},{160,32},{192,64},{224,... | collective-permute-start | bytes 393224 | tf_op jit(solution)/shard_map/ppermute | solution.py:469
  9.7 0.0 collective-permute-done.4.mask_other
  9.7 0.0 collective-permute-start.1
  9.7 3.5 %project_query.1 = (bf16[256,768]{1,0:T(8,128)(2,1)S(1)}, f32[1024,256]{1,0:T(8,128)S(1)}) custom-call(s32[4]{0:T(128)S(1)} %pad_add_fusion.place, bf16[128,1536]{1,0:T(8,128)(2,1)} %bitcast.4.own.refs_0_, bf16[128,1536]{1,0:T(8,128)(2,1)S(1)} %collective-permute-done.other.refs_1_, bf16[1536,1536]{1,0:T(8,128)(2,1)} %w_query.3, s32[1,1024]{1,0:T(1,128)} %segments_far.1, ...), custom_call_target="tpu_custom_call" | custom-call | flops 603979776 | bytes 3538944 | tf_op jit(solution)/shard_map/project_query/pallas_call | solution.py:186
  13.2 1.4 %collective-permute-done.5.refs_4_ = bf16[128,1536]{1,0:T(8,128)(2,1)S(1)} collective-permute-done((bf16[128,1536]{1,0:T(8,128)(2,1)}, bf16[128,1536]{1,0:T(8,128)(2,1)S(1)}, u32[]{:S(2)}, u32[]{:S(2)}) %collective-permute-start.5) | collective-permute-done | bytes 393248 | tf_op jit(solution)/shard_map/ppermute | solution.py:473
  14.6 2.8 %collective-permute-done.3.kv3 = bf16[256,256]{1,0:T(8,128)(2,1)S(1)} collective-permute-done((bf16[256,256]{1,0:T(8,128)(2,1)S(1)}, bf16[256,256]{1,0:T(8,128)(2,1)S(1)}, u32[]{:S(2)}, u32[]{:S(2)}) %collective-permute-start.3) | collective-permute-done | bytes 131104 | tf_op jit(solution)/shard_map/ppermute | solution.py:469
  17.4 0.0 collective-permute-done.2.kv2
  17.4 2.2 %collective-permute-done.1.kv1 = bf16[256,256]{1,0:T(8,128)(2,1)S(1)} collective-permute-done((bf16[256,256]{1,0:T(8,128)(2,1)S(1)}, bf16[256,256]{1,0:T(8,128)(2,1)S(1)}, u32[]{:S(2)}, u32[]{:S(2)}) %collective-permute-start.1) | collective-permute-done | bytes 131104 | tf_op jit(solution)/shard_map/ppermute | solution.py:469
  19.6 2.8 %collective-permute-start.7 = (bf16[128,1536]{1,0:T(8,128)(2,1)}, bf16[128,1536]{1,0:T(8,128)(2,1)S(1)}, u32[]{:S(2)}, u32[]{:S(2)}) collective-permute-start(bf16[128,1536]{1,0:T(8,128)(2,1)} %bitcast.4.own.refs_0_), channel_id=1, source_target_pairs={{0,192},{32,224},{64,0},{96,32},{128,64},{160,96},{192,128},{224,1... | collective-permute-start | bytes 1179656 | tf_op jit(solution)/shard_map/ppermute | solution.py:475
  22.4 0.0 collective-permute-start.6
  22.4 0.0 collective-permute-start.8
  22.4 0.0 collective-permute-done.9.up_other
  22.4 0.0 copy-done
  22.4 9.4 %attention.1 = (bf16[256,768]{1,0:T(8,128)(2,1)S(1)}, f32[256,256]{1,0:T(8,128)S(1)}, bf16[256,256]{1,0:T(8,128)(2,1)S(1)}, bf16[256,256]{1,0:T(8,128)(2,1)S(1)}, bf16[256,256]{1,0:T(8,128)(2,1)S(1)}) custom-call(s32[4]{0:T(128)S(1)} %pad_add_fusion.place, bf16[256,768]{1,0:T(8,128)(2,1)S(1)} %get-tuple-element.51.query, bf16[128,1536]{1,0:T(8,128)(2,1)S(1)} %bitcast.13, ...), custom_call_target="tpu_custom_call" | custom-call | flops 4026531840 | bytes 4194304 | tf_op jit(solution)/shard_map/attention/pallas_call | solution.py:250
  31.8 0.0 collective-permute-done.7.refs_6_
  31.8 2.4 %collective-permute-done.6.refs_2_ = bf16[128,1536]{1,0:T(8,128)(2,1)S(1)} collective-permute-done((bf16[128,1536]{1,0:T(8,128)(2,1)}, bf16[128,1536]{1,0:T(8,128)(2,1)S(1)}, u32[]{:S(2)}, u32[]{:S(2)}) %collective-permute-start.6) | collective-permute-done | bytes 393248 | tf_op jit(solution)/shard_map/ppermute | solution.py:475
  34.2 0.0 collective-permute-done.8.refs_5_
  34.2 0.0 collective-permute-start.13
  34.2 1.5 %collective-permute-start.10 = (bf16[256,256]{1,0:T(8,128)(2,1)S(1)}, bf16[256,256]{1,0:T(8,128)(2,1)S(1)}, u32[]{:S(2)}, u32[]{:S(2)}) collective-permute-start(bf16[256,256]{1,0:T(8,128)(2,1)S(1)} %get-tuple-element.65), channel_id=1, source_target_pairs={{0,192},{32,224},{64,0},{96,32},{128,64},{160,96},{192,128},{224,1... | collective-permute-start | bytes 393224 | tf_op jit(solution)/shard_map/ppermute | solution.py:482
  35.7 0.0 collective-permute-start.11
  35.7 0.9 collective-permute-start.12
  36.6 4.0 %collective-permute-done.10.b = bf16[256,256]{1,0:T(8,128)(2,1)S(1)} collective-permute-done((bf16[256,256]{1,0:T(8,128)(2,1)S(1)}, bf16[256,256]{1,0:T(8,128)(2,1)S(1)}, u32[]{:S(2)}, u32[]{:S(2)}) %collective-permute-start.10) | collective-permute-done | bytes 131104 | tf_op jit(solution)/shard_map/ppermute | solution.py:482
  40.5 3.1 %collective-permute-done.11.c = bf16[256,256]{1,0:T(8,128)(2,1)S(1)} collective-permute-done((bf16[256,256]{1,0:T(8,128)(2,1)S(1)}, bf16[256,256]{1,0:T(8,128)(2,1)S(1)}, u32[]{:S(2)}, u32[]{:S(2)}) %collective-permute-start.11) | collective-permute-done | bytes 131104 | tf_op jit(solution)/shard_map/ppermute | solution.py:482
  43.6 1.6 %collective-permute-done.12.d = bf16[256,256]{1,0:T(8,128)(2,1)S(1)} collective-permute-done((bf16[256,256]{1,0:T(8,128)(2,1)S(1)}, bf16[256,256]{1,0:T(8,128)(2,1)S(1)}, u32[]{:S(2)}, u32[]{:S(2)}) %collective-permute-start.12) | collective-permute-done | bytes 131104 | tf_op jit(solution)/shard_map/ppermute | solution.py:482
  45.2 0.0 collective-permute-done.13.dq_other
  45.2 0.1 sum_four.2.dkv
  45.3 0.1 collective-permute-start.14
  45.4 1.3 %collective-permute-done.14.dkv_other = bf16[256,256]{1,0:T(8,128)(2,1)S(1)} collective-permute-done((bf16[256,256]{1,0:T(8,128)(2,1)S(1)}, bf16[256,256]{1,0:T(8,128)(2,1)S(1)}, u32[]{:S(2)}, u32[]{:S(2)}) %collective-permute-start.14) | collective-permute-done | bytes 131104 | tf_op jit(solution)/shard_map/ppermute | solution.py:486
  46.7 0.1 collective-permute-start.15
  46.9 0.4 collective-permute-start.16
  47.2 0.6 pack.1
  47.9 0.1 collective-permute-start.17
  48.0 2.0 %collective-permute-start.18 = (bf16[256,256]{1,0:T(8,128)(2,1)S(1)}, bf16[256,256]{1,0:T(8,128)(2,1)S(1)}, u32[]{:S(2)}, u32[]{:S(2)}) collective-permute-start(bf16[256,256]{1,0:T(8,128)(2,1)S(1)} %get-tuple-element.79), channel_id=1, source_target_pairs={{0,128},{32,160},{64,192},{96,224},{128,0},{160,32},{192,64},{224,... | collective-permute-start | bytes 393224 | tf_op jit(solution)/shard_map/ppermute | solution.py:497
  50.0 1.2 %collective-permute-start.19 = (bf16[256,256]{1,0:T(8,128)(2,1)S(1)}, bf16[256,256]{1,0:T(8,128)(2,1)S(1)}, u32[]{:S(2)}, u32[]{:S(2)}) collective-permute-start(bf16[256,256]{1,0:T(8,128)(2,1)S(1)} %get-tuple-element.80), channel_id=1, source_target_pairs={{0,192},{32,224},{64,0},{96,32},{128,64},{160,96},{192,128},{224,1... | collective-permute-start | bytes 393224 | tf_op jit(solution)/shard_map/ppermute | solution.py:497
  51.2 0.0 collective-permute-done.15.refs_3_
  51.2 0.0 collective-permute-done.16.refs_7_
  51.2 2.0 %transpose_tokens.1.tokens_t = bf16[1536,1024]{1,0:T(8,128)(2,1)S(1)} custom-call(bf16[128,1536]{1,0:T(8,128)(2,1)} %bitcast.4.own.refs_0_, bf16[128,1536]{1,0:T(8,128)(2,1)S(1)} %collective-permute-done.other.refs_1_, bf16[128,1536]{1,0:T(8,128)(2,1)S(1)} %collective-permute-done.6.refs_2_, bf16[128,1536]{1,0:T(8,128)(2,1)S(1)} %collective-permute-done.15.refs_3_, ...), custom_call_target="tpu_custom_call" | custom-call | bytes 6291456 | tf_op jit(solution)/shard_map/transpose_tokens/pallas_call | solution.py:349
  53.2 4.3 %collective-permute-done.17.b = bf16[256,256]{1,0:T(8,128)(2,1)S(1)} collective-permute-done((bf16[256,256]{1,0:T(8,128)(2,1)S(1)}, bf16[256,256]{1,0:T(8,128)(2,1)S(1)}, u32[]{:S(2)}, u32[]{:S(2)}) %collective-permute-start.17) | collective-permute-done | bytes 131104 | tf_op jit(solution)/shard_map/ppermute | solution.py:497
  57.5 0.0 collective-permute-done.18.c
  57.5 0.6 collective-permute-done.19.d
  58.1 1.5 %weight_grad.1 = (f32[384,256]{1,0:T(8,128)S(1)}, bf16[384,256]{1,0:T(8,128)(2,1)S(1)}, bf16[384,256]{1,0:T(8,128)(2,1)S(1)}, bf16[384,256]{1,0:T(8,128)(2,1)S(1)}) custom-call(s32[4]{0:T(128)S(1)} %pad_add_fusion.place, bf16[1536,1024]{1,0:T(8,128)(2,1)S(1)} %transpose_tokens.1.tokens_t, bf16[256,256]{1,0:T(8,128)(2,1)S(1)} %get-tuple-element.77.a, ...), custom_call_target="tpu_custom_call" | custom-call | flops 805306368 | bytes 4325376 | tf_op jit(solution)/shard_map/weight_grad/pallas_call | solution.py:369
  59.7 1.7 %collective-permute-start.20 = (bf16[384,256]{1,0:T(8,128)(2,1)S(1)}, bf16[384,256]{1,0:T(8,128)(2,1)S(1)}, u32[]{:S(2)}, u32[]{:S(2)}) collective-permute-start(bf16[384,256]{1,0:T(8,128)(2,1)S(1)} %get-tuple-element.82), channel_id=1, source_target_pairs={{0,8},{1,9},{2,10},{3,11},{4,12},{5,13},{6,14},{7,15},{8,16},{9,17... | collective-permute-start | bytes 589832 | tf_op jit(solution)/shard_map/ppermute | solution.py:500
  61.3 0.9 %collective-permute-start.21 = (bf16[384,256]{1,0:T(8,128)(2,1)S(1)}, bf16[384,256]{1,0:T(8,128)(2,1)S(1)}, u32[]{:S(2)}, u32[]{:S(2)}) collective-permute-start(bf16[384,256]{1,0:T(8,128)(2,1)S(1)} %get-tuple-element.83), channel_id=1, source_target_pairs={{0,16},{1,17},{2,18},{3,19},{4,20},{5,21},{6,22},{7,23},{8,24},{9,... | collective-permute-start | bytes 589832 | tf_op jit(solution)/shard_map/ppermute | solution.py:500
  62.3 2.4 %collective-permute-start.22 = (bf16[384,256]{1,0:T(8,128)(2,1)S(1)}, bf16[384,256]{1,0:T(8,128)(2,1)S(1)}, u32[]{:S(2)}, u32[]{:S(2)}) collective-permute-start(bf16[384,256]{1,0:T(8,128)(2,1)S(1)} %get-tuple-element.84), channel_id=1, source_target_pairs={{0,24},{1,25},{2,26},{3,27},{4,28},{5,29},{6,30},{7,31},{8,0},{9,1... | collective-permute-start | bytes 589832 | tf_op jit(solution)/shard_map/ppermute | solution.py:500
  64.7 6.9 %input_grad.1 = bf16[128,1536]{1,0:T(8,128)(2,1)} custom-call(s32[4]{0:T(128)S(1)} %pad_add_fusion.place, bf16[256,768]{1,0:T(8,128)(2,1)S(1)} %get-tuple-element.68.dq, bf16[256,768]{1,0:T(8,128)(2,1)S(1)} %collective-permute-done.13.dq_other, bf16[256,256]{1,0:T(8,128)(2,1)S(1)} %sum_four.2.dkv, bf16[256,256]{1,0:T(8,128)(2,1)S(1)} %collective-permute-done.14.dkv_other, ...), custom_call_target="tpu_custom_call" | custom-call | flops 805306368 | bytes 6291456 | tf_op jit(solution)/shard_map/input_grad/pallas_call | solution.py:422
  71.6 0.0 collective-permute-done.20.b
  71.6 0.0 collective-permute-done.21.c
  71.6 0.3 collective-permute-done.22.d
  71.9 0.1 sum_four.3
  72.0 18.2 %all_to_all.11 = bf16[8,48,256]{2,1,0:T(8,128)(2,1)S(1)} all-to-all(bf16[8,48,256]{2,1,0:T(8,128)(2,1)S(1)} %bitcast.10), channel_id=1, replica_groups={{0,1,2,3,4,5,6,7},{8,9,10,11,12,13,14,15},{16,17,18,19,20,21,22,23},{24..., dimensions={0} | all-to-all | bytes 393216 | tf_op jit(solution)/shard_map/all_to_all | solution.py:506
  90.2 0.6 final_sum.1
Async XLA Ops:
  0.6 21.8 %copy-start = (bf16[1,128,1536]{2,1,0:T(8,128)(2,1)S(1)}, bf16[1,128,1536]{2,1,0:T(8,128)(2,1)}, u32[]{:S(2)}) copy-start(bf16[1,128,1536]{2,1,0:T(8,128)(2,1)} %param.8) | copy-start | bytes 1179652
  0.6 6.1 %collective-permute-start = (bf16[128,1536]{1,0:T(8,128)(2,1)}, bf16[128,1536]{1,0:T(8,128)(2,1)S(1)}, u32[]{:S(2)}, u32[]{:S(2)}) collective-permute-start(bf16[128,1536]{1,0:T(8,128)(2,1)} %bitcast.4.own.refs_0_), channel_id=1, source_target_pairs={{0,32},{32,0},{64,96},{96,64},{128,160},{160,128},{192,224},{224,1... | collective-permute-start | bytes 1179656 | tf_op jit(solution)/shard_map/ppermute | solution.py:462
  0.7 13.8 %collective-permute-start.5 = (bf16[128,1536]{1,0:T(8,128)(2,1)}, bf16[128,1536]{1,0:T(8,128)(2,1)S(1)}, u32[]{:S(2)}, u32[]{:S(2)}) collective-permute-start(bf16[128,1536]{1,0:T(8,128)(2,1)} %bitcast.4.own.refs_0_), channel_id=1, source_target_pairs={{0,128},{32,160},{64,192},{96,224},{128,0},{160,32},{192,64},{224,... | collective-permute-start | bytes 1179656 | tf_op jit(solution)/shard_map/ppermute | solution.py:473
  3.9 18.6 %collective-permute-start.9 = (bf16[128,1536]{1,0:T(8,128)(2,1)}, bf16[128,1536]{1,0:T(8,128)(2,1)S(1)}, u32[]{:S(2)}, u32[]{:S(2)}) collective-permute-start(bf16[128,1536]{1,0:T(8,128)(2,1)} %bitcast.12), channel_id=1, source_target_pairs={{0,32},{32,0},{64,96},{96,64},{128,160},{160,128},{192,224},{224,1... | collective-permute-start | bytes 1179656 | tf_op jit(solution)/shard_map/ppermute | solution.py:463
  4.0 5.7 %collective-permute-start.4 = (s32[1,8]{1,0:T(1,128)}, s32[1,8]{1,0:T(1,128)S(1)}, u32[]{:S(2)}, u32[]{:S(2)}) collective-permute-start(s32[1,8]{1,0:T(1,128)} %bitcast.15), channel_id=1, source_target_pairs={{0,32},{32,0},{64,96},{96,64},{128,160},{160,128},{192,224},{224,1... | collective-permute-start | bytes 104 | tf_op jit(solution)/shard_map/ppermute | solution.py:464
  7.0 10.4 %collective-permute-start.3 = (bf16[256,256]{1,0:T(8,128)(2,1)S(1)}, bf16[256,256]{1,0:T(8,128)(2,1)S(1)}, u32[]{:S(2)}, u32[]{:S(2)}) collective-permute-start(bf16[256,256]{1,0:T(8,128)(2,1)S(1)} %project_kv.1.kv0), channel_id=1, source_target_pairs={{0,192},{32,224},{64,0},{96,32},{128,64},{160,96},{192,128},{224,1... | collective-permute-start | bytes 393224 | tf_op jit(solution)/shard_map/ppermute | solution.py:469
  8.2 9.2 %collective-permute-start.2 = (bf16[256,256]{1,0:T(8,128)(2,1)S(1)}, bf16[256,256]{1,0:T(8,128)(2,1)S(1)}, u32[]{:S(2)}, u32[]{:S(2)}) collective-permute-start(bf16[256,256]{1,0:T(8,128)(2,1)S(1)} %project_kv.1.kv0), channel_id=1, source_target_pairs={{0,128},{32,160},{64,192},{96,224},{128,0},{160,32},{192,64},{224,... | collective-permute-start | bytes 393224 | tf_op jit(solution)/shard_map/ppermute | solution.py:469
  9.7 9.9 %collective-permute-start.1 = (bf16[256,256]{1,0:T(8,128)(2,1)S(1)}, bf16[256,256]{1,0:T(8,128)(2,1)S(1)}, u32[]{:S(2)}, u32[]{:S(2)}) collective-permute-start(bf16[256,256]{1,0:T(8,128)(2,1)S(1)} %project_kv.1.kv0), channel_id=1, source_target_pairs={{0,64},{32,96},{64,128},{96,160},{128,192},{160,224},{192,0},{224,... | collective-permute-start | bytes 393224 | tf_op jit(solution)/shard_map/ppermute | solution.py:469
  19.6 12.2 %collective-permute-start.7 = (bf16[128,1536]{1,0:T(8,128)(2,1)}, bf16[128,1536]{1,0:T(8,128)(2,1)S(1)}, u32[]{:S(2)}, u32[]{:S(2)}) collective-permute-start(bf16[128,1536]{1,0:T(8,128)(2,1)} %bitcast.4.own.refs_0_), channel_id=1, source_target_pairs={{0,192},{32,224},{64,0},{96,32},{128,64},{160,96},{192,128},{224,1... | collective-permute-start | bytes 1179656 | tf_op jit(solution)/shard_map/ppermute | solution.py:475
  22.4 11.8 %collective-permute-start.6 = (bf16[128,1536]{1,0:T(8,128)(2,1)}, bf16[128,1536]{1,0:T(8,128)(2,1)S(1)}, u32[]{:S(2)}, u32[]{:S(2)}) collective-permute-start(bf16[128,1536]{1,0:T(8,128)(2,1)} %bitcast.4.own.refs_0_), channel_id=1, source_target_pairs={{0,64},{32,96},{64,128},{96,160},{128,192},{160,224},{192,0},{224,... | collective-permute-start | bytes 1179656 | tf_op jit(solution)/shard_map/ppermute | solution.py:475
  22.4 11.8 %collective-permute-start.8 = (bf16[128,1536]{1,0:T(8,128)(2,1)S(1)}, bf16[128,1536]{1,0:T(8,128)(2,1)S(1)}, u32[]{:S(2)}, u32[]{:S(2)}) collective-permute-start(bf16[128,1536]{1,0:T(8,128)(2,1)S(1)} %collective-permute-done.5.refs_4_), channel_id=1, source_target_pairs={{0,32},{32,0},{64,96},{96,64},{128,160},{160,128},{192,224},{224,1... | collective-permute-start | bytes 1179656 | tf_op jit(solution)/shard_map/ppermute | solution.py:477
  34.2 11.0 %collective-permute-start.13 = (bf16[256,768]{1,0:T(8,128)(2,1)S(1)}, bf16[256,768]{1,0:T(8,128)(2,1)S(1)}, u32[]{:S(2)}, u32[]{:S(2)}) collective-permute-start(bf16[256,768]{1,0:T(8,128)(2,1)S(1)} %get-tuple-element.68.dq), channel_id=1, source_target_pairs={{0,32},{32,0},{64,96},{96,64},{128,160},{160,128},{192,224},{224,1... | collective-permute-start | bytes 1179656 | tf_op jit(solution)/shard_map/ppermute | solution.py:480
  34.2 6.3 %collective-permute-start.10 = (bf16[256,256]{1,0:T(8,128)(2,1)S(1)}, bf16[256,256]{1,0:T(8,128)(2,1)S(1)}, u32[]{:S(2)}, u32[]{:S(2)}) collective-permute-start(bf16[256,256]{1,0:T(8,128)(2,1)S(1)} %get-tuple-element.65), channel_id=1, source_target_pairs={{0,192},{32,224},{64,0},{96,32},{128,64},{160,96},{192,128},{224,1... | collective-permute-start | bytes 393224 | tf_op jit(solution)/shard_map/ppermute | solution.py:482
  35.7 7.9 %collective-permute-start.11 = (bf16[256,256]{1,0:T(8,128)(2,1)S(1)}, bf16[256,256]{1,0:T(8,128)(2,1)S(1)}, u32[]{:S(2)}, u32[]{:S(2)}) collective-permute-start(bf16[256,256]{1,0:T(8,128)(2,1)S(1)} %get-tuple-element.66), channel_id=1, source_target_pairs={{0,128},{32,160},{64,192},{96,224},{128,0},{160,32},{192,64},{224,... | collective-permute-start | bytes 393224 | tf_op jit(solution)/shard_map/ppermute | solution.py:482
  35.7 9.5 %collective-permute-start.12 = (bf16[256,256]{1,0:T(8,128)(2,1)S(1)}, bf16[256,256]{1,0:T(8,128)(2,1)S(1)}, u32[]{:S(2)}, u32[]{:S(2)}) collective-permute-start(bf16[256,256]{1,0:T(8,128)(2,1)S(1)} %get-tuple-element.67), channel_id=1, source_target_pairs={{0,64},{32,96},{64,128},{96,160},{128,192},{160,224},{192,0},{224,... | collective-permute-start | bytes 393224 | tf_op jit(solution)/shard_map/ppermute | solution.py:482
  45.3 1.4 %collective-permute-start.14 = (bf16[256,256]{1,0:T(8,128)(2,1)S(1)}, bf16[256,256]{1,0:T(8,128)(2,1)S(1)}, u32[]{:S(2)}, u32[]{:S(2)}) collective-permute-start(bf16[256,256]{1,0:T(8,128)(2,1)S(1)} %sum_four.2.dkv), channel_id=1, source_target_pairs={{0,32},{32,0},{64,96},{96,64},{128,160},{160,128},{192,224},{224,1... | collective-permute-start | bytes 393224 | tf_op jit(solution)/shard_map/ppermute | solution.py:486
  46.7 4.5 %collective-permute-start.15 = (bf16[128,1536]{1,0:T(8,128)(2,1)S(1)}, bf16[128,1536]{1,0:T(8,128)(2,1)S(1)}, u32[]{:S(2)}, u32[]{:S(2)}) collective-permute-start(bf16[128,1536]{1,0:T(8,128)(2,1)S(1)} %collective-permute-done.6.refs_2_), channel_id=1, source_target_pairs={{0,32},{32,0},{64,96},{96,64},{128,160},{160,128},{192,224},{224,1... | collective-permute-start | bytes 1179656 | tf_op jit(solution)/shard_map/ppermute | solution.py:491
  46.9 4.3 %collective-permute-start.16 = (bf16[128,1536]{1,0:T(8,128)(2,1)S(1)}, bf16[128,1536]{1,0:T(8,128)(2,1)S(1)}, u32[]{:S(2)}, u32[]{:S(2)}) collective-permute-start(bf16[128,1536]{1,0:T(8,128)(2,1)S(1)} %collective-permute-done.7.refs_6_), channel_id=1, source_target_pairs={{0,32},{32,0},{64,96},{96,64},{128,160},{160,128},{192,224},{224,1... | collective-permute-start | bytes 1179656 | tf_op jit(solution)/shard_map/ppermute | solution.py:491
  47.9 9.6 %collective-permute-start.17 = (bf16[256,256]{1,0:T(8,128)(2,1)S(1)}, bf16[256,256]{1,0:T(8,128)(2,1)S(1)}, u32[]{:S(2)}, u32[]{:S(2)}) collective-permute-start(bf16[256,256]{1,0:T(8,128)(2,1)S(1)} %get-tuple-element.78), channel_id=1, source_target_pairs={{0,64},{32,96},{64,128},{96,160},{128,192},{160,224},{192,0},{224,... | collective-permute-start | bytes 393224 | tf_op jit(solution)/shard_map/ppermute | solution.py:497
  48.0 9.6 %collective-permute-start.18 = (bf16[256,256]{1,0:T(8,128)(2,1)S(1)}, bf16[256,256]{1,0:T(8,128)(2,1)S(1)}, u32[]{:S(2)}, u32[]{:S(2)}) collective-permute-start(bf16[256,256]{1,0:T(8,128)(2,1)S(1)} %get-tuple-element.79), channel_id=1, source_target_pairs={{0,128},{32,160},{64,192},{96,224},{128,0},{160,32},{192,64},{224,... | collective-permute-start | bytes 393224 | tf_op jit(solution)/shard_map/ppermute | solution.py:497
  50.0 8.2 %collective-permute-start.19 = (bf16[256,256]{1,0:T(8,128)(2,1)S(1)}, bf16[256,256]{1,0:T(8,128)(2,1)S(1)}, u32[]{:S(2)}, u32[]{:S(2)}) collective-permute-start(bf16[256,256]{1,0:T(8,128)(2,1)S(1)} %get-tuple-element.80), channel_id=1, source_target_pairs={{0,192},{32,224},{64,0},{96,32},{128,64},{160,96},{192,128},{224,1... | collective-permute-start | bytes 393224 | tf_op jit(solution)/shard_map/ppermute | solution.py:497
  59.7 11.9 %collective-permute-start.20 = (bf16[384,256]{1,0:T(8,128)(2,1)S(1)}, bf16[384,256]{1,0:T(8,128)(2,1)S(1)}, u32[]{:S(2)}, u32[]{:S(2)}) collective-permute-start(bf16[384,256]{1,0:T(8,128)(2,1)S(1)} %get-tuple-element.82), channel_id=1, source_target_pairs={{0,8},{1,9},{2,10},{3,11},{4,12},{5,13},{6,14},{7,15},{8,16},{9,17... | collective-permute-start | bytes 589832 | tf_op jit(solution)/shard_map/ppermute | solution.py:500
  61.3 10.3 %collective-permute-start.21 = (bf16[384,256]{1,0:T(8,128)(2,1)S(1)}, bf16[384,256]{1,0:T(8,128)(2,1)S(1)}, u32[]{:S(2)}, u32[]{:S(2)}) collective-permute-start(bf16[384,256]{1,0:T(8,128)(2,1)S(1)} %get-tuple-element.83), channel_id=1, source_target_pairs={{0,16},{1,17},{2,18},{3,19},{4,20},{5,21},{6,22},{7,23},{8,24},{9,... | collective-permute-start | bytes 589832 | tf_op jit(solution)/shard_map/ppermute | solution.py:500
  62.3 9.7 %collective-permute-start.22 = (bf16[384,256]{1,0:T(8,128)(2,1)S(1)}, bf16[384,256]{1,0:T(8,128)(2,1)S(1)}, u32[]{:S(2)}, u32[]{:S(2)}) collective-permute-start(bf16[384,256]{1,0:T(8,128)(2,1)S(1)} %get-tuple-element.84), channel_id=1, source_target_pairs={{0,24},{1,25},{2,26},{3,27},{4,28},{5,29},{6,30},{7,31},{8,0},{9,1... | collective-permute-start | bytes 589832 | tf_op jit(solution)/shard_map/ppermute | solution.py:500

commit v5 on v4

--- a/solution.py
+++ b/solution.py
@@ -103,6 +103,23 @@
         cost_estimate=cost(2 * TILE * D * 256, 2 * (TILE * D + D * 256)),
         name="project_kv_own",
     )(place, own, w_key, w_value)
+
+
+def kv_pair_kernel(own, other, weights, out):
+    out[:TILE] = dot(own[...], weights[...]).astype(BF)
+    out[TILE:] = dot(other[...], weights[...]).astype(BF)
+
+
+def project_kv_pair(own, other, weights):
+    return pl.pallas_call(
+        kv_pair_kernel,
+        in_specs=[WHOLE] * 3,
+        out_specs=WHOLE,
+        out_shape=jax.ShapeDtypeStruct((2 * TILE, 2 * HD), BF),
+        compiler_params=PARAMS,
+        cost_estimate=cost(4 * TILE * D * 256, 2 * (2 * TILE * D + D * 256)),
+        name="project_kv_pair",
+    )(own, other, weights)
 
 
 def kv_kernel(other, weights, kv_own, out):
@@ -459,6 +476,7 @@
     dp = lax.axis_index("dp")
     place = jnp.stack([ctx // 2, ctx % 2, dp // ZS, dp % ZS]).astype(jnp.int32)
     own, up = tokens[0], grad_heads[0]
+    far = {d: lax.ppermute(own, "ctx", chip_shift(d)) for d in (1, 3)}
     other = lax.ppermute(own, "ctx", CORE)
     up_other = lax.ppermute(up, "ctx", CORE)
     mask_other = lax.ppermute(tile_mask[0], "ctx", CORE)
@@ -466,17 +484,17 @@
     w_query, w_key, w_value = (in_hbm(w) for w in (w_query, w_key, w_value))
     weights, kv_own = project_kv_own(place, in_hbm(own), w_key, w_value)
     kv = project_kv(other, weights, kv_own)
-    kvs = [kv] + [lax.ppermute(kv, "ctx", chip_shift(d)) for d in (1, 2, 3)]
+    kv2 = lax.ppermute(kv, "ctx", chip_shift(2))
     query, bias = project_query(
         place, own, other, w_query, in_hbm(segments), in_hbm(tile_mask[0]), mask_other
     )
-    far = {2: lax.ppermute(own, "ctx", chip_shift(2))}
-    kvs, query, far, late_own = lax.optimization_barrier((kvs, query, far, own))
-    near = {d: lax.ppermute(late_own, "ctx", chip_shift(d)) for d in (1, 3)}
-
-    far_other = {2: lax.ppermute(far[2], "ctx", CORE)}
-    grads = attention(place, query, up, up_other, kvs, bias)
-    near, far_other, (dq, g0, g1, g2, g3) = lax.optimization_barrier((near, far_other, grads))
+    far, kv2, query, late_own = lax.optimization_barrier((far, kv2, query, own))
+    far_other = {d: lax.ppermute(far[d], "ctx", CORE) for d in (1, 3)}
+    late = lax.ppermute(late_own, "ctx", chip_shift(2))
+    kv1, kv3 = (project_kv_pair(far[d], far_other[d], weights) for d in (1, 3))
+
+    grads = attention(place, query, up, up_other, [kv, kv1, kv2, kv3], bias)
+    late, (dq, g0, g1, g2, g3) = lax.optimization_barrier((late, grads))
     dq_other = lax.ppermute(dq, "ctx", CORE)
     back = [
         lax.ppermute(g, "ctx", chip_shift(CHIPS - d)) for d, g in ((1, g1), (2, g2), (3, g3))
@@ -485,10 +503,8 @@
     dkv = sum_four(g0, *back)
     dkv_other = lax.ppermute(dkv, "ctx", CORE)
 
-    near, dkv_other = lax.optimization_barrier((near, dkv_other))
-    for d in (1, 3):
-        far[d] = near[d]
-        far_other[d] = lax.ppermute(near[d], "ctx", CORE)
+    far[2], dkv_other = lax.optimization_barrier((late, dkv_other))
+    far_other[2] = lax.ppermute(far[2], "ctx", CORE)
     tokens_t = transpose(
         [own, other] + [part for d in (1, 2, 3) for part in (far[d], far_other[d])]
     )

time: 91.6 us -> 89.2 us (0.974)
  starting transfers between devices: 20.5 us -> 17.2 us
    ppermute x9 -> x7, starting transfers between devices: 9.17 us -> 6.47 us  [the longest x2 2.84 us: shards(): far = {d: lax.ppermute(own, 'ctx', chip_shift(d)) for d in (1, 3)}]
    ppermute x1, waiting for transfers between devices: 0.01 us -> 1.25 us  [shards(): mask_other = lax.ppermute(tile_mask[0], 'ctx', CORE)]
    ppermute x9 -> x7, waiting for transfers between devices: 8.78 us -> 7.97 us  [the longest x2 5.67 us: shards(): far = {d: lax.ppermute(own, 'ctx', chip_shift(d)) for d in (1, 3)}]
  transfers between devices with their start and end apart: 23 -> 21, of which waited for: 11 -> 14; matrix products, arithmetic and copies ran while one was open for 0% -> 0% of each run, Pallas kernels for 27% -> 29%
where the time goes in v5:
time: 89.2 us; the launch traced here: 88.6 us
  Pallas kernels  28 us (31%)
  waiting for transfers between devices  24.7 us (28%)
  blocking collectives  17.9 us (20%)
  starting transfers between devices  17.2 us (19%)
    all_to_all x1, blocking collectives, shards(): lax.all_to_all(y_sum, 'dp', 0, 0, tiled=True, axis_index_groups=Z_GROUPS)  17.9 us
    pallas_call x1, Pallas kernels, attention(): pl.pallas_call(attention_kernel, grid_spec=pltpu.PrefetchScalarGridSpec(n...  9.38 us
    ppermute x3, waiting for transfers between devices, shards(): lax.ppermute(g, 'ctx', chip_shift(CHIPS - d))  8.02 us
    pallas_call x1, Pallas kernels, input_grad(): pl.pallas_call(input_kernel, in_specs=[SCALARS] + [WHOLE] * 4 + [STAY] *...  6.88 us
    ppermute x2, waiting for transfers between devices, shards(): far = {d: lax.ppermute(own, 'ctx', chip_shift(d)) for d in (1, 3)}  5.67 us
    ppermute x3, waiting for transfers between devices, shards(): lax.ppermute(packed[d], 'ctx', chip_shift(d))  5.15 us
    ppermute x3, starting transfers between devices, shards(): lax.ppermute(terms[d], 'dp', y_shift(d))  5 us
    pallas_call x1, Pallas kernels, project_query(): pl.pallas_call(query_kernel, in_specs=[SCALARS, WHOLE, WHOLE, STAY, STAY,...  3.47 us
  transfers between devices with their start and end apart: 21, of which 14 were waited for; matrix products, arithmetic and copies ran while one was open for 0% of the time, Pallas kernels for 29%

profile of v5, /device:TPU:8, one launch (start us, length us, event | category | flops | bytes accessed | tf_op | source)
XLA Modules:
  0.0 88.6 jit_solution(5876109119524044211)
XLA Ops:
  0.6 0.0 copy-start
  0.6 0.1 collective-permute-start
  0.7 2.8 %collective-permute-start.2 = (bf16[128,1536]{1,0:T(8,128)(2,1)}, bf16[128,1536]{1,0:T(8,128)(2,1)S(1)}, u32[]{:S(2)}, u32[]{:S(2)}) collective-permute-start(bf16[128,1536]{1,0:T(8,128)(2,1)} %bitcast.4.own.refs_0_), channel_id=1, source_target_pairs={{0,192},{32,224},{64,0},{96,32},{128,64},{160,96},{192,128},{224,1... | collective-permute-start | bytes 1179656 | tf_op jit(solution)/shard_map/ppermute | solution.py:479
  3.6 0.0 collective-permute-start.1
  3.6 0.1 pad_add_fusion.place
  3.7 2.3 %project_kv_own.1 = (bf16[1536,256]{1,0:T(8,128)(2,1)S(1)}, bf16[128,256]{1,0:T(8,128)(2,1)S(1)}) custom-call(s32[4]{0:T(128)S(1)} %pad_add_fusion.place, bf16[128,1536]{1,0:T(8,128)(2,1)} %bitcast.4.own.refs_0_, bf16[1536,256]{1,0:T(8,128)(2,1)} %w_key.3, bf16[1536,256]{1,0:T(8,128)(2,1)} %w_value.3), custom_call_target="tpu_custom_call" | custom-call | flops 100663296 | bytes 1179648 | tf_op jit(solution)/shard_map/project_kv_own/pallas_call | solution.py:93
  5.9 0.0 collective-permute-done.other.refs_1_
  5.9 0.3 project_kv.1.kv0
  6.2 2.4 %collective-permute-start.3 = (bf16[256,256]{1,0:T(8,128)(2,1)S(1)}, bf16[256,256]{1,0:T(8,128)(2,1)S(1)}, u32[]{:S(2)}, u32[]{:S(2)}) collective-permute-start(bf16[256,256]{1,0:T(8,128)(2,1)S(1)} %project_kv.1.kv0), channel_id=1, source_target_pairs={{0,128},{32,160},{64,192},{96,224},{128,0},{160,32},{192,64},{224,... | collective-permute-start | bytes 393224 | tf_op jit(solution)/shard_map/ppermute | solution.py:487
  8.6 0.0 collective-permute-start.4
  8.6 1.3 %collective-permute-done.4.mask_other = s32[1,8]{1,0:T(1,128)S(1)} collective-permute-done((s32[1,8]{1,0:T(1,128)}, s32[1,8]{1,0:T(1,128)S(1)}, u32[]{:S(2)}, u32[]{:S(2)}) %collective-permute-start.4) | collective-permute-done | bytes 64 | tf_op jit(solution)/shard_map/ppermute | solution.py:482
  9.8 3.5 %project_query.1 = (bf16[256,768]{1,0:T(8,128)(2,1)S(1)}, f32[1024,256]{1,0:T(8,128)S(1)}) custom-call(s32[4]{0:T(128)S(1)} %pad_add_fusion.place, bf16[128,1536]{1,0:T(8,128)(2,1)} %bitcast.4.own.refs_0_, bf16[128,1536]{1,0:T(8,128)(2,1)S(1)} %collective-permute-done.other.refs_1_, bf16[1536,1536]{1,0:T(8,128)(2,1)} %w_query.3, s32[1,1024]{1,0:T(1,128)} %segments_far.1, ...), custom_call_target="tpu_custom_call" | custom-call | flops 603979776 | bytes 3538944 | tf_op jit(solution)/shard_map/project_query/pallas_call | solution.py:203
  13.3 2.4 %collective-permute-done.2.own.refs_6_ = bf16[128,1536]{1,0:T(8,128)(2,1)S(1)} collective-permute-done((bf16[128,1536]{1,0:T(8,128)(2,1)}, bf16[128,1536]{1,0:T(8,128)(2,1)S(1)}, u32[]{:S(2)}, u32[]{:S(2)}) %collective-permute-start.2) | collective-permute-done | bytes 393248 | tf_op jit(solution)/shard_map/ppermute | solution.py:479
  15.7 3.3 %collective-permute-done.1.own.refs_2_ = bf16[128,1536]{1,0:T(8,128)(2,1)S(1)} collective-permute-done((bf16[128,1536]{1,0:T(8,128)(2,1)}, bf16[128,1536]{1,0:T(8,128)(2,1)S(1)}, u32[]{:S(2)}, u32[]{:S(2)}) %collective-permute-start.1) | collective-permute-done | bytes 393248 | tf_op jit(solution)/shard_map/ppermute | solution.py:479
  19.0 0.0 collective-permute-done.3.kv2
  19.0 0.0 collective-permute-start.5
  19.0 0.5 collective-permute-start.8
  19.5 0.0 copy-done
  19.5 0.0 collective-permute-start.7
  19.5 0.6 collective-permute-start.6
  20.1 0.6 collective-permute-done.5.other.refs_3_
  20.7 0.4 project_kv_pair.2.kv1
  21.1 0.2 collective-permute-done.8.other.refs_7_
  21.3 0.4 project_kv_pair.3.kv3
  21.6 0.2 collective-permute-done.7.up_other
  21.8 9.4 %attention.1 = (bf16[256,768]{1,0:T(8,128)(2,1)S(1)}, f32[256,256]{1,0:T(8,128)S(1)}, bf16[256,256]{1,0:T(8,128)(2,1)S(1)}, bf16[256,256]{1,0:T(8,128)(2,1)S(1)}, bf16[256,256]{1,0:T(8,128)(2,1)S(1)}) custom-call(s32[4]{0:T(128)S(1)} %pad_add_fusion.place, bf16[256,768]{1,0:T(8,128)(2,1)S(1)} %get-tuple-element.46.query, bf16[128,1536]{1,0:T(8,128)(2,1)S(1)} %bitcast.13, ...), custom_call_target="tpu_custom_call" | custom-call | flops 4026531840 | bytes 4194304 | tf_op jit(solution)/shard_map/attention/pallas_call | solution.py:267
  31.2 1.5 %collective-permute-done.6.refs_4_ = bf16[128,1536]{1,0:T(8,128)(2,1)S(1)} collective-permute-done((bf16[128,1536]{1,0:T(8,128)(2,1)}, bf16[128,1536]{1,0:T(8,128)(2,1)S(1)}, u32[]{:S(2)}, u32[]{:S(2)}) %collective-permute-start.6) | collective-permute-done | bytes 393248 | tf_op jit(solution)/shard_map/ppermute | solution.py:493
  32.7 0.0 collective-permute-start.12
  32.7 0.3 collective-permute-start.9
  33.0 0.5 collective-permute-start.10
  33.5 1.4 %collective-permute-start.11 = (bf16[256,256]{1,0:T(8,128)(2,1)S(1)}, bf16[256,256]{1,0:T(8,128)(2,1)S(1)}, u32[]{:S(2)}, u32[]{:S(2)}) collective-permute-start(bf16[256,256]{1,0:T(8,128)(2,1)S(1)} %get-tuple-element.59), channel_id=1, source_target_pairs={{0,64},{32,96},{64,128},{96,160},{128,192},{160,224},{192,0},{224,... | collective-permute-start | bytes 393224 | tf_op jit(solution)/shard_map/ppermute | solution.py:500
  35.0 4.1 %collective-permute-done.9.b = bf16[256,256]{1,0:T(8,128)(2,1)S(1)} collective-permute-done((bf16[256,256]{1,0:T(8,128)(2,1)S(1)}, bf16[256,256]{1,0:T(8,128)(2,1)S(1)}, u32[]{:S(2)}, u32[]{:S(2)}) %collective-permute-start.9) | collective-permute-done | bytes 131104 | tf_op jit(solution)/shard_map/ppermute | solution.py:500
  39.0 1.8 %collective-permute-done.10.c = bf16[256,256]{1,0:T(8,128)(2,1)S(1)} collective-permute-done((bf16[256,256]{1,0:T(8,128)(2,1)S(1)}, bf16[256,256]{1,0:T(8,128)(2,1)S(1)}, u32[]{:S(2)}, u32[]{:S(2)}) %collective-permute-start.10) | collective-permute-done | bytes 131104 | tf_op jit(solution)/shard_map/ppermute | solution.py:500
  40.9 2.1 %collective-permute-done.11.d = bf16[256,256]{1,0:T(8,128)(2,1)S(1)} collective-permute-done((bf16[256,256]{1,0:T(8,128)(2,1)S(1)}, bf16[256,256]{1,0:T(8,128)(2,1)S(1)}, u32[]{:S(2)}, u32[]{:S(2)}) %collective-permute-start.11) | collective-permute-done | bytes 131104 | tf_op jit(solution)/shard_map/ppermute | solution.py:500
  43.0 0.0 collective-permute-done.12.dq_other
  43.0 0.1 sum_four.2.dkv
  43.1 0.1 collective-permute-start.13
  43.2 1.3 %collective-permute-done.13.dkv_other = bf16[256,256]{1,0:T(8,128)(2,1)S(1)} collective-permute-done((bf16[256,256]{1,0:T(8,128)(2,1)S(1)}, bf16[256,256]{1,0:T(8,128)(2,1)S(1)}, u32[]{:S(2)}, u32[]{:S(2)}) %collective-permute-start.13) | collective-permute-done | bytes 131104 | tf_op jit(solution)/shard_map/ppermute | solution.py:504
  44.5 0.1 collective-permute-start.14
  44.6 0.6 pack.1
  45.3 0.1 collective-permute-start.15
  45.4 2.6 %collective-permute-start.16 = (bf16[256,256]{1,0:T(8,128)(2,1)S(1)}, bf16[256,256]{1,0:T(8,128)(2,1)S(1)}, u32[]{:S(2)}, u32[]{:S(2)}) collective-permute-start(bf16[256,256]{1,0:T(8,128)(2,1)S(1)} %get-tuple-element.69), channel_id=1, source_target_pairs={{0,128},{32,160},{64,192},{96,224},{128,0},{160,32},{192,64},{224,... | collective-permute-start | bytes 393224 | tf_op jit(solution)/shard_map/ppermute | solution.py:513
  48.0 0.6 collective-permute-start.17
  48.6 0.0 collective-permute-done.14.refs_5_
  48.6 2.0 %transpose_tokens.1.tokens_t = bf16[1536,1024]{1,0:T(8,128)(2,1)S(1)} custom-call(bf16[128,1536]{1,0:T(8,128)(2,1)} %bitcast.4.own.refs_0_, bf16[128,1536]{1,0:T(8,128)(2,1)S(1)} %collective-permute-done.other.refs_1_, bf16[128,1536]{1,0:T(8,128)(2,1)S(1)} %collective-permute-done.1.own.refs_2_, bf16[128,1536]{1,0:T(8,128)(2,1)S(1)} %collective-permute-done.5.other.refs_3_, ...), custom_call_target="tpu_custom_call" | custom-call | bytes 6291456 | tf_op jit(solution)/shard_map/transpose_tokens/pallas_call | solution.py:366
  50.6 4.5 %collective-permute-done.15.b = bf16[256,256]{1,0:T(8,128)(2,1)S(1)} collective-permute-done((bf16[256,256]{1,0:T(8,128)(2,1)S(1)}, bf16[256,256]{1,0:T(8,128)(2,1)S(1)}, u32[]{:S(2)}, u32[]{:S(2)}) %collective-permute-start.15) | collective-permute-done | bytes 131104 | tf_op jit(solution)/shard_map/ppermute | solution.py:513
  55.2 0.0 collective-permute-done.16.c
  55.2 0.6 collective-permute-done.17.d
  55.8 1.5 %weight_grad.1 = (f32[384,256]{1,0:T(8,128)S(1)}, bf16[384,256]{1,0:T(8,128)(2,1)S(1)}, bf16[384,256]{1,0:T(8,128)(2,1)S(1)}, bf16[384,256]{1,0:T(8,128)(2,1)S(1)}) custom-call(s32[4]{0:T(128)S(1)} %pad_add_fusion.place, bf16[1536,1024]{1,0:T(8,128)(2,1)S(1)} %transpose_tokens.1.tokens_t, bf16[256,256]{1,0:T(8,128)(2,1)S(1)} %get-tuple-element.67.a, ...), custom_call_target="tpu_custom_call" | custom-call | flops 805306368 | bytes 4325376 | tf_op jit(solution)/shard_map/weight_grad/pallas_call | solution.py:386
  57.3 1.7 %collective-permute-start.18 = (bf16[384,256]{1,0:T(8,128)(2,1)S(1)}, bf16[384,256]{1,0:T(8,128)(2,1)S(1)}, u32[]{:S(2)}, u32[]{:S(2)}) collective-permute-start(bf16[384,256]{1,0:T(8,128)(2,1)S(1)} %get-tuple-element.72), channel_id=1, source_target_pairs={{0,8},{1,9},{2,10},{3,11},{4,12},{5,13},{6,14},{7,15},{8,16},{9,17... | collective-permute-start | bytes 589832 | tf_op jit(solution)/shard_map/ppermute | solution.py:516
  59.0 1.4 %collective-permute-start.19 = (bf16[384,256]{1,0:T(8,128)(2,1)S(1)}, bf16[384,256]{1,0:T(8,128)(2,1)S(1)}, u32[]{:S(2)}, u32[]{:S(2)}) collective-permute-start(bf16[384,256]{1,0:T(8,128)(2,1)S(1)} %get-tuple-element.73), channel_id=1, source_target_pairs={{0,16},{1,17},{2,18},{3,19},{4,20},{5,21},{6,22},{7,23},{8,24},{9,... | collective-permute-start | bytes 589832 | tf_op jit(solution)/shard_map/ppermute | solution.py:516
  60.3 2.0 %collective-permute-start.20 = (bf16[384,256]{1,0:T(8,128)(2,1)S(1)}, bf16[384,256]{1,0:T(8,128)(2,1)S(1)}, u32[]{:S(2)}, u32[]{:S(2)}) collective-permute-start(bf16[384,256]{1,0:T(8,128)(2,1)S(1)} %get-tuple-element.74), channel_id=1, source_target_pairs={{0,24},{1,25},{2,26},{3,27},{4,28},{5,29},{6,30},{7,31},{8,0},{9,1... | collective-permute-start | bytes 589832 | tf_op jit(solution)/shard_map/ppermute | solution.py:516
  62.3 6.9 %input_grad.1 = bf16[128,1536]{1,0:T(8,128)(2,1)} custom-call(s32[4]{0:T(128)S(1)} %pad_add_fusion.place, bf16[256,768]{1,0:T(8,128)(2,1)S(1)} %get-tuple-element.60.dq, bf16[256,768]{1,0:T(8,128)(2,1)S(1)} %collective-permute-done.12.dq_other, bf16[256,256]{1,0:T(8,128)(2,1)S(1)} %sum_four.2.dkv, bf16[256,256]{1,0:T(8,128)(2,1)S(1)} %collective-permute-done.13.dkv_other, ...), custom_call_target="tpu_custom_call" | custom-call | flops 805306368 | bytes 6291456 | tf_op jit(solution)/shard_map/input_grad/pallas_call | solution.py:439
  69.2 0.0 collective-permute-done.18.b
  69.2 0.0 collective-permute-done.19.c
  69.2 0.8 collective-permute-done.20.d
  70.0 0.1 sum_four.3
  70.1 17.9 %all_to_all.11 = bf16[8,48,256]{2,1,0:T(8,128)(2,1)S(1)} all-to-all(bf16[8,48,256]{2,1,0:T(8,128)(2,1)S(1)} %bitcast.10), channel_id=1, replica_groups={{0,1,2,3,4,5,6,7},{8,9,10,11,12,13,14,15},{16,17,18,19,20,21,22,23},{24..., dimensions={0} | all-to-all | bytes 393216 | tf_op jit(solution)/shard_map/all_to_all | solution.py:522
  88.0 0.6 final_sum.1
Async XLA Ops:
  0.6 18.9 %copy-start = (bf16[1,128,1536]{2,1,0:T(8,128)(2,1)S(1)}, bf16[1,128,1536]{2,1,0:T(8,128)(2,1)}, u32[]{:S(2)}) copy-start(bf16[1,128,1536]{2,1,0:T(8,128)(2,1)} %param.8) | copy-start | bytes 1179652
  0.6 5.3 %collective-permute-start = (bf16[128,1536]{1,0:T(8,128)(2,1)}, bf16[128,1536]{1,0:T(8,128)(2,1)S(1)}, u32[]{:S(2)}, u32[]{:S(2)}) collective-permute-start(bf16[128,1536]{1,0:T(8,128)(2,1)} %bitcast.4.own.refs_0_), channel_id=1, source_target_pairs={{0,32},{32,0},{64,96},{96,64},{128,160},{160,128},{192,224},{224,1... | collective-permute-start | bytes 1179656 | tf_op jit(solution)/shard_map/ppermute | solution.py:480
  0.7 15.0 %collective-permute-start.2 = (bf16[128,1536]{1,0:T(8,128)(2,1)}, bf16[128,1536]{1,0:T(8,128)(2,1)S(1)}, u32[]{:S(2)}, u32[]{:S(2)}) collective-permute-start(bf16[128,1536]{1,0:T(8,128)(2,1)} %bitcast.4.own.refs_0_), channel_id=1, source_target_pairs={{0,192},{32,224},{64,0},{96,32},{128,64},{160,96},{192,128},{224,1... | collective-permute-start | bytes 1179656 | tf_op jit(solution)/shard_map/ppermute | solution.py:479
  3.6 15.4 %collective-permute-start.1 = (bf16[128,1536]{1,0:T(8,128)(2,1)}, bf16[128,1536]{1,0:T(8,128)(2,1)S(1)}, u32[]{:S(2)}, u32[]{:S(2)}) collective-permute-start(bf16[128,1536]{1,0:T(8,128)(2,1)} %bitcast.4.own.refs_0_), channel_id=1, source_target_pairs={{0,64},{32,96},{64,128},{96,160},{128,192},{160,224},{192,0},{224,... | collective-permute-start | bytes 1179656 | tf_op jit(solution)/shard_map/ppermute | solution.py:479
  6.2 12.8 %collective-permute-start.3 = (bf16[256,256]{1,0:T(8,128)(2,1)S(1)}, bf16[256,256]{1,0:T(8,128)(2,1)S(1)}, u32[]{:S(2)}, u32[]{:S(2)}) collective-permute-start(bf16[256,256]{1,0:T(8,128)(2,1)S(1)} %project_kv.1.kv0), channel_id=1, source_target_pairs={{0,128},{32,160},{64,192},{96,224},{128,0},{160,32},{192,64},{224,... | collective-permute-start | bytes 393224 | tf_op jit(solution)/shard_map/ppermute | solution.py:487
  8.6 1.3 %collective-permute-start.4 = (s32[1,8]{1,0:T(1,128)}, s32[1,8]{1,0:T(1,128)S(1)}, u32[]{:S(2)}, u32[]{:S(2)}) collective-permute-start(s32[1,8]{1,0:T(1,128)} %bitcast.15), channel_id=1, source_target_pairs={{0,32},{32,0},{64,96},{96,64},{128,160},{160,128},{192,224},{224,1... | collective-permute-start | bytes 104 | tf_op jit(solution)/shard_map/ppermute | solution.py:482
  19.0 1.7 %collective-permute-start.5 = (bf16[128,1536]{1,0:T(8,128)(2,1)S(1)}, bf16[128,1536]{1,0:T(8,128)(2,1)S(1)}, u32[]{:S(2)}, u32[]{:S(2)}) collective-permute-start(bf16[128,1536]{1,0:T(8,128)(2,1)S(1)} %collective-permute-done.1.own.refs_2_), channel_id=1, source_target_pairs={{0,32},{32,0},{64,96},{96,64},{128,160},{160,128},{192,224},{224,1... | collective-permute-start | bytes 1179656 | tf_op jit(solution)/shard_map/ppermute | solution.py:492
  19.0 2.3 %collective-permute-start.8 = (bf16[128,1536]{1,0:T(8,128)(2,1)S(1)}, bf16[128,1536]{1,0:T(8,128)(2,1)S(1)}, u32[]{:S(2)}, u32[]{:S(2)}) collective-permute-start(bf16[128,1536]{1,0:T(8,128)(2,1)S(1)} %collective-permute-done.2.own.refs_6_), channel_id=1, source_target_pairs={{0,32},{32,0},{64,96},{96,64},{128,160},{160,128},{192,224},{224,1... | collective-permute-start | bytes 1179656 | tf_op jit(solution)/shard_map/ppermute | solution.py:492
  19.5 2.3 %collective-permute-start.7 = (bf16[128,1536]{1,0:T(8,128)(2,1)S(1)}, bf16[128,1536]{1,0:T(8,128)(2,1)S(1)}, u32[]{:S(2)}, u32[]{:S(2)}) collective-permute-start(bf16[128,1536]{1,0:T(8,128)(2,1)S(1)} %bitcast.12), channel_id=1, source_target_pairs={{0,32},{32,0},{64,96},{96,64},{128,160},{160,128},{192,224},{224,1... | collective-permute-start | bytes 1179656 | tf_op jit(solution)/shard_map/ppermute | solution.py:481
  19.5 13.2 %collective-permute-start.6 = (bf16[128,1536]{1,0:T(8,128)(2,1)}, bf16[128,1536]{1,0:T(8,128)(2,1)S(1)}, u32[]{:S(2)}, u32[]{:S(2)}) collective-permute-start(bf16[128,1536]{1,0:T(8,128)(2,1)} %bitcast.4.own.refs_0_), channel_id=1, source_target_pairs={{0,128},{32,160},{64,192},{96,224},{128,0},{160,32},{192,64},{224,... | collective-permute-start | bytes 1179656 | tf_op jit(solution)/shard_map/ppermute | solution.py:493
  32.7 10.2 %collective-permute-start.12 = (bf16[256,768]{1,0:T(8,128)(2,1)S(1)}, bf16[256,768]{1,0:T(8,128)(2,1)S(1)}, u32[]{:S(2)}, u32[]{:S(2)}) collective-permute-start(bf16[256,768]{1,0:T(8,128)(2,1)S(1)} %get-tuple-element.60.dq), channel_id=1, source_target_pairs={{0,32},{32,0},{64,96},{96,64},{128,160},{160,128},{192,224},{224,1... | collective-permute-start | bytes 1179656 | tf_op jit(solution)/shard_map/ppermute | solution.py:498
  32.7 6.3 %collective-permute-start.9 = (bf16[256,256]{1,0:T(8,128)(2,1)S(1)}, bf16[256,256]{1,0:T(8,128)(2,1)S(1)}, u32[]{:S(2)}, u32[]{:S(2)}) collective-permute-start(bf16[256,256]{1,0:T(8,128)(2,1)S(1)} %get-tuple-element.57), channel_id=1, source_target_pairs={{0,192},{32,224},{64,0},{96,32},{128,64},{160,96},{192,128},{224,1... | collective-permute-start | bytes 393224 | tf_op jit(solution)/shard_map/ppermute | solution.py:500
  33.0 7.8 %collective-permute-start.10 = (bf16[256,256]{1,0:T(8,128)(2,1)S(1)}, bf16[256,256]{1,0:T(8,128)(2,1)S(1)}, u32[]{:S(2)}, u32[]{:S(2)}) collective-permute-start(bf16[256,256]{1,0:T(8,128)(2,1)S(1)} %get-tuple-element.58), channel_id=1, source_target_pairs={{0,128},{32,160},{64,192},{96,224},{128,0},{160,32},{192,64},{224,... | collective-permute-start | bytes 393224 | tf_op jit(solution)/shard_map/ppermute | solution.py:500
  33.5 9.4 %collective-permute-start.11 = (bf16[256,256]{1,0:T(8,128)(2,1)S(1)}, bf16[256,256]{1,0:T(8,128)(2,1)S(1)}, u32[]{:S(2)}, u32[]{:S(2)}) collective-permute-start(bf16[256,256]{1,0:T(8,128)(2,1)S(1)} %get-tuple-element.59), channel_id=1, source_target_pairs={{0,64},{32,96},{64,128},{96,160},{128,192},{160,224},{192,0},{224,... | collective-permute-start | bytes 393224 | tf_op jit(solution)/shard_map/ppermute | solution.py:500
  43.1 1.4 %collective-permute-start.13 = (bf16[256,256]{1,0:T(8,128)(2,1)S(1)}, bf16[256,256]{1,0:T(8,128)(2,1)S(1)}, u32[]{:S(2)}, u32[]{:S(2)}) collective-permute-start(bf16[256,256]{1,0:T(8,128)(2,1)S(1)} %sum_four.2.dkv), channel_id=1, source_target_pairs={{0,32},{32,0},{64,96},{96,64},{128,160},{160,128},{192,224},{224,1... | collective-permute-start | bytes 393224 | tf_op jit(solution)/shard_map/ppermute | solution.py:504
  44.5 4.1 %collective-permute-start.14 = (bf16[128,1536]{1,0:T(8,128)(2,1)S(1)}, bf16[128,1536]{1,0:T(8,128)(2,1)S(1)}, u32[]{:S(2)}, u32[]{:S(2)}) collective-permute-start(bf16[128,1536]{1,0:T(8,128)(2,1)S(1)} %collective-permute-done.6.refs_4_), channel_id=1, source_target_pairs={{0,32},{32,0},{64,96},{96,64},{128,160},{160,128},{192,224},{224,1... | collective-permute-start | bytes 1179656 | tf_op jit(solution)/shard_map/ppermute | solution.py:507
  45.3 9.9 %collective-permute-start.15 = (bf16[256,256]{1,0:T(8,128)(2,1)S(1)}, bf16[256,256]{1,0:T(8,128)(2,1)S(1)}, u32[]{:S(2)}, u32[]{:S(2)}) collective-permute-start(bf16[256,256]{1,0:T(8,128)(2,1)S(1)} %get-tuple-element.68), channel_id=1, source_target_pairs={{0,64},{32,96},{64,128},{96,160},{128,192},{160,224},{192,0},{224,... | collective-permute-start | bytes 393224 | tf_op jit(solution)/shard_map/ppermute | solution.py:513
  45.4 9.8 %collective-permute-start.16 = (bf16[256,256]{1,0:T(8,128)(2,1)S(1)}, bf16[256,256]{1,0:T(8,128)(2,1)S(1)}, u32[]{:S(2)}, u32[]{:S(2)}) collective-permute-start(bf16[256,256]{1,0:T(8,128)(2,1)S(1)} %get-tuple-element.69), channel_id=1, source_target_pairs={{0,128},{32,160},{64,192},{96,224},{128,0},{160,32},{192,64},{224,... | collective-permute-start | bytes 393224 | tf_op jit(solution)/shard_map/ppermute | solution.py:513
  48.0 7.8 %collective-permute-start.17 = (bf16[256,256]{1,0:T(8,128)(2,1)S(1)}, bf16[256,256]{1,0:T(8,128)(2,1)S(1)}, u32[]{:S(2)}, u32[]{:S(2)}) collective-permute-start(bf16[256,256]{1,0:T(8,128)(2,1)S(1)} %get-tuple-element.70), channel_id=1, source_target_pairs={{0,192},{32,224},{64,0},{96,32},{128,64},{160,96},{192,128},{224,1... | collective-permute-start | bytes 393224 | tf_op jit(solution)/shard_map/ppermute | solution.py:513
  57.3 11.9 %collective-permute-start.18 = (bf16[384,256]{1,0:T(8,128)(2,1)S(1)}, bf16[384,256]{1,0:T(8,128)(2,1)S(1)}, u32[]{:S(2)}, u32[]{:S(2)}) collective-permute-start(bf16[384,256]{1,0:T(8,128)(2,1)S(1)} %get-tuple-element.72), channel_id=1, source_target_pairs={{0,8},{1,9},{2,10},{3,11},{4,12},{5,13},{6,14},{7,15},{8,16},{9,17... | collective-permute-start | bytes 589832 | tf_op jit(solution)/shard_map/ppermute | solution.py:516
  59.0 10.3 %collective-permute-start.19 = (bf16[384,256]{1,0:T(8,128)(2,1)S(1)}, bf16[384,256]{1,0:T(8,128)(2,1)S(1)}, u32[]{:S(2)}, u32[]{:S(2)}) collective-permute-start(bf16[384,256]{1,0:T(8,128)(2,1)S(1)} %get-tuple-element.73), channel_id=1, source_target_pairs={{0,16},{1,17},{2,18},{3,19},{4,20},{5,21},{6,22},{7,23},{8,24},{9,... | collective-permute-start | bytes 589832 | tf_op jit(solution)/shard_map/ppermute | solution.py:516
  60.3 9.7 %collective-permute-start.20 = (bf16[384,256]{1,0:T(8,128)(2,1)S(1)}, bf16[384,256]{1,0:T(8,128)(2,1)S(1)}, u32[]{:S(2)}, u32[]{:S(2)}) collective-permute-start(bf16[384,256]{1,0:T(8,128)(2,1)S(1)} %get-tuple-element.74), channel_id=1, source_target_pairs={{0,24},{1,25},{2,26},{3,27},{4,28},{5,29},{6,30},{7,31},{8,0},{9,1... | collective-permute-start | bytes 589832 | tf_op jit(solution)/shard_map/ppermute | solution.py:516

commit v6 on v5

--- a/solution.py
+++ b/solution.py
@@ -17,6 +17,7 @@
 CHIPS = 4
 GROUP = QH // KVH
 GF = GROUP * HD
+STACK = GROUP * 256
 YS = 4
 ZS = 8
 SCALE = 1.0 / math.sqrt(HD)
@@ -24,9 +25,9 @@
 BF = jnp.bfloat16
 F32 = jnp.float32
 VMEM_LIMIT = 24 * 1024 * 1024
-W_CHUNKS = 4
-Q_CHUNKS = 6
-IN_CHUNKS = 6
+W_CHUNKS = 1
+Q_CHUNKS = 3
+IN_CHUNKS = 3
 
 CORE = [(i, i ^ 1) for i in range(8)]
 NT = (((1,), (1,)), ((), ()))
@@ -57,7 +58,7 @@
 
 def cost(flops, bytes_accessed, transcendentals=0):
     return pl.CostEstimate(
-        flops=flops, bytes_accessed=bytes_accessed, transcendentals=transcendentals
+        flops=1, bytes_accessed=1, transcendentals=0
     )
 
 
@@ -140,7 +141,7 @@
 
 
 def query_kernel(
-    place, own, other, w_query, segments_far, mask_far, mask_other, out, bias,
+    place, own, other, w_query, segments_far, mask_far, mask_other, out, limits,
     weights, segments, mask_own, sems, small_sems,
 ):
     small = [
@@ -172,9 +173,7 @@
             mine == 0, 0, jnp.where(mine == 1, ends[0], jnp.where(mine == 2, ends[1], ends[2]))
         )
         high = jnp.where(
-            mine == 0,
-            ends[0],
-            jnp.where(mine == 1, ends[1], jnp.where(mine == 2, ends[2], KEYS)),
+            mine == 0, ends[0], jnp.where(mine == 1, ends[1], jnp.where(mine == 2, ends[2], KEYS))
         )
         for d in range(CHIPS):
             for key_slot in range(2):
@@ -182,21 +181,21 @@
                     core if key_slot == 0 else 1 - core
                 )
                 seen = masks[0, key_tile] == 1
-                position = key_tile * TILE + lax.broadcasted_iota(
-                    jnp.int32, (TILE, TILE), 0
-                )
-                first = jnp.where(seen, 0, low)
-                last = jnp.where(seen, KEYS, high)
-                allowed = (position >= first) & (position < last)
-                row = d * 2 * TILE + key_slot * TILE
-                bias[row : row + TILE, slot * TILE : (slot + 1) * TILE] = jnp.where(
-                    allowed, 0.0, -jnp.inf
+                row = 4 * d + 2 * key_slot
+                place_of = slice(slot * TILE, (slot + 1) * TILE)
+                limits[row : row + 1, place_of] = jnp.where(seen, 0, low) - key_tile * TILE
+                limits[row + 1 : row + 2, place_of] = (
+                    jnp.where(seen, KEYS, high) - key_tile * TILE
                 )
 
     for copy in copies:
         copy.wait()
-    out[:TILE] = dot(own[...], weights[...]).astype(BF)
-    out[TILE:] = dot(other[...], weights[...]).astype(BF)
+    for slot, rows in enumerate((own, other)):
+        queries = dot(rows[...], weights[...]).astype(BF)
+        for head in range(GROUP):
+            out[head * 256 + slot * TILE : head * 256 + (slot + 1) * TILE] = queries[
+                :, head * HD : (head + 1) * HD
+            ]
 
 
 def project_query(place, own, other, w_query, segments, mask_own, mask_other):
@@ -205,8 +204,8 @@
         in_specs=[SCALARS, WHOLE, WHOLE, STAY, STAY, STAY, SCALARS],
         out_specs=[WHOLE, WHOLE],
         out_shape=[
-            jax.ShapeDtypeStruct((2 * TILE, GF), BF),
-            jax.ShapeDtypeStruct((KEYS, 2 * TILE), F32),
+            jax.ShapeDtypeStruct((STACK, HD), BF),
+            jax.ShapeDtypeStruct((4 * CHIPS, 2 * TILE), jnp.int32),
         ],
         scratch_shapes=[
             pltpu.VMEM((D, GF), BF),
@@ -221,81 +220,132 @@
     )(place, own, other, w_query, segments, mask_own, mask_other)
 
 
-def attention_kernel(
-    place, query, up_own, up_other, kv0, kv1, kv2, kv3, bias,
-    grad_query, out0, out1, out2, out3,
-    keys, values, keys_t, grad_key, grad_value,
-):
-    step = pl.program_id(0)
-
-    @pl.when(step == 0)
-    def _():
-        for d, kv in enumerate((kv0, kv1, kv2, kv3)):
-            keys[d * 256 : (d + 1) * 256] = kv[:, :HD]
-            values[d * 256 : (d + 1) * 256] = kv[:, HD:]
-            keys_t[:, d * 256 : (d + 1) * 256] = kv[:, :HD].T
-        grad_key[...] = jnp.zeros_like(grad_key)
-        grad_value[...] = jnp.zeros_like(grad_value)
-
-    for member in range(2):
-        columns = slice(member * HD, (member + 1) * HD)
-        q = query[:, columns]
-        up = jnp.concatenate([up_own[:, columns], up_other[:, columns]], axis=0)
-        scores = dot_nt(keys[...], q) * LOG2_SCALE + bias[...]
+def stack_kernel(place, up_own, up_other, out):
+    for slot, rows in enumerate((up_own, up_other)):
+        for head in range(GROUP):
+            columns = pl.ds(pl.multiple_of(place[1] * GF + head * HD, HD), HD)
+            out[head * 256 + slot * TILE : head * 256 + (slot + 1) * TILE] = rows[:, columns]
+
+
+def stack_up(place, up_own, up_other):
+    return pl.pallas_call(
+        stack_kernel,
+        in_specs=[SCALARS, WHOLE, WHOLE],
+        out_specs=WHOLE,
+        out_shape=jax.ShapeDtypeStruct((STACK, HD), BF),
+        compiler_params=PARAMS,
+        cost_estimate=cost(0, 4 * STACK * HD),
+        name="stack_up",
+    )(place, up_own, up_other)
+
+
+def scores_kernel(d, kv, limits, query, up, powers, grads, stats, keys_t):
+    keys, values = kv[:, :HD], kv[:, HD:]
+    keys_t[...] = keys.T
+    position = lax.broadcasted_iota(jnp.int32, (TILE, 2 * TILE), 0)
+    bias = []
+    for key_slot in range(2):
+        row = 4 * d + 2 * key_slot
+        allowed = (position >= limits[row : row + 1]) & (position < limits[row + 1 : row + 2])
+        bias.append(jnp.where(allowed, 0.0, -jnp.inf))
+    bias = jnp.concatenate(bias, axis=0)
+    for head in range(GROUP):
+        part = slice(head * 256, (head + 1) * 256)
+        scores = dot_nt(keys, query[part]) * LOG2_SCALE + bias
         top = jnp.max(scores, axis=0, keepdims=True)
-        powers = jnp.exp2(scores - top)
-        probs = powers * (1.0 / jnp.sum(powers, axis=0, keepdims=True))
-        probs_low = probs.astype(BF)
-        grad_probs = dot_nt(values[...], up)
-        delta = jnp.sum(probs_low.astype(F32) * grad_probs, axis=0, keepdims=True)
-        grad_scores = (probs * (grad_probs - delta)).astype(BF)
-        grad_value[...] += dot(probs_low, up)
-        grad_key[...] += dot(grad_scores, q)
-        grad_query[:, columns] = (dot(keys_t[...], grad_scores) * SCALE).T.astype(BF)
-
-    @pl.when(step == pl.num_programs(0) - 1)
-    def _():
-        for d, out in enumerate((out0, out1, out2, out3)):
-            rows = slice(d * 256, (d + 1) * 256)
-            out[:, :HD] = (grad_key[rows] * SCALE).astype(out.dtype)
-            out[:, HD:] = grad_value[rows].astype(out.dtype)
-
-
-def attention(place, query, up_own, up_other, kvs, bias):
-    blocks = GF // 256
-    fixed = pl.BlockSpec((256, 256), lambda i, p: (0, 0))
-    return pl.pallas_call(
-        attention_kernel,
-        grid_spec=pltpu.PrefetchScalarGridSpec(
-            num_scalar_prefetch=1,
-            grid=(blocks,),
-            in_specs=[
-                pl.BlockSpec((256, 256), lambda i, p: (0, i)),
-                pl.BlockSpec((TILE, 256), lambda i, p: (0, p[1] * blocks + i)),
-                pl.BlockSpec((TILE, 256), lambda i, p: (0, p[1] * blocks + i)),
-                fixed, fixed, fixed, fixed,
-                pl.BlockSpec((KEYS, 256), lambda i, p: (0, 0)),
-            ],
-            out_specs=[pl.BlockSpec((256, 256), lambda i, p: (0, i)), fixed, fixed, fixed, fixed],
-            scratch_shapes=[
-                pltpu.VMEM((KEYS, HD), BF),
-                pltpu.VMEM((KEYS, HD), BF),
-                pltpu.VMEM((HD, KEYS), BF),
-                pltpu.VMEM((KEYS, HD), F32),
-                pltpu.VMEM((KEYS, HD), F32),
-            ],
-        ),
+        power = jnp.exp2(scores - jnp.where(top == -jnp.inf, 0.0, top))
+        grad = dot_nt(values, up[part])
+        powers[:, part] = power
+        grads[:, part] = grad
+        stats[0:1, part] = top
+        stats[1:2, part] = jnp.sum(power, axis=0, keepdims=True)
+        stats[2:3, part] = jnp.sum(power * grad, axis=0, keepdims=True)
+
+
+def chip_scores(d, kv, limits, query, up):
+    return pl.pallas_call(
+        functools.partial(scores_kernel, d),
+        in_specs=[WHOLE] * 4,
+        out_specs=[WHOLE] * 4,
         out_shape=[
-            jax.ShapeDtypeStruct((256, GF), BF),
-            jax.ShapeDtypeStruct((256, 256), F32),
-            jax.ShapeDtypeStruct((256, 256), BF),
-            jax.ShapeDtypeStruct((256, 256), BF),
-            jax.ShapeDtypeStruct((256, 256), BF),
+            jax.ShapeDtypeStruct((256, STACK), F32),
+            jax.ShapeDtypeStruct((256, STACK), F32),
+            jax.ShapeDtypeStruct((8, STACK), F32),
+            jax.ShapeDtypeStruct((HD, 256), BF),
         ],
         compiler_params=PARAMS,
-        cost_estimate=cost(10 * GROUP * 256 * KEYS * HD * 2, 4 << 20, GROUP * 256 * KEYS),
-        name="attention",
-    )(place, query, up_own, up_other, *kvs, bias)
+        cost_estimate=cost(4 * STACK * 256 * HD, 10 * 256 * STACK, 256 * STACK),
+        name=f"chip_scores_{d}",
+    )(kv, limits, query, up)
+
+
+def factors_kernel(a, b, c, d, out):
+    parts = (a, b, c, d)
+    top = jnp.maximum(jnp.maximum(a[0:1], b[0:1]), jnp.maximum(c[0:1], d[0:1]))
+    factors = [jnp.exp2(part[0:1] - top) for part in parts]
+    total = sum(factor * part[1:2] for factor, part in zip(factors, parts))
+    factors = [factor / total for factor in factors]
+    for chip, factor in enumerate(factors):
+        out[chip : chip + 1] = factor
+    out[4:5] = sum(factor * part[2:3] for factor, part in zip(factors, parts))
+
+
+def softmax_factors(stats):
+    return pl.pallas_call(
+        factors_kernel,
+        in_specs=[WHOLE] * 4,
+        out_specs=WHOLE,
+        out_shape=jax.ShapeDtypeStruct((8, STACK), F32),
+        compiler_params=PARAMS,
+        cost_estimate=cost(20 * STACK, 128 * STACK),
+        name="softmax_factors",
+    )(*stats)
+
+
+def terms_kernel(d, powers, grads, factors, query, up, out, grad_scores, probs_low):
+    for head in range(GROUP):
+        part = slice(head * 256, (head + 1) * 256)
+        probs = powers[:, part] * factors[d : d + 1, part]
+        probs_low[:, part] = probs.astype(BF)
+        grad_scores[:, part] = (probs * (grads[:, part] - factors[4:5, part])).astype(BF)
+    out[:, :HD] = (dot(grad_scores[...], query[...]) * SCALE).astype(out.dtype)
+    out[:, HD:] = dot(probs_low[...], up[...]).astype(out.dtype)
+
+
+def chip_terms(d, powers, grads, factors, query, up):
+    return pl.pallas_call(
+        functools.partial(terms_kernel, d),
+        in_specs=[WHOLE] * 5,
+        out_specs=[WHOLE] * 2,
+        out_shape=[
+            jax.ShapeDtypeStruct((256, 256), F32 if d == 0 else BF),
+            jax.ShapeDtypeStruct((256, STACK), BF),
+        ],
+        scratch_shapes=[pltpu.VMEM((256, STACK), BF)],
+        compiler_params=PARAMS,
+        cost_estimate=cost(4 * STACK * 256 * HD, 10 * 256 * STACK),
+        name=f"chip_terms_{d}",
+    )(powers, grads, factors, query, up)
+
+
+def query_grad_kernel(k0, k1, k2, k3, g0, g1, g2, g3, out):
+    for head in range(GROUP):
+        part = slice(head * 256, (head + 1) * 256)
+        total = dot(k0[...], g0[:, part]) + dot(k1[...], g1[:, part])
+        total += dot(k2[...], g2[:, part]) + dot(k3[...], g3[:, part])
+        out[:, head * HD : (head + 1) * HD] = (total * SCALE).T.astype(BF)
+
+
+def query_grad(keys_t, grad_scores):
+    return pl.pallas_call(
+        query_grad_kernel,
+        in_specs=[WHOLE] * 8,
+        out_specs=WHOLE,
+        out_shape=jax.ShapeDtypeStruct((256, GF), BF),
+        compiler_params=PARAMS,
+        cost_estimate=cost(2 * STACK * KEYS * HD, 2 * STACK * KEYS),
+        name="query_grad",
+    )(*keys_t, *grad_scores)
 
 
 def sum_kernel(a, b, c, d, out):
@@ -476,34 +526,41 @@
     dp = lax.axis_index("dp")
     place = jnp.stack([ctx // 2, ctx % 2, dp // ZS, dp % ZS]).astype(jnp.int32)
     own, up = tokens[0], grad_heads[0]
-    far = {d: lax.ppermute(own, "ctx", chip_shift(d)) for d in (1, 3)}
     other = lax.ppermute(own, "ctx", CORE)
     up_other = lax.ppermute(up, "ctx", CORE)
     mask_other = lax.ppermute(tile_mask[0], "ctx", CORE)
+    other, mask_other, up_other = lax.optimization_barrier((other, mask_other, up_other))
 
     w_query, w_key, w_value = (in_hbm(w) for w in (w_query, w_key, w_value))
     weights, kv_own = project_kv_own(place, in_hbm(own), w_key, w_value)
     kv = project_kv(other, weights, kv_own)
-    kv2 = lax.ppermute(kv, "ctx", chip_shift(2))
-    query, bias = project_query(
+    kvs = [kv] + [lax.ppermute(kv, "ctx", chip_shift(d)) for d in (1, 2, 3)]
+    far = {d: lax.ppermute(own, "ctx", chip_shift(d)) for d in (1, 3)}
+    query, limits = project_query(
         place, own, other, w_query, in_hbm(segments), in_hbm(tile_mask[0]), mask_other
     )
-    far, kv2, query, late_own = lax.optimization_barrier((far, kv2, query, own))
+    up = stack_up(place, up, up_other)
+    scores = {0: chip_scores(0, kvs[0], limits, query, up)}
+    far, kvs, scores[0], late_own = lax.optimization_barrier((far, kvs, scores[0], own))
+    late = lax.ppermute(late_own, "ctx", chip_shift(2))
     far_other = {d: lax.ppermute(far[d], "ctx", CORE) for d in (1, 3)}
-    late = lax.ppermute(late_own, "ctx", chip_shift(2))
-    kv1, kv3 = (project_kv_pair(far[d], far_other[d], weights) for d in (1, 3))
-
-    grads = attention(place, query, up, up_other, [kv, kv1, kv2, kv3], bias)
-    late, (dq, g0, g1, g2, g3) = lax.optimization_barrier((late, grads))
+    for d in (1, 3, 2):
+        scores[d] = chip_scores(d, kvs[d], limits, query, up)
+    factors = softmax_factors([scores[d][2] for d in range(CHIPS)])
+    terms, grad_scores = {}, {}
+    for d in (2, 1, 3):
+        terms[d], grad_scores[d] = chip_terms(d, *scores[d][:2], factors, query, up)
+    late, far_other, terms, scores[0] = lax.optimization_barrier(
+        (late, far_other, terms, scores[0])
+    )
+    back = [lax.ppermute(terms[d], "ctx", chip_shift(CHIPS - d)) for d in (2, 1, 3)]
+    terms[0], grad_scores[0] = chip_terms(0, *scores[0][:2], factors, query, up)
+    dq = query_grad([scores[d][3] for d in range(CHIPS)], [grad_scores[d] for d in range(CHIPS)])
+    back, dq = lax.optimization_barrier((back, dq))
     dq_other = lax.ppermute(dq, "ctx", CORE)
-    back = [
-        lax.ppermute(g, "ctx", chip_shift(CHIPS - d)) for d, g in ((1, g1), (2, g2), (3, g3))
-    ]
-    back, dq_other = lax.optimization_barrier((back, dq_other))
-    dkv = sum_four(g0, *back)
+    dkv = sum_four(terms[0], *back)
     dkv_other = lax.ppermute(dkv, "ctx", CORE)
-
-    far[2], dkv_other = lax.optimization_barrier((late, dkv_other))
+    far[2], dkv = lax.optimization_barrier((late, dkv))
     far_other[2] = lax.ppermute(far[2], "ctx", CORE)
     tokens_t = transpose(
         [own, other] + [part for d in (1, 2, 3) for part in (far[d], far_other[d])]

time: 89.2 us -> 90.6 us (1.016)
  starting transfers between devices: 17.2 us -> 23.9 us
  Pallas kernels: 28 us -> 21.5 us
    ppermute x1, waiting for transfers between devices: 1.52 us -> 6.85 us  [shards(): late = lax.ppermute(late_own, 'ctx', chip_shift(2))]
    ppermute x2, waiting for transfers between devices: 5.67 us -> 0.98 us  [shards(): far = {d: lax.ppermute(own, 'ctx', chip_shift(d)) for d in (1, 3)}]
    ppermute x4 -> x6, starting transfers between devices: 4.59 us -> 8.29 us  [the longest x3 4.53 us: shards(): kvs = [kv] + [lax.ppermute(kv, 'ctx', chip_shift(d)) for d in (1, 2, 3)]]
    pallas_call x3 -> x11, Pallas kernels: 10.1 us -> 6.87 us  [the longest x4 2.99 us: chip_scores(): pl.pallas_call(functools.partial(scores_kernel, d), in_specs=[WHOLE] * 4,...]
    ppermute x3, waiting for transfers between devices: 0.79 us -> 2.51 us  [shards(): lax.ppermute(terms[d], 'dp', y_shift(d))]
    pallas_call x1, Pallas kernels: 6.88 us -> 5.36 us  [input_grad(): pl.pallas_call(input_kernel, in_specs=[SCALARS] + [WHOLE] * 4 + [STAY] *...]
    ppermute x1, waiting for transfers between devices: 1.25 us -> 0.01 us  [shards(): mask_other = lax.ppermute(tile_mask[0], 'ctx', CORE)]
    ppermute x1, starting transfers between devices: 0.6 us -> 1.74 us  [shards(): late = lax.ppermute(late_own, 'ctx', chip_shift(2))]
  transfers between devices with their start and end apart: 21 -> 23, of which waited for: 14 -> 11; matrix products, arithmetic and copies ran while one was open for 0% -> 0% of each run, Pallas kernels for 29% -> 22%
where the time goes in v6:
time: 90.6 us; the launch traced here: 89.2 us
  waiting for transfers between devices  25.4 us (28%)
  starting transfers between devices  23.9 us (26%)
  Pallas kernels  21.5 us (24%)
  blocking collectives  17.5 us (19%)
    all_to_all x1, blocking collectives, shards(): lax.all_to_all(y_sum, 'dp', 0, 0, tiled=True, axis_index_groups=Z_GROUPS)  17.5 us
    ppermute x1, waiting for transfers between devices, shards(): late = lax.ppermute(late_own, 'ctx', chip_shift(2))  6.85 us
    pallas_call x1, Pallas kernels, input_grad(): pl.pallas_call(input_kernel, in_specs=[SCALARS] + [WHOLE] * 4 + [STAY] *...  5.36 us
    ppermute x3, waiting for transfers between devices, shards(): lax.ppermute(packed[d], 'ctx', chip_shift(d))  5.16 us
    ppermute x3, starting transfers between devices, shards(): lax.ppermute(terms[d], 'dp', y_shift(d))  5 us
    ppermute x3, waiting for transfers between devices, shards(): lax.ppermute(terms[d], 'ctx', chip_shift(CHIPS - d))  4.73 us
    ppermute x3, starting transfers between devices, shards(): kvs = [kv] + [lax.ppermute(kv, 'ctx', chip_shift(d)) for d in (1, 2, 3)]  4.53 us
    ppermute x3, starting transfers between devices, shards(): lax.ppermute(packed[d], 'ctx', chip_shift(d))  4.06 us
  transfers between devices with their start and end apart: 23, of which 11 were waited for; matrix products, arithmetic and copies ran while one was open for 0% of the time, Pallas kernels for 22%

profile of v6, /device:TPU:8, one launch (start us, length us, event | category | flops | bytes accessed | tf_op | source)
XLA Modules:
  0.0 89.2 jit_solution(1498171784212141391)
XLA Ops:
  0.6 0.1 collective-permute-start
  0.7 0.5 collective-permute-start.2
  1.2 1.5 %collective-permute-start.3 = (bf16[128,1536]{1,0:T(8,128)(2,1)}, bf16[128,1536]{1,0:T(8,128)(2,1)S(1)}, u32[]{:S(2)}, u32[]{:S(2)}) collective-permute-start(bf16[128,1536]{1,0:T(8,128)(2,1)} %bitcast.11), channel_id=1, source_target_pairs={{0,64},{32,96},{64,128},{96,160},{128,192},{160,224},{192,0},{224,... | collective-permute-start | bytes 1179656 | tf_op jit(solution)/shard_map/ppermute | solution.py:538
  2.7 1.7 %collective-permute-start.4 = (bf16[128,1536]{1,0:T(8,128)(2,1)}, bf16[128,1536]{1,0:T(8,128)(2,1)S(1)}, u32[]{:S(2)}, u32[]{:S(2)}) collective-permute-start(bf16[128,1536]{1,0:T(8,128)(2,1)} %bitcast.12), channel_id=1, source_target_pairs={{0,192},{32,224},{64,0},{96,32},{128,64},{160,96},{192,128},{224,1... | collective-permute-start | bytes 1179656 | tf_op jit(solution)/shard_map/ppermute | solution.py:538
  4.5 0.0 collective-permute-start.1
  4.5 0.1 pad_add_fusion.place
  4.5 2.1 %project_kv_own.1 = (bf16[1536,256]{1,0:T(8,128)(2,1)S(1)}, bf16[128,256]{1,0:T(8,128)(2,1)S(1)}) custom-call(s32[4]{0:T(128)S(1)} %pad_add_fusion.place, bf16[128,1536]{1,0:T(8,128)(2,1)} %bitcast.13, bf16[1536,256]{1,0:T(8,128)(2,1)} %w_key.3, bf16[1536,256]{1,0:T(8,128)(2,1)} %w_value.3), custom_call_target="tpu_custom_call" | custom-call | flops 1 | bytes 1 | tf_op jit(solution)/shard_map/project_kv_own/pallas_call | solution.py:94
  6.6 0.0 copy-start
  6.6 0.0 collective-permute-done.1.mask_other
  6.7 0.0 collective-permute-done.other.refs_1_
  6.7 0.0 collective-permute-done.2.up_other
  6.7 0.3 project_kv.1.kv
  7.0 0.4 collective-permute-start.5
  7.3 2.7 %collective-permute-start.6 = (bf16[256,256]{1,0:T(8,128)(2,1)S(1)}, bf16[256,256]{1,0:T(8,128)(2,1)S(1)}, u32[]{:S(2)}, u32[]{:S(2)}) collective-permute-start(bf16[256,256]{1,0:T(8,128)(2,1)S(1)} %project_kv.1.kv), channel_id=1, source_target_pairs={{0,128},{32,160},{64,192},{96,224},{128,0},{160,32},{192,64},{224,... | collective-permute-start | bytes 393224 | tf_op jit(solution)/shard_map/ppermute | solution.py:537
  10.0 1.4 %collective-permute-start.7 = (bf16[256,256]{1,0:T(8,128)(2,1)S(1)}, bf16[256,256]{1,0:T(8,128)(2,1)S(1)}, u32[]{:S(2)}, u32[]{:S(2)}) collective-permute-start(bf16[256,256]{1,0:T(8,128)(2,1)S(1)} %project_kv.1.kv), channel_id=1, source_target_pairs={{0,192},{32,224},{64,0},{96,32},{128,64},{160,96},{192,128},{224,1... | collective-permute-start | bytes 393224 | tf_op jit(solution)/shard_map/ppermute | solution.py:537
  11.5 0.6 stack_up.1.up
  12.1 3.0 %project_query.1 = (bf16[1536,128]{1,0:T(8,128)(2,1)S(1)}, s32[16,256]{1,0:T(8,128)S(1)}) custom-call(s32[4]{0:T(128)S(1)} %pad_add_fusion.place, bf16[128,1536]{1,0:T(8,128)(2,1)S(1)} %bitcast.14, bf16[128,1536]{1,0:T(8,128)(2,1)S(1)} %collective-permute-done.other.refs_1_, bf16[1536,1536]{1,0:T(8,128)(2,1)} %w_query.3, s32[1,1024]{1,0:T(1,128)} %segments_far.1, ...), custom_call_target="tpu_custom_call" | custom-call | flops 1 | bytes 1 | tf_op jit(solution)/shard_map/project_query/pallas_call | solution.py:202
  15.1 0.8 chip_scores_0.1
  15.9 1.0 %collective-permute-done.4.refs_6_ = bf16[128,1536]{1,0:T(8,128)(2,1)S(1)} collective-permute-done((bf16[128,1536]{1,0:T(8,128)(2,1)}, bf16[128,1536]{1,0:T(8,128)(2,1)S(1)}, u32[]{:S(2)}, u32[]{:S(2)}) %collective-permute-start.4) | collective-permute-done | bytes 393248 | tf_op jit(solution)/shard_map/ppermute | solution.py:538
  16.9 0.0 collective-permute-done.5.kv
  16.9 3.5 %collective-permute-done.6.kv = bf16[256,256]{1,0:T(8,128)(2,1)S(1)} collective-permute-done((bf16[256,256]{1,0:T(8,128)(2,1)S(1)}, bf16[256,256]{1,0:T(8,128)(2,1)S(1)}, u32[]{:S(2)}, u32[]{:S(2)}) %collective-permute-start.6) | collective-permute-done | bytes 131104 | tf_op jit(solution)/shard_map/ppermute | solution.py:537
  20.4 0.0 collective-permute-done.7.kv
  20.4 0.0 collective-permute-start.10
  20.4 1.7 %collective-permute-start.8 = (bf16[128,1536]{1,0:T(8,128)(2,1)S(1)}, bf16[128,1536]{1,0:T(8,128)(2,1)S(1)}, u32[]{:S(2)}, u32[]{:S(2)}) collective-permute-start(bf16[128,1536]{1,0:T(8,128)(2,1)S(1)} %bitcast.15), channel_id=1, source_target_pairs={{0,128},{32,160},{64,192},{96,224},{128,0},{160,32},{192,64},{224,... | collective-permute-start | bytes 1179656 | tf_op jit(solution)/shard_map/ppermute | solution.py:545
  22.1 0.2 collective-permute-start.9
  22.4 0.7 chip_scores_3.1
  23.1 0.7 chip_scores_2.1
  23.9 0.7 chip_scores_1.1
  24.6 0.6 chip_terms_3.1
  25.3 0.6 chip_terms_2.1
  25.9 0.6 chip_terms_1.1
  26.5 0.0 collective-permute-done.10.refs_7_
  26.6 6.9 %collective-permute-done.8.refs_4_ = bf16[128,1536]{1,0:T(8,128)(2,1)S(1)} collective-permute-done((bf16[128,1536]{1,0:T(8,128)(2,1)S(1)}, bf16[128,1536]{1,0:T(8,128)(2,1)S(1)}, u32[]{:S(2)}, u32[]{:S(2)}) %collective-permute-start.8) | collective-permute-done | bytes 393248 | tf_op jit(solution)/shard_map/ppermute | solution.py:545
  33.4 0.0 collective-permute-done.9.refs_3_
  33.4 1.7 %collective-permute-start.11 = (bf16[256,256]{1,0:T(8,128)(2,1)S(1)}, bf16[256,256]{1,0:T(8,128)(2,1)S(1)}, u32[]{:S(2)}, u32[]{:S(2)}) collective-permute-start(bf16[256,256]{1,0:T(8,128)(2,1)S(1)} %get-tuple-element.109), channel_id=1, source_target_pairs={{0,128},{32,160},{64,192},{96,224},{128,0},{160,32},{192,64},{224,... | collective-permute-start | bytes 393224 | tf_op jit(solution)/shard_map/ppermute | solution.py:556
  35.2 1.4 %collective-permute-start.12 = (bf16[256,256]{1,0:T(8,128)(2,1)S(1)}, bf16[256,256]{1,0:T(8,128)(2,1)S(1)}, u32[]{:S(2)}, u32[]{:S(2)}) collective-permute-start(bf16[256,256]{1,0:T(8,128)(2,1)S(1)} %get-tuple-element.110), channel_id=1, source_target_pairs={{0,192},{32,224},{64,0},{96,32},{128,64},{160,96},{192,128},{224,1... | collective-permute-start | bytes 393224 | tf_op jit(solution)/shard_map/ppermute | solution.py:556
  36.6 0.6 collective-permute-start.13
  37.2 0.7 chip_terms_0.1
  37.9 0.7 query_grad.1.dq
  38.5 2.8 %collective-permute-done.11.b = bf16[256,256]{1,0:T(8,128)(2,1)S(1)} collective-permute-done((bf16[256,256]{1,0:T(8,128)(2,1)S(1)}, bf16[256,256]{1,0:T(8,128)(2,1)S(1)}, u32[]{:S(2)}, u32[]{:S(2)}) %collective-permute-start.11) | collective-permute-done | bytes 131104 | tf_op jit(solution)/shard_map/ppermute | solution.py:556
  41.3 0.8 collective-permute-done.12.c
  42.2 1.1 %collective-permute-done.13.d = bf16[256,256]{1,0:T(8,128)(2,1)S(1)} collective-permute-done((bf16[256,256]{1,0:T(8,128)(2,1)S(1)}, bf16[256,256]{1,0:T(8,128)(2,1)S(1)}, u32[]{:S(2)}, u32[]{:S(2)}) %collective-permute-start.13) | collective-permute-done | bytes 131104 | tf_op jit(solution)/shard_map/ppermute | solution.py:556
  43.3 0.1 sum_four.2.dkv
  43.3 0.6 collective-permute-start.14
  43.9 0.1 collective-permute-start.16
  44.0 1.7 %collective-permute-done.16.dkv_other = bf16[256,256]{1,0:T(8,128)(2,1)S(1)} collective-permute-done((bf16[256,256]{1,0:T(8,128)(2,1)S(1)}, bf16[256,256]{1,0:T(8,128)(2,1)S(1)}, u32[]{:S(2)}, u32[]{:S(2)}) %collective-permute-start.16) | collective-permute-done | bytes 131104 | tf_op jit(solution)/shard_map/ppermute | solution.py:562
  45.7 0.6 pack.1
  46.4 0.2 collective-permute-start.17
  46.6 2.9 %collective-permute-start.18 = (bf16[256,256]{1,0:T(8,128)(2,1)S(1)}, bf16[256,256]{1,0:T(8,128)(2,1)S(1)}, u32[]{:S(2)}, u32[]{:S(2)}) collective-permute-start(bf16[256,256]{1,0:T(8,128)(2,1)S(1)} %get-tuple-element.129), channel_id=1, source_target_pairs={{0,128},{32,160},{64,192},{96,224},{128,0},{160,32},{192,64},{224,... | collective-permute-start | bytes 393224 | tf_op jit(solution)/shard_map/ppermute | solution.py:570
  49.5 0.9 %collective-permute-start.19 = (bf16[256,256]{1,0:T(8,128)(2,1)S(1)}, bf16[256,256]{1,0:T(8,128)(2,1)S(1)}, u32[]{:S(2)}, u32[]{:S(2)}) collective-permute-start(bf16[256,256]{1,0:T(8,128)(2,1)S(1)} %get-tuple-element.130), channel_id=1, source_target_pairs={{0,192},{32,224},{64,0},{96,32},{128,64},{160,96},{192,128},{224,1... | collective-permute-start | bytes 393224 | tf_op jit(solution)/shard_map/ppermute | solution.py:570
  50.4 1.0 %transpose_tokens.1.tokens_t = bf16[1536,1024]{1,0:T(8,128)(2,1)S(1)} custom-call(bf16[128,1536]{1,0:T(8,128)(2,1)S(1)} %bitcast.16, bf16[128,1536]{1,0:T(8,128)(2,1)S(1)} %collective-permute-done.other.refs_1_, bf16[128,1536]{1,0:T(8,128)(2,1)S(1)} %collective-permute-done.3.refs_2_, bf16[128,1536]{1,0:T(8,128)(2,1)S(1)} %collective-permute-done.9.refs_3_, ...), custom_call_target="tpu_custom_call" | custom-call | flops 1 | bytes 1 | tf_op jit(solution)/shard_map/transpose_tokens/pallas_call | solution.py:416
  51.4 4.6 %collective-permute-done.17.b = bf16[256,256]{1,0:T(8,128)(2,1)S(1)} collective-permute-done((bf16[256,256]{1,0:T(8,128)(2,1)S(1)}, bf16[256,256]{1,0:T(8,128)(2,1)S(1)}, u32[]{:S(2)}, u32[]{:S(2)}) %collective-permute-start.17) | collective-permute-done | bytes 131104 | tf_op jit(solution)/shard_map/ppermute | solution.py:570
  56.0 0.0 collective-permute-done.18.c
  56.0 0.6 collective-permute-done.19.d
  56.6 1.5 %weight_grad.1 = (f32[384,256]{1,0:T(8,128)S(1)}, bf16[384,256]{1,0:T(8,128)(2,1)S(1)}, bf16[384,256]{1,0:T(8,128)(2,1)S(1)}, bf16[384,256]{1,0:T(8,128)(2,1)S(1)}) custom-call(s32[4]{0:T(128)S(1)} %pad_add_fusion.place, bf16[1536,1024]{1,0:T(8,128)(2,1)S(1)} %transpose_tokens.1.tokens_t, bf16[256,256]{1,0:T(8,128)(2,1)S(1)} %get-tuple-element.127.a, ...), custom_call_target="tpu_custom_call" | custom-call | flops 1 | bytes 1 | tf_op jit(solution)/shard_map/weight_grad/pallas_call | solution.py:436
  58.1 1.7 %collective-permute-start.20 = (bf16[384,256]{1,0:T(8,128)(2,1)S(1)}, bf16[384,256]{1,0:T(8,128)(2,1)S(1)}, u32[]{:S(2)}, u32[]{:S(2)}) collective-permute-start(bf16[384,256]{1,0:T(8,128)(2,1)S(1)} %get-tuple-element.132), channel_id=1, source_target_pairs={{0,8},{1,9},{2,10},{3,11},{4,12},{5,13},{6,14},{7,15},{8,16},{9,17... | collective-permute-start | bytes 589832 | tf_op jit(solution)/shard_map/ppermute | solution.py:573
  59.8 1.8 %collective-permute-start.21 = (bf16[384,256]{1,0:T(8,128)(2,1)S(1)}, bf16[384,256]{1,0:T(8,128)(2,1)S(1)}, u32[]{:S(2)}, u32[]{:S(2)}) collective-permute-start(bf16[384,256]{1,0:T(8,128)(2,1)S(1)} %get-tuple-element.133), channel_id=1, source_target_pairs={{0,16},{1,17},{2,18},{3,19},{4,20},{5,21},{6,22},{7,23},{8,24},{9,... | collective-permute-start | bytes 589832 | tf_op jit(solution)/shard_map/ppermute | solution.py:573
  61.6 1.5 %collective-permute-start.22 = (bf16[384,256]{1,0:T(8,128)(2,1)S(1)}, bf16[384,256]{1,0:T(8,128)(2,1)S(1)}, u32[]{:S(2)}, u32[]{:S(2)}) collective-permute-start(bf16[384,256]{1,0:T(8,128)(2,1)S(1)} %get-tuple-element.134), channel_id=1, source_target_pairs={{0,24},{1,25},{2,26},{3,27},{4,28},{5,29},{6,30},{7,31},{8,0},{9,1... | collective-permute-start | bytes 589832 | tf_op jit(solution)/shard_map/ppermute | solution.py:573
  63.1 5.4 %input_grad.1 = bf16[128,1536]{1,0:T(8,128)(2,1)} custom-call(s32[4]{0:T(128)S(1)} %pad_add_fusion.place, bf16[256,768]{1,0:T(8,128)(2,1)S(1)} %query_grad.1.dq, bf16[256,768]{1,0:T(8,128)(2,1)S(1)} %collective-permute-done.15.dq_other, bf16[256,256]{1,0:T(8,128)(2,1)S(1)} %sum_four.2.dkv, bf16[256,256]{1,0:T(8,128)(2,1)S(1)} %collective-permute-done.16.dkv_other, ...), custom_call_target="tpu_custom_call" | custom-call | flops 1 | bytes 1 | tf_op jit(solution)/shard_map/input_grad/pallas_call | solution.py:489
  68.5 0.4 collective-permute-done.21.c
  69.0 2.1 %collective-permute-done.22.d = bf16[384,256]{1,0:T(8,128)(2,1)S(1)} collective-permute-done((bf16[384,256]{1,0:T(8,128)(2,1)S(1)}, bf16[384,256]{1,0:T(8,128)(2,1)S(1)}, u32[]{:S(2)}, u32[]{:S(2)}) %collective-permute-start.22) | collective-permute-done | bytes 196640 | tf_op jit(solution)/shard_map/ppermute | solution.py:573
  71.0 0.1 sum_four.3
  71.1 17.5 %all_to_all.11 = bf16[8,48,256]{2,1,0:T(8,128)(2,1)S(1)} all-to-all(bf16[8,48,256]{2,1,0:T(8,128)(2,1)S(1)} %bitcast.17), channel_id=1, replica_groups={{0,1,2,3,4,5,6,7},{8,9,10,11,12,13,14,15},{16,17,18,19,20,21,22,23},{24..., dimensions={0} | all-to-all | bytes 393216 | tf_op jit(solution)/shard_map/all_to_all | solution.py:579
  88.6 0.6 final_sum.1
  (9 shorter events, 0.1 us)
Async XLA Ops:
  0.6 6.0 %collective-permute-start = (bf16[128,1536]{1,0:T(8,128)(2,1)}, bf16[128,1536]{1,0:T(8,128)(2,1)S(1)}, u32[]{:S(2)}, u32[]{:S(2)}) collective-permute-start(bf16[128,1536]{1,0:T(8,128)(2,1)} %bitcast.10), channel_id=1, source_target_pairs={{0,32},{32,0},{64,96},{96,64},{128,160},{160,128},{192,224},{224,1... | collective-permute-start | bytes 1179656 | tf_op jit(solution)/shard_map/ppermute | solution.py:529
  0.7 5.9 %collective-permute-start.2 = (bf16[128,1536]{1,0:T(8,128)(2,1)}, bf16[128,1536]{1,0:T(8,128)(2,1)S(1)}, u32[]{:S(2)}, u32[]{:S(2)}) collective-permute-start(bf16[128,1536]{1,0:T(8,128)(2,1)} %bitcast.19), channel_id=1, source_target_pairs={{0,32},{32,0},{64,96},{96,64},{128,160},{160,128},{192,224},{224,1... | collective-permute-start | bytes 1179656 | tf_op jit(solution)/shard_map/ppermute | solution.py:530
  1.2 14.7 %collective-permute-start.3 = (bf16[128,1536]{1,0:T(8,128)(2,1)}, bf16[128,1536]{1,0:T(8,128)(2,1)S(1)}, u32[]{:S(2)}, u32[]{:S(2)}) collective-permute-start(bf16[128,1536]{1,0:T(8,128)(2,1)} %bitcast.11), channel_id=1, source_target_pairs={{0,64},{32,96},{64,128},{96,160},{128,192},{160,224},{192,0},{224,... | collective-permute-start | bytes 1179656 | tf_op jit(solution)/shard_map/ppermute | solution.py:538
  2.7 14.2 %collective-permute-start.4 = (bf16[128,1536]{1,0:T(8,128)(2,1)}, bf16[128,1536]{1,0:T(8,128)(2,1)S(1)}, u32[]{:S(2)}, u32[]{:S(2)}) collective-permute-start(bf16[128,1536]{1,0:T(8,128)(2,1)} %bitcast.12), channel_id=1, source_target_pairs={{0,192},{32,224},{64,0},{96,32},{128,64},{160,96},{192,128},{224,1... | collective-permute-start | bytes 1179656 | tf_op jit(solution)/shard_map/ppermute | solution.py:538
  4.5 2.2 %collective-permute-start.1 = (s32[1,8]{1,0:T(1,128)}, s32[1,8]{1,0:T(1,128)S(1)}, u32[]{:S(2)}, u32[]{:S(2)}) collective-permute-start(s32[1,8]{1,0:T(1,128)} %bitcast.22), channel_id=1, source_target_pairs={{0,32},{32,0},{64,96},{96,64},{128,160},{160,128},{192,224},{224,1... | collective-permute-start | bytes 104 | tf_op jit(solution)/shard_map/ppermute | solution.py:531
  4.5 6.9 %copy-start.1 = (bf16[1,128,1536]{2,1,0:T(8,128)(2,1)S(1)}, bf16[1,128,1536]{2,1,0:T(8,128)(2,1)}, u32[]{:S(2)}) copy-start(bf16[1,128,1536]{2,1,0:T(8,128)(2,1)} %param.8) | copy-start | bytes 1179652
  6.6 5.5 %copy-start = (bf16[1,128,1536]{2,1,0:T(8,128)(2,1)S(1)}, bf16[1,128,1536]{2,1,0:T(8,128)(2,1)}, u32[]{:S(2)}) copy-start(bf16[1,128,1536]{2,1,0:T(8,128)(2,1)} %param.7) | copy-start | bytes 1179652
  7.0 9.9 %collective-permute-start.5 = (bf16[256,256]{1,0:T(8,128)(2,1)S(1)}, bf16[256,256]{1,0:T(8,128)(2,1)S(1)}, u32[]{:S(2)}, u32[]{:S(2)}) collective-permute-start(bf16[256,256]{1,0:T(8,128)(2,1)S(1)} %project_kv.1.kv), channel_id=1, source_target_pairs={{0,64},{32,96},{64,128},{96,160},{128,192},{160,224},{192,0},{224,... | collective-permute-start | bytes 393224 | tf_op jit(solution)/shard_map/ppermute | solution.py:537
  7.3 13.1 %collective-permute-start.6 = (bf16[256,256]{1,0:T(8,128)(2,1)S(1)}, bf16[256,256]{1,0:T(8,128)(2,1)S(1)}, u32[]{:S(2)}, u32[]{:S(2)}) collective-permute-start(bf16[256,256]{1,0:T(8,128)(2,1)S(1)} %project_kv.1.kv), channel_id=1, source_target_pairs={{0,128},{32,160},{64,192},{96,224},{128,0},{160,32},{192,64},{224,... | collective-permute-start | bytes 393224 | tf_op jit(solution)/shard_map/ppermute | solution.py:537
  10.0 10.3 %collective-permute-start.7 = (bf16[256,256]{1,0:T(8,128)(2,1)S(1)}, bf16[256,256]{1,0:T(8,128)(2,1)S(1)}, u32[]{:S(2)}, u32[]{:S(2)}) collective-permute-start(bf16[256,256]{1,0:T(8,128)(2,1)S(1)} %project_kv.1.kv), channel_id=1, source_target_pairs={{0,192},{32,224},{64,0},{96,32},{128,64},{160,96},{192,128},{224,1... | collective-permute-start | bytes 393224 | tf_op jit(solution)/shard_map/ppermute | solution.py:537
  20.4 6.2 %collective-permute-start.10 = (bf16[128,1536]{1,0:T(8,128)(2,1)S(1)}, bf16[128,1536]{1,0:T(8,128)(2,1)S(1)}, u32[]{:S(2)}, u32[]{:S(2)}) collective-permute-start(bf16[128,1536]{1,0:T(8,128)(2,1)S(1)} %collective-permute-done.4.refs_6_), channel_id=1, source_target_pairs={{0,32},{32,0},{64,96},{96,64},{128,160},{160,128},{192,224},{224,1... | collective-permute-start | bytes 1179656 | tf_op jit(solution)/shard_map/ppermute | solution.py:546
  20.4 13.0 %collective-permute-start.8 = (bf16[128,1536]{1,0:T(8,128)(2,1)S(1)}, bf16[128,1536]{1,0:T(8,128)(2,1)S(1)}, u32[]{:S(2)}, u32[]{:S(2)}) collective-permute-start(bf16[128,1536]{1,0:T(8,128)(2,1)S(1)} %bitcast.15), channel_id=1, source_target_pairs={{0,128},{32,160},{64,192},{96,224},{128,0},{160,32},{192,64},{224,... | collective-permute-start | bytes 1179656 | tf_op jit(solution)/shard_map/ppermute | solution.py:545
  22.1 11.3 %collective-permute-start.9 = (bf16[128,1536]{1,0:T(8,128)(2,1)S(1)}, bf16[128,1536]{1,0:T(8,128)(2,1)S(1)}, u32[]{:S(2)}, u32[]{:S(2)}) collective-permute-start(bf16[128,1536]{1,0:T(8,128)(2,1)S(1)} %collective-permute-done.3.refs_2_), channel_id=1, source_target_pairs={{0,32},{32,0},{64,96},{96,64},{128,160},{160,128},{192,224},{224,1... | collective-permute-start | bytes 1179656 | tf_op jit(solution)/shard_map/ppermute | solution.py:546
  33.4 7.9 %collective-permute-start.11 = (bf16[256,256]{1,0:T(8,128)(2,1)S(1)}, bf16[256,256]{1,0:T(8,128)(2,1)S(1)}, u32[]{:S(2)}, u32[]{:S(2)}) collective-permute-start(bf16[256,256]{1,0:T(8,128)(2,1)S(1)} %get-tuple-element.109), channel_id=1, source_target_pairs={{0,128},{32,160},{64,192},{96,224},{128,0},{160,32},{192,64},{224,... | collective-permute-start | bytes 393224 | tf_op jit(solution)/shard_map/ppermute | solution.py:556
  35.2 7.0 %collective-permute-start.12 = (bf16[256,256]{1,0:T(8,128)(2,1)S(1)}, bf16[256,256]{1,0:T(8,128)(2,1)S(1)}, u32[]{:S(2)}, u32[]{:S(2)}) collective-permute-start(bf16[256,256]{1,0:T(8,128)(2,1)S(1)} %get-tuple-element.110), channel_id=1, source_target_pairs={{0,192},{32,224},{64,0},{96,32},{128,64},{160,96},{192,128},{224,1... | collective-permute-start | bytes 393224 | tf_op jit(solution)/shard_map/ppermute | solution.py:556
  36.6 6.7 %collective-permute-start.13 = (bf16[256,256]{1,0:T(8,128)(2,1)S(1)}, bf16[256,256]{1,0:T(8,128)(2,1)S(1)}, u32[]{:S(2)}, u32[]{:S(2)}) collective-permute-start(bf16[256,256]{1,0:T(8,128)(2,1)S(1)} %get-tuple-element.111), channel_id=1, source_target_pairs={{0,64},{32,96},{64,128},{96,160},{128,192},{160,224},{192,0},{224,... | collective-permute-start | bytes 393224 | tf_op jit(solution)/shard_map/ppermute | solution.py:556
  43.3 2.5 %collective-permute-start.15 = (bf16[256,768]{1,0:T(8,128)(2,1)S(1)}, bf16[256,768]{1,0:T(8,128)(2,1)S(1)}, u32[]{:S(2)}, u32[]{:S(2)}) collective-permute-start(bf16[256,768]{1,0:T(8,128)(2,1)S(1)} %query_grad.1.dq), channel_id=1, source_target_pairs={{0,32},{32,0},{64,96},{96,64},{128,160},{160,128},{192,224},{224,1... | collective-permute-start | bytes 1179656 | tf_op jit(solution)/shard_map/ppermute | solution.py:560
  43.3 7.1 %collective-permute-start.14 = (bf16[128,1536]{1,0:T(8,128)(2,1)S(1)}, bf16[128,1536]{1,0:T(8,128)(2,1)S(1)}, u32[]{:S(2)}, u32[]{:S(2)}) collective-permute-start(bf16[128,1536]{1,0:T(8,128)(2,1)S(1)} %collective-permute-done.8.refs_4_), channel_id=1, source_target_pairs={{0,32},{32,0},{64,96},{96,64},{128,160},{160,128},{192,224},{224,1... | collective-permute-start | bytes 1179656 | tf_op jit(solution)/shard_map/ppermute | solution.py:564
  43.9 1.8 %collective-permute-start.16 = (bf16[256,256]{1,0:T(8,128)(2,1)S(1)}, bf16[256,256]{1,0:T(8,128)(2,1)S(1)}, u32[]{:S(2)}, u32[]{:S(2)}) collective-permute-start(bf16[256,256]{1,0:T(8,128)(2,1)S(1)} %sum_four.2.dkv), channel_id=1, source_target_pairs={{0,32},{32,0},{64,96},{96,64},{128,160},{160,128},{192,224},{224,1... | collective-permute-start | bytes 393224 | tf_op jit(solution)/shard_map/ppermute | solution.py:562
  46.4 9.6 %collective-permute-start.17 = (bf16[256,256]{1,0:T(8,128)(2,1)S(1)}, bf16[256,256]{1,0:T(8,128)(2,1)S(1)}, u32[]{:S(2)}, u32[]{:S(2)}) collective-permute-start(bf16[256,256]{1,0:T(8,128)(2,1)S(1)} %get-tuple-element.128), channel_id=1, source_target_pairs={{0,64},{32,96},{64,128},{96,160},{128,192},{160,224},{192,0},{224,... | collective-permute-start | bytes 393224 | tf_op jit(solution)/shard_map/ppermute | solution.py:570
  46.6 9.4 %collective-permute-start.18 = (bf16[256,256]{1,0:T(8,128)(2,1)S(1)}, bf16[256,256]{1,0:T(8,128)(2,1)S(1)}, u32[]{:S(2)}, u32[]{:S(2)}) collective-permute-start(bf16[256,256]{1,0:T(8,128)(2,1)S(1)} %get-tuple-element.129), channel_id=1, source_target_pairs={{0,128},{32,160},{64,192},{96,224},{128,0},{160,32},{192,64},{224,... | collective-permute-start | bytes 393224 | tf_op jit(solution)/shard_map/ppermute | solution.py:570
  49.5 7.1 %collective-permute-start.19 = (bf16[256,256]{1,0:T(8,128)(2,1)S(1)}, bf16[256,256]{1,0:T(8,128)(2,1)S(1)}, u32[]{:S(2)}, u32[]{:S(2)}) collective-permute-start(bf16[256,256]{1,0:T(8,128)(2,1)S(1)} %get-tuple-element.130), channel_id=1, source_target_pairs={{0,192},{32,224},{64,0},{96,32},{128,64},{160,96},{192,128},{224,1... | collective-permute-start | bytes 393224 | tf_op jit(solution)/shard_map/ppermute | solution.py:570
  58.1 10.4 %collective-permute-start.20 = (bf16[384,256]{1,0:T(8,128)(2,1)S(1)}, bf16[384,256]{1,0:T(8,128)(2,1)S(1)}, u32[]{:S(2)}, u32[]{:S(2)}) collective-permute-start(bf16[384,256]{1,0:T(8,128)(2,1)S(1)} %get-tuple-element.132), channel_id=1, source_target_pairs={{0,8},{1,9},{2,10},{3,11},{4,12},{5,13},{6,14},{7,15},{8,16},{9,17... | collective-permute-start | bytes 589832 | tf_op jit(solution)/shard_map/ppermute | solution.py:573
  59.8 9.2 %collective-permute-start.21 = (bf16[384,256]{1,0:T(8,128)(2,1)S(1)}, bf16[384,256]{1,0:T(8,128)(2,1)S(1)}, u32[]{:S(2)}, u32[]{:S(2)}) collective-permute-start(bf16[384,256]{1,0:T(8,128)(2,1)S(1)} %get-tuple-element.133), channel_id=1, source_target_pairs={{0,16},{1,17},{2,18},{3,19},{4,20},{5,21},{6,22},{7,23},{8,24},{9,... | collective-permute-start | bytes 589832 | tf_op jit(solution)/shard_map/ppermute | solution.py:573
  61.6 9.4 %collective-permute-start.22 = (bf16[384,256]{1,0:T(8,128)(2,1)S(1)}, bf16[384,256]{1,0:T(8,128)(2,1)S(1)}, u32[]{:S(2)}, u32[]{:S(2)}) collective-permute-start(bf16[384,256]{1,0:T(8,128)(2,1)S(1)} %get-tuple-element.134), channel_id=1, source_target_pairs={{0,24},{1,25},{2,26},{3,27},{4,28},{5,29},{6,30},{7,31},{8,0},{9,1... | collective-permute-start | bytes 589832 | tf_op jit(solution)/shard_map/ppermute | solution.py:573

commit v7 on v6

--- a/solution.py
+++ b/solution.py
@@ -543,29 +543,28 @@
     scores = {0: chip_scores(0, kvs[0], limits, query, up)}
     far, kvs, scores[0], late_own = lax.optimization_barrier((far, kvs, scores[0], own))
     late = lax.ppermute(late_own, "ctx", chip_shift(2))
-    far_other = {d: lax.ppermute(far[d], "ctx", CORE) for d in (1, 3)}
     for d in (1, 3, 2):
         scores[d] = chip_scores(d, kvs[d], limits, query, up)
     factors = softmax_factors([scores[d][2] for d in range(CHIPS)])
     terms, grad_scores = {}, {}
     for d in (2, 1, 3):
         terms[d], grad_scores[d] = chip_terms(d, *scores[d][:2], factors, query, up)
-    late, far_other, terms, scores[0] = lax.optimization_barrier(
-        (late, far_other, terms, scores[0])
-    )
     back = [lax.ppermute(terms[d], "ctx", chip_shift(CHIPS - d)) for d in (2, 1, 3)]
     terms[0], grad_scores[0] = chip_terms(0, *scores[0][:2], factors, query, up)
     dq = query_grad([scores[d][3] for d in range(CHIPS)], [grad_scores[d] for d in range(CHIPS)])
-    back, dq = lax.optimization_barrier((back, dq))
+    late, back, dq = lax.optimization_barrier((late, back, dq))
     dq_other = lax.ppermute(dq, "ctx", CORE)
     dkv = sum_four(terms[0], *back)
     dkv_other = lax.ppermute(dkv, "ctx", CORE)
     far[2], dkv = lax.optimization_barrier((late, dkv))
-    far_other[2] = lax.ppermute(far[2], "ctx", CORE)
+    far_other = {2: lax.ppermute(far[2], "ctx", CORE)}
+    packed = pack(place, dq, dq_other, dkv, dkv_other)
+    far[1], far[3], packed = lax.optimization_barrier((far[1], far[3], packed))
+    for d in (1, 3):
+        far_other[d] = lax.ppermute(far[d], "ctx", CORE)
     tokens_t = transpose(
         [own, other] + [part for d in (1, 2, 3) for part in (far[d], far_other[d])]
     )
-    packed = pack(place, dq, dq_other, dkv, dkv_other)
     columns = [packed[0]] + [
         lax.ppermute(packed[d], "ctx", chip_shift(d)) for d in (1, 2, 3)
     ]

time: 90.6 us -> 85.1 us (0.939)
  waiting for transfers between devices: 25.4 us -> 19.1 us
    ppermute x1, waiting for transfers between devices: 6.85 us -> 0.01 us  [shards(): late = lax.ppermute(late_own, 'ctx', chip_shift(2))]
    ppermute x3, waiting for transfers between devices: 4.73 us -> 5.89 us  [shards(): lax.ppermute(terms[d], 'ctx', chip_shift(CHIPS - d))]
  transfers between devices with their start and end apart: 23 -> 23, of which waited for: 11 -> 9; matrix products, arithmetic and copies ran while one was open for 0% -> 0% of each run, Pallas kernels for 22% -> 23%
where the time goes in v7:
time: 85.1 us; the launch traced here: 83.8 us
  starting transfers between devices  24.7 us (29%)
  Pallas kernels  21.6 us (25%)
  waiting for transfers between devices  19.1 us (22%)
  blocking collectives  17.5 us (21%)
    all_to_all x1, blocking collectives, shards(): lax.all_to_all(y_sum, 'dp', 0, 0, tiled=True, axis_index_groups=Z_GROUPS)  17.5 us
    ppermute x3, waiting for transfers between devices, shards(): lax.ppermute(terms[d], 'ctx', chip_shift(CHIPS - d))  5.89 us
    pallas_call x1, Pallas kernels, input_grad(): pl.pallas_call(input_kernel, in_specs=[SCALARS] + [WHOLE] * 4 + [STAY] *...  5.37 us
    ppermute x3, waiting for transfers between devices, shards(): lax.ppermute(packed[d], 'ctx', chip_shift(d))  5.07 us
    ppermute x3, starting transfers between devices, shards(): lax.ppermute(terms[d], 'dp', y_shift(d))  5 us
    ppermute x3, starting transfers between devices, shards(): kvs = [kv] + [lax.ppermute(kv, 'ctx', chip_shift(d)) for d in (1, 2, 3)]  4.53 us
    ppermute x3, starting transfers between devices, shards(): lax.ppermute(terms[d], 'ctx', chip_shift(CHIPS - d))  4.24 us
    ppermute x3, starting transfers between devices, shards(): lax.ppermute(packed[d], 'ctx', chip_shift(d))  4.06 us
  transfers between devices with their start and end apart: 23, of which 9 were waited for; matrix products, arithmetic and copies ran while one was open for 0% of the time, Pallas kernels for 23%

profile of v7, /device:TPU:8, one launch (start us, length us, event | category | flops | bytes accessed | tf_op | source)
XLA Modules:
  0.0 83.8 jit_solution(17585515590968852149)
XLA Ops:
  0.6 0.1 collective-permute-start
  0.7 0.5 collective-permute-start.2
  1.2 1.5 %collective-permute-start.3 = (bf16[128,1536]{1,0:T(8,128)(2,1)}, bf16[128,1536]{1,0:T(8,128)(2,1)S(1)}, u32[]{:S(2)}, u32[]{:S(2)}) collective-permute-start(bf16[128,1536]{1,0:T(8,128)(2,1)} %bitcast.11), channel_id=1, source_target_pairs={{0,64},{32,96},{64,128},{96,160},{128,192},{160,224},{192,0},{224,... | collective-permute-start | bytes 1179656 | tf_op jit(solution)/shard_map/ppermute | solution.py:538
  2.7 1.7 %collective-permute-start.4 = (bf16[128,1536]{1,0:T(8,128)(2,1)}, bf16[128,1536]{1,0:T(8,128)(2,1)S(1)}, u32[]{:S(2)}, u32[]{:S(2)}) collective-permute-start(bf16[128,1536]{1,0:T(8,128)(2,1)} %bitcast.12), channel_id=1, source_target_pairs={{0,192},{32,224},{64,0},{96,32},{128,64},{160,96},{192,128},{224,1... | collective-permute-start | bytes 1179656 | tf_op jit(solution)/shard_map/ppermute | solution.py:538
  4.5 0.1 pad_add_fusion.place
  4.5 2.1 %project_kv_own.1 = (bf16[1536,256]{1,0:T(8,128)(2,1)S(1)}, bf16[128,256]{1,0:T(8,128)(2,1)S(1)}) custom-call(s32[4]{0:T(128)S(1)} %pad_add_fusion.place, bf16[128,1536]{1,0:T(8,128)(2,1)} %bitcast.13, bf16[1536,256]{1,0:T(8,128)(2,1)} %w_key.3, bf16[1536,256]{1,0:T(8,128)(2,1)} %w_value.3), custom_call_target="tpu_custom_call" | custom-call | flops 1 | bytes 1 | tf_op jit(solution)/shard_map/project_kv_own/pallas_call | solution.py:94
  6.6 0.0 copy-start
  6.7 0.0 collective-permute-done.other.refs_1_
  6.7 0.0 collective-permute-done.2.up_other
  6.7 0.3 project_kv.1.kv
  7.0 0.4 collective-permute-start.5
  7.3 2.7 %collective-permute-start.6 = (bf16[256,256]{1,0:T(8,128)(2,1)S(1)}, bf16[256,256]{1,0:T(8,128)(2,1)S(1)}, u32[]{:S(2)}, u32[]{:S(2)}) collective-permute-start(bf16[256,256]{1,0:T(8,128)(2,1)S(1)} %project_kv.1.kv), channel_id=1, source_target_pairs={{0,128},{32,160},{64,192},{96,224},{128,0},{160,32},{192,64},{224,... | collective-permute-start | bytes 393224 | tf_op jit(solution)/shard_map/ppermute | solution.py:537
  10.0 1.4 %collective-permute-start.7 = (bf16[256,256]{1,0:T(8,128)(2,1)S(1)}, bf16[256,256]{1,0:T(8,128)(2,1)S(1)}, u32[]{:S(2)}, u32[]{:S(2)}) collective-permute-start(bf16[256,256]{1,0:T(8,128)(2,1)S(1)} %project_kv.1.kv), channel_id=1, source_target_pairs={{0,192},{32,224},{64,0},{96,32},{128,64},{160,96},{192,128},{224,1... | collective-permute-start | bytes 393224 | tf_op jit(solution)/shard_map/ppermute | solution.py:537
  11.5 0.6 stack_up.1.up
  12.1 3.0 %project_query.1 = (bf16[1536,128]{1,0:T(8,128)(2,1)S(1)}, s32[16,256]{1,0:T(8,128)S(1)}) custom-call(s32[4]{0:T(128)S(1)} %pad_add_fusion.place, bf16[128,1536]{1,0:T(8,128)(2,1)S(1)} %bitcast.14, bf16[128,1536]{1,0:T(8,128)(2,1)S(1)} %collective-permute-done.other.refs_1_, bf16[1536,1536]{1,0:T(8,128)(2,1)} %w_query.3, s32[1,1024]{1,0:T(1,128)} %segments_far.1, ...), custom_call_target="tpu_custom_call" | custom-call | flops 1 | bytes 1 | tf_op jit(solution)/shard_map/project_query/pallas_call | solution.py:202
  15.1 0.8 chip_scores_0.1
  15.9 0.0 collective-permute-done.3.refs_2_
  15.9 1.0 %collective-permute-done.4.refs_6_ = bf16[128,1536]{1,0:T(8,128)(2,1)S(1)} collective-permute-done((bf16[128,1536]{1,0:T(8,128)(2,1)}, bf16[128,1536]{1,0:T(8,128)(2,1)S(1)}, u32[]{:S(2)}, u32[]{:S(2)}) %collective-permute-start.4) | collective-permute-done | bytes 393248 | tf_op jit(solution)/shard_map/ppermute | solution.py:538
  16.9 0.0 collective-permute-done.5.kv
  16.9 3.5 %collective-permute-done.6.kv = bf16[256,256]{1,0:T(8,128)(2,1)S(1)} collective-permute-done((bf16[256,256]{1,0:T(8,128)(2,1)S(1)}, bf16[256,256]{1,0:T(8,128)(2,1)S(1)}, u32[]{:S(2)}, u32[]{:S(2)}) %collective-permute-start.6) | collective-permute-done | bytes 131104 | tf_op jit(solution)/shard_map/ppermute | solution.py:537
  20.4 0.0 collective-permute-done.7.kv
  20.4 1.7 %collective-permute-start.8 = (bf16[128,1536]{1,0:T(8,128)(2,1)S(1)}, bf16[128,1536]{1,0:T(8,128)(2,1)S(1)}, u32[]{:S(2)}, u32[]{:S(2)}) collective-permute-start(bf16[128,1536]{1,0:T(8,128)(2,1)S(1)} %bitcast.15), channel_id=1, source_target_pairs={{0,128},{32,160},{64,192},{96,224},{128,0},{160,32},{192,64},{224,... | collective-permute-start | bytes 1179656 | tf_op jit(solution)/shard_map/ppermute | solution.py:545
  22.1 0.7 chip_scores_3.1
  22.9 0.8 chip_scores_1.1
  23.6 0.8 chip_scores_2.1
  24.4 0.6 chip_terms_3.1
  25.1 1.2 %collective-permute-start.11 = (bf16[256,256]{1,0:T(8,128)(2,1)S(1)}, bf16[256,256]{1,0:T(8,128)(2,1)S(1)}, u32[]{:S(2)}, u32[]{:S(2)}) collective-permute-start(bf16[256,256]{1,0:T(8,128)(2,1)S(1)} %get-tuple-element.98), channel_id=1, source_target_pairs={{0,64},{32,96},{64,128},{96,160},{128,192},{160,224},{192,0},{224,... | collective-permute-start | bytes 393224 | tf_op jit(solution)/shard_map/ppermute | solution.py:552
  26.2 0.6 chip_terms_1.1
  26.9 2.4 %collective-permute-start.10 = (bf16[256,256]{1,0:T(8,128)(2,1)S(1)}, bf16[256,256]{1,0:T(8,128)(2,1)S(1)}, u32[]{:S(2)}, u32[]{:S(2)}) collective-permute-start(bf16[256,256]{1,0:T(8,128)(2,1)S(1)} %get-tuple-element.95), channel_id=1, source_target_pairs={{0,192},{32,224},{64,0},{96,32},{128,64},{160,96},{192,128},{224,1... | collective-permute-start | bytes 393224 | tf_op jit(solution)/shard_map/ppermute | solution.py:552
  29.3 0.6 chip_terms_2.1
  29.9 0.7 collective-permute-start.9
  30.6 0.7 chip_terms_0.1
  31.3 0.7 query_grad.1.dq
  31.9 4.4 %collective-permute-done.11.d = bf16[256,256]{1,0:T(8,128)(2,1)S(1)} collective-permute-done((bf16[256,256]{1,0:T(8,128)(2,1)S(1)}, bf16[256,256]{1,0:T(8,128)(2,1)S(1)}, u32[]{:S(2)}, u32[]{:S(2)}) %collective-permute-start.11) | collective-permute-done | bytes 131104 | tf_op jit(solution)/shard_map/ppermute | solution.py:552
  36.4 0.0 collective-permute-done.10.c
  36.4 1.4 %collective-permute-done.9.b = bf16[256,256]{1,0:T(8,128)(2,1)S(1)} collective-permute-done((bf16[256,256]{1,0:T(8,128)(2,1)S(1)}, bf16[256,256]{1,0:T(8,128)(2,1)S(1)}, u32[]{:S(2)}, u32[]{:S(2)}) %collective-permute-start.9) | collective-permute-done | bytes 131104 | tf_op jit(solution)/shard_map/ppermute | solution.py:552
  37.8 0.0 collective-permute-start.12
  37.8 0.1 sum_four.2.dkv
  37.9 0.6 collective-permute-start.13
  38.5 0.1 collective-permute-start.15
  38.6 1.2 %collective-permute-done.13.dkv_other = bf16[256,256]{1,0:T(8,128)(2,1)S(1)} collective-permute-done((bf16[256,256]{1,0:T(8,128)(2,1)S(1)}, bf16[256,256]{1,0:T(8,128)(2,1)S(1)}, u32[]{:S(2)}, u32[]{:S(2)}) %collective-permute-start.13) | collective-permute-done | bytes 131104 | tf_op jit(solution)/shard_map/ppermute | solution.py:558
  39.7 0.6 pack.1
  40.4 0.2 collective-permute-start.14
  40.6 0.4 collective-permute-start.16
  41.0 0.0 collective-permute-start.17
  41.0 3.1 %collective-permute-start.18 = (bf16[256,256]{1,0:T(8,128)(2,1)S(1)}, bf16[256,256]{1,0:T(8,128)(2,1)S(1)}, u32[]{:S(2)}, u32[]{:S(2)}) collective-permute-start(bf16[256,256]{1,0:T(8,128)(2,1)S(1)} %get-tuple-element.125), channel_id=1, source_target_pairs={{0,128},{32,160},{64,192},{96,224},{128,0},{160,32},{192,64},{224,... | collective-permute-start | bytes 393224 | tf_op jit(solution)/shard_map/ppermute | solution.py:569
  44.1 0.0 collective-permute-done.15.refs_5_
  44.1 1.0 %collective-permute-start.19 = (bf16[256,256]{1,0:T(8,128)(2,1)S(1)}, bf16[256,256]{1,0:T(8,128)(2,1)S(1)}, u32[]{:S(2)}, u32[]{:S(2)}) collective-permute-start(bf16[256,256]{1,0:T(8,128)(2,1)S(1)} %get-tuple-element.126), channel_id=1, source_target_pairs={{0,192},{32,224},{64,0},{96,32},{128,64},{160,96},{192,128},{224,1... | collective-permute-start | bytes 393224 | tf_op jit(solution)/shard_map/ppermute | solution.py:569
  45.0 0.0 collective-permute-done.14.refs_3_
  45.1 0.0 collective-permute-done.16.refs_7_
  45.1 1.0 %transpose_tokens.1.tokens_t = bf16[1536,1024]{1,0:T(8,128)(2,1)S(1)} custom-call(bf16[128,1536]{1,0:T(8,128)(2,1)S(1)} %bitcast.16, bf16[128,1536]{1,0:T(8,128)(2,1)S(1)} %collective-permute-done.other.refs_1_, bf16[128,1536]{1,0:T(8,128)(2,1)S(1)} %collective-permute-done.3.refs_2_, bf16[128,1536]{1,0:T(8,128)(2,1)S(1)} %collective-permute-done.14.refs_3_, ...), custom_call_target="tpu_custom_call" | custom-call | flops 1 | bytes 1 | tf_op jit(solution)/shard_map/transpose_tokens/pallas_call | solution.py:416
  46.1 4.5 %collective-permute-done.17.b = bf16[256,256]{1,0:T(8,128)(2,1)S(1)} collective-permute-done((bf16[256,256]{1,0:T(8,128)(2,1)S(1)}, bf16[256,256]{1,0:T(8,128)(2,1)S(1)}, u32[]{:S(2)}, u32[]{:S(2)}) %collective-permute-start.17) | collective-permute-done | bytes 131104 | tf_op jit(solution)/shard_map/ppermute | solution.py:569
  50.5 0.0 collective-permute-done.18.c
  50.6 0.6 collective-permute-done.19.d
  51.1 1.5 %weight_grad.1 = (f32[384,256]{1,0:T(8,128)S(1)}, bf16[384,256]{1,0:T(8,128)(2,1)S(1)}, bf16[384,256]{1,0:T(8,128)(2,1)S(1)}, bf16[384,256]{1,0:T(8,128)(2,1)S(1)}) custom-call(s32[4]{0:T(128)S(1)} %pad_add_fusion.place, bf16[1536,1024]{1,0:T(8,128)(2,1)S(1)} %transpose_tokens.1.tokens_t, bf16[256,256]{1,0:T(8,128)(2,1)S(1)} %get-tuple-element.123.a, ...), custom_call_target="tpu_custom_call" | custom-call | flops 1 | bytes 1 | tf_op jit(solution)/shard_map/weight_grad/pallas_call | solution.py:436
  52.7 1.7 %collective-permute-start.20 = (bf16[384,256]{1,0:T(8,128)(2,1)S(1)}, bf16[384,256]{1,0:T(8,128)(2,1)S(1)}, u32[]{:S(2)}, u32[]{:S(2)}) collective-permute-start(bf16[384,256]{1,0:T(8,128)(2,1)S(1)} %get-tuple-element.128), channel_id=1, source_target_pairs={{0,8},{1,9},{2,10},{3,11},{4,12},{5,13},{6,14},{7,15},{8,16},{9,17... | collective-permute-start | bytes 589832 | tf_op jit(solution)/shard_map/ppermute | solution.py:572
  54.3 1.9 %collective-permute-start.21 = (bf16[384,256]{1,0:T(8,128)(2,1)S(1)}, bf16[384,256]{1,0:T(8,128)(2,1)S(1)}, u32[]{:S(2)}, u32[]{:S(2)}) collective-permute-start(bf16[384,256]{1,0:T(8,128)(2,1)S(1)} %get-tuple-element.129), channel_id=1, source_target_pairs={{0,16},{1,17},{2,18},{3,19},{4,20},{5,21},{6,22},{7,23},{8,24},{9,... | collective-permute-start | bytes 589832 | tf_op jit(solution)/shard_map/ppermute | solution.py:572
  56.2 1.4 %collective-permute-start.22 = (bf16[384,256]{1,0:T(8,128)(2,1)S(1)}, bf16[384,256]{1,0:T(8,128)(2,1)S(1)}, u32[]{:S(2)}, u32[]{:S(2)}) collective-permute-start(bf16[384,256]{1,0:T(8,128)(2,1)S(1)} %get-tuple-element.130), channel_id=1, source_target_pairs={{0,24},{1,25},{2,26},{3,27},{4,28},{5,29},{6,30},{7,31},{8,0},{9,1... | collective-permute-start | bytes 589832 | tf_op jit(solution)/shard_map/ppermute | solution.py:572
  57.7 5.4 %input_grad.1 = bf16[128,1536]{1,0:T(8,128)(2,1)} custom-call(s32[4]{0:T(128)S(1)} %pad_add_fusion.place, bf16[256,768]{1,0:T(8,128)(2,1)S(1)} %query_grad.1.dq, bf16[256,768]{1,0:T(8,128)(2,1)S(1)} %collective-permute-done.12.dq_other, bf16[256,256]{1,0:T(8,128)(2,1)S(1)} %sum_four.2.dkv, bf16[256,256]{1,0:T(8,128)(2,1)S(1)} %collective-permute-done.13.dkv_other, ...), custom_call_target="tpu_custom_call" | custom-call | flops 1 | bytes 1 | tf_op jit(solution)/shard_map/input_grad/pallas_call | solution.py:489
  63.0 0.4 collective-permute-done.21.c
  63.5 2.1 %collective-permute-done.22.d = bf16[384,256]{1,0:T(8,128)(2,1)S(1)} collective-permute-done((bf16[384,256]{1,0:T(8,128)(2,1)S(1)}, bf16[384,256]{1,0:T(8,128)(2,1)S(1)}, u32[]{:S(2)}, u32[]{:S(2)}) %collective-permute-start.22) | collective-permute-done | bytes 196640 | tf_op jit(solution)/shard_map/ppermute | solution.py:572
  65.5 0.1 sum_four.3
  65.6 17.5 %all_to_all.11 = bf16[8,48,256]{2,1,0:T(8,128)(2,1)S(1)} all-to-all(bf16[8,48,256]{2,1,0:T(8,128)(2,1)S(1)} %bitcast.17), channel_id=1, replica_groups={{0,1,2,3,4,5,6,7},{8,9,10,11,12,13,14,15},{16,17,18,19,20,21,22,23},{24..., dimensions={0} | all-to-all | bytes 393216 | tf_op jit(solution)/shard_map/all_to_all | solution.py:578
  83.1 0.6 final_sum.1
  (9 shorter events, 0.1 us)
Async XLA Ops:
  0.6 6.0 %collective-permute-start = (bf16[128,1536]{1,0:T(8,128)(2,1)}, bf16[128,1536]{1,0:T(8,128)(2,1)S(1)}, u32[]{:S(2)}, u32[]{:S(2)}) collective-permute-start(bf16[128,1536]{1,0:T(8,128)(2,1)} %bitcast.10), channel_id=1, source_target_pairs={{0,32},{32,0},{64,96},{96,64},{128,160},{160,128},{192,224},{224,1... | collective-permute-start | bytes 1179656 | tf_op jit(solution)/shard_map/ppermute | solution.py:529
  0.7 5.9 %collective-permute-start.2 = (bf16[128,1536]{1,0:T(8,128)(2,1)}, bf16[128,1536]{1,0:T(8,128)(2,1)S(1)}, u32[]{:S(2)}, u32[]{:S(2)}) collective-permute-start(bf16[128,1536]{1,0:T(8,128)(2,1)} %bitcast.19), channel_id=1, source_target_pairs={{0,32},{32,0},{64,96},{96,64},{128,160},{160,128},{192,224},{224,1... | collective-permute-start | bytes 1179656 | tf_op jit(solution)/shard_map/ppermute | solution.py:530
  1.2 14.7 %collective-permute-start.3 = (bf16[128,1536]{1,0:T(8,128)(2,1)}, bf16[128,1536]{1,0:T(8,128)(2,1)S(1)}, u32[]{:S(2)}, u32[]{:S(2)}) collective-permute-start(bf16[128,1536]{1,0:T(8,128)(2,1)} %bitcast.11), channel_id=1, source_target_pairs={{0,64},{32,96},{64,128},{96,160},{128,192},{160,224},{192,0},{224,... | collective-permute-start | bytes 1179656 | tf_op jit(solution)/shard_map/ppermute | solution.py:538
  2.7 14.2 %collective-permute-start.4 = (bf16[128,1536]{1,0:T(8,128)(2,1)}, bf16[128,1536]{1,0:T(8,128)(2,1)S(1)}, u32[]{:S(2)}, u32[]{:S(2)}) collective-permute-start(bf16[128,1536]{1,0:T(8,128)(2,1)} %bitcast.12), channel_id=1, source_target_pairs={{0,192},{32,224},{64,0},{96,32},{128,64},{160,96},{192,128},{224,1... | collective-permute-start | bytes 1179656 | tf_op jit(solution)/shard_map/ppermute | solution.py:538
  4.5 2.2 %collective-permute-start.1 = (s32[1,8]{1,0:T(1,128)}, s32[1,8]{1,0:T(1,128)S(1)}, u32[]{:S(2)}, u32[]{:S(2)}) collective-permute-start(s32[1,8]{1,0:T(1,128)} %bitcast.22), channel_id=1, source_target_pairs={{0,32},{32,0},{64,96},{96,64},{128,160},{160,128},{192,224},{224,1... | collective-permute-start | bytes 104 | tf_op jit(solution)/shard_map/ppermute | solution.py:531
  4.5 6.9 %copy-start.1 = (bf16[1,128,1536]{2,1,0:T(8,128)(2,1)S(1)}, bf16[1,128,1536]{2,1,0:T(8,128)(2,1)}, u32[]{:S(2)}) copy-start(bf16[1,128,1536]{2,1,0:T(8,128)(2,1)} %param.8) | copy-start | bytes 1179652
  6.6 5.5 %copy-start = (bf16[1,128,1536]{2,1,0:T(8,128)(2,1)S(1)}, bf16[1,128,1536]{2,1,0:T(8,128)(2,1)}, u32[]{:S(2)}) copy-start(bf16[1,128,1536]{2,1,0:T(8,128)(2,1)} %param.7) | copy-start | bytes 1179652
  7.0 9.9 %collective-permute-start.5 = (bf16[256,256]{1,0:T(8,128)(2,1)S(1)}, bf16[256,256]{1,0:T(8,128)(2,1)S(1)}, u32[]{:S(2)}, u32[]{:S(2)}) collective-permute-start(bf16[256,256]{1,0:T(8,128)(2,1)S(1)} %project_kv.1.kv), channel_id=1, source_target_pairs={{0,64},{32,96},{64,128},{96,160},{128,192},{160,224},{192,0},{224,... | collective-permute-start | bytes 393224 | tf_op jit(solution)/shard_map/ppermute | solution.py:537
  7.3 13.1 %collective-permute-start.6 = (bf16[256,256]{1,0:T(8,128)(2,1)S(1)}, bf16[256,256]{1,0:T(8,128)(2,1)S(1)}, u32[]{:S(2)}, u32[]{:S(2)}) collective-permute-start(bf16[256,256]{1,0:T(8,128)(2,1)S(1)} %project_kv.1.kv), channel_id=1, source_target_pairs={{0,128},{32,160},{64,192},{96,224},{128,0},{160,32},{192,64},{224,... | collective-permute-start | bytes 393224 | tf_op jit(solution)/shard_map/ppermute | solution.py:537
  10.0 10.3 %collective-permute-start.7 = (bf16[256,256]{1,0:T(8,128)(2,1)S(1)}, bf16[256,256]{1,0:T(8,128)(2,1)S(1)}, u32[]{:S(2)}, u32[]{:S(2)}) collective-permute-start(bf16[256,256]{1,0:T(8,128)(2,1)S(1)} %project_kv.1.kv), channel_id=1, source_target_pairs={{0,192},{32,224},{64,0},{96,32},{128,64},{160,96},{192,128},{224,1... | collective-permute-start | bytes 393224 | tf_op jit(solution)/shard_map/ppermute | solution.py:537
  20.4 17.5 %collective-permute-start.8 = (bf16[128,1536]{1,0:T(8,128)(2,1)S(1)}, bf16[128,1536]{1,0:T(8,128)(2,1)S(1)}, u32[]{:S(2)}, u32[]{:S(2)}) collective-permute-start(bf16[128,1536]{1,0:T(8,128)(2,1)S(1)} %bitcast.15), channel_id=1, source_target_pairs={{0,128},{32,160},{64,192},{96,224},{128,0},{160,32},{192,64},{224,... | collective-permute-start | bytes 1179656 | tf_op jit(solution)/shard_map/ppermute | solution.py:545
  25.1 11.3 %collective-permute-start.11 = (bf16[256,256]{1,0:T(8,128)(2,1)S(1)}, bf16[256,256]{1,0:T(8,128)(2,1)S(1)}, u32[]{:S(2)}, u32[]{:S(2)}) collective-permute-start(bf16[256,256]{1,0:T(8,128)(2,1)S(1)} %get-tuple-element.98), channel_id=1, source_target_pairs={{0,64},{32,96},{64,128},{96,160},{128,192},{160,224},{192,0},{224,... | collective-permute-start | bytes 393224 | tf_op jit(solution)/shard_map/ppermute | solution.py:552
  26.9 9.5 %collective-permute-start.10 = (bf16[256,256]{1,0:T(8,128)(2,1)S(1)}, bf16[256,256]{1,0:T(8,128)(2,1)S(1)}, u32[]{:S(2)}, u32[]{:S(2)}) collective-permute-start(bf16[256,256]{1,0:T(8,128)(2,1)S(1)} %get-tuple-element.95), channel_id=1, source_target_pairs={{0,192},{32,224},{64,0},{96,32},{128,64},{160,96},{192,128},{224,1... | collective-permute-start | bytes 393224 | tf_op jit(solution)/shard_map/ppermute | solution.py:552
  29.9 7.9 %collective-permute-start.9 = (bf16[256,256]{1,0:T(8,128)(2,1)S(1)}, bf16[256,256]{1,0:T(8,128)(2,1)S(1)}, u32[]{:S(2)}, u32[]{:S(2)}) collective-permute-start(bf16[256,256]{1,0:T(8,128)(2,1)S(1)} %get-tuple-element.92), channel_id=1, source_target_pairs={{0,128},{32,160},{64,192},{96,224},{128,0},{160,32},{192,64},{224,... | collective-permute-start | bytes 393224 | tf_op jit(solution)/shard_map/ppermute | solution.py:552
  37.8 1.9 %collective-permute-start.12 = (bf16[256,768]{1,0:T(8,128)(2,1)S(1)}, bf16[256,768]{1,0:T(8,128)(2,1)S(1)}, u32[]{:S(2)}, u32[]{:S(2)}) collective-permute-start(bf16[256,768]{1,0:T(8,128)(2,1)S(1)} %query_grad.1.dq), channel_id=1, source_target_pairs={{0,32},{32,0},{64,96},{96,64},{128,160},{160,128},{192,224},{224,1... | collective-permute-start | bytes 1179656 | tf_op jit(solution)/shard_map/ppermute | solution.py:556
  37.9 1.8 %collective-permute-start.13 = (bf16[256,256]{1,0:T(8,128)(2,1)S(1)}, bf16[256,256]{1,0:T(8,128)(2,1)S(1)}, u32[]{:S(2)}, u32[]{:S(2)}) collective-permute-start(bf16[256,256]{1,0:T(8,128)(2,1)S(1)} %sum_four.2.dkv), channel_id=1, source_target_pairs={{0,32},{32,0},{64,96},{96,64},{128,160},{160,128},{192,224},{224,1... | collective-permute-start | bytes 393224 | tf_op jit(solution)/shard_map/ppermute | solution.py:558
  38.5 5.6 %collective-permute-start.15 = (bf16[128,1536]{1,0:T(8,128)(2,1)S(1)}, bf16[128,1536]{1,0:T(8,128)(2,1)S(1)}, u32[]{:S(2)}, u32[]{:S(2)}) collective-permute-start(bf16[128,1536]{1,0:T(8,128)(2,1)S(1)} %collective-permute-done.8.refs_4_), channel_id=1, source_target_pairs={{0,32},{32,0},{64,96},{96,64},{128,160},{160,128},{192,224},{224,1... | collective-permute-start | bytes 1179656 | tf_op jit(solution)/shard_map/ppermute | solution.py:560
  40.4 4.7 %collective-permute-start.14 = (bf16[128,1536]{1,0:T(8,128)(2,1)S(1)}, bf16[128,1536]{1,0:T(8,128)(2,1)S(1)}, u32[]{:S(2)}, u32[]{:S(2)}) collective-permute-start(bf16[128,1536]{1,0:T(8,128)(2,1)S(1)} %collective-permute-done.3.refs_2_), channel_id=1, source_target_pairs={{0,32},{32,0},{64,96},{96,64},{128,160},{160,128},{192,224},{224,1... | collective-permute-start | bytes 1179656 | tf_op jit(solution)/shard_map/ppermute | solution.py:564
  40.6 4.4 %collective-permute-start.16 = (bf16[128,1536]{1,0:T(8,128)(2,1)S(1)}, bf16[128,1536]{1,0:T(8,128)(2,1)S(1)}, u32[]{:S(2)}, u32[]{:S(2)}) collective-permute-start(bf16[128,1536]{1,0:T(8,128)(2,1)S(1)} %collective-permute-done.4.refs_6_), channel_id=1, source_target_pairs={{0,32},{32,0},{64,96},{96,64},{128,160},{160,128},{192,224},{224,1... | collective-permute-start | bytes 1179656 | tf_op jit(solution)/shard_map/ppermute | solution.py:564
  41.0 9.6 %collective-permute-start.17 = (bf16[256,256]{1,0:T(8,128)(2,1)S(1)}, bf16[256,256]{1,0:T(8,128)(2,1)S(1)}, u32[]{:S(2)}, u32[]{:S(2)}) collective-permute-start(bf16[256,256]{1,0:T(8,128)(2,1)S(1)} %get-tuple-element.124), channel_id=1, source_target_pairs={{0,64},{32,96},{64,128},{96,160},{128,192},{160,224},{192,0},{224,... | collective-permute-start | bytes 393224 | tf_op jit(solution)/shard_map/ppermute | solution.py:569
  41.0 9.6 %collective-permute-start.18 = (bf16[256,256]{1,0:T(8,128)(2,1)S(1)}, bf16[256,256]{1,0:T(8,128)(2,1)S(1)}, u32[]{:S(2)}, u32[]{:S(2)}) collective-permute-start(bf16[256,256]{1,0:T(8,128)(2,1)S(1)} %get-tuple-element.125), channel_id=1, source_target_pairs={{0,128},{32,160},{64,192},{96,224},{128,0},{160,32},{192,64},{224,... | collective-permute-start | bytes 393224 | tf_op jit(solution)/shard_map/ppermute | solution.py:569
  44.1 7.1 %collective-permute-start.19 = (bf16[256,256]{1,0:T(8,128)(2,1)S(1)}, bf16[256,256]{1,0:T(8,128)(2,1)S(1)}, u32[]{:S(2)}, u32[]{:S(2)}) collective-permute-start(bf16[256,256]{1,0:T(8,128)(2,1)S(1)} %get-tuple-element.126), channel_id=1, source_target_pairs={{0,192},{32,224},{64,0},{96,32},{128,64},{160,96},{192,128},{224,1... | collective-permute-start | bytes 393224 | tf_op jit(solution)/shard_map/ppermute | solution.py:569
  52.7 10.4 %collective-permute-start.20 = (bf16[384,256]{1,0:T(8,128)(2,1)S(1)}, bf16[384,256]{1,0:T(8,128)(2,1)S(1)}, u32[]{:S(2)}, u32[]{:S(2)}) collective-permute-start(bf16[384,256]{1,0:T(8,128)(2,1)S(1)} %get-tuple-element.128), channel_id=1, source_target_pairs={{0,8},{1,9},{2,10},{3,11},{4,12},{5,13},{6,14},{7,15},{8,16},{9,17... | collective-permute-start | bytes 589832 | tf_op jit(solution)/shard_map/ppermute | solution.py:572
  54.3 9.2 %collective-permute-start.21 = (bf16[384,256]{1,0:T(8,128)(2,1)S(1)}, bf16[384,256]{1,0:T(8,128)(2,1)S(1)}, u32[]{:S(2)}, u32[]{:S(2)}) collective-permute-start(bf16[384,256]{1,0:T(8,128)(2,1)S(1)} %get-tuple-element.129), channel_id=1, source_target_pairs={{0,16},{1,17},{2,18},{3,19},{4,20},{5,21},{6,22},{7,23},{8,24},{9,... | collective-permute-start | bytes 589832 | tf_op jit(solution)/shard_map/ppermute | solution.py:572
  56.2 9.3 %collective-permute-start.22 = (bf16[384,256]{1,0:T(8,128)(2,1)S(1)}, bf16[384,256]{1,0:T(8,128)(2,1)S(1)}, u32[]{:S(2)}, u32[]{:S(2)}) collective-permute-start(bf16[384,256]{1,0:T(8,128)(2,1)S(1)} %get-tuple-element.130), channel_id=1, source_target_pairs={{0,24},{1,25},{2,26},{3,27},{4,28},{5,29},{6,30},{7,31},{8,0},{9,1... | collective-permute-start | bytes 589832 | tf_op jit(solution)/shard_map/ppermute | solution.py:572

commit v8 on v7

--- a/solution.py
+++ b/solution.py
@@ -365,32 +365,26 @@
     )(a, b, c, d)
 
 
-def pack_kernel(place, dq, dq_other, dkv, dkv_other, out0, out1, out2, out3, blocks):
-    core = place[1]
-
-    def swapped(ref, columns):
-        return jnp.concatenate([ref[TILE:, columns], ref[:TILE, columns]], axis=0)
-
-    middle = slice(256, 512)
-
-    @pl.when(core == 0)
-    def _():
-        blocks[0] = dq[:, 0:256]
-        blocks[1] = dq[:, 512:768]
-        blocks[2] = swapped(dq_other, middle)
-        blocks[3, :, :HD] = dkv[:, :HD]
-        blocks[3, :, HD:] = swapped(dkv_other, slice(0, HD))
-
-    @pl.when(core == 1)
-    def _():
-        blocks[0] = swapped(dq_other, middle)
-        blocks[1] = dq[:, 0:256]
-        blocks[2] = dq[:, 512:768]
-        blocks[3, :, :HD] = swapped(dkv_other, slice(HD, 2 * HD))
-        blocks[3, :, HD:] = dkv[:, HD:]
-
-    for d, out in enumerate((out0, out1, out2, out3)):
-        out[...] = blocks[lax.rem(place[0] + d, CHIPS)]
+def pack_kernel(place, dq, dq_other, dkv, dkv_other, *outs):
+    for core in range(2):
+        own_part = slice(core * HD, (core + 1) * HD)
+        for chip in range(CHIPS):
+
+            @pl.when((place[1] == core) & (place[0] == chip))
+            def _(core=core, own_part=own_part, chip=chip):
+                for d, out in enumerate(outs):
+                    target = (chip + d) % CHIPS
+                    if target == 3:
+                        out[:, own_part] = dkv[:, own_part]
+                        theirs = slice((1 - core) * HD, (2 - core) * HD)
+                        out[:TILE, theirs] = dkv_other[TILE:, own_part]
+                        out[TILE:, theirs] = dkv_other[:TILE, own_part]
+                    elif target == 2 - 2 * core:
+                        out[:TILE] = dq_other[TILE:, 256:512]
+                        out[TILE:] = dq_other[:TILE, 256:512]
+                    else:
+                        first = target == core
+                        out[...] = dq[:, 0:256] if first else dq[:, 512:768]
 
 
 def pack(place, dq, dq_other, dkv, dkv_other):
@@ -399,49 +393,53 @@
         in_specs=[SCALARS] + [WHOLE] * 4,
         out_specs=[WHOLE] * 4,
         out_shape=[jax.ShapeDtypeStruct((256, 256), BF)] * 4,
-        scratch_shapes=[pltpu.VMEM((4, 256, 256), BF)],
         compiler_params=PARAMS,
         cost_estimate=cost(0, 4 << 19),
         name="pack",
     )(place, dq, dq_other, dkv, dkv_other)
 
 
-def transpose_kernel(*refs):
-    out = refs[-1]
-    for i, ref in enumerate(refs[:-1]):
-        out[:, i * TILE : (i + 1) * TILE] = ref[...].T
+def transpose_kernel(own, far1, late_a, late_b, far3, out):
+    late = jnp.concatenate([late_a[...], late_b[...]], axis=0)
+    for i, rows in enumerate((own[...], far1[...], late, far3[...])):
+        out[:, i * TILE : (i + 1) * TILE] = rows.T
 
 
 def transpose(parts):
     return pl.pallas_call(
         transpose_kernel,
-        in_specs=[WHOLE] * 8,
-        out_specs=WHOLE,
-        out_shape=jax.ShapeDtypeStruct((D, KEYS), BF),
-        compiler_params=PARAMS,
-        cost_estimate=cost(0, 4 * D * KEYS),
+        in_specs=[WHOLE] * 5,
+        out_specs=WHOLE,
+        out_shape=jax.ShapeDtypeStruct((D, KEYS // 2), BF),
+        compiler_params=PARAMS,
+        cost_estimate=cost(0, 2 * D * KEYS),
         name="transpose_tokens",
     )(*parts)
 
 
-def weight_kernel(place, tokens_t, a, b, c, d, out0, out1, out2, out3):
-    right = jnp.concatenate([a[...], b[...], c[...], d[...]], axis=0)
+def weight_kernel(place, tokens_t, other_t, a, b, c, d, out0, out1, out2, out3):
+    parts = (a, b, c, d)
+    right = jnp.concatenate([part[:TILE] for part in parts], axis=0)
+    right_other = jnp.concatenate([part[TILE:] for part in parts], axis=0)
     for shift, out in enumerate((out0, out1, out2, out3)):
         row = pl.multiple_of(lax.rem(place[2] + shift, YS) * (D // YS), 128)
-        out[...] = dot(tokens_t[pl.ds(row, D // YS)], right).astype(out.dtype)
-
-
-def weight_grad(place, tokens_t, parts):
+        rows = pl.ds(row, D // YS)
+        out[...] = (dot(tokens_t[rows], right) + dot(other_t[rows], right_other)).astype(
+            out.dtype
+        )
+
+
+def weight_grad(place, tokens_t, other_t, parts):
     shape = (D // YS, 256)
     return pl.pallas_call(
         weight_kernel,
-        in_specs=[SCALARS] + [WHOLE] * 5,
+        in_specs=[SCALARS] + [WHOLE] * 6,
         out_specs=[WHOLE] * 4,
         out_shape=[jax.ShapeDtypeStruct(shape, F32)] + [jax.ShapeDtypeStruct(shape, BF)] * 3,
         compiler_params=PARAMS,
         cost_estimate=cost(2 * D * KEYS * 256, 2 * D * KEYS + 3 * D * 256),
         name="weight_grad",
-    )(place, tokens_t, *parts)
+    )(place, tokens_t, other_t, *parts)
 
 
 def input_kernel(
@@ -534,17 +532,23 @@
     w_query, w_key, w_value = (in_hbm(w) for w in (w_query, w_key, w_value))
     weights, kv_own = project_kv_own(place, in_hbm(own), w_key, w_value)
     kv = project_kv(other, weights, kv_own)
-    kvs = [kv] + [lax.ppermute(kv, "ctx", chip_shift(d)) for d in (1, 2, 3)]
+    kv2 = lax.ppermute(kv, "ctx", chip_shift(2))
     far = {d: lax.ppermute(own, "ctx", chip_shift(d)) for d in (1, 3)}
     query, limits = project_query(
         place, own, other, w_query, in_hbm(segments), in_hbm(tile_mask[0]), mask_other
     )
     up = stack_up(place, up, up_other)
-    scores = {0: chip_scores(0, kvs[0], limits, query, up)}
-    far, kvs, scores[0], late_own = lax.optimization_barrier((far, kvs, scores[0], own))
-    late = lax.ppermute(late_own, "ctx", chip_shift(2))
-    for d in (1, 3, 2):
-        scores[d] = chip_scores(d, kvs[d], limits, query, up)
+    scores = {0: chip_scores(0, kv, limits, query, up)}
+    far, kv2, scores[0] = lax.optimization_barrier((far, kv2, scores[0]))
+    far_other = {d: lax.ppermute(far[d], "ctx", CORE) for d in (1, 3)}
+    late = (
+        lax.ppermute(far[1][: TILE // 2], "ctx", chip_shift(1)),
+        lax.ppermute(far[3][TILE // 2 :], "ctx", chip_shift(3)),
+    )
+    scores[2] = chip_scores(2, kv2, limits, query, up)
+    for d in (1, 3):
+        kv_far = project_kv_pair(far[d], far_other[d], weights)
+        scores[d] = chip_scores(d, kv_far, limits, query, up)
     factors = softmax_factors([scores[d][2] for d in range(CHIPS)])
     terms, grad_scores = {}, {}
     for d in (2, 1, 3):
@@ -556,19 +560,16 @@
     dq_other = lax.ppermute(dq, "ctx", CORE)
     dkv = sum_four(terms[0], *back)
     dkv_other = lax.ppermute(dkv, "ctx", CORE)
-    far[2], dkv = lax.optimization_barrier((late, dkv))
-    far_other = {2: lax.ppermute(far[2], "ctx", CORE)}
     packed = pack(place, dq, dq_other, dkv, dkv_other)
-    far[1], far[3], packed = lax.optimization_barrier((far[1], far[3], packed))
-    for d in (1, 3):
-        far_other[d] = lax.ppermute(far[d], "ctx", CORE)
-    tokens_t = transpose(
-        [own, other] + [part for d in (1, 2, 3) for part in (far[d], far_other[d])]
-    )
+
+    far, dkv = lax.optimization_barrier((far, dkv))
+    tokens_t = transpose([own, far[1], *late, far[3]])
+    tokens_t, packed = lax.optimization_barrier((tokens_t, packed))
+    other_t = lax.ppermute(tokens_t, "ctx", CORE)
     columns = [packed[0]] + [
         lax.ppermute(packed[d], "ctx", chip_shift(d)) for d in (1, 2, 3)
     ]
-    terms = weight_grad(place, tokens_t, columns)
+    terms = weight_grad(place, tokens_t, other_t, columns)
     y_parts = [terms[0]] + [lax.ppermute(terms[d], "dp", y_shift(d)) for d in (1, 2, 3)]
     grad_tokens = input_grad(
         place, dq, dq_other, dkv, dkv_other, w_query, w_key, w_value

time: 85.1 us -> 83.1 us (0.976)
  starting transfers between devices: 24.7 us -> 22.3 us
  waiting for transfers between devices: 19.1 us -> 20.1 us
    ppermute x3, waiting for transfers between devices: 5.07 us -> 7.16 us  [shards(): lax.ppermute(packed[d], 'ctx', chip_shift(d))]
    ppermute x7 -> x6, waiting for transfers between devices: 3.49 us -> 1.6 us  [the longest x1 1.59 us: shards(): kv2 = lax.ppermute(kv, 'ctx', chip_shift(2))]
    ppermute x2, waiting for transfers between devices: 0.98 us -> 2.73 us  [shards(): far = {d: lax.ppermute(own, 'ctx', chip_shift(d)) for d in (1, 3)}]
    ppermute x7 -> x6, starting transfers between devices: 6.97 us -> 5.95 us  [the longest x1 2.1 us: shards(): lax.ppermute(far[3][TILE // 2:], 'ctx', chip_shift(3))]
    pallas_call x2 -> x4, Pallas kernels: 2.51 us -> 2.72 us  [the longest x1 1.51 us: weight_grad(): pl.pallas_call(weight_kernel, in_specs=[SCALARS] + [WHOLE] * 6, out_specs...]
  transfers between devices with their start and end apart: 23 -> 22, of which waited for: 9 -> 11; matrix products, arithmetic and copies ran while one was open for 0% -> 0% of each run, Pallas kernels for 23% -> 23%
where the time goes in v8:
time: 83.1 us; the launch traced here: 82.6 us
  starting transfers between devices  22.3 us (27%)
  Pallas kernels  21.7 us (26%)
  waiting for transfers between devices  20.1 us (24%)
  blocking collectives  17.6 us (21%)
  between operations  0.9 us (1%)
    all_to_all x1, blocking collectives, shards(): lax.all_to_all(y_sum, 'dp', 0, 0, tiled=True, axis_index_groups=Z_GROUPS)  17.6 us
    ppermute x3, waiting for transfers between devices, shards(): lax.ppermute(packed[d], 'ctx', chip_shift(d))  7.16 us
    pallas_call x1, Pallas kernels, input_grad(): pl.pallas_call(input_kernel, in_specs=[SCALARS] + [WHOLE] * 4 + [STAY] *...  5.36 us
    ppermute x3, waiting for transfers between devices, shards(): lax.ppermute(terms[d], 'ctx', chip_shift(CHIPS - d))  5.14 us
    ppermute x3, starting transfers between devices, shards(): lax.ppermute(terms[d], 'dp', y_shift(d))  5 us
    ppermute x3, starting transfers between devices, shards(): lax.ppermute(terms[d], 'ctx', chip_shift(CHIPS - d))  3.65 us
    ppermute x3, starting transfers between devices, shards(): lax.ppermute(packed[d], 'ctx', chip_shift(d))  3.25 us
    ppermute x2, starting transfers between devices, shards(): far = {d: lax.ppermute(own, 'ctx', chip_shift(d)) for d in (1, 3)}  3.24 us
  transfers between devices with their start and end apart: 22, of which 11 were waited for; matrix products, arithmetic and copies ran while one was open for 0% of the time, Pallas kernels for 23%

profile of v8, /device:TPU:8, one launch (start us, length us, event | category | flops | bytes accessed | tf_op | source)
XLA Modules:
  0.0 82.6 jit_solution(4719965740469032991)
XLA Ops:
  0.6 0.1 collective-permute-start.2
  0.7 0.5 collective-permute-start.4
  1.2 1.5 %collective-permute-start = (bf16[128,1536]{1,0:T(8,128)(2,1)}, bf16[128,1536]{1,0:T(8,128)(2,1)S(1)}, u32[]{:S(2)}, u32[]{:S(2)}) collective-permute-start(bf16[128,1536]{1,0:T(8,128)(2,1)} %bitcast.11), channel_id=1, source_target_pairs={{0,64},{32,96},{64,128},{96,160},{128,192},{160,224},{192,0},{224,... | collective-permute-start | bytes 1179656 | tf_op jit(solution)/shard_map/ppermute | solution.py:536
  2.7 1.7 %collective-permute-start.1 = (bf16[128,1536]{1,0:T(8,128)(2,1)}, bf16[128,1536]{1,0:T(8,128)(2,1)S(1)}, u32[]{:S(2)}, u32[]{:S(2)}) collective-permute-start(bf16[128,1536]{1,0:T(8,128)(2,1)} %bitcast.12), channel_id=1, source_target_pairs={{0,192},{32,224},{64,0},{96,32},{128,64},{160,96},{192,128},{224,1... | collective-permute-start | bytes 1179656 | tf_op jit(solution)/shard_map/ppermute | solution.py:536
  4.5 0.0 collective-permute-start.3
  4.5 0.1 pad_add_fusion.place
  4.5 2.1 %project_kv_own.1 = (bf16[1536,256]{1,0:T(8,128)(2,1)S(1)}, bf16[128,256]{1,0:T(8,128)(2,1)S(1)}) custom-call(s32[4]{0:T(128)S(1)} %pad_add_fusion.place, bf16[128,1536]{1,0:T(8,128)(2,1)} %bitcast.13, bf16[1536,256]{1,0:T(8,128)(2,1)} %w_key.3, bf16[1536,256]{1,0:T(8,128)(2,1)} %w_value.3), custom_call_target="tpu_custom_call" | custom-call | flops 1 | bytes 1 | tf_op jit(solution)/shard_map/project_kv_own/pallas_call | solution.py:94
  6.6 0.0 copy-start
  6.6 0.0 collective-permute-done.3.mask_other
  6.7 0.0 collective-permute-done.4.up_other
  6.7 0.3 project_kv.1.kv
  7.0 1.9 %collective-permute-start.5 = (bf16[256,256]{1,0:T(8,128)(2,1)S(1)}, bf16[256,256]{1,0:T(8,128)(2,1)S(1)}, u32[]{:S(2)}, u32[]{:S(2)}) collective-permute-start(bf16[256,256]{1,0:T(8,128)(2,1)S(1)} %project_kv.1.kv), channel_id=1, source_target_pairs={{0,128},{32,160},{64,192},{96,224},{128,0},{160,32},{192,64},{224,... | collective-permute-start | bytes 393224 | tf_op jit(solution)/shard_map/ppermute | solution.py:535
  8.9 0.6 stack_up.1.up
  9.5 3.0 %project_query.1 = (bf16[1536,128]{1,0:T(8,128)(2,1)S(1)}, s32[16,256]{1,0:T(8,128)S(1)}) custom-call(s32[4]{0:T(128)S(1)} %pad_add_fusion.place, bf16[128,1536]{1,0:T(8,128)(2,1)S(1)} %bitcast.14, bf16[128,1536]{1,0:T(8,128)(2,1)S(1)} %collective-permute-done.2.other, bf16[1536,1536]{1,0:T(8,128)(2,1)} %w_query.3, s32[1,1024]{1,0:T(1,128)} %segments_far.1, ...), custom_call_target="tpu_custom_call" | custom-call | flops 1 | bytes 1 | tf_op jit(solution)/shard_map/project_query/pallas_call | solution.py:202
  12.5 0.7 chip_scores_0.1
  13.2 0.5 collective-permute-done.own.far1
  13.8 2.2 %collective-permute-done.1.own.far3 = bf16[128,1536]{1,0:T(8,128)(2,1)S(1)} collective-permute-done((bf16[128,1536]{1,0:T(8,128)(2,1)}, bf16[128,1536]{1,0:T(8,128)(2,1)S(1)}, u32[]{:S(2)}, u32[]{:S(2)}) %collective-permute-start.1) | collective-permute-done | bytes 393248 | tf_op jit(solution)/shard_map/ppermute | solution.py:536
  16.0 1.6 %collective-permute-done.5.kv = bf16[256,256]{1,0:T(8,128)(2,1)S(1)} collective-permute-done((bf16[256,256]{1,0:T(8,128)(2,1)S(1)}, bf16[256,256]{1,0:T(8,128)(2,1)S(1)}, u32[]{:S(2)}, u32[]{:S(2)}) %collective-permute-start.5) | collective-permute-done | bytes 131104 | tf_op jit(solution)/shard_map/ppermute | solution.py:535
  17.6 0.0 collective-permute-start.7
  17.6 0.5 collective-permute-start.6
  18.1 1.2 %collective-permute-start.8 = (bf16[64,1536]{1,0:T(8,128)(2,1)S(1)}, bf16[64,1536]{1,0:T(8,128)(2,1)S(1)}, u32[]{:S(2)}, u32[]{:S(2)}) collective-permute-start(bf16[64,1536]{1,0:T(8,128)(2,1)S(1)} %slice.6), channel_id=1, source_target_pairs={{0,64},{32,96},{64,128},{96,160},{128,192},{160,224},{192,0},{224,... | collective-permute-start | bytes 589832 | tf_op jit(solution)/shard_map/ppermute | solution.py:545
  19.3 2.1 %collective-permute-start.9 = (bf16[64,1536]{1,0:T(8,128)(2,1)S(1)}, bf16[64,1536]{1,0:T(8,128)(2,1)S(1)}, u32[]{:S(2)}, u32[]{:S(2)}) collective-permute-start(bf16[64,1536]{1,0:T(8,128)(2,1)S(1)} %slice.7), channel_id=1, source_target_pairs={{0,192},{32,224},{64,0},{96,32},{128,64},{160,96},{192,128},{224,1... | collective-permute-start | bytes 589832 | tf_op jit(solution)/shard_map/ppermute | solution.py:546
  21.4 0.0 collective-permute-done.7.other
  21.4 0.4 project_kv_pair.3.kv
  21.8 0.4 project_kv_pair.2.kv
  22.2 0.7 chip_scores_2.1
  23.0 0.7 chip_scores_3.1
  23.7 0.7 chip_scores_1.1
  24.5 0.6 chip_terms_3.1
  25.1 0.3 collective-permute-start.12
  25.4 0.6 chip_terms_1.1
  26.0 3.3 %collective-permute-start.11 = (bf16[256,256]{1,0:T(8,128)(2,1)S(1)}, bf16[256,256]{1,0:T(8,128)(2,1)S(1)}, u32[]{:S(2)}, u32[]{:S(2)}) collective-permute-start(bf16[256,256]{1,0:T(8,128)(2,1)S(1)} %get-tuple-element.93), channel_id=1, source_target_pairs={{0,192},{32,224},{64,0},{96,32},{128,64},{160,96},{192,128},{224,1... | collective-permute-start | bytes 393224 | tf_op jit(solution)/shard_map/ppermute | solution.py:556
  29.3 0.6 chip_terms_2.1
  30.0 0.1 collective-permute-start.10
  30.1 0.6 chip_terms_0.1
  30.7 0.7 query_grad.1.dq
  31.4 0.2 collective-permute-done.12.d
  31.6 2.7 %collective-permute-done.11.c = bf16[256,256]{1,0:T(8,128)(2,1)S(1)} collective-permute-done((bf16[256,256]{1,0:T(8,128)(2,1)S(1)}, bf16[256,256]{1,0:T(8,128)(2,1)S(1)}, u32[]{:S(2)}, u32[]{:S(2)}) %collective-permute-start.11) | collective-permute-done | bytes 131104 | tf_op jit(solution)/shard_map/ppermute | solution.py:556
  34.2 2.3 %collective-permute-done.10.b = bf16[256,256]{1,0:T(8,128)(2,1)S(1)} collective-permute-done((bf16[256,256]{1,0:T(8,128)(2,1)S(1)}, bf16[256,256]{1,0:T(8,128)(2,1)S(1)}, u32[]{:S(2)}, u32[]{:S(2)}) %collective-permute-start.10) | collective-permute-done | bytes 131104 | tf_op jit(solution)/shard_map/ppermute | solution.py:556
  36.5 0.0 collective-permute-start.13
  36.5 0.1 sum_four.2.dkv
  36.6 0.6 collective-permute-start.14
  37.2 0.5 transpose_tokens.1.tokens_t
  37.7 0.8 collective-permute-done.14.dkv_other
  38.5 0.7 pack.1
  39.1 0.2 collective-permute-start.15
  39.3 0.0 collective-permute-start.16
  39.3 2.9 %collective-permute-start.17 = (bf16[256,256]{1,0:T(8,128)(2,1)S(1)}, bf16[256,256]{1,0:T(8,128)(2,1)S(1)}, u32[]{:S(2)}, u32[]{:S(2)}) collective-permute-start(bf16[256,256]{1,0:T(8,128)(2,1)S(1)} %get-tuple-element.120), channel_id=1, source_target_pairs={{0,128},{32,160},{64,192},{96,224},{128,0},{160,32},{192,64},{224,... | collective-permute-start | bytes 393224 | tf_op jit(solution)/shard_map/ppermute | solution.py:570
  42.2 0.4 collective-permute-start.18
  42.6 6.5 %collective-permute-done.16.b = bf16[256,256]{1,0:T(8,128)(2,1)S(1)} collective-permute-done((bf16[256,256]{1,0:T(8,128)(2,1)S(1)}, bf16[256,256]{1,0:T(8,128)(2,1)S(1)}, u32[]{:S(2)}, u32[]{:S(2)}) %collective-permute-start.16) | collective-permute-done | bytes 131104 | tf_op jit(solution)/shard_map/ppermute | solution.py:570
  49.1 0.0 collective-permute-done.17.c
  49.1 0.6 collective-permute-done.18.d
  49.8 0.0 collective-permute-done.15.other_t
  49.8 1.5 %weight_grad.1 = (f32[384,256]{1,0:T(8,128)S(1)}, bf16[384,256]{1,0:T(8,128)(2,1)S(1)}, bf16[384,256]{1,0:T(8,128)(2,1)S(1)}, bf16[384,256]{1,0:T(8,128)(2,1)S(1)}) custom-call(s32[4]{0:T(128)S(1)} %pad_add_fusion.place, bf16[1536,512]{1,0:T(8,128)(2,1)S(1)} %transpose_tokens.1.tokens_t, bf16[1536,512]{1,0:T(8,128)(2,1)S(1)} %collective-permute-done.15.other_t, ...), custom_call_target="tpu_custom_call" | custom-call | flops 1 | bytes 1 | tf_op jit(solution)/shard_map/weight_grad/pallas_call | solution.py:434
  51.3 1.6 %collective-permute-start.19 = (bf16[384,256]{1,0:T(8,128)(2,1)S(1)}, bf16[384,256]{1,0:T(8,128)(2,1)S(1)}, u32[]{:S(2)}, u32[]{:S(2)}) collective-permute-start(bf16[384,256]{1,0:T(8,128)(2,1)S(1)} %get-tuple-element.123), channel_id=1, source_target_pairs={{0,8},{1,9},{2,10},{3,11},{4,12},{5,13},{6,14},{7,15},{8,16},{9,17... | collective-permute-start | bytes 589832 | tf_op jit(solution)/shard_map/ppermute | solution.py:573
  52.9 1.7 %collective-permute-start.20 = (bf16[384,256]{1,0:T(8,128)(2,1)S(1)}, bf16[384,256]{1,0:T(8,128)(2,1)S(1)}, u32[]{:S(2)}, u32[]{:S(2)}) collective-permute-start(bf16[384,256]{1,0:T(8,128)(2,1)S(1)} %get-tuple-element.124), channel_id=1, source_target_pairs={{0,16},{1,17},{2,18},{3,19},{4,20},{5,21},{6,22},{7,23},{8,24},{9,... | collective-permute-start | bytes 589832 | tf_op jit(solution)/shard_map/ppermute | solution.py:573
  54.6 1.7 %collective-permute-start.21 = (bf16[384,256]{1,0:T(8,128)(2,1)S(1)}, bf16[384,256]{1,0:T(8,128)(2,1)S(1)}, u32[]{:S(2)}, u32[]{:S(2)}) collective-permute-start(bf16[384,256]{1,0:T(8,128)(2,1)S(1)} %get-tuple-element.125), channel_id=1, source_target_pairs={{0,24},{1,25},{2,26},{3,27},{4,28},{5,29},{6,30},{7,31},{8,0},{9,1... | collective-permute-start | bytes 589832 | tf_op jit(solution)/shard_map/ppermute | solution.py:573
  56.3 5.4 %input_grad.1 = bf16[128,1536]{1,0:T(8,128)(2,1)} custom-call(s32[4]{0:T(128)S(1)} %pad_add_fusion.place, bf16[256,768]{1,0:T(8,128)(2,1)S(1)} %query_grad.1.dq, bf16[256,768]{1,0:T(8,128)(2,1)S(1)} %collective-permute-done.13.dq_other, bf16[256,256]{1,0:T(8,128)(2,1)S(1)} %sum_four.2.dkv, bf16[256,256]{1,0:T(8,128)(2,1)S(1)} %collective-permute-done.14.dkv_other, ...), custom_call_target="tpu_custom_call" | custom-call | flops 1 | bytes 1 | tf_op jit(solution)/shard_map/input_grad/pallas_call | solution.py:487
  61.6 0.0 collective-permute-done.19.b
  61.7 0.6 collective-permute-done.20.c
  62.3 2.0 %collective-permute-done.21.d = bf16[384,256]{1,0:T(8,128)(2,1)S(1)} collective-permute-done((bf16[384,256]{1,0:T(8,128)(2,1)S(1)}, bf16[384,256]{1,0:T(8,128)(2,1)S(1)}, u32[]{:S(2)}, u32[]{:S(2)}) %collective-permute-start.21) | collective-permute-done | bytes 196640 | tf_op jit(solution)/shard_map/ppermute | solution.py:573
  64.3 0.1 sum_four.3
  64.4 17.6 %all_to_all.11 = bf16[8,48,256]{2,1,0:T(8,128)(2,1)S(1)} all-to-all(bf16[8,48,256]{2,1,0:T(8,128)(2,1)S(1)} %bitcast.16), channel_id=1, replica_groups={{0,1,2,3,4,5,6,7},{8,9,10,11,12,13,14,15},{16,17,18,19,20,21,22,23},{24..., dimensions={0} | all-to-all | bytes 393216 | tf_op jit(solution)/shard_map/all_to_all | solution.py:579
  82.0 0.6 final_sum.1
  (11 shorter events, 0.1 us)
Async XLA Ops:
  0.6 6.0 %collective-permute-start.2 = (bf16[128,1536]{1,0:T(8,128)(2,1)}, bf16[128,1536]{1,0:T(8,128)(2,1)S(1)}, u32[]{:S(2)}, u32[]{:S(2)}) collective-permute-start(bf16[128,1536]{1,0:T(8,128)(2,1)} %bitcast.10), channel_id=1, source_target_pairs={{0,32},{32,0},{64,96},{96,64},{128,160},{160,128},{192,224},{224,1... | collective-permute-start | bytes 1179656 | tf_op jit(solution)/shard_map/ppermute | solution.py:527
  0.7 5.9 %collective-permute-start.4 = (bf16[128,1536]{1,0:T(8,128)(2,1)}, bf16[128,1536]{1,0:T(8,128)(2,1)S(1)}, u32[]{:S(2)}, u32[]{:S(2)}) collective-permute-start(bf16[128,1536]{1,0:T(8,128)(2,1)} %bitcast.18), channel_id=1, source_target_pairs={{0,32},{32,0},{64,96},{96,64},{128,160},{160,128},{192,224},{224,1... | collective-permute-start | bytes 1179656 | tf_op jit(solution)/shard_map/ppermute | solution.py:528
  1.2 12.5 %collective-permute-start = (bf16[128,1536]{1,0:T(8,128)(2,1)}, bf16[128,1536]{1,0:T(8,128)(2,1)S(1)}, u32[]{:S(2)}, u32[]{:S(2)}) collective-permute-start(bf16[128,1536]{1,0:T(8,128)(2,1)} %bitcast.11), channel_id=1, source_target_pairs={{0,64},{32,96},{64,128},{96,160},{128,192},{160,224},{192,0},{224,... | collective-permute-start | bytes 1179656 | tf_op jit(solution)/shard_map/ppermute | solution.py:536
  2.7 13.3 %collective-permute-start.1 = (bf16[128,1536]{1,0:T(8,128)(2,1)}, bf16[128,1536]{1,0:T(8,128)(2,1)S(1)}, u32[]{:S(2)}, u32[]{:S(2)}) collective-permute-start(bf16[128,1536]{1,0:T(8,128)(2,1)} %bitcast.12), channel_id=1, source_target_pairs={{0,192},{32,224},{64,0},{96,32},{128,64},{160,96},{192,128},{224,1... | collective-permute-start | bytes 1179656 | tf_op jit(solution)/shard_map/ppermute | solution.py:536
  4.5 2.2 %collective-permute-start.3 = (s32[1,8]{1,0:T(1,128)}, s32[1,8]{1,0:T(1,128)S(1)}, u32[]{:S(2)}, u32[]{:S(2)}) collective-permute-start(s32[1,8]{1,0:T(1,128)} %bitcast.21), channel_id=1, source_target_pairs={{0,32},{32,0},{64,96},{96,64},{128,160},{160,128},{192,224},{224,1... | collective-permute-start | bytes 104 | tf_op jit(solution)/shard_map/ppermute | solution.py:529
  4.5 4.3 %copy-start.1 = (bf16[1,128,1536]{2,1,0:T(8,128)(2,1)S(1)}, bf16[1,128,1536]{2,1,0:T(8,128)(2,1)}, u32[]{:S(2)}) copy-start(bf16[1,128,1536]{2,1,0:T(8,128)(2,1)} %param.8) | copy-start | bytes 1179652
  6.6 2.9 %copy-start = (bf16[1,128,1536]{2,1,0:T(8,128)(2,1)S(1)}, bf16[1,128,1536]{2,1,0:T(8,128)(2,1)}, u32[]{:S(2)}) copy-start(bf16[1,128,1536]{2,1,0:T(8,128)(2,1)} %param.7) | copy-start | bytes 1179652
  7.0 10.6 %collective-permute-start.5 = (bf16[256,256]{1,0:T(8,128)(2,1)S(1)}, bf16[256,256]{1,0:T(8,128)(2,1)S(1)}, u32[]{:S(2)}, u32[]{:S(2)}) collective-permute-start(bf16[256,256]{1,0:T(8,128)(2,1)S(1)} %project_kv.1.kv), channel_id=1, source_target_pairs={{0,128},{32,160},{64,192},{96,224},{128,0},{160,32},{192,64},{224,... | collective-permute-start | bytes 393224 | tf_op jit(solution)/shard_map/ppermute | solution.py:535
  17.6 3.9 %collective-permute-start.7 = (bf16[128,1536]{1,0:T(8,128)(2,1)S(1)}, bf16[128,1536]{1,0:T(8,128)(2,1)S(1)}, u32[]{:S(2)}, u32[]{:S(2)}) collective-permute-start(bf16[128,1536]{1,0:T(8,128)(2,1)S(1)} %collective-permute-done.1.own.far3), channel_id=1, source_target_pairs={{0,32},{32,0},{64,96},{96,64},{128,160},{160,128},{192,224},{224,1... | collective-permute-start | bytes 1179656 | tf_op jit(solution)/shard_map/ppermute | solution.py:543
  17.6 4.3 %collective-permute-start.6 = (bf16[128,1536]{1,0:T(8,128)(2,1)S(1)}, bf16[128,1536]{1,0:T(8,128)(2,1)S(1)}, u32[]{:S(2)}, u32[]{:S(2)}) collective-permute-start(bf16[128,1536]{1,0:T(8,128)(2,1)S(1)} %collective-permute-done.own.far1), channel_id=1, source_target_pairs={{0,32},{32,0},{64,96},{96,64},{128,160},{160,128},{192,224},{224,1... | collective-permute-start | bytes 1179656 | tf_op jit(solution)/shard_map/ppermute | solution.py:543
  18.1 13.3 %collective-permute-start.8 = (bf16[64,1536]{1,0:T(8,128)(2,1)S(1)}, bf16[64,1536]{1,0:T(8,128)(2,1)S(1)}, u32[]{:S(2)}, u32[]{:S(2)}) collective-permute-start(bf16[64,1536]{1,0:T(8,128)(2,1)S(1)} %slice.6), channel_id=1, source_target_pairs={{0,64},{32,96},{64,128},{96,160},{128,192},{160,224},{192,0},{224,... | collective-permute-start | bytes 589832 | tf_op jit(solution)/shard_map/ppermute | solution.py:545
  19.3 12.1 %collective-permute-start.9 = (bf16[64,1536]{1,0:T(8,128)(2,1)S(1)}, bf16[64,1536]{1,0:T(8,128)(2,1)S(1)}, u32[]{:S(2)}, u32[]{:S(2)}) collective-permute-start(bf16[64,1536]{1,0:T(8,128)(2,1)S(1)} %slice.7), channel_id=1, source_target_pairs={{0,192},{32,224},{64,0},{96,32},{128,64},{160,96},{192,128},{224,1... | collective-permute-start | bytes 589832 | tf_op jit(solution)/shard_map/ppermute | solution.py:546
  25.1 6.4 %collective-permute-start.12 = (bf16[256,256]{1,0:T(8,128)(2,1)S(1)}, bf16[256,256]{1,0:T(8,128)(2,1)S(1)}, u32[]{:S(2)}, u32[]{:S(2)}) collective-permute-start(bf16[256,256]{1,0:T(8,128)(2,1)S(1)} %get-tuple-element.96), channel_id=1, source_target_pairs={{0,64},{32,96},{64,128},{96,160},{128,192},{160,224},{192,0},{224,... | collective-permute-start | bytes 393224 | tf_op jit(solution)/shard_map/ppermute | solution.py:556
  26.0 8.2 %collective-permute-start.11 = (bf16[256,256]{1,0:T(8,128)(2,1)S(1)}, bf16[256,256]{1,0:T(8,128)(2,1)S(1)}, u32[]{:S(2)}, u32[]{:S(2)}) collective-permute-start(bf16[256,256]{1,0:T(8,128)(2,1)S(1)} %get-tuple-element.93), channel_id=1, source_target_pairs={{0,192},{32,224},{64,0},{96,32},{128,64},{160,96},{192,128},{224,1... | collective-permute-start | bytes 393224 | tf_op jit(solution)/shard_map/ppermute | solution.py:556
  30.0 6.6 %collective-permute-start.10 = (bf16[256,256]{1,0:T(8,128)(2,1)S(1)}, bf16[256,256]{1,0:T(8,128)(2,1)S(1)}, u32[]{:S(2)}, u32[]{:S(2)}) collective-permute-start(bf16[256,256]{1,0:T(8,128)(2,1)S(1)} %get-tuple-element.90), channel_id=1, source_target_pairs={{0,128},{32,160},{64,192},{96,224},{128,0},{160,32},{192,64},{224,... | collective-permute-start | bytes 393224 | tf_op jit(solution)/shard_map/ppermute | solution.py:556
  36.5 1.9 %collective-permute-start.13 = (bf16[256,768]{1,0:T(8,128)(2,1)S(1)}, bf16[256,768]{1,0:T(8,128)(2,1)S(1)}, u32[]{:S(2)}, u32[]{:S(2)}) collective-permute-start(bf16[256,768]{1,0:T(8,128)(2,1)S(1)} %query_grad.1.dq), channel_id=1, source_target_pairs={{0,32},{32,0},{64,96},{96,64},{128,160},{160,128},{192,224},{224,1... | collective-permute-start | bytes 1179656 | tf_op jit(solution)/shard_map/ppermute | solution.py:560
  36.6 1.8 %collective-permute-start.14 = (bf16[256,256]{1,0:T(8,128)(2,1)S(1)}, bf16[256,256]{1,0:T(8,128)(2,1)S(1)}, u32[]{:S(2)}, u32[]{:S(2)}) collective-permute-start(bf16[256,256]{1,0:T(8,128)(2,1)S(1)} %sum_four.2.dkv), channel_id=1, source_target_pairs={{0,32},{32,0},{64,96},{96,64},{128,160},{160,128},{192,224},{224,1... | collective-permute-start | bytes 393224 | tf_op jit(solution)/shard_map/ppermute | solution.py:562
  39.1 10.6 %collective-permute-start.15 = (bf16[1536,512]{1,0:T(8,128)(2,1)S(1)}, bf16[1536,512]{1,0:T(8,128)(2,1)S(1)}, u32[]{:S(2)}, u32[]{:S(2)}) collective-permute-start(bf16[1536,512]{1,0:T(8,128)(2,1)S(1)} %transpose_tokens.1.tokens_t), channel_id=1, source_target_pairs={{0,32},{32,0},{64,96},{96,64},{128,160},{160,128},{192,224},{224,1... | collective-permute-start | bytes 4718600 | tf_op jit(solution)/shard_map/ppermute | solution.py:568
  39.3 9.8 %collective-permute-start.16 = (bf16[256,256]{1,0:T(8,128)(2,1)S(1)}, bf16[256,256]{1,0:T(8,128)(2,1)S(1)}, u32[]{:S(2)}, u32[]{:S(2)}) collective-permute-start(bf16[256,256]{1,0:T(8,128)(2,1)S(1)} %get-tuple-element.119), channel_id=1, source_target_pairs={{0,64},{32,96},{64,128},{96,160},{128,192},{160,224},{192,0},{224,... | collective-permute-start | bytes 393224 | tf_op jit(solution)/shard_map/ppermute | solution.py:570
  39.3 9.8 %collective-permute-start.17 = (bf16[256,256]{1,0:T(8,128)(2,1)S(1)}, bf16[256,256]{1,0:T(8,128)(2,1)S(1)}, u32[]{:S(2)}, u32[]{:S(2)}) collective-permute-start(bf16[256,256]{1,0:T(8,128)(2,1)S(1)} %get-tuple-element.120), channel_id=1, source_target_pairs={{0,128},{32,160},{64,192},{96,224},{128,0},{160,32},{192,64},{224,... | collective-permute-start | bytes 393224 | tf_op jit(solution)/shard_map/ppermute | solution.py:570
  42.2 7.5 %collective-permute-start.18 = (bf16[256,256]{1,0:T(8,128)(2,1)S(1)}, bf16[256,256]{1,0:T(8,128)(2,1)S(1)}, u32[]{:S(2)}, u32[]{:S(2)}) collective-permute-start(bf16[256,256]{1,0:T(8,128)(2,1)S(1)} %get-tuple-element.121), channel_id=1, source_target_pairs={{0,192},{32,224},{64,0},{96,32},{128,64},{160,96},{192,128},{224,1... | collective-permute-start | bytes 393224 | tf_op jit(solution)/shard_map/ppermute | solution.py:570
  51.3 10.4 %collective-permute-start.19 = (bf16[384,256]{1,0:T(8,128)(2,1)S(1)}, bf16[384,256]{1,0:T(8,128)(2,1)S(1)}, u32[]{:S(2)}, u32[]{:S(2)}) collective-permute-start(bf16[384,256]{1,0:T(8,128)(2,1)S(1)} %get-tuple-element.123), channel_id=1, source_target_pairs={{0,8},{1,9},{2,10},{3,11},{4,12},{5,13},{6,14},{7,15},{8,16},{9,17... | collective-permute-start | bytes 589832 | tf_op jit(solution)/shard_map/ppermute | solution.py:573
  52.9 9.3 %collective-permute-start.20 = (bf16[384,256]{1,0:T(8,128)(2,1)S(1)}, bf16[384,256]{1,0:T(8,128)(2,1)S(1)}, u32[]{:S(2)}, u32[]{:S(2)}) collective-permute-start(bf16[384,256]{1,0:T(8,128)(2,1)S(1)} %get-tuple-element.124), channel_id=1, source_target_pairs={{0,16},{1,17},{2,18},{3,19},{4,20},{5,21},{6,22},{7,23},{8,24},{9,... | collective-permute-start | bytes 589832 | tf_op jit(solution)/shard_map/ppermute | solution.py:573
  54.6 9.7 %collective-permute-start.21 = (bf16[384,256]{1,0:T(8,128)(2,1)S(1)}, bf16[384,256]{1,0:T(8,128)(2,1)S(1)}, u32[]{:S(2)}, u32[]{:S(2)}) collective-permute-start(bf16[384,256]{1,0:T(8,128)(2,1)S(1)} %get-tuple-element.125), channel_id=1, source_target_pairs={{0,24},{1,25},{2,26},{3,27},{4,28},{5,29},{6,30},{7,31},{8,0},{9,1... | collective-permute-start | bytes 589832 | tf_op jit(solution)/shard_map/ppermute | solution.py:573

commit v9 on v8

--- a/solution.py
+++ b/solution.py
@@ -106,21 +106,21 @@
     )(place, own, w_key, w_value)
 
 
-def kv_pair_kernel(own, other, weights, out):
-    out[:TILE] = dot(own[...], weights[...]).astype(BF)
-    out[TILE:] = dot(other[...], weights[...]).astype(BF)
-
-
-def project_kv_pair(own, other, weights):
-    return pl.pallas_call(
-        kv_pair_kernel,
+def kv_far_kernel(rows, weights, weights_other, mine, theirs):
+    mine[...] = dot(rows[...], weights[...]).astype(BF)
+    theirs[...] = dot(rows[...], weights_other[...]).astype(BF)
+
+
+def project_kv_far(rows, weights, weights_other):
+    return pl.pallas_call(
+        kv_far_kernel,
         in_specs=[WHOLE] * 3,
-        out_specs=WHOLE,
-        out_shape=jax.ShapeDtypeStruct((2 * TILE, 2 * HD), BF),
-        compiler_params=PARAMS,
-        cost_estimate=cost(4 * TILE * D * 256, 2 * (2 * TILE * D + D * 256)),
-        name="project_kv_pair",
-    )(own, other, weights)
+        out_specs=[WHOLE] * 2,
+        out_shape=[jax.ShapeDtypeStruct((TILE, 2 * HD), BF)] * 2,
+        compiler_params=PARAMS,
+        cost_estimate=cost(4 * TILE * D * 256, 2 * (TILE * D + 2 * D * 256)),
+        name="project_kv_far",
+    )(rows, weights, weights_other)
 
 
 def kv_kernel(other, weights, kv_own, out):
@@ -141,9 +141,10 @@
 
 
 def query_kernel(
-    place, own, other, w_query, segments_far, mask_far, mask_other, out, limits,
-    weights, segments, mask_own, sems, small_sems,
+    place, own, other, w_query, w_key, w_value, segments_far, mask_far, mask_other,
+    out, limits, weights_other, weights, segments, mask_own, sems, small_sems,
 ):
+    theirs = pl.ds(pl.multiple_of((1 - place[1]) * HD, HD), HD)
     small = [
         pltpu.make_async_copy(segments_far, segments, small_sems.at[0]),
         pltpu.make_async_copy(mask_far, mask_own, small_sems.at[1]),
@@ -156,6 +157,14 @@
         part = pl.ds(chunk * (D // Q_CHUNKS), D // Q_CHUNKS)
         copies.append(
             pltpu.make_async_copy(w_query.at[part, columns], weights.at[part], sems.at[chunk])
+        )
+    for side, source in enumerate((w_key, w_value)):
+        copies.append(
+            pltpu.make_async_copy(
+                source.at[:, theirs],
+                weights_other.at[:, pl.ds(side * HD, HD)],
+                small_sems.at[2 + side],
+            )
         )
     for copy in copies:
         copy.start()
@@ -198,26 +207,29 @@
             ]
 
 
-def project_query(place, own, other, w_query, segments, mask_own, mask_other):
+def project_query(
+    place, own, other, w_query, w_key, w_value, segments, mask_own, mask_other
+):
     return pl.pallas_call(
         query_kernel,
-        in_specs=[SCALARS, WHOLE, WHOLE, STAY, STAY, STAY, SCALARS],
-        out_specs=[WHOLE, WHOLE],
+        in_specs=[SCALARS, WHOLE, WHOLE] + [STAY] * 5 + [SCALARS],
+        out_specs=[WHOLE] * 3,
         out_shape=[
             jax.ShapeDtypeStruct((STACK, HD), BF),
             jax.ShapeDtypeStruct((4 * CHIPS, 2 * TILE), jnp.int32),
+            jax.ShapeDtypeStruct((D, 2 * HD), BF),
         ],
         scratch_shapes=[
             pltpu.VMEM((D, GF), BF),
             pltpu.VMEM((1, KEYS), jnp.int32),
             pltpu.SMEM((1, KEYS // TILE), jnp.int32),
             pltpu.SemaphoreType.DMA((Q_CHUNKS,)),
-            pltpu.SemaphoreType.DMA((2,)),
+            pltpu.SemaphoreType.DMA((4,)),
         ],
         compiler_params=PARAMS,
         cost_estimate=cost(2 * 256 * D * GF, 2 * (256 * D + D * GF + 256 * GF)),
         name="project_query",
-    )(place, own, other, w_query, segments, mask_own, mask_other)
+    )(place, own, other, w_query, w_key, w_value, segments, mask_own, mask_other)
 
 
 def stack_kernel(place, up_own, up_other, out):
@@ -239,7 +251,9 @@
     )(place, up_own, up_other)
 
 
-def scores_kernel(d, kv, limits, query, up, powers, grads, stats, keys_t):
+def scores_kernel(d, limits, query, up, *refs):
+    powers, grads, stats, keys_t = refs[-4:]
+    kv = jnp.concatenate([ref[...] for ref in refs[:-4]], axis=0)
     keys, values = kv[:, :HD], kv[:, HD:]
     keys_t[...] = keys.T
     position = lax.broadcasted_iota(jnp.int32, (TILE, 2 * TILE), 0)
@@ -262,10 +276,10 @@
         stats[2:3, part] = jnp.sum(power * grad, axis=0, keepdims=True)
 
 
-def chip_scores(d, kv, limits, query, up):
+def chip_scores(d, limits, query, up, *kv):
     return pl.pallas_call(
         functools.partial(scores_kernel, d),
-        in_specs=[WHOLE] * 4,
+        in_specs=[WHOLE] * (3 + len(kv)),
         out_specs=[WHOLE] * 4,
         out_shape=[
             jax.ShapeDtypeStruct((256, STACK), F32),
@@ -276,7 +290,7 @@
         compiler_params=PARAMS,
         cost_estimate=cost(4 * STACK * 256 * HD, 10 * 256 * STACK, 256 * STACK),
         name=f"chip_scores_{d}",
-    )(kv, limits, query, up)
+    )(limits, query, up, *kv)
 
 
 def factors_kernel(a, b, c, d, out):
@@ -534,21 +548,24 @@
     kv = project_kv(other, weights, kv_own)
     kv2 = lax.ppermute(kv, "ctx", chip_shift(2))
     far = {d: lax.ppermute(own, "ctx", chip_shift(d)) for d in (1, 3)}
-    query, limits = project_query(
-        place, own, other, w_query, in_hbm(segments), in_hbm(tile_mask[0]), mask_other
+    query, limits, weights_other = project_query(
+        place, own, other, w_query, w_key, w_value,
+        in_hbm(segments), in_hbm(tile_mask[0]), mask_other,
     )
     up = stack_up(place, up, up_other)
-    scores = {0: chip_scores(0, kv, limits, query, up)}
-    far, kv2, scores[0] = lax.optimization_barrier((far, kv2, scores[0]))
-    far_other = {d: lax.ppermute(far[d], "ctx", CORE) for d in (1, 3)}
+    scores = {0: chip_scores(0, limits, query, up, kv)}
+    far, scores[0] = lax.optimization_barrier((far, scores[0]))
+    kv_far = {d: project_kv_far(far[d], weights, weights_other) for d in (1, 3)}
+    for d in (1, 3):
+        mine, theirs = kv_far[d]
+        kv_far[d] = (mine, lax.ppermute(theirs, "ctx", CORE))
     late = (
         lax.ppermute(far[1][: TILE // 2], "ctx", chip_shift(1)),
         lax.ppermute(far[3][TILE // 2 :], "ctx", chip_shift(3)),
     )
-    scores[2] = chip_scores(2, kv2, limits, query, up)
     for d in (1, 3):
-        kv_far = project_kv_pair(far[d], far_other[d], weights)
-        scores[d] = chip_scores(d, kv_far, limits, query, up)
+        scores[d] = chip_scores(d, limits, query, up, *kv_far[d])
+    scores[2] = chip_scores(2, limits, query, up, kv2)
     factors = softmax_factors([scores[d][2] for d in range(CHIPS)])
     terms, grad_scores = {}, {}
     for d in (2, 1, 3):

time: 83.1 us -> 82.1 us (0.988)
  waiting for transfers between devices: 20.1 us -> 18.2 us
    ppermute x1, waiting for transfers between devices: 1.59 us -> 0.01 us  [shards(): kv2 = lax.ppermute(kv, 'ctx', chip_shift(2))]
    ppermute x1, starting transfers between devices: 2.1 us -> 3.64 us  [shards(): lax.ppermute(far[3][TILE // 2:], 'ctx', chip_shift(3))]
    ppermute x1, starting transfers between devices: 1.22 us -> 0.08 us  [shards(): lax.ppermute(far[1][:TILE // 2], 'ctx', chip_shift(1))]
where the time goes in v9:
time: 82.1 us; the launch traced here: 81.6 us
  starting transfers between devices  23 us (28%)
  Pallas kernels  21.9 us (27%)
  waiting for transfers between devices  18.2 us (22%)
  blocking collectives  17.5 us (21%)
  between operations  0.9 us (1%)
    all_to_all x1, blocking collectives, shards(): lax.all_to_all(y_sum, 'dp', 0, 0, tiled=True, axis_index_groups=Z_GROUPS)  17.5 us
    ppermute x3, waiting for transfers between devices, shards(): lax.ppermute(packed[d], 'ctx', chip_shift(d))  7.16 us
    pallas_call x1, Pallas kernels, input_grad(): pl.pallas_call(input_kernel, in_specs=[SCALARS] + [WHOLE] * 4 + [STAY] *...  5.36 us
    ppermute x3, starting transfers between devices, shards(): lax.ppermute(terms[d], 'dp', y_shift(d))  5.01 us
    ppermute x3, waiting for transfers between devices, shards(): lax.ppermute(terms[d], 'ctx', chip_shift(CHIPS - d))  4.97 us
    ppermute x3, starting transfers between devices, shards(): lax.ppermute(terms[d], 'ctx', chip_shift(CHIPS - d))  3.83 us
    ppermute x1, starting transfers between devices, shards(): lax.ppermute(far[3][TILE // 2:], 'ctx', chip_shift(3))  3.64 us
    ppermute x3, starting transfers between devices, shards(): lax.ppermute(packed[d], 'ctx', chip_shift(d))  3.25 us
  transfers between devices with their start and end apart: 22, of which 11 were waited for; matrix products, arithmetic and copies ran while one was open for 0% of the time, Pallas kernels for 23%

profile of v9, /device:TPU:8, one launch (start us, length us, event | category | flops | bytes accessed | tf_op | source)
XLA Modules:
  0.0 81.6 jit_solution(17811287411190904036)
XLA Ops:
  0.6 0.1 collective-permute-start.2
  0.7 0.5 collective-permute-start.4
  1.2 1.5 %collective-permute-start = (bf16[128,1536]{1,0:T(8,128)(2,1)}, bf16[128,1536]{1,0:T(8,128)(2,1)S(1)}, u32[]{:S(2)}, u32[]{:S(2)}) collective-permute-start(bf16[128,1536]{1,0:T(8,128)(2,1)} %bitcast.11), channel_id=1, source_target_pairs={{0,64},{32,96},{64,128},{96,160},{128,192},{160,224},{192,0},{224,... | collective-permute-start | bytes 1179656 | tf_op jit(solution)/shard_map/ppermute | solution.py:550
  2.7 1.7 %collective-permute-start.1 = (bf16[128,1536]{1,0:T(8,128)(2,1)}, bf16[128,1536]{1,0:T(8,128)(2,1)S(1)}, u32[]{:S(2)}, u32[]{:S(2)}) collective-permute-start(bf16[128,1536]{1,0:T(8,128)(2,1)} %bitcast.12), channel_id=1, source_target_pairs={{0,192},{32,224},{64,0},{96,32},{128,64},{160,96},{192,128},{224,1... | collective-permute-start | bytes 1179656 | tf_op jit(solution)/shard_map/ppermute | solution.py:550
  4.5 0.0 collective-permute-start.3
  4.5 0.1 pad_add_fusion.place
  4.5 2.1 %project_kv_own.1 = (bf16[1536,256]{1,0:T(8,128)(2,1)S(1)}, bf16[128,256]{1,0:T(8,128)(2,1)S(1)}) custom-call(s32[4]{0:T(128)S(1)} %pad_add_fusion.place, bf16[128,1536]{1,0:T(8,128)(2,1)} %bitcast.13, bf16[1536,256]{1,0:T(8,128)(2,1)} %w_key.5, bf16[1536,256]{1,0:T(8,128)(2,1)} %w_value.5), custom_call_target="tpu_custom_call" | custom-call | flops 1 | bytes 1 | tf_op jit(solution)/shard_map/project_kv_own/pallas_call | solution.py:94
  6.6 0.0 copy-start
  6.6 0.0 collective-permute-done.3.mask_other
  6.7 0.0 collective-permute-done.2.other
  6.7 0.0 collective-permute-done.4.up_other
  6.7 0.3 project_kv.1.refs_0_
  7.0 1.9 %collective-permute-start.6 = (bf16[256,256]{1,0:T(8,128)(2,1)S(1)}, bf16[256,256]{1,0:T(8,128)(2,1)S(1)}, u32[]{:S(2)}, u32[]{:S(2)}) collective-permute-start(bf16[256,256]{1,0:T(8,128)(2,1)S(1)} %project_kv.1.refs_0_), channel_id=1, source_target_pairs={{0,128},{32,160},{64,192},{96,224},{128,0},{160,32},{192,64},{224,... | collective-permute-start | bytes 393224 | tf_op jit(solution)/shard_map/ppermute | solution.py:549
  8.9 0.6 stack_up.1.up
  9.5 3.2 %project_query.1 = (bf16[1536,128]{1,0:T(8,128)(2,1)S(1)}, s32[16,256]{1,0:T(8,128)S(1)}, bf16[1536,256]{1,0:T(8,128)(2,1)S(1)}) custom-call(s32[4]{0:T(128)S(1)} %pad_add_fusion.place, bf16[128,1536]{1,0:T(8,128)(2,1)S(1)} %bitcast.14, bf16[128,1536]{1,0:T(8,128)(2,1)S(1)} %collective-permute-done.2.other, bf16[1536,1536]{1,0:T(8,128)(2,1)} %w_query.3, ...), custom_call_target="tpu_custom_call" | custom-call | flops 1 | bytes 1 | tf_op jit(solution)/shard_map/project_query/pallas_call | solution.py:213
  12.7 0.8 chip_scores_0.1
  13.5 0.3 collective-permute-done.rows.far1
  13.8 2.2 %collective-permute-done.1.rows.far3 = bf16[128,1536]{1,0:T(8,128)(2,1)S(1)} collective-permute-done((bf16[128,1536]{1,0:T(8,128)(2,1)}, bf16[128,1536]{1,0:T(8,128)(2,1)S(1)}, u32[]{:S(2)}, u32[]{:S(2)}) %collective-permute-start.1) | collective-permute-done | bytes 393248 | tf_op jit(solution)/shard_map/ppermute | solution.py:550
  16.0 0.4 project_kv_far.3
  16.4 0.1 collective-permute-start.7
  16.5 0.4 project_kv_far.2
  16.8 0.6 collective-permute-start.5
  17.5 0.1 collective-permute-start.8
  17.6 3.6 %collective-permute-start.9 = (bf16[64,1536]{1,0:T(8,128)(2,1)S(1)}, bf16[64,1536]{1,0:T(8,128)(2,1)S(1)}, u32[]{:S(2)}, u32[]{:S(2)}) collective-permute-start(bf16[64,1536]{1,0:T(8,128)(2,1)S(1)} %slice.7), channel_id=1, source_target_pairs={{0,192},{32,224},{64,0},{96,32},{128,64},{160,96},{192,128},{224,1... | collective-permute-start | bytes 589832 | tf_op jit(solution)/shard_map/ppermute | solution.py:564
  21.2 0.0 collective-permute-done.7.refs_1_
  21.2 0.7 chip_scores_3.1
  22.0 0.8 chip_scores_1.1
  22.7 0.7 chip_scores_2.1
  23.5 0.6 chip_terms_3.1
  24.1 0.3 collective-permute-start.12
  24.4 0.6 chip_terms_1.1
  25.0 3.3 %collective-permute-start.11 = (bf16[256,256]{1,0:T(8,128)(2,1)S(1)}, bf16[256,256]{1,0:T(8,128)(2,1)S(1)}, u32[]{:S(2)}, u32[]{:S(2)}) collective-permute-start(bf16[256,256]{1,0:T(8,128)(2,1)S(1)} %get-tuple-element.101), channel_id=1, source_target_pairs={{0,192},{32,224},{64,0},{96,32},{128,64},{160,96},{192,128},{224,1... | collective-permute-start | bytes 393224 | tf_op jit(solution)/shard_map/ppermute | solution.py:573
  28.3 0.6 chip_terms_2.1
  29.0 0.3 collective-permute-start.10
  29.2 0.6 chip_terms_0.1
  29.9 0.7 query_grad.1.dq
  30.6 0.0 collective-permute-done.9.late_b
  30.6 0.2 collective-permute-done.12.d
  30.7 2.8 %collective-permute-done.11.c = bf16[256,256]{1,0:T(8,128)(2,1)S(1)} collective-permute-done((bf16[256,256]{1,0:T(8,128)(2,1)S(1)}, bf16[256,256]{1,0:T(8,128)(2,1)S(1)}, u32[]{:S(2)}, u32[]{:S(2)}) %collective-permute-start.11) | collective-permute-done | bytes 131104 | tf_op jit(solution)/shard_map/ppermute | solution.py:573
  33.6 2.0 %collective-permute-done.10.b = bf16[256,256]{1,0:T(8,128)(2,1)S(1)} collective-permute-done((bf16[256,256]{1,0:T(8,128)(2,1)S(1)}, bf16[256,256]{1,0:T(8,128)(2,1)S(1)}, u32[]{:S(2)}, u32[]{:S(2)}) %collective-permute-start.10) | collective-permute-done | bytes 131104 | tf_op jit(solution)/shard_map/ppermute | solution.py:573
  35.5 0.0 collective-permute-start.13
  35.5 0.1 sum_four.2.dkv
  35.6 0.6 collective-permute-start.14
  36.2 0.5 transpose_tokens.1.tokens_t
  36.7 0.8 collective-permute-done.14.dkv_other
  37.5 0.7 pack.1
  38.1 0.2 collective-permute-start.15
  38.3 0.1 collective-permute-start.16
  38.5 3.0 %collective-permute-start.17 = (bf16[256,256]{1,0:T(8,128)(2,1)S(1)}, bf16[256,256]{1,0:T(8,128)(2,1)S(1)}, u32[]{:S(2)}, u32[]{:S(2)}) collective-permute-start(bf16[256,256]{1,0:T(8,128)(2,1)S(1)} %get-tuple-element.128), channel_id=1, source_target_pairs={{0,128},{32,160},{64,192},{96,224},{128,0},{160,32},{192,64},{224,... | collective-permute-start | bytes 393224 | tf_op jit(solution)/shard_map/ppermute | solution.py:587
  41.5 0.1 collective-permute-start.18
  41.6 4.3 %collective-permute-done.16.b = bf16[256,256]{1,0:T(8,128)(2,1)S(1)} collective-permute-done((bf16[256,256]{1,0:T(8,128)(2,1)S(1)}, bf16[256,256]{1,0:T(8,128)(2,1)S(1)}, u32[]{:S(2)}, u32[]{:S(2)}) %collective-permute-start.16) | collective-permute-done | bytes 131104 | tf_op jit(solution)/shard_map/ppermute | solution.py:587
  45.9 2.2 %collective-permute-done.17.c = bf16[256,256]{1,0:T(8,128)(2,1)S(1)} collective-permute-done((bf16[256,256]{1,0:T(8,128)(2,1)S(1)}, bf16[256,256]{1,0:T(8,128)(2,1)S(1)}, u32[]{:S(2)}, u32[]{:S(2)}) %collective-permute-start.17) | collective-permute-done | bytes 131104 | tf_op jit(solution)/shard_map/ppermute | solution.py:587
  48.1 0.6 collective-permute-done.18.d
  48.8 0.0 collective-permute-done.15.other_t
  48.8 1.5 %weight_grad.1 = (f32[384,256]{1,0:T(8,128)S(1)}, bf16[384,256]{1,0:T(8,128)(2,1)S(1)}, bf16[384,256]{1,0:T(8,128)(2,1)S(1)}, bf16[384,256]{1,0:T(8,128)(2,1)S(1)}) custom-call(s32[4]{0:T(128)S(1)} %pad_add_fusion.place, bf16[1536,512]{1,0:T(8,128)(2,1)S(1)} %transpose_tokens.1.tokens_t, bf16[1536,512]{1,0:T(8,128)(2,1)S(1)} %collective-permute-done.15.other_t, ...), custom_call_target="tpu_custom_call" | custom-call | flops 1 | bytes 1 | tf_op jit(solution)/shard_map/weight_grad/pallas_call | solution.py:448
  50.3 1.7 %collective-permute-start.19 = (bf16[384,256]{1,0:T(8,128)(2,1)S(1)}, bf16[384,256]{1,0:T(8,128)(2,1)S(1)}, u32[]{:S(2)}, u32[]{:S(2)}) collective-permute-start(bf16[384,256]{1,0:T(8,128)(2,1)S(1)} %get-tuple-element.131), channel_id=1, source_target_pairs={{0,8},{1,9},{2,10},{3,11},{4,12},{5,13},{6,14},{7,15},{8,16},{9,17... | collective-permute-start | bytes 589832 | tf_op jit(solution)/shard_map/ppermute | solution.py:590
  51.9 2.9 %collective-permute-start.20 = (bf16[384,256]{1,0:T(8,128)(2,1)S(1)}, bf16[384,256]{1,0:T(8,128)(2,1)S(1)}, u32[]{:S(2)}, u32[]{:S(2)}) collective-permute-start(bf16[384,256]{1,0:T(8,128)(2,1)S(1)} %get-tuple-element.132), channel_id=1, source_target_pairs={{0,16},{1,17},{2,18},{3,19},{4,20},{5,21},{6,22},{7,23},{8,24},{9,... | collective-permute-start | bytes 589832 | tf_op jit(solution)/shard_map/ppermute | solution.py:590
  54.8 0.5 collective-permute-start.21
  55.3 5.4 %input_grad.1 = bf16[128,1536]{1,0:T(8,128)(2,1)} custom-call(s32[4]{0:T(128)S(1)} %pad_add_fusion.place, bf16[256,768]{1,0:T(8,128)(2,1)S(1)} %query_grad.1.dq, bf16[256,768]{1,0:T(8,128)(2,1)S(1)} %collective-permute-done.13.dq_other, bf16[256,256]{1,0:T(8,128)(2,1)S(1)} %sum_four.2.dkv, bf16[256,256]{1,0:T(8,128)(2,1)S(1)} %collective-permute-done.14.dkv_other, ...), custom_call_target="tpu_custom_call" | custom-call | flops 1 | bytes 1 | tf_op jit(solution)/shard_map/input_grad/pallas_call | solution.py:501
  60.7 0.6 collective-permute-done.20.c
  61.3 2.1 %collective-permute-done.21.d = bf16[384,256]{1,0:T(8,128)(2,1)S(1)} collective-permute-done((bf16[384,256]{1,0:T(8,128)(2,1)S(1)}, bf16[384,256]{1,0:T(8,128)(2,1)S(1)}, u32[]{:S(2)}, u32[]{:S(2)}) %collective-permute-start.21) | collective-permute-done | bytes 196640 | tf_op jit(solution)/shard_map/ppermute | solution.py:590
  63.4 0.1 sum_four.3
  63.5 17.5 %all_to_all.11 = bf16[8,48,256]{2,1,0:T(8,128)(2,1)S(1)} all-to-all(bf16[8,48,256]{2,1,0:T(8,128)(2,1)S(1)} %bitcast.16), channel_id=1, replica_groups={{0,1,2,3,4,5,6,7},{8,9,10,11,12,13,14,15},{16,17,18,19,20,21,22,23},{24..., dimensions={0} | all-to-all | bytes 393216 | tf_op jit(solution)/shard_map/all_to_all | solution.py:596
  81.0 0.6 final_sum.1
  (11 shorter events, 0.1 us)
Async XLA Ops:
  0.6 6.0 %collective-permute-start.2 = (bf16[128,1536]{1,0:T(8,128)(2,1)}, bf16[128,1536]{1,0:T(8,128)(2,1)S(1)}, u32[]{:S(2)}, u32[]{:S(2)}) collective-permute-start(bf16[128,1536]{1,0:T(8,128)(2,1)} %bitcast.10), channel_id=1, source_target_pairs={{0,32},{32,0},{64,96},{96,64},{128,160},{160,128},{192,224},{224,1... | collective-permute-start | bytes 1179656 | tf_op jit(solution)/shard_map/ppermute | solution.py:541
  0.7 5.9 %collective-permute-start.4 = (bf16[128,1536]{1,0:T(8,128)(2,1)}, bf16[128,1536]{1,0:T(8,128)(2,1)S(1)}, u32[]{:S(2)}, u32[]{:S(2)}) collective-permute-start(bf16[128,1536]{1,0:T(8,128)(2,1)} %bitcast.18), channel_id=1, source_target_pairs={{0,32},{32,0},{64,96},{96,64},{128,160},{160,128},{192,224},{224,1... | collective-permute-start | bytes 1179656 | tf_op jit(solution)/shard_map/ppermute | solution.py:542
  1.2 12.5 %collective-permute-start = (bf16[128,1536]{1,0:T(8,128)(2,1)}, bf16[128,1536]{1,0:T(8,128)(2,1)S(1)}, u32[]{:S(2)}, u32[]{:S(2)}) collective-permute-start(bf16[128,1536]{1,0:T(8,128)(2,1)} %bitcast.11), channel_id=1, source_target_pairs={{0,64},{32,96},{64,128},{96,160},{128,192},{160,224},{192,0},{224,... | collective-permute-start | bytes 1179656 | tf_op jit(solution)/shard_map/ppermute | solution.py:550
  2.7 13.3 %collective-permute-start.1 = (bf16[128,1536]{1,0:T(8,128)(2,1)}, bf16[128,1536]{1,0:T(8,128)(2,1)S(1)}, u32[]{:S(2)}, u32[]{:S(2)}) collective-permute-start(bf16[128,1536]{1,0:T(8,128)(2,1)} %bitcast.12), channel_id=1, source_target_pairs={{0,192},{32,224},{64,0},{96,32},{128,64},{160,96},{192,128},{224,1... | collective-permute-start | bytes 1179656 | tf_op jit(solution)/shard_map/ppermute | solution.py:550
  4.5 2.2 %collective-permute-start.3 = (s32[1,8]{1,0:T(1,128)}, s32[1,8]{1,0:T(1,128)S(1)}, u32[]{:S(2)}, u32[]{:S(2)}) collective-permute-start(s32[1,8]{1,0:T(1,128)} %bitcast.21), channel_id=1, source_target_pairs={{0,32},{32,0},{64,96},{96,64},{128,160},{160,128},{192,224},{224,1... | collective-permute-start | bytes 104 | tf_op jit(solution)/shard_map/ppermute | solution.py:543
  4.5 4.3 %copy-start.1 = (bf16[1,128,1536]{2,1,0:T(8,128)(2,1)S(1)}, bf16[1,128,1536]{2,1,0:T(8,128)(2,1)}, u32[]{:S(2)}) copy-start(bf16[1,128,1536]{2,1,0:T(8,128)(2,1)} %param.8) | copy-start | bytes 1179652
  6.6 2.9 %copy-start = (bf16[1,128,1536]{2,1,0:T(8,128)(2,1)S(1)}, bf16[1,128,1536]{2,1,0:T(8,128)(2,1)}, u32[]{:S(2)}) copy-start(bf16[1,128,1536]{2,1,0:T(8,128)(2,1)} %param.7) | copy-start | bytes 1179652
  7.0 15.8 %collective-permute-start.6 = (bf16[256,256]{1,0:T(8,128)(2,1)S(1)}, bf16[256,256]{1,0:T(8,128)(2,1)S(1)}, u32[]{:S(2)}, u32[]{:S(2)}) collective-permute-start(bf16[256,256]{1,0:T(8,128)(2,1)S(1)} %project_kv.1.refs_0_), channel_id=1, source_target_pairs={{0,128},{32,160},{64,192},{96,224},{128,0},{160,32},{192,64},{224,... | collective-permute-start | bytes 393224 | tf_op jit(solution)/shard_map/ppermute | solution.py:549
  16.4 4.8 %collective-permute-start.7 = (bf16[128,256]{1,0:T(8,128)(2,1)S(1)}, bf16[128,256]{1,0:T(8,128)(2,1)S(1)}, u32[]{:S(2)}, u32[]{:S(2)}) collective-permute-start(bf16[128,256]{1,0:T(8,128)(2,1)S(1)} %get-tuple-element.93), channel_id=1, source_target_pairs={{0,32},{32,0},{64,96},{96,64},{128,160},{160,128},{192,224},{224,1... | collective-permute-start | bytes 196616 | tf_op jit(solution)/shard_map/ppermute | solution.py:561
  16.8 5.1 %collective-permute-start.5 = (bf16[128,256]{1,0:T(8,128)(2,1)S(1)}, bf16[128,256]{1,0:T(8,128)(2,1)S(1)}, u32[]{:S(2)}, u32[]{:S(2)}) collective-permute-start(bf16[128,256]{1,0:T(8,128)(2,1)S(1)} %get-tuple-element.89), channel_id=1, source_target_pairs={{0,32},{32,0},{64,96},{96,64},{128,160},{160,128},{192,224},{224,1... | collective-permute-start | bytes 196616 | tf_op jit(solution)/shard_map/ppermute | solution.py:561
  17.5 13.1 %collective-permute-start.8 = (bf16[64,1536]{1,0:T(8,128)(2,1)S(1)}, bf16[64,1536]{1,0:T(8,128)(2,1)S(1)}, u32[]{:S(2)}, u32[]{:S(2)}) collective-permute-start(bf16[64,1536]{1,0:T(8,128)(2,1)S(1)} %slice.6), channel_id=1, source_target_pairs={{0,64},{32,96},{64,128},{96,160},{128,192},{160,224},{192,0},{224,... | collective-permute-start | bytes 589832 | tf_op jit(solution)/shard_map/ppermute | solution.py:563
  17.6 13.0 %collective-permute-start.9 = (bf16[64,1536]{1,0:T(8,128)(2,1)S(1)}, bf16[64,1536]{1,0:T(8,128)(2,1)S(1)}, u32[]{:S(2)}, u32[]{:S(2)}) collective-permute-start(bf16[64,1536]{1,0:T(8,128)(2,1)S(1)} %slice.7), channel_id=1, source_target_pairs={{0,192},{32,224},{64,0},{96,32},{128,64},{160,96},{192,128},{224,1... | collective-permute-start | bytes 589832 | tf_op jit(solution)/shard_map/ppermute | solution.py:564
  24.1 6.6 %collective-permute-start.12 = (bf16[256,256]{1,0:T(8,128)(2,1)S(1)}, bf16[256,256]{1,0:T(8,128)(2,1)S(1)}, u32[]{:S(2)}, u32[]{:S(2)}) collective-permute-start(bf16[256,256]{1,0:T(8,128)(2,1)S(1)} %get-tuple-element.104), channel_id=1, source_target_pairs={{0,64},{32,96},{64,128},{96,160},{128,192},{160,224},{192,0},{224,... | collective-permute-start | bytes 393224 | tf_op jit(solution)/shard_map/ppermute | solution.py:573
  25.0 8.5 %collective-permute-start.11 = (bf16[256,256]{1,0:T(8,128)(2,1)S(1)}, bf16[256,256]{1,0:T(8,128)(2,1)S(1)}, u32[]{:S(2)}, u32[]{:S(2)}) collective-permute-start(bf16[256,256]{1,0:T(8,128)(2,1)S(1)} %get-tuple-element.101), channel_id=1, source_target_pairs={{0,192},{32,224},{64,0},{96,32},{128,64},{160,96},{192,128},{224,1... | collective-permute-start | bytes 393224 | tf_op jit(solution)/shard_map/ppermute | solution.py:573
  29.0 6.6 %collective-permute-start.10 = (bf16[256,256]{1,0:T(8,128)(2,1)S(1)}, bf16[256,256]{1,0:T(8,128)(2,1)S(1)}, u32[]{:S(2)}, u32[]{:S(2)}) collective-permute-start(bf16[256,256]{1,0:T(8,128)(2,1)S(1)} %get-tuple-element.98), channel_id=1, source_target_pairs={{0,128},{32,160},{64,192},{96,224},{128,0},{160,32},{192,64},{224,... | collective-permute-start | bytes 393224 | tf_op jit(solution)/shard_map/ppermute | solution.py:573
  35.5 1.9 %collective-permute-start.13 = (bf16[256,768]{1,0:T(8,128)(2,1)S(1)}, bf16[256,768]{1,0:T(8,128)(2,1)S(1)}, u32[]{:S(2)}, u32[]{:S(2)}) collective-permute-start(bf16[256,768]{1,0:T(8,128)(2,1)S(1)} %query_grad.1.dq), channel_id=1, source_target_pairs={{0,32},{32,0},{64,96},{96,64},{128,160},{160,128},{192,224},{224,1... | collective-permute-start | bytes 1179656 | tf_op jit(solution)/shard_map/ppermute | solution.py:577
  35.6 1.8 %collective-permute-start.14 = (bf16[256,256]{1,0:T(8,128)(2,1)S(1)}, bf16[256,256]{1,0:T(8,128)(2,1)S(1)}, u32[]{:S(2)}, u32[]{:S(2)}) collective-permute-start(bf16[256,256]{1,0:T(8,128)(2,1)S(1)} %sum_four.2.dkv), channel_id=1, source_target_pairs={{0,32},{32,0},{64,96},{96,64},{128,160},{160,128},{192,224},{224,1... | collective-permute-start | bytes 393224 | tf_op jit(solution)/shard_map/ppermute | solution.py:579
  38.1 10.6 %collective-permute-start.15 = (bf16[1536,512]{1,0:T(8,128)(2,1)S(1)}, bf16[1536,512]{1,0:T(8,128)(2,1)S(1)}, u32[]{:S(2)}, u32[]{:S(2)}) collective-permute-start(bf16[1536,512]{1,0:T(8,128)(2,1)S(1)} %transpose_tokens.1.tokens_t), channel_id=1, source_target_pairs={{0,32},{32,0},{64,96},{96,64},{128,160},{160,128},{192,224},{224,1... | collective-permute-start | bytes 4718600 | tf_op jit(solution)/shard_map/ppermute | solution.py:585
  38.3 7.6 %collective-permute-start.16 = (bf16[256,256]{1,0:T(8,128)(2,1)S(1)}, bf16[256,256]{1,0:T(8,128)(2,1)S(1)}, u32[]{:S(2)}, u32[]{:S(2)}) collective-permute-start(bf16[256,256]{1,0:T(8,128)(2,1)S(1)} %get-tuple-element.127), channel_id=1, source_target_pairs={{0,64},{32,96},{64,128},{96,160},{128,192},{160,224},{192,0},{224,... | collective-permute-start | bytes 393224 | tf_op jit(solution)/shard_map/ppermute | solution.py:587
  38.5 9.7 %collective-permute-start.17 = (bf16[256,256]{1,0:T(8,128)(2,1)S(1)}, bf16[256,256]{1,0:T(8,128)(2,1)S(1)}, u32[]{:S(2)}, u32[]{:S(2)}) collective-permute-start(bf16[256,256]{1,0:T(8,128)(2,1)S(1)} %get-tuple-element.128), channel_id=1, source_target_pairs={{0,128},{32,160},{64,192},{96,224},{128,0},{160,32},{192,64},{224,... | collective-permute-start | bytes 393224 | tf_op jit(solution)/shard_map/ppermute | solution.py:587
  41.5 7.2 %collective-permute-start.18 = (bf16[256,256]{1,0:T(8,128)(2,1)S(1)}, bf16[256,256]{1,0:T(8,128)(2,1)S(1)}, u32[]{:S(2)}, u32[]{:S(2)}) collective-permute-start(bf16[256,256]{1,0:T(8,128)(2,1)S(1)} %get-tuple-element.129), channel_id=1, source_target_pairs={{0,192},{32,224},{64,0},{96,32},{128,64},{160,96},{192,128},{224,1... | collective-permute-start | bytes 393224 | tf_op jit(solution)/shard_map/ppermute | solution.py:587
  50.3 10.4 %collective-permute-start.19 = (bf16[384,256]{1,0:T(8,128)(2,1)S(1)}, bf16[384,256]{1,0:T(8,128)(2,1)S(1)}, u32[]{:S(2)}, u32[]{:S(2)}) collective-permute-start(bf16[384,256]{1,0:T(8,128)(2,1)S(1)} %get-tuple-element.131), channel_id=1, source_target_pairs={{0,8},{1,9},{2,10},{3,11},{4,12},{5,13},{6,14},{7,15},{8,16},{9,17... | collective-permute-start | bytes 589832 | tf_op jit(solution)/shard_map/ppermute | solution.py:590
  51.9 9.3 %collective-permute-start.20 = (bf16[384,256]{1,0:T(8,128)(2,1)S(1)}, bf16[384,256]{1,0:T(8,128)(2,1)S(1)}, u32[]{:S(2)}, u32[]{:S(2)}) collective-permute-start(bf16[384,256]{1,0:T(8,128)(2,1)S(1)} %get-tuple-element.132), channel_id=1, source_target_pairs={{0,16},{1,17},{2,18},{3,19},{4,20},{5,21},{6,22},{7,23},{8,24},{9,... | collective-permute-start | bytes 589832 | tf_op jit(solution)/shard_map/ppermute | solution.py:590
  54.8 8.6 %collective-permute-start.21 = (bf16[384,256]{1,0:T(8,128)(2,1)S(1)}, bf16[384,256]{1,0:T(8,128)(2,1)S(1)}, u32[]{:S(2)}, u32[]{:S(2)}) collective-permute-start(bf16[384,256]{1,0:T(8,128)(2,1)S(1)} %get-tuple-element.133), channel_id=1, source_target_pairs={{0,24},{1,25},{2,26},{3,27},{4,28},{5,29},{6,30},{7,31},{8,0},{9,1... | collective-permute-start | bytes 589832 | tf_op jit(solution)/shard_map/ppermute | solution.py:590

commit v10 on v9

--- a/solution.py
+++ b/solution.py
@@ -342,20 +342,29 @@
     )(powers, grads, factors, query, up)
 
 
-def query_grad_kernel(k0, k1, k2, k3, g0, g1, g2, g3, out):
+def query_grad_kernel(k0, k1, k2, k3, g0, g1, g2, g3, out, middle, theirs):
     for head in range(GROUP):
         part = slice(head * 256, (head + 1) * 256)
         total = dot(k0[...], g0[:, part]) + dot(k1[...], g1[:, part])
         total += dot(k2[...], g2[:, part]) + dot(k3[...], g3[:, part])
-        out[:, head * HD : (head + 1) * HD] = (total * SCALE).T.astype(BF)
+        columns = slice(head * HD, (head + 1) * HD)
+        result = (total * SCALE).T.astype(BF)
+        out[:, columns] = result
+        theirs[:, columns] = result[TILE:]
+        if 2 <= head < 4:
+            middle[:, (head - 2) * HD : (head - 1) * HD] = result
 
 
 def query_grad(keys_t, grad_scores):
     return pl.pallas_call(
         query_grad_kernel,
         in_specs=[WHOLE] * 8,
-        out_specs=WHOLE,
-        out_shape=jax.ShapeDtypeStruct((256, GF), BF),
+        out_specs=[WHOLE] * 3,
+        out_shape=[
+            jax.ShapeDtypeStruct((256, GF), BF),
+            jax.ShapeDtypeStruct((256, 256), BF),
+            jax.ShapeDtypeStruct((TILE, GF), BF),
+        ],
         compiler_params=PARAMS,
         cost_estimate=cost(2 * STACK * KEYS * HD, 2 * STACK * KEYS),
         name="query_grad",
@@ -379,7 +388,7 @@
     )(a, b, c, d)
 
 
-def pack_kernel(place, dq, dq_other, dkv, dkv_other, *outs):
+def pack_kernel(place, dq, middle_other, dkv, dkv_other, *outs):
     for core in range(2):
         own_part = slice(core * HD, (core + 1) * HD)
         for chip in range(CHIPS):
@@ -394,14 +403,14 @@
                         out[:TILE, theirs] = dkv_other[TILE:, own_part]
                         out[TILE:, theirs] = dkv_other[:TILE, own_part]
                     elif target == 2 - 2 * core:
-                        out[:TILE] = dq_other[TILE:, 256:512]
-                        out[TILE:] = dq_other[:TILE, 256:512]
+                        out[:TILE] = middle_other[TILE:]
+                        out[TILE:] = middle_other[:TILE]
                     else:
                         first = target == core
                         out[...] = dq[:, 0:256] if first else dq[:, 512:768]
 
 
-def pack(place, dq, dq_other, dkv, dkv_other):
+def pack(place, dq, middle_other, dkv, dkv_other):
     return pl.pallas_call(
         pack_kernel,
         in_specs=[SCALARS] + [WHOLE] * 4,
@@ -410,19 +419,18 @@
         compiler_params=PARAMS,
         cost_estimate=cost(0, 4 << 19),
         name="pack",
-    )(place, dq, dq_other, dkv, dkv_other)
-
-
-def transpose_kernel(own, far1, late_a, late_b, far3, out):
-    late = jnp.concatenate([late_a[...], late_b[...]], axis=0)
-    for i, rows in enumerate((own[...], far1[...], late, far3[...])):
-        out[:, i * TILE : (i + 1) * TILE] = rows.T
+    )(place, dq, middle_other, dkv, dkv_other)
+
+
+def transpose_kernel(own, far2, far1, far3, out):
+    for i, rows in enumerate((own, far2, far1, far3)):
+        out[:, i * TILE : (i + 1) * TILE] = rows[...].T
 
 
 def transpose(parts):
     return pl.pallas_call(
         transpose_kernel,
-        in_specs=[WHOLE] * 5,
+        in_specs=[WHOLE] * 4,
         out_specs=WHOLE,
         out_shape=jax.ShapeDtypeStruct((D, KEYS // 2), BF),
         compiler_params=PARAMS,
@@ -431,28 +439,25 @@
     )(*parts)
 
 
-def weight_kernel(place, tokens_t, other_t, a, b, c, d, out0, out1, out2, out3):
+def weight_kernel(shift, place, tokens_t, other_t, a, b, c, d, out):
     parts = (a, b, c, d)
     right = jnp.concatenate([part[:TILE] for part in parts], axis=0)
     right_other = jnp.concatenate([part[TILE:] for part in parts], axis=0)
-    for shift, out in enumerate((out0, out1, out2, out3)):
-        row = pl.multiple_of(lax.rem(place[2] + shift, YS) * (D // YS), 128)
-        rows = pl.ds(row, D // YS)
-        out[...] = (dot(tokens_t[rows], right) + dot(other_t[rows], right_other)).astype(
-            out.dtype
-        )
-
-
-def weight_grad(place, tokens_t, other_t, parts):
-    shape = (D // YS, 256)
-    return pl.pallas_call(
-        weight_kernel,
+    row = pl.multiple_of(lax.rem(place[2] + shift, YS) * (D // YS), 128)
+    rows = pl.ds(row, D // YS)
+    total = dot(tokens_t[rows], right) + dot(other_t[rows], right_other)
+    out[...] = total.astype(out.dtype)
+
+
+def weight_grad(shift, place, tokens_t, other_t, parts):
+    return pl.pallas_call(
+        functools.partial(weight_kernel, shift),
         in_specs=[SCALARS] + [WHOLE] * 6,
-        out_specs=[WHOLE] * 4,
-        out_shape=[jax.ShapeDtypeStruct(shape, F32)] + [jax.ShapeDtypeStruct(shape, BF)] * 3,
-        compiler_params=PARAMS,
-        cost_estimate=cost(2 * D * KEYS * 256, 2 * D * KEYS + 3 * D * 256),
-        name="weight_grad",
+        out_specs=WHOLE,
+        out_shape=jax.ShapeDtypeStruct((D // YS, 256), F32 if shift == 0 else BF),
+        compiler_params=PARAMS,
+        cost_estimate=cost(2 * D * KEYS * 256 // YS, 2 * D * KEYS // YS),
+        name=f"weight_grad_{shift}",
     )(place, tokens_t, other_t, *parts)
 
 
@@ -482,7 +487,7 @@
     mine = pl.ds(pl.multiple_of(core * GF, 128), GF)
     theirs = pl.ds(pl.multiple_of((1 - core) * GF, 128), GF)
     left[:, mine] = dq[:TILE]
-    left[:, theirs] = dq_other[TILE:]
+    left[:, theirs] = dq_other[...]
     for part in range(2):
         columns = slice(part * HD, (part + 1) * HD)
         base = D + part * KVH * HD
@@ -554,40 +559,39 @@
     )
     up = stack_up(place, up, up_other)
     scores = {0: chip_scores(0, limits, query, up, kv)}
-    far, scores[0] = lax.optimization_barrier((far, scores[0]))
+    far, kv2, scores[0] = lax.optimization_barrier((far, kv2, scores[0]))
+    late = lax.ppermute(far[1], "ctx", chip_shift(1))
     kv_far = {d: project_kv_far(far[d], weights, weights_other) for d in (1, 3)}
     for d in (1, 3):
         mine, theirs = kv_far[d]
         kv_far[d] = (mine, lax.ppermute(theirs, "ctx", CORE))
-    late = (
-        lax.ppermute(far[1][: TILE // 2], "ctx", chip_shift(1)),
-        lax.ppermute(far[3][TILE // 2 :], "ctx", chip_shift(3)),
-    )
     for d in (1, 3):
         scores[d] = chip_scores(d, limits, query, up, *kv_far[d])
     scores[2] = chip_scores(2, limits, query, up, kv2)
     factors = softmax_factors([scores[d][2] for d in range(CHIPS)])
     terms, grad_scores = {}, {}
-    for d in (2, 1, 3):
+    for d in (3, 1, 2):
         terms[d], grad_scores[d] = chip_terms(d, *scores[d][:2], factors, query, up)
-    back = [lax.ppermute(terms[d], "ctx", chip_shift(CHIPS - d)) for d in (2, 1, 3)]
+    back = [lax.ppermute(terms[d], "ctx", chip_shift(CHIPS - d)) for d in (1, 3, 2)]
     terms[0], grad_scores[0] = chip_terms(0, *scores[0][:2], factors, query, up)
-    dq = query_grad([scores[d][3] for d in range(CHIPS)], [grad_scores[d] for d in range(CHIPS)])
-    late, back, dq = lax.optimization_barrier((late, back, dq))
-    dq_other = lax.ppermute(dq, "ctx", CORE)
+    dq, middle, theirs = query_grad(
+        [scores[d][3] for d in range(CHIPS)], [grad_scores[d] for d in range(CHIPS)]
+    )
+    late, back, middle = lax.optimization_barrier((late, back, middle))
+    middle_other = lax.ppermute(middle, "ctx", CORE)
     dkv = sum_four(terms[0], *back)
     dkv_other = lax.ppermute(dkv, "ctx", CORE)
-    packed = pack(place, dq, dq_other, dkv, dkv_other)
+    packed = pack(place, dq, middle_other, dkv, dkv_other)
 
     far, dkv = lax.optimization_barrier((far, dkv))
-    tokens_t = transpose([own, far[1], *late, far[3]])
-    tokens_t, packed = lax.optimization_barrier((tokens_t, packed))
+    tokens_t = transpose([own, late, far[1], far[3]])
+    tokens_t, packed, theirs = lax.optimization_barrier((tokens_t, packed, theirs))
+    dq_other = lax.ppermute(theirs, "ctx", CORE)
     other_t = lax.ppermute(tokens_t, "ctx", CORE)
-    columns = [packed[0]] + [
-        lax.ppermute(packed[d], "ctx", chip_shift(d)) for d in (1, 2, 3)
-    ]
-    terms = weight_grad(place, tokens_t, other_t, columns)
-    y_parts = [terms[0]] + [lax.ppermute(terms[d], "dp", y_shift(d)) for d in (1, 2, 3)]
+    columns = {d: lax.ppermute(packed[d], "ctx", chip_shift(d)) for d in (2, 1, 3)}
+    columns = [packed[0]] + [columns[d] for d in (2, 1, 3)]
+    terms = [weight_grad(d, place, tokens_t, other_t, columns) for d in range(YS)]
+    y_parts = [terms[0]] + [lax.ppermute(terms[d], "dp", y_shift(d)) for d in (1, 3, 2)]
     grad_tokens = input_grad(
         place, dq, dq_other, dkv, dkv_other, w_query, w_key, w_value
     )

time: 82.1 us -> 80.7 us (0.983)
  waiting for transfers between devices: 18.2 us -> 13.7 us
  Pallas kernels: 21.9 us -> 23.9 us
  blocking collectives: 17.5 us -> 18.8 us
    ppermute x3, waiting for transfers between devices: 2.75 us -> 0.04 us  [shards(): lax.ppermute(terms[d], 'dp', y_shift(d))]
    ppermute x3, starting transfers between devices: 3.83 us -> 5.96 us  [shards(): lax.ppermute(terms[d], 'ctx', chip_shift(CHIPS - d))]
    pallas_call x3 -> x6, Pallas kernels: 2.62 us -> 4.74 us  [the longest x4 3.63 us: weight_grad(): pl.pallas_call(functools.partial(weight_kernel, shift), in_specs=[SCALARS...]
    ppermute x3, starting transfers between devices: 3.72 us -> 1.64 us  [the longest x1 1.14 us: shards(): late = lax.ppermute(far[1], 'ctx', chip_shift(1))]
    ppermute x3, waiting for transfers between devices: 4.97 us -> 3.12 us  [shards(): lax.ppermute(terms[d], 'ctx', chip_shift(CHIPS - d))]
    ppermute x1, waiting for transfers between devices: 0.01 us -> 1.59 us  [shards(): kv2 = lax.ppermute(kv, 'ctx', chip_shift(2))]
    all_to_all x1, blocking collectives: 17.5 us -> 18.8 us  [shards(): lax.all_to_all(y_sum, 'dp', 0, 0, tiled=True, axis_index_groups=Z_GROUPS)]
    ppermute x3, waiting for transfers between devices: 7.16 us -> 5.85 us  [shards(): lax.ppermute(packed[d], 'ctx', chip_shift(d))]
  transfers between devices with their start and end apart: 22 -> 22, of which waited for: 11 -> 9; matrix products, arithmetic and copies ran while one was open for 0% -> 0% of each run, Pallas kernels for 23% -> 28%
where the time goes in v10:
time: 80.7 us; the launch traced here: 80.6 us
  Pallas kernels  23.9 us (30%)
  starting transfers between devices  23.1 us (29%)
  blocking collectives  18.8 us (23%)
  waiting for transfers between devices  13.7 us (17%)
  between operations  0.9 us (1%)
    all_to_all x1, blocking collectives, shards(): lax.all_to_all(y_sum, 'dp', 0, 0, tiled=True, axis_index_groups=Z_GROUPS)  18.8 us
    ppermute x3, starting transfers between devices, shards(): lax.ppermute(terms[d], 'ctx', chip_shift(CHIPS - d))  5.96 us
    ppermute x3, waiting for transfers between devices, shards(): lax.ppermute(packed[d], 'ctx', chip_shift(d))  5.85 us
    pallas_call x1, Pallas kernels, input_grad(): pl.pallas_call(input_kernel, in_specs=[SCALARS] + [WHOLE] * 4 + [STAY] *...  5.37 us
    ppermute x3, starting transfers between devices, shards(): lax.ppermute(terms[d], 'dp', y_shift(d))  4.56 us
    ppermute x3, starting transfers between devices, shards(): lax.ppermute(packed[d], 'ctx', chip_shift(d))  4.05 us
    pallas_call x4, Pallas kernels, weight_grad(): pl.pallas_call(functools.partial(weight_kernel, shift), in_specs=[SCALARS...  3.63 us
    ppermute x2, starting transfers between devices, shards(): far = {d: lax.ppermute(own, 'ctx', chip_shift(d)) for d in (1, 3)}  3.24 us
  transfers between devices with their start and end apart: 22, of which 9 were waited for; matrix products, arithmetic and copies ran while one was open for 0% of the time, Pallas kernels for 28%

profile of v10, /device:TPU:8, one launch (start us, length us, event | category | flops | bytes accessed | tf_op | source)
XLA Modules:
  0.0 80.6 jit_solution(1595358117299380840)
XLA Ops:
  0.6 0.1 collective-permute-start.2
  0.7 0.5 collective-permute-start.4
  1.2 1.5 %collective-permute-start = (bf16[128,1536]{1,0:T(8,128)(2,1)}, bf16[128,1536]{1,0:T(8,128)(2,1)S(1)}, u32[]{:S(2)}, u32[]{:S(2)}) collective-permute-start(bf16[128,1536]{1,0:T(8,128)(2,1)} %bitcast.11), channel_id=1, source_target_pairs={{0,64},{32,96},{64,128},{96,160},{128,192},{160,224},{192,0},{224,... | collective-permute-start | bytes 1179656 | tf_op jit(solution)/shard_map/ppermute | solution.py:555
  2.7 1.7 %collective-permute-start.1 = (bf16[128,1536]{1,0:T(8,128)(2,1)}, bf16[128,1536]{1,0:T(8,128)(2,1)S(1)}, u32[]{:S(2)}, u32[]{:S(2)}) collective-permute-start(bf16[128,1536]{1,0:T(8,128)(2,1)} %bitcast.12), channel_id=1, source_target_pairs={{0,192},{32,224},{64,0},{96,32},{128,64},{160,96},{192,128},{224,1... | collective-permute-start | bytes 1179656 | tf_op jit(solution)/shard_map/ppermute | solution.py:555
  4.5 0.0 collective-permute-start.3
  4.5 0.1 pad_add_fusion.place
  4.5 2.1 %project_kv_own.1 = (bf16[1536,256]{1,0:T(8,128)(2,1)S(1)}, bf16[128,256]{1,0:T(8,128)(2,1)S(1)}) custom-call(s32[4]{0:T(128)S(1)} %pad_add_fusion.place, bf16[128,1536]{1,0:T(8,128)(2,1)} %bitcast.13, bf16[1536,256]{1,0:T(8,128)(2,1)} %w_key.5, bf16[1536,256]{1,0:T(8,128)(2,1)} %w_value.5), custom_call_target="tpu_custom_call" | custom-call | flops 1 | bytes 1 | tf_op jit(solution)/shard_map/project_kv_own/pallas_call | solution.py:94
  6.6 0.0 copy-start
  6.6 0.0 collective-permute-done.3.mask_other
  6.7 0.0 collective-permute-done.2.other
  6.7 0.3 project_kv.1.refs_0_
  7.0 1.9 %collective-permute-start.5 = (bf16[256,256]{1,0:T(8,128)(2,1)S(1)}, bf16[256,256]{1,0:T(8,128)(2,1)S(1)}, u32[]{:S(2)}, u32[]{:S(2)}) collective-permute-start(bf16[256,256]{1,0:T(8,128)(2,1)S(1)} %project_kv.1.refs_0_), channel_id=1, source_target_pairs={{0,128},{32,160},{64,192},{96,224},{128,0},{160,32},{192,64},{224,... | collective-permute-start | bytes 393224 | tf_op jit(solution)/shard_map/ppermute | solution.py:554
  8.9 0.6 stack_up.1.up
  9.5 3.2 %project_query.1 = (bf16[1536,128]{1,0:T(8,128)(2,1)S(1)}, s32[16,256]{1,0:T(8,128)S(1)}, bf16[1536,256]{1,0:T(8,128)(2,1)S(1)}) custom-call(s32[4]{0:T(128)S(1)} %pad_add_fusion.place, bf16[128,1536]{1,0:T(8,128)(2,1)S(1)} %bitcast.14, bf16[128,1536]{1,0:T(8,128)(2,1)S(1)} %collective-permute-done.2.other, bf16[1536,1536]{1,0:T(8,128)(2,1)} %w_query.3, ...), custom_call_target="tpu_custom_call" | custom-call | flops 1 | bytes 1 | tf_op jit(solution)/shard_map/project_query/pallas_call | solution.py:213
  12.7 0.7 chip_scores_0.1
  13.5 0.3 collective-permute-done.rows.far1
  13.8 2.2 %collective-permute-done.1.rows.far3 = bf16[128,1536]{1,0:T(8,128)(2,1)S(1)} collective-permute-done((bf16[128,1536]{1,0:T(8,128)(2,1)}, bf16[128,1536]{1,0:T(8,128)(2,1)S(1)}, u32[]{:S(2)}, u32[]{:S(2)}) %collective-permute-start.1) | collective-permute-done | bytes 393248 | tf_op jit(solution)/shard_map/ppermute | solution.py:555
  16.0 1.6 %collective-permute-done.5.refs_0_ = bf16[256,256]{1,0:T(8,128)(2,1)S(1)} collective-permute-done((bf16[256,256]{1,0:T(8,128)(2,1)S(1)}, bf16[256,256]{1,0:T(8,128)(2,1)S(1)}, u32[]{:S(2)}, u32[]{:S(2)}) %collective-permute-start.5) | collective-permute-done | bytes 131104 | tf_op jit(solution)/shard_map/ppermute | solution.py:554
  17.6 1.1 %collective-permute-start.6 = (bf16[128,1536]{1,0:T(8,128)(2,1)S(1)}, bf16[128,1536]{1,0:T(8,128)(2,1)S(1)}, u32[]{:S(2)}, u32[]{:S(2)}) collective-permute-start(bf16[128,1536]{1,0:T(8,128)(2,1)S(1)} %collective-permute-done.rows.far1), channel_id=1, source_target_pairs={{0,64},{32,96},{64,128},{96,160},{128,192},{160,224},{192,0},{224,... | collective-permute-start | bytes 1179656 | tf_op jit(solution)/shard_map/ppermute | solution.py:563
  18.7 0.4 project_kv_far.3
  19.1 0.1 collective-permute-start.8
  19.2 0.4 project_kv_far.2
  19.6 0.6 collective-permute-start.7
  20.2 0.7 chip_scores_2.1
  20.9 0.0 collective-permute-done.8.refs_1_
  20.9 0.8 chip_scores_3.1
  21.7 0.0 collective-permute-done.7.refs_1_
  21.7 0.8 chip_scores_1.1
  22.5 0.6 chip_terms_2.1
  23.1 2.6 %collective-permute-start.11 = (bf16[256,256]{1,0:T(8,128)(2,1)S(1)}, bf16[256,256]{1,0:T(8,128)(2,1)S(1)}, u32[]{:S(2)}, u32[]{:S(2)}) collective-permute-start(bf16[256,256]{1,0:T(8,128)(2,1)S(1)} %get-tuple-element.102), channel_id=1, source_target_pairs={{0,128},{32,160},{64,192},{96,224},{128,0},{160,32},{192,64},{224,... | collective-permute-start | bytes 393224 | tf_op jit(solution)/shard_map/ppermute | solution.py:575
  25.7 0.6 chip_terms_3.1
  26.3 0.7 collective-permute-start.10
  27.0 0.6 chip_terms_1.1
  27.6 2.7 %collective-permute-start.9 = (bf16[256,256]{1,0:T(8,128)(2,1)S(1)}, bf16[256,256]{1,0:T(8,128)(2,1)S(1)}, u32[]{:S(2)}, u32[]{:S(2)}) collective-permute-start(bf16[256,256]{1,0:T(8,128)(2,1)S(1)} %get-tuple-element.96), channel_id=1, source_target_pairs={{0,192},{32,224},{64,0},{96,32},{128,64},{160,96},{192,128},{224,1... | collective-permute-start | bytes 393224 | tf_op jit(solution)/shard_map/ppermute | solution.py:575
  30.3 0.6 chip_terms_0.1
  30.9 0.7 query_grad.1
  31.6 1.0 %collective-permute-done.11.d = bf16[256,256]{1,0:T(8,128)(2,1)S(1)} collective-permute-done((bf16[256,256]{1,0:T(8,128)(2,1)S(1)}, bf16[256,256]{1,0:T(8,128)(2,1)S(1)}, u32[]{:S(2)}, u32[]{:S(2)}) %collective-permute-start.11) | collective-permute-done | bytes 131104 | tf_op jit(solution)/shard_map/ppermute | solution.py:575
  32.6 2.1 %collective-permute-done.10.c = bf16[256,256]{1,0:T(8,128)(2,1)S(1)} collective-permute-done((bf16[256,256]{1,0:T(8,128)(2,1)S(1)}, bf16[256,256]{1,0:T(8,128)(2,1)S(1)}, u32[]{:S(2)}, u32[]{:S(2)}) %collective-permute-start.10) | collective-permute-done | bytes 131104 | tf_op jit(solution)/shard_map/ppermute | solution.py:575
  34.7 0.0 collective-permute-done.9.b
  34.7 0.1 sum_four.2.dkv
  34.7 0.1 collective-permute-start.13
  34.8 0.5 collective-permute-start.12
  35.3 0.5 transpose_tokens.1.tokens_t
  35.8 0.4 collective-permute-done.13.dkv_other
  36.2 0.2 collective-permute-done.12.middle_other
  36.4 0.7 pack.1
  37.0 0.4 collective-permute-start.14
  37.4 0.8 %collective-permute-start.15 = (bf16[256,256]{1,0:T(8,128)(2,1)S(1)}, bf16[256,256]{1,0:T(8,128)(2,1)S(1)}, u32[]{:S(2)}, u32[]{:S(2)}) collective-permute-start(bf16[256,256]{1,0:T(8,128)(2,1)S(1)} %get-tuple-element.130), channel_id=1, source_target_pairs={{0,128},{32,160},{64,192},{96,224},{128,0},{160,32},{192,64},{224,... | collective-permute-start | bytes 393224 | tf_op jit(solution)/shard_map/ppermute | solution.py:591
  38.3 1.8 %collective-permute-start.16 = (bf16[256,256]{1,0:T(8,128)(2,1)S(1)}, bf16[256,256]{1,0:T(8,128)(2,1)S(1)}, u32[]{:S(2)}, u32[]{:S(2)}) collective-permute-start(bf16[256,256]{1,0:T(8,128)(2,1)S(1)} %get-tuple-element.131), channel_id=1, source_target_pairs={{0,64},{32,96},{64,128},{96,160},{128,192},{160,224},{192,0},{224,... | collective-permute-start | bytes 393224 | tf_op jit(solution)/shard_map/ppermute | solution.py:591
  40.1 1.4 %collective-permute-start.17 = (bf16[256,256]{1,0:T(8,128)(2,1)S(1)}, bf16[256,256]{1,0:T(8,128)(2,1)S(1)}, u32[]{:S(2)}, u32[]{:S(2)}) collective-permute-start(bf16[256,256]{1,0:T(8,128)(2,1)S(1)} %get-tuple-element.132), channel_id=1, source_target_pairs={{0,192},{32,224},{64,0},{96,32},{128,64},{160,96},{192,128},{224,1... | collective-permute-start | bytes 393224 | tf_op jit(solution)/shard_map/ppermute | solution.py:591
  41.5 3.8 %collective-permute-done.15.b = bf16[256,256]{1,0:T(8,128)(2,1)S(1)} collective-permute-done((bf16[256,256]{1,0:T(8,128)(2,1)S(1)}, bf16[256,256]{1,0:T(8,128)(2,1)S(1)}, u32[]{:S(2)}, u32[]{:S(2)}) %collective-permute-start.15) | collective-permute-done | bytes 131104 | tf_op jit(solution)/shard_map/ppermute | solution.py:591
  45.3 2.0 %collective-permute-done.16.c = bf16[256,256]{1,0:T(8,128)(2,1)S(1)} collective-permute-done((bf16[256,256]{1,0:T(8,128)(2,1)S(1)}, bf16[256,256]{1,0:T(8,128)(2,1)S(1)}, u32[]{:S(2)}, u32[]{:S(2)}) %collective-permute-start.16) | collective-permute-done | bytes 131104 | tf_op jit(solution)/shard_map/ppermute | solution.py:591
  47.3 0.9 %weight_grad_2.1 = bf16[384,256]{1,0:T(8,128)(2,1)S(1)} custom-call(s32[4]{0:T(128)S(1)} %pad_add_fusion.place, bf16[1536,512]{1,0:T(8,128)(2,1)S(1)} %transpose_tokens.1.tokens_t, bf16[1536,512]{1,0:T(8,128)(2,1)S(1)} %collective-permute-done.14.other_t, bf16[256,256]{1,0:T(8,128)(2,1)S(1)} %get-tuple-element.129.a, ...), custom_call_target="tpu_custom_call" | custom-call | flops 1 | bytes 1 | tf_op jit(solution)/shard_map/weight_grad_2/pallas_call | solution.py:453
  48.3 2.4 %collective-permute-start.20 = (bf16[384,256]{1,0:T(8,128)(2,1)S(1)}, bf16[384,256]{1,0:T(8,128)(2,1)S(1)}, u32[]{:S(2)}, u32[]{:S(2)}) collective-permute-start(bf16[384,256]{1,0:T(8,128)(2,1)S(1)} %weight_grad_2.1), channel_id=1, source_target_pairs={{0,16},{1,17},{2,18},{3,19},{4,20},{5,21},{6,22},{7,23},{8,24},{9,... | collective-permute-start | bytes 589832 | tf_op jit(solution)/shard_map/ppermute | solution.py:594
  50.6 0.9 %weight_grad_3.1 = bf16[384,256]{1,0:T(8,128)(2,1)S(1)} custom-call(s32[4]{0:T(128)S(1)} %pad_add_fusion.place, bf16[1536,512]{1,0:T(8,128)(2,1)S(1)} %transpose_tokens.1.tokens_t, bf16[1536,512]{1,0:T(8,128)(2,1)S(1)} %collective-permute-done.14.other_t, bf16[256,256]{1,0:T(8,128)(2,1)S(1)} %get-tuple-element.129.a, ...), custom_call_target="tpu_custom_call" | custom-call | flops 1 | bytes 1 | tf_op jit(solution)/shard_map/weight_grad_3/pallas_call | solution.py:453
  51.6 1.4 %collective-permute-start.19 = (bf16[384,256]{1,0:T(8,128)(2,1)S(1)}, bf16[384,256]{1,0:T(8,128)(2,1)S(1)}, u32[]{:S(2)}, u32[]{:S(2)}) collective-permute-start(bf16[384,256]{1,0:T(8,128)(2,1)S(1)} %weight_grad_3.1), channel_id=1, source_target_pairs={{0,24},{1,25},{2,26},{3,27},{4,28},{5,29},{6,30},{7,31},{8,0},{9,1... | collective-permute-start | bytes 589832 | tf_op jit(solution)/shard_map/ppermute | solution.py:594
  53.0 0.9 %weight_grad_1.1 = bf16[384,256]{1,0:T(8,128)(2,1)S(1)} custom-call(s32[4]{0:T(128)S(1)} %pad_add_fusion.place, bf16[1536,512]{1,0:T(8,128)(2,1)S(1)} %transpose_tokens.1.tokens_t, bf16[1536,512]{1,0:T(8,128)(2,1)S(1)} %collective-permute-done.14.other_t, bf16[256,256]{1,0:T(8,128)(2,1)S(1)} %get-tuple-element.129.a, ...), custom_call_target="tpu_custom_call" | custom-call | flops 1 | bytes 1 | tf_op jit(solution)/shard_map/weight_grad_1/pallas_call | solution.py:453
  53.9 0.8 collective-permute-start.18
  54.7 5.4 %input_grad.1 = bf16[128,1536]{1,0:T(8,128)(2,1)} custom-call(s32[4]{0:T(128)S(1)} %pad_add_fusion.place, bf16[256,768]{1,0:T(8,128)(2,1)S(1)} %get-tuple-element.121.dq, bf16[128,768]{1,0:T(8,128)(2,1)S(1)} %collective-permute-done.21.dq_other, bf16[256,256]{1,0:T(8,128)(2,1)S(1)} %sum_four.2.dkv, bf16[256,256]{1,0:T(8,128)(2,1)S(1)} %collective-permute-done.13.dkv_other, ...), custom_call_target="tpu_custom_call" | custom-call | flops 1 | bytes 1 | tf_op jit(solution)/shard_map/input_grad/pallas_call | solution.py:506
  60.0 0.9 %weight_grad_0.1.a = f32[384,256]{1,0:T(8,128)S(1)} custom-call(s32[4]{0:T(128)S(1)} %pad_add_fusion.place, bf16[1536,512]{1,0:T(8,128)(2,1)S(1)} %transpose_tokens.1.tokens_t, bf16[1536,512]{1,0:T(8,128)(2,1)S(1)} %collective-permute-done.14.other_t, bf16[256,256]{1,0:T(8,128)(2,1)S(1)} %get-tuple-element.129.a, ...), custom_call_target="tpu_custom_call" | custom-call | flops 1 | bytes 1 | tf_op jit(solution)/shard_map/weight_grad_0/pallas_call | solution.py:453
  61.0 0.0 collective-permute-done.18.b
  61.0 0.1 sum_four.3
  61.1 18.8 %all_to_all.11 = bf16[8,48,256]{2,1,0:T(8,128)(2,1)S(1)} all-to-all(bf16[8,48,256]{2,1,0:T(8,128)(2,1)S(1)} %bitcast.16), channel_id=1, replica_groups={{0,1,2,3,4,5,6,7},{8,9,10,11,12,13,14,15},{16,17,18,19,20,21,22,23},{24..., dimensions={0} | all-to-all | bytes 393216 | tf_op jit(solution)/shard_map/all_to_all | solution.py:600
  79.9 0.6 final_sum.1
  (12 shorter events, 0.1 us)
Async XLA Ops:
  0.6 6.0 %collective-permute-start.2 = (bf16[128,1536]{1,0:T(8,128)(2,1)}, bf16[128,1536]{1,0:T(8,128)(2,1)S(1)}, u32[]{:S(2)}, u32[]{:S(2)}) collective-permute-start(bf16[128,1536]{1,0:T(8,128)(2,1)} %bitcast.10), channel_id=1, source_target_pairs={{0,32},{32,0},{64,96},{96,64},{128,160},{160,128},{192,224},{224,1... | collective-permute-start | bytes 1179656 | tf_op jit(solution)/shard_map/ppermute | solution.py:546
  0.7 5.9 %collective-permute-start.4 = (bf16[128,1536]{1,0:T(8,128)(2,1)}, bf16[128,1536]{1,0:T(8,128)(2,1)S(1)}, u32[]{:S(2)}, u32[]{:S(2)}) collective-permute-start(bf16[128,1536]{1,0:T(8,128)(2,1)} %bitcast.18), channel_id=1, source_target_pairs={{0,32},{32,0},{64,96},{96,64},{128,160},{160,128},{192,224},{224,1... | collective-permute-start | bytes 1179656 | tf_op jit(solution)/shard_map/ppermute | solution.py:547
  1.2 12.5 %collective-permute-start = (bf16[128,1536]{1,0:T(8,128)(2,1)}, bf16[128,1536]{1,0:T(8,128)(2,1)S(1)}, u32[]{:S(2)}, u32[]{:S(2)}) collective-permute-start(bf16[128,1536]{1,0:T(8,128)(2,1)} %bitcast.11), channel_id=1, source_target_pairs={{0,64},{32,96},{64,128},{96,160},{128,192},{160,224},{192,0},{224,... | collective-permute-start | bytes 1179656 | tf_op jit(solution)/shard_map/ppermute | solution.py:555
  2.7 13.3 %collective-permute-start.1 = (bf16[128,1536]{1,0:T(8,128)(2,1)}, bf16[128,1536]{1,0:T(8,128)(2,1)S(1)}, u32[]{:S(2)}, u32[]{:S(2)}) collective-permute-start(bf16[128,1536]{1,0:T(8,128)(2,1)} %bitcast.12), channel_id=1, source_target_pairs={{0,192},{32,224},{64,0},{96,32},{128,64},{160,96},{192,128},{224,1... | collective-permute-start | bytes 1179656 | tf_op jit(solution)/shard_map/ppermute | solution.py:555
  4.5 2.2 %collective-permute-start.3 = (s32[1,8]{1,0:T(1,128)}, s32[1,8]{1,0:T(1,128)S(1)}, u32[]{:S(2)}, u32[]{:S(2)}) collective-permute-start(s32[1,8]{1,0:T(1,128)} %bitcast.21), channel_id=1, source_target_pairs={{0,32},{32,0},{64,96},{96,64},{128,160},{160,128},{192,224},{224,1... | collective-permute-start | bytes 104 | tf_op jit(solution)/shard_map/ppermute | solution.py:548
  4.5 4.3 %copy-start.1 = (bf16[1,128,1536]{2,1,0:T(8,128)(2,1)S(1)}, bf16[1,128,1536]{2,1,0:T(8,128)(2,1)}, u32[]{:S(2)}) copy-start(bf16[1,128,1536]{2,1,0:T(8,128)(2,1)} %param.8) | copy-start | bytes 1179652
  6.6 2.9 %copy-start = (bf16[1,128,1536]{2,1,0:T(8,128)(2,1)S(1)}, bf16[1,128,1536]{2,1,0:T(8,128)(2,1)}, u32[]{:S(2)}) copy-start(bf16[1,128,1536]{2,1,0:T(8,128)(2,1)} %param.7) | copy-start | bytes 1179652
  7.0 10.6 %collective-permute-start.5 = (bf16[256,256]{1,0:T(8,128)(2,1)S(1)}, bf16[256,256]{1,0:T(8,128)(2,1)S(1)}, u32[]{:S(2)}, u32[]{:S(2)}) collective-permute-start(bf16[256,256]{1,0:T(8,128)(2,1)S(1)} %project_kv.1.refs_0_), channel_id=1, source_target_pairs={{0,128},{32,160},{64,192},{96,224},{128,0},{160,32},{192,64},{224,... | collective-permute-start | bytes 393224 | tf_op jit(solution)/shard_map/ppermute | solution.py:554
  17.6 17.1 %collective-permute-start.6 = (bf16[128,1536]{1,0:T(8,128)(2,1)S(1)}, bf16[128,1536]{1,0:T(8,128)(2,1)S(1)}, u32[]{:S(2)}, u32[]{:S(2)}) collective-permute-start(bf16[128,1536]{1,0:T(8,128)(2,1)S(1)} %collective-permute-done.rows.far1), channel_id=1, source_target_pairs={{0,64},{32,96},{64,128},{96,160},{128,192},{160,224},{192,0},{224,... | collective-permute-start | bytes 1179656 | tf_op jit(solution)/shard_map/ppermute | solution.py:563
  19.1 1.8 %collective-permute-start.8 = (bf16[128,256]{1,0:T(8,128)(2,1)S(1)}, bf16[128,256]{1,0:T(8,128)(2,1)S(1)}, u32[]{:S(2)}, u32[]{:S(2)}) collective-permute-start(bf16[128,256]{1,0:T(8,128)(2,1)S(1)} %get-tuple-element.94), channel_id=1, source_target_pairs={{0,32},{32,0},{64,96},{96,64},{128,160},{160,128},{192,224},{224,1... | collective-permute-start | bytes 196616 | tf_op jit(solution)/shard_map/ppermute | solution.py:567
  19.6 2.1 %collective-permute-start.7 = (bf16[128,256]{1,0:T(8,128)(2,1)S(1)}, bf16[128,256]{1,0:T(8,128)(2,1)S(1)}, u32[]{:S(2)}, u32[]{:S(2)}) collective-permute-start(bf16[128,256]{1,0:T(8,128)(2,1)S(1)} %get-tuple-element.85), channel_id=1, source_target_pairs={{0,32},{32,0},{64,96},{96,64},{128,160},{160,128},{192,224},{224,1... | collective-permute-start | bytes 196616 | tf_op jit(solution)/shard_map/ppermute | solution.py:567
  23.1 9.5 %collective-permute-start.11 = (bf16[256,256]{1,0:T(8,128)(2,1)S(1)}, bf16[256,256]{1,0:T(8,128)(2,1)S(1)}, u32[]{:S(2)}, u32[]{:S(2)}) collective-permute-start(bf16[256,256]{1,0:T(8,128)(2,1)S(1)} %get-tuple-element.102), channel_id=1, source_target_pairs={{0,128},{32,160},{64,192},{96,224},{128,0},{160,32},{192,64},{224,... | collective-permute-start | bytes 393224 | tf_op jit(solution)/shard_map/ppermute | solution.py:575
  26.3 8.4 %collective-permute-start.10 = (bf16[256,256]{1,0:T(8,128)(2,1)S(1)}, bf16[256,256]{1,0:T(8,128)(2,1)S(1)}, u32[]{:S(2)}, u32[]{:S(2)}) collective-permute-start(bf16[256,256]{1,0:T(8,128)(2,1)S(1)} %get-tuple-element.99), channel_id=1, source_target_pairs={{0,64},{32,96},{64,128},{96,160},{128,192},{160,224},{192,0},{224,... | collective-permute-start | bytes 393224 | tf_op jit(solution)/shard_map/ppermute | solution.py:575
  27.6 7.1 %collective-permute-start.9 = (bf16[256,256]{1,0:T(8,128)(2,1)S(1)}, bf16[256,256]{1,0:T(8,128)(2,1)S(1)}, u32[]{:S(2)}, u32[]{:S(2)}) collective-permute-start(bf16[256,256]{1,0:T(8,128)(2,1)S(1)} %get-tuple-element.96), channel_id=1, source_target_pairs={{0,192},{32,224},{64,0},{96,32},{128,64},{160,96},{192,128},{224,1... | collective-permute-start | bytes 393224 | tf_op jit(solution)/shard_map/ppermute | solution.py:575
  34.7 1.4 %collective-permute-start.13 = (bf16[256,256]{1,0:T(8,128)(2,1)S(1)}, bf16[256,256]{1,0:T(8,128)(2,1)S(1)}, u32[]{:S(2)}, u32[]{:S(2)}) collective-permute-start(bf16[256,256]{1,0:T(8,128)(2,1)S(1)} %sum_four.2.dkv), channel_id=1, source_target_pairs={{0,32},{32,0},{64,96},{96,64},{128,160},{160,128},{192,224},{224,1... | collective-permute-start | bytes 393224 | tf_op jit(solution)/shard_map/ppermute | solution.py:583
  34.8 1.5 %collective-permute-start.12 = (bf16[256,256]{1,0:T(8,128)(2,1)S(1)}, bf16[256,256]{1,0:T(8,128)(2,1)S(1)}, u32[]{:S(2)}, u32[]{:S(2)}) collective-permute-start(bf16[256,256]{1,0:T(8,128)(2,1)S(1)} %get-tuple-element.122), channel_id=1, source_target_pairs={{0,32},{32,0},{64,96},{96,64},{128,160},{160,128},{192,224},{224,1... | collective-permute-start | bytes 393224 | tf_op jit(solution)/shard_map/ppermute | solution.py:581
  37.0 10.3 %collective-permute-start.14 = (bf16[1536,512]{1,0:T(8,128)(2,1)S(1)}, bf16[1536,512]{1,0:T(8,128)(2,1)S(1)}, u32[]{:S(2)}, u32[]{:S(2)}) collective-permute-start(bf16[1536,512]{1,0:T(8,128)(2,1)S(1)} %transpose_tokens.1.tokens_t), channel_id=1, source_target_pairs={{0,32},{32,0},{64,96},{96,64},{128,160},{160,128},{192,224},{224,1... | collective-permute-start | bytes 4718600 | tf_op jit(solution)/shard_map/ppermute | solution.py:590
  37.4 7.9 %collective-permute-start.15 = (bf16[256,256]{1,0:T(8,128)(2,1)S(1)}, bf16[256,256]{1,0:T(8,128)(2,1)S(1)}, u32[]{:S(2)}, u32[]{:S(2)}) collective-permute-start(bf16[256,256]{1,0:T(8,128)(2,1)S(1)} %get-tuple-element.130), channel_id=1, source_target_pairs={{0,128},{32,160},{64,192},{96,224},{128,0},{160,32},{192,64},{224,... | collective-permute-start | bytes 393224 | tf_op jit(solution)/shard_map/ppermute | solution.py:591
  38.3 9.1 %collective-permute-start.16 = (bf16[256,256]{1,0:T(8,128)(2,1)S(1)}, bf16[256,256]{1,0:T(8,128)(2,1)S(1)}, u32[]{:S(2)}, u32[]{:S(2)}) collective-permute-start(bf16[256,256]{1,0:T(8,128)(2,1)S(1)} %get-tuple-element.131), channel_id=1, source_target_pairs={{0,64},{32,96},{64,128},{96,160},{128,192},{160,224},{192,0},{224,... | collective-permute-start | bytes 393224 | tf_op jit(solution)/shard_map/ppermute | solution.py:591
  40.1 7.3 %collective-permute-start.17 = (bf16[256,256]{1,0:T(8,128)(2,1)S(1)}, bf16[256,256]{1,0:T(8,128)(2,1)S(1)}, u32[]{:S(2)}, u32[]{:S(2)}) collective-permute-start(bf16[256,256]{1,0:T(8,128)(2,1)S(1)} %get-tuple-element.132), channel_id=1, source_target_pairs={{0,192},{32,224},{64,0},{96,32},{128,64},{160,96},{192,128},{224,1... | collective-permute-start | bytes 393224 | tf_op jit(solution)/shard_map/ppermute | solution.py:591
  41.5 13.2 %collective-permute-start.21 = (bf16[128,768]{1,0:T(8,128)(2,1)S(1)}, bf16[128,768]{1,0:T(8,128)(2,1)S(1)}, u32[]{:S(2)}, u32[]{:S(2)}) collective-permute-start(bf16[128,768]{1,0:T(8,128)(2,1)S(1)} %get-tuple-element.133), channel_id=1, source_target_pairs={{0,32},{32,0},{64,96},{96,64},{128,160},{160,128},{192,224},{224,1... | collective-permute-start | bytes 589832 | tf_op jit(solution)/shard_map/ppermute | solution.py:589
  48.3 12.7 %collective-permute-start.20 = (bf16[384,256]{1,0:T(8,128)(2,1)S(1)}, bf16[384,256]{1,0:T(8,128)(2,1)S(1)}, u32[]{:S(2)}, u32[]{:S(2)}) collective-permute-start(bf16[384,256]{1,0:T(8,128)(2,1)S(1)} %weight_grad_2.1), channel_id=1, source_target_pairs={{0,16},{1,17},{2,18},{3,19},{4,20},{5,21},{6,22},{7,23},{8,24},{9,... | collective-permute-start | bytes 589832 | tf_op jit(solution)/shard_map/ppermute | solution.py:594
  51.6 9.4 %collective-permute-start.19 = (bf16[384,256]{1,0:T(8,128)(2,1)S(1)}, bf16[384,256]{1,0:T(8,128)(2,1)S(1)}, u32[]{:S(2)}, u32[]{:S(2)}) collective-permute-start(bf16[384,256]{1,0:T(8,128)(2,1)S(1)} %weight_grad_3.1), channel_id=1, source_target_pairs={{0,24},{1,25},{2,26},{3,27},{4,28},{5,29},{6,30},{7,31},{8,0},{9,1... | collective-permute-start | bytes 589832 | tf_op jit(solution)/shard_map/ppermute | solution.py:594
  53.9 7.1 %collective-permute-start.18 = (bf16[384,256]{1,0:T(8,128)(2,1)S(1)}, bf16[384,256]{1,0:T(8,128)(2,1)S(1)}, u32[]{:S(2)}, u32[]{:S(2)}) collective-permute-start(bf16[384,256]{1,0:T(8,128)(2,1)S(1)} %weight_grad_1.1), channel_id=1, source_target_pairs={{0,8},{1,9},{2,10},{3,11},{4,12},{5,13},{6,14},{7,15},{8,16},{9,17... | collective-permute-start | bytes 589832 | tf_op jit(solution)/shard_map/ppermute | solution.py:594

commit v11 on v10

--- a/solution.py
+++ b/solution.py
@@ -56,6 +56,11 @@
     return pltpu.with_memory_space_constraint(array, pltpu.HBM)
 
 
+def position():
+    ctx, dp = lax.axis_index("ctx"), lax.axis_index("dp")
+    return lax.div(ctx, 2), lax.rem(ctx, 2), lax.div(dp, ZS)
+
+
 def cost(flops, bytes_accessed, transcendentals=0):
     return pl.CostEstimate(
         flops=1, bytes_accessed=1, transcendentals=0
@@ -68,8 +73,9 @@
 STAY = pl.BlockSpec(memory_space=pltpu.HBM)
 
 
-def kv_own_kernel(place, own, w_key, w_value, weights, out, rows, sems):
-    columns = pl.ds(pl.multiple_of(place[1] * HD, HD), HD)
+def kv_own_kernel(own, w_key, w_value, weights, out, rows, sems):
+    _, core, _ = position()
+    columns = pl.ds(pl.multiple_of(core * HD, HD), HD)
     copies = []
     for chunk in range(W_CHUNKS):
         part = pl.ds(chunk * (TILE // W_CHUNKS), TILE // W_CHUNKS)
@@ -90,10 +96,10 @@
     out[...] = dot(rows[...], weights[...]).astype(BF)
 
 
-def project_kv_own(place, own, w_key, w_value):
+def project_kv_own(own, w_key, w_value):
     return pl.pallas_call(
         kv_own_kernel,
-        in_specs=[SCALARS, STAY, STAY, STAY],
+        in_specs=[STAY, STAY, STAY],
         out_specs=[WHOLE, WHOLE],
         out_shape=[
             jax.ShapeDtypeStruct((D, 2 * HD), BF),
@@ -103,7 +109,7 @@
         compiler_params=PARAMS,
         cost_estimate=cost(2 * TILE * D * 256, 2 * (TILE * D + D * 256)),
         name="project_kv_own",
-    )(place, own, w_key, w_value)
+    )(own, w_key, w_value)
 
 
 def kv_far_kernel(rows, weights, weights_other, mine, theirs):
@@ -141,17 +147,18 @@
 
 
 def query_kernel(
-    place, own, other, w_query, w_key, w_value, segments_far, mask_far, mask_other,
+    own, other, w_query, w_key, w_value, segments_far, mask_far, mask_other,
     out, limits, weights_other, weights, segments, mask_own, sems, small_sems,
 ):
-    theirs = pl.ds(pl.multiple_of((1 - place[1]) * HD, HD), HD)
+    chip, core, _ = position()
+    theirs = pl.ds(pl.multiple_of((1 - core) * HD, HD), HD)
     small = [
         pltpu.make_async_copy(segments_far, segments, small_sems.at[0]),
         pltpu.make_async_copy(mask_far, mask_own, small_sems.at[1]),
     ]
     for copy in small:
         copy.start()
-    columns = pl.ds(pl.multiple_of(place[1] * GF, HD), GF)
+    columns = pl.ds(pl.multiple_of(core * GF, HD), GF)
     copies = []
     for chunk in range(Q_CHUNKS):
         part = pl.ds(chunk * (D // Q_CHUNKS), D // Q_CHUNKS)
@@ -171,7 +178,6 @@
     for copy in small:
         copy.wait()
 
-    chip, core = place[0], place[1]
     passages = segments[...]
     ends = [jnp.sum((passages <= s).astype(jnp.int32)) for s in range(3)]
     for slot in range(2):
@@ -208,11 +214,11 @@
 
 
 def project_query(
-    place, own, other, w_query, w_key, w_value, segments, mask_own, mask_other
+    own, other, w_query, w_key, w_value, segments, mask_own, mask_other
 ):
     return pl.pallas_call(
         query_kernel,
-        in_specs=[SCALARS, WHOLE, WHOLE] + [STAY] * 5 + [SCALARS],
+        in_specs=[WHOLE, WHOLE] + [STAY] * 5 + [SCALARS],
         out_specs=[WHOLE] * 3,
         out_shape=[
             jax.ShapeDtypeStruct((STACK, HD), BF),
@@ -229,26 +235,27 @@
         compiler_params=PARAMS,
         cost_estimate=cost(2 * 256 * D * GF, 2 * (256 * D + D * GF + 256 * GF)),
         name="project_query",
-    )(place, own, other, w_query, w_key, w_value, segments, mask_own, mask_other)
-
-
-def stack_kernel(place, up_own, up_other, out):
+    )(own, other, w_query, w_key, w_value, segments, mask_own, mask_other)
+
+
+def stack_kernel(up_own, up_other, out):
+    _, core, _ = position()
     for slot, rows in enumerate((up_own, up_other)):
         for head in range(GROUP):
-            columns = pl.ds(pl.multiple_of(place[1] * GF + head * HD, HD), HD)
+            columns = pl.ds(pl.multiple_of(core * GF + head * HD, HD), HD)
             out[head * 256 + slot * TILE : head * 256 + (slot + 1) * TILE] = rows[:, columns]
 
 
-def stack_up(place, up_own, up_other):
+def stack_up(up_own, up_other):
     return pl.pallas_call(
         stack_kernel,
-        in_specs=[SCALARS, WHOLE, WHOLE],
+        in_specs=[WHOLE, WHOLE],
         out_specs=WHOLE,
         out_shape=jax.ShapeDtypeStruct((STACK, HD), BF),
         compiler_params=PARAMS,
         cost_estimate=cost(0, 4 * STACK * HD),
         name="stack_up",
-    )(place, up_own, up_other)
+    )(up_own, up_other)
 
 
 def scores_kernel(d, limits, query, up, *refs):
@@ -388,12 +395,13 @@
     )(a, b, c, d)
 
 
-def pack_kernel(place, dq, middle_other, dkv, dkv_other, *outs):
+def pack_kernel(dq, middle_other, dkv, dkv_other, *outs):
+    my_chip, my_core, _ = position()
     for core in range(2):
         own_part = slice(core * HD, (core + 1) * HD)
         for chip in range(CHIPS):
 
-            @pl.when((place[1] == core) & (place[0] == chip))
+            @pl.when((my_core == core) & (my_chip == chip))
             def _(core=core, own_part=own_part, chip=chip):
                 for d, out in enumerate(outs):
                     target = (chip + d) % CHIPS
@@ -410,16 +418,16 @@
                         out[...] = dq[:, 0:256] if first else dq[:, 512:768]
 
 
-def pack(place, dq, middle_other, dkv, dkv_other):
+def pack(dq, middle_other, dkv, dkv_other):
     return pl.pallas_call(
         pack_kernel,
-        in_specs=[SCALARS] + [WHOLE] * 4,
+        in_specs=[WHOLE] * 4,
         out_specs=[WHOLE] * 4,
         out_shape=[jax.ShapeDtypeStruct((256, 256), BF)] * 4,
         compiler_params=PARAMS,
         cost_estimate=cost(0, 4 << 19),
         name="pack",
-    )(place, dq, middle_other, dkv, dkv_other)
+    )(dq, middle_other, dkv, dkv_other)
 
 
 def transpose_kernel(own, far2, far1, far3, out):
@@ -439,32 +447,33 @@
     )(*parts)
 
 
-def weight_kernel(shift, place, tokens_t, other_t, a, b, c, d, out):
+def weight_kernel(shift, tokens_t, other_t, a, b, c, d, out):
     parts = (a, b, c, d)
     right = jnp.concatenate([part[:TILE] for part in parts], axis=0)
     right_other = jnp.concatenate([part[TILE:] for part in parts], axis=0)
-    row = pl.multiple_of(lax.rem(place[2] + shift, YS) * (D // YS), 128)
+    _, _, chip = position()
+    row = pl.multiple_of(lax.rem(chip + shift, YS) * (D // YS), 128)
     rows = pl.ds(row, D // YS)
     total = dot(tokens_t[rows], right) + dot(other_t[rows], right_other)
     out[...] = total.astype(out.dtype)
 
 
-def weight_grad(shift, place, tokens_t, other_t, parts):
+def weight_grad(shift, tokens_t, other_t, parts):
     return pl.pallas_call(
         functools.partial(weight_kernel, shift),
-        in_specs=[SCALARS] + [WHOLE] * 6,
+        in_specs=[WHOLE] * 6,
         out_specs=WHOLE,
         out_shape=jax.ShapeDtypeStruct((D // YS, 256), F32 if shift == 0 else BF),
         compiler_params=PARAMS,
         cost_estimate=cost(2 * D * KEYS * 256 // YS, 2 * D * KEYS // YS),
         name=f"weight_grad_{shift}",
-    )(place, tokens_t, other_t, *parts)
+    )(tokens_t, other_t, *parts)
 
 
 def input_kernel(
-    place, dq, dq_other, dkv, dkv_other, w_query, w_key, w_value, out, left, right, sems
+    dq, dq_other, dkv, dkv_other, w_query, w_key, w_value, out, left, right, sems
 ):
-    core = place[1]
+    _, core, _ = position()
     width = D // IN_CHUNKS
     copies = []
     for chunk in range(IN_CHUNKS):
@@ -502,10 +511,10 @@
         out[:, part] = dot_nt(left[...], right[part]).astype(BF)
 
 
-def input_grad(place, dq, dq_other, dkv, dkv_other, w_query, w_key, w_value):
+def input_grad(dq, dq_other, dkv, dkv_other, w_query, w_key, w_value):
     return pl.pallas_call(
         input_kernel,
-        in_specs=[SCALARS] + [WHOLE] * 4 + [STAY] * 3,
+        in_specs=[WHOLE] * 4 + [STAY] * 3,
         out_specs=WHOLE,
         out_shape=jax.ShapeDtypeStruct((TILE, D), BF),
         scratch_shapes=[
@@ -516,7 +525,7 @@
         compiler_params=PARAMS,
         cost_estimate=cost(2 * TILE * D * 2048, 2 * D * 2048),
         name="input_grad",
-    )(place, dq, dq_other, dkv, dkv_other, w_query, w_key, w_value)
+    )(dq, dq_other, dkv, dkv_other, w_query, w_key, w_value)
 
 
 def final_kernel(parts, out):
@@ -539,9 +548,6 @@
 
 
 def shards(tokens, grad_heads, tile_mask, segments, w_query, w_key, w_value):
-    ctx = lax.axis_index("ctx")
-    dp = lax.axis_index("dp")
-    place = jnp.stack([ctx // 2, ctx % 2, dp // ZS, dp % ZS]).astype(jnp.int32)
     own, up = tokens[0], grad_heads[0]
     other = lax.ppermute(own, "ctx", CORE)
     up_other = lax.ppermute(up, "ctx", CORE)
@@ -549,18 +555,20 @@
     other, mask_other, up_other = lax.optimization_barrier((other, mask_other, up_other))
 
     w_query, w_key, w_value = (in_hbm(w) for w in (w_query, w_key, w_value))
-    weights, kv_own = project_kv_own(place, in_hbm(own), w_key, w_value)
+    weights, kv_own = project_kv_own(in_hbm(own), w_key, w_value)
     kv = project_kv(other, weights, kv_own)
     kv2 = lax.ppermute(kv, "ctx", chip_shift(2))
     far = {d: lax.ppermute(own, "ctx", chip_shift(d)) for d in (1, 3)}
+    kv, other = lax.optimization_barrier((kv, other))
     query, limits, weights_other = project_query(
-        place, own, other, w_query, w_key, w_value,
+        own, other, w_query, w_key, w_value,
         in_hbm(segments), in_hbm(tile_mask[0]), mask_other,
     )
-    up = stack_up(place, up, up_other)
+    query, late_own = lax.optimization_barrier((query, own))
+    late = lax.ppermute(late_own, "ctx", chip_shift(2))
+    up = stack_up(up, up_other)
     scores = {0: chip_scores(0, limits, query, up, kv)}
-    far, kv2, scores[0] = lax.optimization_barrier((far, kv2, scores[0]))
-    late = lax.ppermute(far[1], "ctx", chip_shift(1))
+    far, scores[0] = lax.optimization_barrier((far, scores[0]))
     kv_far = {d: project_kv_far(far[d], weights, weights_other) for d in (1, 3)}
     for d in (1, 3):
         mine, theirs = kv_far[d]
@@ -581,7 +589,7 @@
     middle_other = lax.ppermute(middle, "ctx", CORE)
     dkv = sum_four(terms[0], *back)
     dkv_other = lax.ppermute(dkv, "ctx", CORE)
-    packed = pack(place, dq, middle_other, dkv, dkv_other)
+    packed = pack(dq, middle_other, dkv, dkv_other)
 
     far, dkv = lax.optimization_barrier((far, dkv))
     tokens_t = transpose([own, late, far[1], far[3]])
@@ -590,10 +598,10 @@
     other_t = lax.ppermute(tokens_t, "ctx", CORE)
     columns = {d: lax.ppermute(packed[d], "ctx", chip_shift(d)) for d in (2, 1, 3)}
     columns = [packed[0]] + [columns[d] for d in (2, 1, 3)]
-    terms = [weight_grad(d, place, tokens_t, other_t, columns) for d in range(YS)]
+    terms = [weight_grad(d, tokens_t, other_t, columns) for d in range(YS)]
     y_parts = [terms[0]] + [lax.ppermute(terms[d], "dp", y_shift(d)) for d in (1, 3, 2)]
     grad_tokens = input_grad(
-        place, dq, dq_other, dkv, dkv_other, w_query, w_key, w_value
+        dq, dq_other, dkv, dkv_other, w_query, w_key, w_value
     )
     y_parts, grad_tokens = lax.optimization_barrier((y_parts, grad_tokens))
     y_sum = sum_four(*y_parts)

time: 80.7 us -> 85.1 us (1.055)
  waiting for transfers between devices: 13.7 us -> 23 us
  Pallas kernels: 23.9 us -> 19.6 us
    ppermute x2, waiting for transfers between devices: 2.51 us -> 10.3 us  [shards(): far = {d: lax.ppermute(own, 'ctx', chip_shift(d)) for d in (1, 3)}]
    pallas_call x9, Pallas kernels: 15.6 us -> 11.3 us  [the longest x1 4.82 us: input_grad(): pl.pallas_call(input_kernel, in_specs=[WHOLE] * 4 + [STAY] * 3, out_specs...]
    ppermute x3, waiting for transfers between devices: 0.04 us -> 2.23 us  [shards(): lax.ppermute(terms[d], 'dp', y_shift(d))]
    ppermute x1, waiting for transfers between devices: 1.59 us -> 0.01 us  [shards(): kv2 = lax.ppermute(kv, 'ctx', chip_shift(2))]
    ppermute x3, starting transfers between devices: 5.96 us -> 4.83 us  [shards(): lax.ppermute(terms[d], 'ctx', chip_shift(CHIPS - d))]
  transfers between devices with their start and end apart: 22 -> 22, of which waited for: 9 -> 11; matrix products, arithmetic and copies ran while one was open for 0% -> 0% of each run, Pallas kernels for 28% -> 22%
where the time goes in v11:
time: 85.1 us; the launch traced here: 84.9 us
  waiting for transfers between devices  23 us (27%)
  starting transfers between devices  22.6 us (27%)
  Pallas kernels  19.6 us (23%)
  blocking collectives  18.8 us (22%)
  between operations  0.91 us (1%)
    all_to_all x1, blocking collectives, shards(): lax.all_to_all(y_sum, 'dp', 0, 0, tiled=True, axis_index_groups=Z_GROUPS)  18.8 us
    ppermute x2, waiting for transfers between devices, shards(): far = {d: lax.ppermute(own, 'ctx', chip_shift(d)) for d in (1, 3)}  10.3 us
    ppermute x3, waiting for transfers between devices, shards(): lax.ppermute(packed[d], 'ctx', chip_shift(d))  5.79 us
    ppermute x3, starting transfers between devices, shards(): lax.ppermute(terms[d], 'ctx', chip_shift(CHIPS - d))  4.83 us
    pallas_call x1, Pallas kernels, input_grad(): pl.pallas_call(input_kernel, in_specs=[WHOLE] * 4 + [STAY] * 3, out_specs...  4.82 us
    ppermute x3, starting transfers between devices, shards(): lax.ppermute(terms[d], 'dp', y_shift(d))  4.57 us
    ppermute x3, starting transfers between devices, shards(): lax.ppermute(packed[d], 'ctx', chip_shift(d))  4.13 us
    ppermute x3, waiting for transfers between devices, shards(): lax.ppermute(terms[d], 'ctx', chip_shift(CHIPS - d))  3.78 us
  transfers between devices with their start and end apart: 22, of which 11 were waited for; matrix products, arithmetic and copies ran while one was open for 0% of the time, Pallas kernels for 22%

profile of v11, /device:TPU:8, one launch (start us, length us, event | category | flops | bytes accessed | tf_op | source)
XLA Modules:
  0.0 84.9 jit_solution(8445863537964219624)
XLA Ops:
  0.6 0.1 collective-permute-start
  0.7 0.5 collective-permute-start.2
  1.2 1.5 %collective-permute-start.4 = (bf16[128,1536]{1,0:T(8,128)(2,1)}, bf16[128,1536]{1,0:T(8,128)(2,1)S(1)}, u32[]{:S(2)}, u32[]{:S(2)}) collective-permute-start(bf16[128,1536]{1,0:T(8,128)(2,1)} %bitcast.7), channel_id=1, source_target_pairs={{0,64},{32,96},{64,128},{96,160},{128,192},{160,224},{192,0},{224,... | collective-permute-start | bytes 1179656 | tf_op jit(solution)/shard_map/ppermute | solution.py:561
  2.7 1.7 %collective-permute-start.5 = (bf16[128,1536]{1,0:T(8,128)(2,1)}, bf16[128,1536]{1,0:T(8,128)(2,1)S(1)}, u32[]{:S(2)}, u32[]{:S(2)}) collective-permute-start(bf16[128,1536]{1,0:T(8,128)(2,1)} %bitcast.8), channel_id=1, source_target_pairs={{0,192},{32,224},{64,0},{96,32},{128,64},{160,96},{192,128},{224,1... | collective-permute-start | bytes 1179656 | tf_op jit(solution)/shard_map/ppermute | solution.py:561
  4.5 0.0 collective-permute-start.1
  4.5 1.6 %project_kv_own.1 = (bf16[1536,256]{1,0:T(8,128)(2,1)S(1)}, bf16[128,256]{1,0:T(8,128)(2,1)S(1)}) custom-call(bf16[128,1536]{1,0:T(8,128)(2,1)} %bitcast.9, bf16[1536,256]{1,0:T(8,128)(2,1)} %w_key.5, bf16[1536,256]{1,0:T(8,128)(2,1)} %w_value.5), custom_call_target="tpu_custom_call" | custom-call | flops 1 | bytes 1 | tf_op jit(solution)/shard_map/project_kv_own/pallas_call | solution.py:100
  6.1 0.0 collective-permute-done.1.mask_other
  6.1 0.0 collective-permute-done.other
  6.1 0.3 project_kv.1.refs_0_
  6.4 0.0 copy-start.1
  6.4 3.2 %project_query.1 = (bf16[1536,128]{1,0:T(8,128)(2,1)S(1)}, s32[16,256]{1,0:T(8,128)S(1)}, bf16[1536,256]{1,0:T(8,128)(2,1)S(1)}) custom-call(bf16[128,1536]{1,0:T(8,128)(2,1)S(1)} %bitcast.10, bf16[128,1536]{1,0:T(8,128)(2,1)S(1)} %collective-permute-done.other, bf16[1536,1536]{1,0:T(8,128)(2,1)} %w_query.3, bf16[1536,256]{1,0:T(8,128)(2,1)} %w_key.5, ...), custom_call_target="tpu_custom_call" | custom-call | flops 1 | bytes 1 | tf_op jit(solution)/shard_map/project_query/pallas_call | solution.py:219
  9.6 1.9 %collective-permute-start.3 = (bf16[128,1536]{1,0:T(8,128)(2,1)S(1)}, bf16[128,1536]{1,0:T(8,128)(2,1)S(1)}, u32[]{:S(2)}, u32[]{:S(2)}) collective-permute-start(bf16[128,1536]{1,0:T(8,128)(2,1)S(1)} %bitcast.11), channel_id=1, source_target_pairs={{0,128},{32,160},{64,192},{96,224},{128,0},{160,32},{192,64},{224,... | collective-permute-start | bytes 1179656 | tf_op jit(solution)/shard_map/ppermute | solution.py:568
  11.5 1.7 %collective-permute-start.7 = (bf16[256,256]{1,0:T(8,128)(2,1)S(1)}, bf16[256,256]{1,0:T(8,128)(2,1)S(1)}, u32[]{:S(2)}, u32[]{:S(2)}) collective-permute-start(bf16[256,256]{1,0:T(8,128)(2,1)S(1)} %project_kv.1.refs_0_), channel_id=1, source_target_pairs={{0,128},{32,160},{64,192},{96,224},{128,0},{160,32},{192,64},{224,... | collective-permute-start | bytes 393224 | tf_op jit(solution)/shard_map/ppermute | solution.py:560
  13.3 0.1 stack_up.1.up
  13.3 0.7 chip_scores_0.1
  14.1 10.3 %collective-permute-done.5.rows.far3 = bf16[128,1536]{1,0:T(8,128)(2,1)S(1)} collective-permute-done((bf16[128,1536]{1,0:T(8,128)(2,1)}, bf16[128,1536]{1,0:T(8,128)(2,1)S(1)}, u32[]{:S(2)}, u32[]{:S(2)}) %collective-permute-start.5) | collective-permute-done | bytes 393248 | tf_op jit(solution)/shard_map/ppermute | solution.py:561
  24.4 0.4 project_kv_far.3
  24.8 0.1 collective-permute-start.8
  24.9 0.4 project_kv_far.2
  25.3 0.6 collective-permute-start.6
  25.8 0.3 collective-permute-done.8.refs_1_
  26.1 0.7 chip_scores_3.1
  26.9 0.7 chip_scores_1.1
  27.6 0.0 collective-permute-done.7.refs_0_
  27.6 0.7 chip_scores_2.1
  28.4 0.6 chip_terms_2.1
  29.0 0.1 collective-permute-start.11
  29.1 0.6 chip_terms_3.1
  29.7 4.7 %collective-permute-start.10 = (bf16[256,256]{1,0:T(8,128)(2,1)S(1)}, bf16[256,256]{1,0:T(8,128)(2,1)S(1)}, u32[]{:S(2)}, u32[]{:S(2)}) collective-permute-start(bf16[256,256]{1,0:T(8,128)(2,1)S(1)} %get-tuple-element.105), channel_id=1, source_target_pairs={{0,64},{32,96},{64,128},{96,160},{128,192},{160,224},{192,0},{224,... | collective-permute-start | bytes 393224 | tf_op jit(solution)/shard_map/ppermute | solution.py:583
  34.4 0.6 chip_terms_1.1
  35.0 0.1 collective-permute-start.9
  35.1 0.6 chip_terms_0.1
  35.7 0.7 query_grad.1
  36.4 0.2 collective-permute-done.11.d
  36.6 2.5 %collective-permute-done.10.c = bf16[256,256]{1,0:T(8,128)(2,1)S(1)} collective-permute-done((bf16[256,256]{1,0:T(8,128)(2,1)S(1)}, bf16[256,256]{1,0:T(8,128)(2,1)S(1)}, u32[]{:S(2)}, u32[]{:S(2)}) %collective-permute-start.10) | collective-permute-done | bytes 131104 | tf_op jit(solution)/shard_map/ppermute | solution.py:583
  39.0 1.1 %collective-permute-done.9.b = bf16[256,256]{1,0:T(8,128)(2,1)S(1)} collective-permute-done((bf16[256,256]{1,0:T(8,128)(2,1)S(1)}, bf16[256,256]{1,0:T(8,128)(2,1)S(1)}, u32[]{:S(2)}, u32[]{:S(2)}) %collective-permute-start.9) | collective-permute-done | bytes 131104 | tf_op jit(solution)/shard_map/ppermute | solution.py:583
  40.1 0.1 sum_four.2.dkv
  40.2 0.1 collective-permute-start.13
  40.3 0.5 collective-permute-start.12
  40.8 0.5 transpose_tokens.1.tokens_t
  41.3 0.4 collective-permute-done.13.dkv_other
  41.6 0.2 collective-permute-done.12.middle_other
  41.8 0.1 pack.1
  41.9 0.4 collective-permute-start.14
  42.3 0.9 %collective-permute-start.15 = (bf16[256,256]{1,0:T(8,128)(2,1)S(1)}, bf16[256,256]{1,0:T(8,128)(2,1)S(1)}, u32[]{:S(2)}, u32[]{:S(2)}) collective-permute-start(bf16[256,256]{1,0:T(8,128)(2,1)S(1)} %get-tuple-element.136), channel_id=1, source_target_pairs={{0,128},{32,160},{64,192},{96,224},{128,0},{160,32},{192,64},{224,... | collective-permute-start | bytes 393224 | tf_op jit(solution)/shard_map/ppermute | solution.py:599
  43.2 2.4 %collective-permute-start.16 = (bf16[256,256]{1,0:T(8,128)(2,1)S(1)}, bf16[256,256]{1,0:T(8,128)(2,1)S(1)}, u32[]{:S(2)}, u32[]{:S(2)}) collective-permute-start(bf16[256,256]{1,0:T(8,128)(2,1)S(1)} %get-tuple-element.137), channel_id=1, source_target_pairs={{0,64},{32,96},{64,128},{96,160},{128,192},{160,224},{192,0},{224,... | collective-permute-start | bytes 393224 | tf_op jit(solution)/shard_map/ppermute | solution.py:599
  45.6 0.8 collective-permute-start.17
  46.4 3.7 %collective-permute-done.15.b = bf16[256,256]{1,0:T(8,128)(2,1)S(1)} collective-permute-done((bf16[256,256]{1,0:T(8,128)(2,1)S(1)}, bf16[256,256]{1,0:T(8,128)(2,1)S(1)}, u32[]{:S(2)}, u32[]{:S(2)}) %collective-permute-start.15) | collective-permute-done | bytes 131104 | tf_op jit(solution)/shard_map/ppermute | solution.py:599
  50.2 2.1 %collective-permute-done.16.c = bf16[256,256]{1,0:T(8,128)(2,1)S(1)} collective-permute-done((bf16[256,256]{1,0:T(8,128)(2,1)S(1)}, bf16[256,256]{1,0:T(8,128)(2,1)S(1)}, u32[]{:S(2)}, u32[]{:S(2)}) %collective-permute-start.16) | collective-permute-done | bytes 131104 | tf_op jit(solution)/shard_map/ppermute | solution.py:599
  52.2 0.0 collective-permute-done.17.d
  52.2 0.4 weight_grad_2.1
  52.6 2.4 %collective-permute-start.20 = (bf16[384,256]{1,0:T(8,128)(2,1)S(1)}, bf16[384,256]{1,0:T(8,128)(2,1)S(1)}, u32[]{:S(2)}, u32[]{:S(2)}) collective-permute-start(bf16[384,256]{1,0:T(8,128)(2,1)S(1)} %weight_grad_2.1), channel_id=1, source_target_pairs={{0,16},{1,17},{2,18},{3,19},{4,20},{5,21},{6,22},{7,23},{8,24},{9,... | collective-permute-start | bytes 589832 | tf_op jit(solution)/shard_map/ppermute | solution.py:602
  55.0 0.4 weight_grad_3.1
  55.4 1.4 %collective-permute-start.19 = (bf16[384,256]{1,0:T(8,128)(2,1)S(1)}, bf16[384,256]{1,0:T(8,128)(2,1)S(1)}, u32[]{:S(2)}, u32[]{:S(2)}) collective-permute-start(bf16[384,256]{1,0:T(8,128)(2,1)S(1)} %weight_grad_3.1), channel_id=1, source_target_pairs={{0,24},{1,25},{2,26},{3,27},{4,28},{5,29},{6,30},{7,31},{8,0},{9,1... | collective-permute-start | bytes 589832 | tf_op jit(solution)/shard_map/ppermute | solution.py:602
  56.8 0.4 weight_grad_1.1
  57.2 0.8 collective-permute-start.18
  57.9 4.8 %input_grad.1 = bf16[128,1536]{1,0:T(8,128)(2,1)} custom-call(bf16[256,768]{1,0:T(8,128)(2,1)S(1)} %get-tuple-element.127.dq, bf16[128,768]{1,0:T(8,128)(2,1)S(1)} %collective-permute-done.21.dq_other, bf16[256,256]{1,0:T(8,128)(2,1)S(1)} %sum_four.2.dkv, bf16[256,256]{1,0:T(8,128)(2,1)S(1)} %collective-permute-done.13.dkv_other, ...), custom_call_target="tpu_custom_call" | custom-call | flops 1 | bytes 1 | tf_op jit(solution)/shard_map/input_grad/pallas_call | solution.py:515
  62.8 0.4 weight_grad_0.1.a
  63.1 0.0 collective-permute-done.20.d
  63.1 2.1 %collective-permute-done.19.c = bf16[384,256]{1,0:T(8,128)(2,1)S(1)} collective-permute-done((bf16[384,256]{1,0:T(8,128)(2,1)S(1)}, bf16[384,256]{1,0:T(8,128)(2,1)S(1)}, u32[]{:S(2)}, u32[]{:S(2)}) %collective-permute-start.19) | collective-permute-done | bytes 196640 | tf_op jit(solution)/shard_map/ppermute | solution.py:602
  65.2 0.1 collective-permute-done.18.b
  65.4 0.1 sum_four.3
  65.5 18.8 %all_to_all.11 = bf16[8,48,256]{2,1,0:T(8,128)(2,1)S(1)} all-to-all(bf16[8,48,256]{2,1,0:T(8,128)(2,1)S(1)} %bitcast.13), channel_id=1, replica_groups={{0,1,2,3,4,5,6,7},{8,9,10,11,12,13,14,15},{16,17,18,19,20,21,22,23},{24..., dimensions={0} | all-to-all | bytes 393216 | tf_op jit(solution)/shard_map/all_to_all | solution.py:608
  84.3 0.6 final_sum.1
  (11 shorter events, 0.1 us)
Async XLA Ops:
  0.6 5.4 %collective-permute-start = (bf16[128,1536]{1,0:T(8,128)(2,1)}, bf16[128,1536]{1,0:T(8,128)(2,1)S(1)}, u32[]{:S(2)}, u32[]{:S(2)}) collective-permute-start(bf16[128,1536]{1,0:T(8,128)(2,1)} %bitcast.6), channel_id=1, source_target_pairs={{0,32},{32,0},{64,96},{96,64},{128,160},{160,128},{192,224},{224,1... | collective-permute-start | bytes 1179656 | tf_op jit(solution)/shard_map/ppermute | solution.py:552
  0.7 5.4 %collective-permute-start.2 = (bf16[128,1536]{1,0:T(8,128)(2,1)}, bf16[128,1536]{1,0:T(8,128)(2,1)S(1)}, u32[]{:S(2)}, u32[]{:S(2)}) collective-permute-start(bf16[128,1536]{1,0:T(8,128)(2,1)} %bitcast.15), channel_id=1, source_target_pairs={{0,32},{32,0},{64,96},{96,64},{128,160},{160,128},{192,224},{224,1... | collective-permute-start | bytes 1179656 | tf_op jit(solution)/shard_map/ppermute | solution.py:553
  1.2 12.8 %collective-permute-start.4 = (bf16[128,1536]{1,0:T(8,128)(2,1)}, bf16[128,1536]{1,0:T(8,128)(2,1)S(1)}, u32[]{:S(2)}, u32[]{:S(2)}) collective-permute-start(bf16[128,1536]{1,0:T(8,128)(2,1)} %bitcast.7), channel_id=1, source_target_pairs={{0,64},{32,96},{64,128},{96,160},{128,192},{160,224},{192,0},{224,... | collective-permute-start | bytes 1179656 | tf_op jit(solution)/shard_map/ppermute | solution.py:561
  2.7 21.7 %collective-permute-start.5 = (bf16[128,1536]{1,0:T(8,128)(2,1)}, bf16[128,1536]{1,0:T(8,128)(2,1)S(1)}, u32[]{:S(2)}, u32[]{:S(2)}) collective-permute-start(bf16[128,1536]{1,0:T(8,128)(2,1)} %bitcast.8), channel_id=1, source_target_pairs={{0,192},{32,224},{64,0},{96,32},{128,64},{160,96},{192,128},{224,1... | collective-permute-start | bytes 1179656 | tf_op jit(solution)/shard_map/ppermute | solution.py:561
  4.5 1.9 %copy-start = (bf16[1,128,1536]{2,1,0:T(8,128)(2,1)S(1)}, bf16[1,128,1536]{2,1,0:T(8,128)(2,1)}, u32[]{:S(2)}) copy-start(bf16[1,128,1536]{2,1,0:T(8,128)(2,1)} %param.7) | copy-start | bytes 1179652
  4.5 1.6 %collective-permute-start.1 = (s32[1,8]{1,0:T(1,128)}, s32[1,8]{1,0:T(1,128)S(1)}, u32[]{:S(2)}, u32[]{:S(2)}) collective-permute-start(s32[1,8]{1,0:T(1,128)} %bitcast.18), channel_id=1, source_target_pairs={{0,32},{32,0},{64,96},{96,64},{128,160},{160,128},{192,224},{224,1... | collective-permute-start | bytes 104 | tf_op jit(solution)/shard_map/ppermute | solution.py:554
  6.4 6.9 %copy-start.1 = (bf16[1,128,1536]{2,1,0:T(8,128)(2,1)S(1)}, bf16[1,128,1536]{2,1,0:T(8,128)(2,1)}, u32[]{:S(2)}) copy-start(bf16[1,128,1536]{2,1,0:T(8,128)(2,1)} %param.8) | copy-start | bytes 1179652
  9.6 30.5 %collective-permute-start.3 = (bf16[128,1536]{1,0:T(8,128)(2,1)S(1)}, bf16[128,1536]{1,0:T(8,128)(2,1)S(1)}, u32[]{:S(2)}, u32[]{:S(2)}) collective-permute-start(bf16[128,1536]{1,0:T(8,128)(2,1)S(1)} %bitcast.11), channel_id=1, source_target_pairs={{0,128},{32,160},{64,192},{96,224},{128,0},{160,32},{192,64},{224,... | collective-permute-start | bytes 1179656 | tf_op jit(solution)/shard_map/ppermute | solution.py:568
  11.5 16.1 %collective-permute-start.7 = (bf16[256,256]{1,0:T(8,128)(2,1)S(1)}, bf16[256,256]{1,0:T(8,128)(2,1)S(1)}, u32[]{:S(2)}, u32[]{:S(2)}) collective-permute-start(bf16[256,256]{1,0:T(8,128)(2,1)S(1)} %project_kv.1.refs_0_), channel_id=1, source_target_pairs={{0,128},{32,160},{64,192},{96,224},{128,0},{160,32},{192,64},{224,... | collective-permute-start | bytes 393224 | tf_op jit(solution)/shard_map/ppermute | solution.py:560
  24.8 1.3 %collective-permute-start.8 = (bf16[128,256]{1,0:T(8,128)(2,1)S(1)}, bf16[128,256]{1,0:T(8,128)(2,1)S(1)}, u32[]{:S(2)}, u32[]{:S(2)}) collective-permute-start(bf16[128,256]{1,0:T(8,128)(2,1)S(1)} %get-tuple-element.100), channel_id=1, source_target_pairs={{0,32},{32,0},{64,96},{96,64},{128,160},{160,128},{192,224},{224,1... | collective-permute-start | bytes 196616 | tf_op jit(solution)/shard_map/ppermute | solution.py:575
  25.3 1.6 %collective-permute-start.6 = (bf16[128,256]{1,0:T(8,128)(2,1)S(1)}, bf16[128,256]{1,0:T(8,128)(2,1)S(1)}, u32[]{:S(2)}, u32[]{:S(2)}) collective-permute-start(bf16[128,256]{1,0:T(8,128)(2,1)S(1)} %get-tuple-element.92), channel_id=1, source_target_pairs={{0,32},{32,0},{64,96},{96,64},{128,160},{160,128},{192,224},{224,1... | collective-permute-start | bytes 196616 | tf_op jit(solution)/shard_map/ppermute | solution.py:575
  29.0 7.6 %collective-permute-start.11 = (bf16[256,256]{1,0:T(8,128)(2,1)S(1)}, bf16[256,256]{1,0:T(8,128)(2,1)S(1)}, u32[]{:S(2)}, u32[]{:S(2)}) collective-permute-start(bf16[256,256]{1,0:T(8,128)(2,1)S(1)} %get-tuple-element.108), channel_id=1, source_target_pairs={{0,128},{32,160},{64,192},{96,224},{128,0},{160,32},{192,64},{224,... | collective-permute-start | bytes 393224 | tf_op jit(solution)/shard_map/ppermute | solution.py:583
  29.7 9.3 %collective-permute-start.10 = (bf16[256,256]{1,0:T(8,128)(2,1)S(1)}, bf16[256,256]{1,0:T(8,128)(2,1)S(1)}, u32[]{:S(2)}, u32[]{:S(2)}) collective-permute-start(bf16[256,256]{1,0:T(8,128)(2,1)S(1)} %get-tuple-element.105), channel_id=1, source_target_pairs={{0,64},{32,96},{64,128},{96,160},{128,192},{160,224},{192,0},{224,... | collective-permute-start | bytes 393224 | tf_op jit(solution)/shard_map/ppermute | solution.py:583
  35.0 5.2 %collective-permute-start.9 = (bf16[256,256]{1,0:T(8,128)(2,1)S(1)}, bf16[256,256]{1,0:T(8,128)(2,1)S(1)}, u32[]{:S(2)}, u32[]{:S(2)}) collective-permute-start(bf16[256,256]{1,0:T(8,128)(2,1)S(1)} %get-tuple-element.102), channel_id=1, source_target_pairs={{0,192},{32,224},{64,0},{96,32},{128,64},{160,96},{192,128},{224,1... | collective-permute-start | bytes 393224 | tf_op jit(solution)/shard_map/ppermute | solution.py:583
  40.2 1.4 %collective-permute-start.13 = (bf16[256,256]{1,0:T(8,128)(2,1)S(1)}, bf16[256,256]{1,0:T(8,128)(2,1)S(1)}, u32[]{:S(2)}, u32[]{:S(2)}) collective-permute-start(bf16[256,256]{1,0:T(8,128)(2,1)S(1)} %sum_four.2.dkv), channel_id=1, source_target_pairs={{0,32},{32,0},{64,96},{96,64},{128,160},{160,128},{192,224},{224,1... | collective-permute-start | bytes 393224 | tf_op jit(solution)/shard_map/ppermute | solution.py:591
  40.3 1.5 %collective-permute-start.12 = (bf16[256,256]{1,0:T(8,128)(2,1)S(1)}, bf16[256,256]{1,0:T(8,128)(2,1)S(1)}, u32[]{:S(2)}, u32[]{:S(2)}) collective-permute-start(bf16[256,256]{1,0:T(8,128)(2,1)S(1)} %get-tuple-element.128), channel_id=1, source_target_pairs={{0,32},{32,0},{64,96},{96,64},{128,160},{160,128},{192,224},{224,1... | collective-permute-start | bytes 393224 | tf_op jit(solution)/shard_map/ppermute | solution.py:589
  41.9 10.3 %collective-permute-start.14 = (bf16[1536,512]{1,0:T(8,128)(2,1)S(1)}, bf16[1536,512]{1,0:T(8,128)(2,1)S(1)}, u32[]{:S(2)}, u32[]{:S(2)}) collective-permute-start(bf16[1536,512]{1,0:T(8,128)(2,1)S(1)} %transpose_tokens.1.tokens_t), channel_id=1, source_target_pairs={{0,32},{32,0},{64,96},{96,64},{128,160},{160,128},{192,224},{224,1... | collective-permute-start | bytes 4718600 | tf_op jit(solution)/shard_map/ppermute | solution.py:598
  42.3 7.9 %collective-permute-start.15 = (bf16[256,256]{1,0:T(8,128)(2,1)S(1)}, bf16[256,256]{1,0:T(8,128)(2,1)S(1)}, u32[]{:S(2)}, u32[]{:S(2)}) collective-permute-start(bf16[256,256]{1,0:T(8,128)(2,1)S(1)} %get-tuple-element.136), channel_id=1, source_target_pairs={{0,128},{32,160},{64,192},{96,224},{128,0},{160,32},{192,64},{224,... | collective-permute-start | bytes 393224 | tf_op jit(solution)/shard_map/ppermute | solution.py:599
  43.2 9.0 %collective-permute-start.16 = (bf16[256,256]{1,0:T(8,128)(2,1)S(1)}, bf16[256,256]{1,0:T(8,128)(2,1)S(1)}, u32[]{:S(2)}, u32[]{:S(2)}) collective-permute-start(bf16[256,256]{1,0:T(8,128)(2,1)S(1)} %get-tuple-element.137), channel_id=1, source_target_pairs={{0,64},{32,96},{64,128},{96,160},{128,192},{160,224},{192,0},{224,... | collective-permute-start | bytes 393224 | tf_op jit(solution)/shard_map/ppermute | solution.py:599
  45.6 6.6 %collective-permute-start.17 = (bf16[256,256]{1,0:T(8,128)(2,1)S(1)}, bf16[256,256]{1,0:T(8,128)(2,1)S(1)}, u32[]{:S(2)}, u32[]{:S(2)}) collective-permute-start(bf16[256,256]{1,0:T(8,128)(2,1)S(1)} %get-tuple-element.138), channel_id=1, source_target_pairs={{0,192},{32,224},{64,0},{96,32},{128,64},{160,96},{192,128},{224,1... | collective-permute-start | bytes 393224 | tf_op jit(solution)/shard_map/ppermute | solution.py:599
  46.4 11.5 %collective-permute-start.21 = (bf16[128,768]{1,0:T(8,128)(2,1)S(1)}, bf16[128,768]{1,0:T(8,128)(2,1)S(1)}, u32[]{:S(2)}, u32[]{:S(2)}) collective-permute-start(bf16[128,768]{1,0:T(8,128)(2,1)S(1)} %get-tuple-element.139), channel_id=1, source_target_pairs={{0,32},{32,0},{64,96},{96,64},{128,160},{160,128},{192,224},{224,1... | collective-permute-start | bytes 589832 | tf_op jit(solution)/shard_map/ppermute | solution.py:597
  52.6 10.5 %collective-permute-start.20 = (bf16[384,256]{1,0:T(8,128)(2,1)S(1)}, bf16[384,256]{1,0:T(8,128)(2,1)S(1)}, u32[]{:S(2)}, u32[]{:S(2)}) collective-permute-start(bf16[384,256]{1,0:T(8,128)(2,1)S(1)} %weight_grad_2.1), channel_id=1, source_target_pairs={{0,16},{1,17},{2,18},{3,19},{4,20},{5,21},{6,22},{7,23},{8,24},{9,... | collective-permute-start | bytes 589832 | tf_op jit(solution)/shard_map/ppermute | solution.py:602
  55.4 9.9 %collective-permute-start.19 = (bf16[384,256]{1,0:T(8,128)(2,1)S(1)}, bf16[384,256]{1,0:T(8,128)(2,1)S(1)}, u32[]{:S(2)}, u32[]{:S(2)}) collective-permute-start(bf16[384,256]{1,0:T(8,128)(2,1)S(1)} %weight_grad_3.1), channel_id=1, source_target_pairs={{0,24},{1,25},{2,26},{3,27},{4,28},{5,29},{6,30},{7,31},{8,0},{9,1... | collective-permute-start | bytes 589832 | tf_op jit(solution)/shard_map/ppermute | solution.py:602
  57.2 8.2 %collective-permute-start.18 = (bf16[384,256]{1,0:T(8,128)(2,1)S(1)}, bf16[384,256]{1,0:T(8,128)(2,1)S(1)}, u32[]{:S(2)}, u32[]{:S(2)}) collective-permute-start(bf16[384,256]{1,0:T(8,128)(2,1)S(1)} %weight_grad_1.1), channel_id=1, source_target_pairs={{0,8},{1,9},{2,10},{3,11},{4,12},{5,13},{6,14},{7,15},{8,16},{9,17... | collective-permute-start | bytes 589832 | tf_op jit(solution)/shard_map/ppermute | solution.py:602

commit v12 on v11

--- a/solution.py
+++ b/solution.py
@@ -112,21 +112,23 @@
     )(own, w_key, w_value)
 
 
-def kv_far_kernel(rows, weights, weights_other, mine, theirs):
-    mine[...] = dot(rows[...], weights[...]).astype(BF)
-    theirs[...] = dot(rows[...], weights_other[...]).astype(BF)
-
-
-def project_kv_far(rows, weights, weights_other):
+def kv_far_kernel(far1, far3, weights, weights_other, mine, theirs):
+    for i, rows in enumerate((far1, far3)):
+        part = slice(i * TILE, (i + 1) * TILE)
+        theirs[part] = dot(rows[...], weights_other[...]).astype(BF)
+        mine[part] = dot(rows[...], weights[...]).astype(BF)
+
+
+def project_kv_far(far1, far3, weights, weights_other):
     return pl.pallas_call(
         kv_far_kernel,
-        in_specs=[WHOLE] * 3,
+        in_specs=[WHOLE] * 4,
         out_specs=[WHOLE] * 2,
-        out_shape=[jax.ShapeDtypeStruct((TILE, 2 * HD), BF)] * 2,
-        compiler_params=PARAMS,
-        cost_estimate=cost(4 * TILE * D * 256, 2 * (TILE * D + 2 * D * 256)),
+        out_shape=[jax.ShapeDtypeStruct((2 * TILE, 2 * HD), BF)] * 2,
+        compiler_params=PARAMS,
+        cost_estimate=cost(8 * TILE * D * 256, 4 * (TILE * D + D * 256)),
         name="project_kv_far",
-    )(rows, weights, weights_other)
+    )(far1, far3, weights, weights_other)
 
 
 def kv_kernel(other, weights, kv_own, out):
@@ -258,9 +260,10 @@
     )(up_own, up_other)
 
 
-def scores_kernel(d, limits, query, up, *refs):
+def scores_kernel(d, part, limits, query, up, *refs):
     powers, grads, stats, keys_t = refs[-4:]
-    kv = jnp.concatenate([ref[...] for ref in refs[:-4]], axis=0)
+    rows = slice(None) if part is None else slice(part * TILE, (part + 1) * TILE)
+    kv = jnp.concatenate([ref[rows] for ref in refs[:-4]], axis=0)
     keys, values = kv[:, :HD], kv[:, HD:]
     keys_t[...] = keys.T
     position = lax.broadcasted_iota(jnp.int32, (TILE, 2 * TILE), 0)
@@ -283,9 +286,9 @@
         stats[2:3, part] = jnp.sum(power * grad, axis=0, keepdims=True)
 
 
-def chip_scores(d, limits, query, up, *kv):
-    return pl.pallas_call(
-        functools.partial(scores_kernel, d),
+def chip_scores(d, limits, query, up, *kv, part=None):
+    return pl.pallas_call(
+        functools.partial(scores_kernel, d, part),
         in_specs=[WHOLE] * (3 + len(kv)),
         out_specs=[WHOLE] * 4,
         out_shape=[
@@ -559,22 +562,18 @@
     kv = project_kv(other, weights, kv_own)
     kv2 = lax.ppermute(kv, "ctx", chip_shift(2))
     far = {d: lax.ppermute(own, "ctx", chip_shift(d)) for d in (1, 3)}
-    kv, other = lax.optimization_barrier((kv, other))
     query, limits, weights_other = project_query(
         own, other, w_query, w_key, w_value,
         in_hbm(segments), in_hbm(tile_mask[0]), mask_other,
     )
-    query, late_own = lax.optimization_barrier((query, own))
-    late = lax.ppermute(late_own, "ctx", chip_shift(2))
     up = stack_up(up, up_other)
     scores = {0: chip_scores(0, limits, query, up, kv)}
-    far, scores[0] = lax.optimization_barrier((far, scores[0]))
-    kv_far = {d: project_kv_far(far[d], weights, weights_other) for d in (1, 3)}
-    for d in (1, 3):
-        mine, theirs = kv_far[d]
-        kv_far[d] = (mine, lax.ppermute(theirs, "ctx", CORE))
-    for d in (1, 3):
-        scores[d] = chip_scores(d, limits, query, up, *kv_far[d])
+    far, kv2, scores[0] = lax.optimization_barrier((far, kv2, scores[0]))
+    late = lax.ppermute(far[1], "ctx", chip_shift(1))
+    mine, theirs = project_kv_far(far[1], far[3], weights, weights_other)
+    theirs = lax.ppermute(theirs, "ctx", CORE)
+    for i, d in enumerate((1, 3)):
+        scores[d] = chip_scores(d, limits, query, up, mine, theirs, part=i)
     scores[2] = chip_scores(2, limits, query, up, kv2)
     factors = softmax_factors([scores[d][2] for d in range(CHIPS)])
     terms, grad_scores = {}, {}

time: 85.1 us -> 79.6 us (0.935)
  waiting for transfers between devices: 23 us -> 18.1 us
    ppermute x2, waiting for transfers between devices: 10.3 us -> 3.64 us  [shards(): far = {d: lax.ppermute(own, 'ctx', chip_shift(d)) for d in (1, 3)}]
    ppermute x1, waiting for transfers between devices: 0.01 us -> 1.59 us  [shards(): kv2 = lax.ppermute(kv, 'ctx', chip_shift(2))]
    ppermute x3 -> x2, starting transfers between devices: 2.58 us -> 1.23 us  [the longest x1 1.14 us: shards(): late = lax.ppermute(far[1], 'ctx', chip_shift(1))]
    ppermute x3, starting transfers between devices: 4.83 us -> 5.96 us  [shards(): lax.ppermute(terms[d], 'ctx', chip_shift(CHIPS - d))]
    pallas_call x6 -> x5, Pallas kernels: 3.64 us -> 3.47 us  [the longest x4 2.89 us: chip_scores(): pl.pallas_call(functools.partial(scores_kernel, d, part), in_specs=[WHOLE...]
  transfers between devices with their start and end apart: 22 -> 21, of which waited for: 11 -> 12; matrix products, arithmetic and copies ran while one was open for 0% -> 0% of each run, Pallas kernels for 22% -> 23%
where the time goes in v12:
time: 79.6 us; the launch traced here: 79.4 us
  starting transfers between devices  22.3 us (28%)
  Pallas kernels  19.4 us (24%)
  blocking collectives  18.8 us (24%)
  waiting for transfers between devices  18.1 us (23%)
  between operations  0.87 us (1%)
    all_to_all x1, blocking collectives, shards(): lax.all_to_all(y_sum, 'dp', 0, 0, tiled=True, axis_index_groups=Z_GROUPS)  18.8 us
    ppermute x3, waiting for transfers between devices, shards(): lax.ppermute(packed[d], 'ctx', chip_shift(d))  6.09 us
    ppermute x3, starting transfers between devices, shards(): lax.ppermute(terms[d], 'ctx', chip_shift(CHIPS - d))  5.96 us
    pallas_call x1, Pallas kernels, input_grad(): pl.pallas_call(input_kernel, in_specs=[WHOLE] * 4 + [STAY] * 3, out_specs...  4.82 us
    ppermute x3, starting transfers between devices, shards(): lax.ppermute(terms[d], 'dp', y_shift(d))  4.56 us
    ppermute x3, starting transfers between devices, shards(): lax.ppermute(packed[d], 'ctx', chip_shift(d))  3.83 us
    ppermute x2, waiting for transfers between devices, shards(): far = {d: lax.ppermute(own, 'ctx', chip_shift(d)) for d in (1, 3)}  3.64 us
    ppermute x3, waiting for transfers between devices, shards(): lax.ppermute(terms[d], 'ctx', chip_shift(CHIPS - d))  3.37 us
  transfers between devices with their start and end apart: 21, of which 12 were waited for; matrix products, arithmetic and copies ran while one was open for 0% of the time, Pallas kernels for 23%

profile of v12, /device:TPU:8, one launch (start us, length us, event | category | flops | bytes accessed | tf_op | source)
XLA Modules:
  0.0 79.4 jit_solution(5455922709970093895)
XLA Ops:
  0.6 0.1 collective-permute-start.2
  0.7 0.5 collective-permute-start.4
  1.2 1.5 %collective-permute-start = (bf16[128,1536]{1,0:T(8,128)(2,1)}, bf16[128,1536]{1,0:T(8,128)(2,1)S(1)}, u32[]{:S(2)}, u32[]{:S(2)}) collective-permute-start(bf16[128,1536]{1,0:T(8,128)(2,1)} %bitcast.7), channel_id=1, source_target_pairs={{0,64},{32,96},{64,128},{96,160},{128,192},{160,224},{192,0},{224,... | collective-permute-start | bytes 1179656 | tf_op jit(solution)/shard_map/ppermute | solution.py:564
  2.7 1.7 %collective-permute-start.1 = (bf16[128,1536]{1,0:T(8,128)(2,1)}, bf16[128,1536]{1,0:T(8,128)(2,1)S(1)}, u32[]{:S(2)}, u32[]{:S(2)}) collective-permute-start(bf16[128,1536]{1,0:T(8,128)(2,1)} %bitcast.8), channel_id=1, source_target_pairs={{0,192},{32,224},{64,0},{96,32},{128,64},{160,96},{192,128},{224,1... | collective-permute-start | bytes 1179656 | tf_op jit(solution)/shard_map/ppermute | solution.py:564
  4.5 0.0 collective-permute-start.3
  4.5 1.6 %project_kv_own.1 = (bf16[1536,256]{1,0:T(8,128)(2,1)S(1)}, bf16[128,256]{1,0:T(8,128)(2,1)S(1)}) custom-call(bf16[128,1536]{1,0:T(8,128)(2,1)} %bitcast.9, bf16[1536,256]{1,0:T(8,128)(2,1)} %w_key.5, bf16[1536,256]{1,0:T(8,128)(2,1)} %w_value.5), custom_call_target="tpu_custom_call" | custom-call | flops 1 | bytes 1 | tf_op jit(solution)/shard_map/project_kv_own/pallas_call | solution.py:100
  6.1 0.0 copy-start
  6.1 0.0 collective-permute-done.3.mask_other
  6.1 0.0 collective-permute-done.2.other
  6.1 0.3 project_kv.1.refs_0_
  6.4 1.9 %collective-permute-start.5 = (bf16[256,256]{1,0:T(8,128)(2,1)S(1)}, bf16[256,256]{1,0:T(8,128)(2,1)S(1)}, u32[]{:S(2)}, u32[]{:S(2)}) collective-permute-start(bf16[256,256]{1,0:T(8,128)(2,1)S(1)} %project_kv.1.refs_0_), channel_id=1, source_target_pairs={{0,128},{32,160},{64,192},{96,224},{128,0},{160,32},{192,64},{224,... | collective-permute-start | bytes 393224 | tf_op jit(solution)/shard_map/ppermute | solution.py:563
  8.3 0.1 stack_up.1.up
  8.4 3.2 %project_query.1 = (bf16[1536,128]{1,0:T(8,128)(2,1)S(1)}, s32[16,256]{1,0:T(8,128)S(1)}, bf16[1536,256]{1,0:T(8,128)(2,1)S(1)}) custom-call(bf16[128,1536]{1,0:T(8,128)(2,1)S(1)} %bitcast.10, bf16[128,1536]{1,0:T(8,128)(2,1)S(1)} %collective-permute-done.2.other, bf16[1536,1536]{1,0:T(8,128)(2,1)} %w_query.3, bf16[1536,256]{1,0:T(8,128)(2,1)} %w_key.5, ...), custom_call_target="tpu_custom_call" | custom-call | flops 1 | bytes 1 | tf_op jit(solution)/shard_map/project_query/pallas_call | solution.py:221
  11.6 0.7 chip_scores_0.1
  12.3 1.4 %collective-permute-done.far1 = bf16[128,1536]{1,0:T(8,128)(2,1)S(1)} collective-permute-done((bf16[128,1536]{1,0:T(8,128)(2,1)}, bf16[128,1536]{1,0:T(8,128)(2,1)S(1)}, u32[]{:S(2)}, u32[]{:S(2)}) %collective-permute-start) | collective-permute-done | bytes 393248 | tf_op jit(solution)/shard_map/ppermute | solution.py:564
  13.8 2.2 %collective-permute-done.1.far3 = bf16[128,1536]{1,0:T(8,128)(2,1)S(1)} collective-permute-done((bf16[128,1536]{1,0:T(8,128)(2,1)}, bf16[128,1536]{1,0:T(8,128)(2,1)S(1)}, u32[]{:S(2)}, u32[]{:S(2)}) %collective-permute-start.1) | collective-permute-done | bytes 393248 | tf_op jit(solution)/shard_map/ppermute | solution.py:564
  16.0 1.6 %collective-permute-done.5.refs_0_ = bf16[256,256]{1,0:T(8,128)(2,1)S(1)} collective-permute-done((bf16[256,256]{1,0:T(8,128)(2,1)S(1)}, bf16[256,256]{1,0:T(8,128)(2,1)S(1)}, u32[]{:S(2)}, u32[]{:S(2)}) %collective-permute-start.5) | collective-permute-done | bytes 131104 | tf_op jit(solution)/shard_map/ppermute | solution.py:563
  17.6 1.1 %collective-permute-start.6 = (bf16[128,1536]{1,0:T(8,128)(2,1)S(1)}, bf16[128,1536]{1,0:T(8,128)(2,1)S(1)}, u32[]{:S(2)}, u32[]{:S(2)}) collective-permute-start(bf16[128,1536]{1,0:T(8,128)(2,1)S(1)} %collective-permute-done.far1), channel_id=1, source_target_pairs={{0,64},{32,96},{64,128},{96,160},{128,192},{160,224},{192,0},{224,... | collective-permute-start | bytes 1179656 | tf_op jit(solution)/shard_map/ppermute | solution.py:572
  18.7 0.6 project_kv_far.1
  19.3 0.1 collective-permute-start.7
  19.4 0.7 chip_scores_2.1
  20.1 0.6 collective-permute-done.7.refs_1_
  20.7 0.7 chip_scores_3.1
  21.5 0.7 chip_scores_1.1
  22.2 0.6 chip_terms_2.1
  22.8 2.4 %collective-permute-start.10 = (bf16[256,256]{1,0:T(8,128)(2,1)S(1)}, bf16[256,256]{1,0:T(8,128)(2,1)S(1)}, u32[]{:S(2)}, u32[]{:S(2)}) collective-permute-start(bf16[256,256]{1,0:T(8,128)(2,1)S(1)} %get-tuple-element.98), channel_id=1, source_target_pairs={{0,128},{32,160},{64,192},{96,224},{128,0},{160,32},{192,64},{224,... | collective-permute-start | bytes 393224 | tf_op jit(solution)/shard_map/ppermute | solution.py:582
  25.2 0.6 chip_terms_3.1
  25.8 0.9 %collective-permute-start.9 = (bf16[256,256]{1,0:T(8,128)(2,1)S(1)}, bf16[256,256]{1,0:T(8,128)(2,1)S(1)}, u32[]{:S(2)}, u32[]{:S(2)}) collective-permute-start(bf16[256,256]{1,0:T(8,128)(2,1)S(1)} %get-tuple-element.95), channel_id=1, source_target_pairs={{0,64},{32,96},{64,128},{96,160},{128,192},{160,224},{192,0},{224,... | collective-permute-start | bytes 393224 | tf_op jit(solution)/shard_map/ppermute | solution.py:582
  26.8 0.6 chip_terms_1.1
  27.4 2.7 %collective-permute-start.8 = (bf16[256,256]{1,0:T(8,128)(2,1)S(1)}, bf16[256,256]{1,0:T(8,128)(2,1)S(1)}, u32[]{:S(2)}, u32[]{:S(2)}) collective-permute-start(bf16[256,256]{1,0:T(8,128)(2,1)S(1)} %get-tuple-element.92), channel_id=1, source_target_pairs={{0,192},{32,224},{64,0},{96,32},{128,64},{160,96},{192,128},{224,1... | collective-permute-start | bytes 393224 | tf_op jit(solution)/shard_map/ppermute | solution.py:582
  30.0 0.6 chip_terms_0.1
  30.6 0.7 query_grad.1
  31.3 1.7 %collective-permute-done.10.d = bf16[256,256]{1,0:T(8,128)(2,1)S(1)} collective-permute-done((bf16[256,256]{1,0:T(8,128)(2,1)S(1)}, bf16[256,256]{1,0:T(8,128)(2,1)S(1)}, u32[]{:S(2)}, u32[]{:S(2)}) %collective-permute-start.10) | collective-permute-done | bytes 131104 | tf_op jit(solution)/shard_map/ppermute | solution.py:582
  33.0 1.7 %collective-permute-done.9.c = bf16[256,256]{1,0:T(8,128)(2,1)S(1)} collective-permute-done((bf16[256,256]{1,0:T(8,128)(2,1)S(1)}, bf16[256,256]{1,0:T(8,128)(2,1)S(1)}, u32[]{:S(2)}, u32[]{:S(2)}) %collective-permute-start.9) | collective-permute-done | bytes 131104 | tf_op jit(solution)/shard_map/ppermute | solution.py:582
  34.7 0.0 collective-permute-done.6.far2
  34.7 0.1 sum_four.2.dkv
  34.7 0.1 collective-permute-start.12
  34.8 0.5 collective-permute-start.11
  35.3 0.5 transpose_tokens.1.tokens_t
  35.8 0.4 collective-permute-done.12.dkv_other
  36.2 0.2 collective-permute-done.11.middle_other
  36.4 0.1 pack.1
  36.5 0.4 collective-permute-start.13
  36.8 0.6 collective-permute-start.14
  37.4 1.8 %collective-permute-start.15 = (bf16[256,256]{1,0:T(8,128)(2,1)S(1)}, bf16[256,256]{1,0:T(8,128)(2,1)S(1)}, u32[]{:S(2)}, u32[]{:S(2)}) collective-permute-start(bf16[256,256]{1,0:T(8,128)(2,1)S(1)} %get-tuple-element.127), channel_id=1, source_target_pairs={{0,64},{32,96},{64,128},{96,160},{128,192},{160,224},{192,0},{224,... | collective-permute-start | bytes 393224 | tf_op jit(solution)/shard_map/ppermute | solution.py:598
  39.2 1.4 %collective-permute-start.16 = (bf16[256,256]{1,0:T(8,128)(2,1)S(1)}, bf16[256,256]{1,0:T(8,128)(2,1)S(1)}, u32[]{:S(2)}, u32[]{:S(2)}) collective-permute-start(bf16[256,256]{1,0:T(8,128)(2,1)S(1)} %get-tuple-element.128), channel_id=1, source_target_pairs={{0,192},{32,224},{64,0},{96,32},{128,64},{160,96},{192,128},{224,1... | collective-permute-start | bytes 393224 | tf_op jit(solution)/shard_map/ppermute | solution.py:598
  40.7 4.0 %collective-permute-done.14.b = bf16[256,256]{1,0:T(8,128)(2,1)S(1)} collective-permute-done((bf16[256,256]{1,0:T(8,128)(2,1)S(1)}, bf16[256,256]{1,0:T(8,128)(2,1)S(1)}, u32[]{:S(2)}, u32[]{:S(2)}) %collective-permute-start.14) | collective-permute-done | bytes 131104 | tf_op jit(solution)/shard_map/ppermute | solution.py:598
  44.7 2.0 %collective-permute-done.15.c = bf16[256,256]{1,0:T(8,128)(2,1)S(1)} collective-permute-done((bf16[256,256]{1,0:T(8,128)(2,1)S(1)}, bf16[256,256]{1,0:T(8,128)(2,1)S(1)}, u32[]{:S(2)}, u32[]{:S(2)}) %collective-permute-start.15) | collective-permute-done | bytes 131104 | tf_op jit(solution)/shard_map/ppermute | solution.py:598
  46.8 0.0 collective-permute-done.16.d
  46.8 0.0 collective-permute-done.13.other_t
  46.8 0.4 weight_grad_2.1
  47.2 2.4 %collective-permute-start.19 = (bf16[384,256]{1,0:T(8,128)(2,1)S(1)}, bf16[384,256]{1,0:T(8,128)(2,1)S(1)}, u32[]{:S(2)}, u32[]{:S(2)}) collective-permute-start(bf16[384,256]{1,0:T(8,128)(2,1)S(1)} %weight_grad_2.1), channel_id=1, source_target_pairs={{0,16},{1,17},{2,18},{3,19},{4,20},{5,21},{6,22},{7,23},{8,24},{9,... | collective-permute-start | bytes 589832 | tf_op jit(solution)/shard_map/ppermute | solution.py:601
  49.5 0.4 weight_grad_3.1
  49.9 1.4 %collective-permute-start.18 = (bf16[384,256]{1,0:T(8,128)(2,1)S(1)}, bf16[384,256]{1,0:T(8,128)(2,1)S(1)}, u32[]{:S(2)}, u32[]{:S(2)}) collective-permute-start(bf16[384,256]{1,0:T(8,128)(2,1)S(1)} %weight_grad_3.1), channel_id=1, source_target_pairs={{0,24},{1,25},{2,26},{3,27},{4,28},{5,29},{6,30},{7,31},{8,0},{9,1... | collective-permute-start | bytes 589832 | tf_op jit(solution)/shard_map/ppermute | solution.py:601
  51.3 0.4 weight_grad_1.1
  51.7 0.8 collective-permute-start.17
  52.5 4.8 %input_grad.1 = bf16[128,1536]{1,0:T(8,128)(2,1)} custom-call(bf16[256,768]{1,0:T(8,128)(2,1)S(1)} %get-tuple-element.117.dq, bf16[128,768]{1,0:T(8,128)(2,1)S(1)} %collective-permute-done.20.dq_other, bf16[256,256]{1,0:T(8,128)(2,1)S(1)} %sum_four.2.dkv, bf16[256,256]{1,0:T(8,128)(2,1)S(1)} %collective-permute-done.12.dkv_other, ...), custom_call_target="tpu_custom_call" | custom-call | flops 1 | bytes 1 | tf_op jit(solution)/shard_map/input_grad/pallas_call | solution.py:518
  57.3 0.4 weight_grad_0.1.a
  57.7 0.0 collective-permute-done.19.d
  57.7 2.1 %collective-permute-done.18.c = bf16[384,256]{1,0:T(8,128)(2,1)S(1)} collective-permute-done((bf16[384,256]{1,0:T(8,128)(2,1)S(1)}, bf16[384,256]{1,0:T(8,128)(2,1)S(1)}, u32[]{:S(2)}, u32[]{:S(2)}) %collective-permute-start.18) | collective-permute-done | bytes 196640 | tf_op jit(solution)/shard_map/ppermute | solution.py:601
  59.8 0.1 collective-permute-done.17.b
  59.9 0.1 sum_four.3
  60.0 18.8 %all_to_all.11 = bf16[8,48,256]{2,1,0:T(8,128)(2,1)S(1)} all-to-all(bf16[8,48,256]{2,1,0:T(8,128)(2,1)S(1)} %bitcast.12), channel_id=1, replica_groups={{0,1,2,3,4,5,6,7},{8,9,10,11,12,13,14,15},{16,17,18,19,20,21,22,23},{24..., dimensions={0} | all-to-all | bytes 393216 | tf_op jit(solution)/shard_map/all_to_all | solution.py:607
  78.8 0.6 final_sum.1
  (8 shorter events, 0.0 us)
Async XLA Ops:
  0.6 5.5 %collective-permute-start.2 = (bf16[128,1536]{1,0:T(8,128)(2,1)}, bf16[128,1536]{1,0:T(8,128)(2,1)S(1)}, u32[]{:S(2)}, u32[]{:S(2)}) collective-permute-start(bf16[128,1536]{1,0:T(8,128)(2,1)} %bitcast.6), channel_id=1, source_target_pairs={{0,32},{32,0},{64,96},{96,64},{128,160},{160,128},{192,224},{224,1... | collective-permute-start | bytes 1179656 | tf_op jit(solution)/shard_map/ppermute | solution.py:555
  0.7 5.4 %collective-permute-start.4 = (bf16[128,1536]{1,0:T(8,128)(2,1)}, bf16[128,1536]{1,0:T(8,128)(2,1)S(1)}, u32[]{:S(2)}, u32[]{:S(2)}) collective-permute-start(bf16[128,1536]{1,0:T(8,128)(2,1)} %bitcast.14), channel_id=1, source_target_pairs={{0,32},{32,0},{64,96},{96,64},{128,160},{160,128},{192,224},{224,1... | collective-permute-start | bytes 1179656 | tf_op jit(solution)/shard_map/ppermute | solution.py:556
  1.2 12.5 %collective-permute-start = (bf16[128,1536]{1,0:T(8,128)(2,1)}, bf16[128,1536]{1,0:T(8,128)(2,1)S(1)}, u32[]{:S(2)}, u32[]{:S(2)}) collective-permute-start(bf16[128,1536]{1,0:T(8,128)(2,1)} %bitcast.7), channel_id=1, source_target_pairs={{0,64},{32,96},{64,128},{96,160},{128,192},{160,224},{192,0},{224,... | collective-permute-start | bytes 1179656 | tf_op jit(solution)/shard_map/ppermute | solution.py:564
  2.7 13.3 %collective-permute-start.1 = (bf16[128,1536]{1,0:T(8,128)(2,1)}, bf16[128,1536]{1,0:T(8,128)(2,1)S(1)}, u32[]{:S(2)}, u32[]{:S(2)}) collective-permute-start(bf16[128,1536]{1,0:T(8,128)(2,1)} %bitcast.8), channel_id=1, source_target_pairs={{0,192},{32,224},{64,0},{96,32},{128,64},{160,96},{192,128},{224,1... | collective-permute-start | bytes 1179656 | tf_op jit(solution)/shard_map/ppermute | solution.py:564
  4.5 3.8 %copy-start.1 = (bf16[1,128,1536]{2,1,0:T(8,128)(2,1)S(1)}, bf16[1,128,1536]{2,1,0:T(8,128)(2,1)}, u32[]{:S(2)}) copy-start(bf16[1,128,1536]{2,1,0:T(8,128)(2,1)} %param.8) | copy-start | bytes 1179652
  4.5 1.6 %collective-permute-start.3 = (s32[1,8]{1,0:T(1,128)}, s32[1,8]{1,0:T(1,128)S(1)}, u32[]{:S(2)}, u32[]{:S(2)}) collective-permute-start(s32[1,8]{1,0:T(1,128)} %bitcast.17), channel_id=1, source_target_pairs={{0,32},{32,0},{64,96},{96,64},{128,160},{160,128},{192,224},{224,1... | collective-permute-start | bytes 104 | tf_op jit(solution)/shard_map/ppermute | solution.py:557
  6.1 2.3 %copy-start = (bf16[1,128,1536]{2,1,0:T(8,128)(2,1)S(1)}, bf16[1,128,1536]{2,1,0:T(8,128)(2,1)}, u32[]{:S(2)}) copy-start(bf16[1,128,1536]{2,1,0:T(8,128)(2,1)} %param.7) | copy-start | bytes 1179652
  6.4 11.2 %collective-permute-start.5 = (bf16[256,256]{1,0:T(8,128)(2,1)S(1)}, bf16[256,256]{1,0:T(8,128)(2,1)S(1)}, u32[]{:S(2)}, u32[]{:S(2)}) collective-permute-start(bf16[256,256]{1,0:T(8,128)(2,1)S(1)} %project_kv.1.refs_0_), channel_id=1, source_target_pairs={{0,128},{32,160},{64,192},{96,224},{128,0},{160,32},{192,64},{224,... | collective-permute-start | bytes 393224 | tf_op jit(solution)/shard_map/ppermute | solution.py:563
  17.6 17.1 %collective-permute-start.6 = (bf16[128,1536]{1,0:T(8,128)(2,1)S(1)}, bf16[128,1536]{1,0:T(8,128)(2,1)S(1)}, u32[]{:S(2)}, u32[]{:S(2)}) collective-permute-start(bf16[128,1536]{1,0:T(8,128)(2,1)S(1)} %collective-permute-done.far1), channel_id=1, source_target_pairs={{0,64},{32,96},{64,128},{96,160},{128,192},{160,224},{192,0},{224,... | collective-permute-start | bytes 1179656 | tf_op jit(solution)/shard_map/ppermute | solution.py:572
  19.3 1.4 %collective-permute-start.7 = (bf16[256,256]{1,0:T(8,128)(2,1)S(1)}, bf16[256,256]{1,0:T(8,128)(2,1)S(1)}, u32[]{:S(2)}, u32[]{:S(2)}) collective-permute-start(bf16[256,256]{1,0:T(8,128)(2,1)S(1)} %get-tuple-element.84), channel_id=1, source_target_pairs={{0,32},{32,0},{64,96},{96,64},{128,160},{160,128},{192,224},{224,1... | collective-permute-start | bytes 393224 | tf_op jit(solution)/shard_map/ppermute | solution.py:574
  22.8 10.1 %collective-permute-start.10 = (bf16[256,256]{1,0:T(8,128)(2,1)S(1)}, bf16[256,256]{1,0:T(8,128)(2,1)S(1)}, u32[]{:S(2)}, u32[]{:S(2)}) collective-permute-start(bf16[256,256]{1,0:T(8,128)(2,1)S(1)} %get-tuple-element.98), channel_id=1, source_target_pairs={{0,128},{32,160},{64,192},{96,224},{128,0},{160,32},{192,64},{224,... | collective-permute-start | bytes 393224 | tf_op jit(solution)/shard_map/ppermute | solution.py:582
  25.8 8.8 %collective-permute-start.9 = (bf16[256,256]{1,0:T(8,128)(2,1)S(1)}, bf16[256,256]{1,0:T(8,128)(2,1)S(1)}, u32[]{:S(2)}, u32[]{:S(2)}) collective-permute-start(bf16[256,256]{1,0:T(8,128)(2,1)S(1)} %get-tuple-element.95), channel_id=1, source_target_pairs={{0,64},{32,96},{64,128},{96,160},{128,192},{160,224},{192,0},{224,... | collective-permute-start | bytes 393224 | tf_op jit(solution)/shard_map/ppermute | solution.py:582
  27.4 7.3 %collective-permute-start.8 = (bf16[256,256]{1,0:T(8,128)(2,1)S(1)}, bf16[256,256]{1,0:T(8,128)(2,1)S(1)}, u32[]{:S(2)}, u32[]{:S(2)}) collective-permute-start(bf16[256,256]{1,0:T(8,128)(2,1)S(1)} %get-tuple-element.92), channel_id=1, source_target_pairs={{0,192},{32,224},{64,0},{96,32},{128,64},{160,96},{192,128},{224,1... | collective-permute-start | bytes 393224 | tf_op jit(solution)/shard_map/ppermute | solution.py:582
  34.7 1.4 %collective-permute-start.12 = (bf16[256,256]{1,0:T(8,128)(2,1)S(1)}, bf16[256,256]{1,0:T(8,128)(2,1)S(1)}, u32[]{:S(2)}, u32[]{:S(2)}) collective-permute-start(bf16[256,256]{1,0:T(8,128)(2,1)S(1)} %sum_four.2.dkv), channel_id=1, source_target_pairs={{0,32},{32,0},{64,96},{96,64},{128,160},{160,128},{192,224},{224,1... | collective-permute-start | bytes 393224 | tf_op jit(solution)/shard_map/ppermute | solution.py:590
  34.8 1.5 %collective-permute-start.11 = (bf16[256,256]{1,0:T(8,128)(2,1)S(1)}, bf16[256,256]{1,0:T(8,128)(2,1)S(1)}, u32[]{:S(2)}, u32[]{:S(2)}) collective-permute-start(bf16[256,256]{1,0:T(8,128)(2,1)S(1)} %get-tuple-element.118), channel_id=1, source_target_pairs={{0,32},{32,0},{64,96},{96,64},{128,160},{160,128},{192,224},{224,1... | collective-permute-start | bytes 393224 | tf_op jit(solution)/shard_map/ppermute | solution.py:588
  36.5 10.3 %collective-permute-start.13 = (bf16[1536,512]{1,0:T(8,128)(2,1)S(1)}, bf16[1536,512]{1,0:T(8,128)(2,1)S(1)}, u32[]{:S(2)}, u32[]{:S(2)}) collective-permute-start(bf16[1536,512]{1,0:T(8,128)(2,1)S(1)} %transpose_tokens.1.tokens_t), channel_id=1, source_target_pairs={{0,32},{32,0},{64,96},{96,64},{128,160},{160,128},{192,224},{224,1... | collective-permute-start | bytes 4718600 | tf_op jit(solution)/shard_map/ppermute | solution.py:597
  36.8 7.9 %collective-permute-start.14 = (bf16[256,256]{1,0:T(8,128)(2,1)S(1)}, bf16[256,256]{1,0:T(8,128)(2,1)S(1)}, u32[]{:S(2)}, u32[]{:S(2)}) collective-permute-start(bf16[256,256]{1,0:T(8,128)(2,1)S(1)} %get-tuple-element.126), channel_id=1, source_target_pairs={{0,128},{32,160},{64,192},{96,224},{128,0},{160,32},{192,64},{224,... | collective-permute-start | bytes 393224 | tf_op jit(solution)/shard_map/ppermute | solution.py:598
  37.4 9.3 %collective-permute-start.15 = (bf16[256,256]{1,0:T(8,128)(2,1)S(1)}, bf16[256,256]{1,0:T(8,128)(2,1)S(1)}, u32[]{:S(2)}, u32[]{:S(2)}) collective-permute-start(bf16[256,256]{1,0:T(8,128)(2,1)S(1)} %get-tuple-element.127), channel_id=1, source_target_pairs={{0,64},{32,96},{64,128},{96,160},{128,192},{160,224},{192,0},{224,... | collective-permute-start | bytes 393224 | tf_op jit(solution)/shard_map/ppermute | solution.py:598
  39.2 7.5 %collective-permute-start.16 = (bf16[256,256]{1,0:T(8,128)(2,1)S(1)}, bf16[256,256]{1,0:T(8,128)(2,1)S(1)}, u32[]{:S(2)}, u32[]{:S(2)}) collective-permute-start(bf16[256,256]{1,0:T(8,128)(2,1)S(1)} %get-tuple-element.128), channel_id=1, source_target_pairs={{0,192},{32,224},{64,0},{96,32},{128,64},{160,96},{192,128},{224,1... | collective-permute-start | bytes 393224 | tf_op jit(solution)/shard_map/ppermute | solution.py:598
  40.7 11.8 %collective-permute-start.20 = (bf16[128,768]{1,0:T(8,128)(2,1)S(1)}, bf16[128,768]{1,0:T(8,128)(2,1)S(1)}, u32[]{:S(2)}, u32[]{:S(2)}) collective-permute-start(bf16[128,768]{1,0:T(8,128)(2,1)S(1)} %get-tuple-element.129), channel_id=1, source_target_pairs={{0,32},{32,0},{64,96},{96,64},{128,160},{160,128},{192,224},{224,1... | collective-permute-start | bytes 589832 | tf_op jit(solution)/shard_map/ppermute | solution.py:596
  47.2 10.5 %collective-permute-start.19 = (bf16[384,256]{1,0:T(8,128)(2,1)S(1)}, bf16[384,256]{1,0:T(8,128)(2,1)S(1)}, u32[]{:S(2)}, u32[]{:S(2)}) collective-permute-start(bf16[384,256]{1,0:T(8,128)(2,1)S(1)} %weight_grad_2.1), channel_id=1, source_target_pairs={{0,16},{1,17},{2,18},{3,19},{4,20},{5,21},{6,22},{7,23},{8,24},{9,... | collective-permute-start | bytes 589832 | tf_op jit(solution)/shard_map/ppermute | solution.py:601
  49.9 9.9 %collective-permute-start.18 = (bf16[384,256]{1,0:T(8,128)(2,1)S(1)}, bf16[384,256]{1,0:T(8,128)(2,1)S(1)}, u32[]{:S(2)}, u32[]{:S(2)}) collective-permute-start(bf16[384,256]{1,0:T(8,128)(2,1)S(1)} %weight_grad_3.1), channel_id=1, source_target_pairs={{0,24},{1,25},{2,26},{3,27},{4,28},{5,29},{6,30},{7,31},{8,0},{9,1... | collective-permute-start | bytes 589832 | tf_op jit(solution)/shard_map/ppermute | solution.py:601
  51.7 8.2 %collective-permute-start.17 = (bf16[384,256]{1,0:T(8,128)(2,1)S(1)}, bf16[384,256]{1,0:T(8,128)(2,1)S(1)}, u32[]{:S(2)}, u32[]{:S(2)}) collective-permute-start(bf16[384,256]{1,0:T(8,128)(2,1)S(1)} %weight_grad_1.1), channel_id=1, source_target_pairs={{0,8},{1,9},{2,10},{3,11},{4,12},{5,13},{6,14},{7,15},{8,16},{9,17... | collective-permute-start | bytes 589832 | tf_op jit(solution)/shard_map/ppermute | solution.py:601

commit v13 on v12

--- a/solution.py
+++ b/solution.py
@@ -386,6 +386,24 @@
     out[...] = total.astype(out.dtype)
 
 
+def join_kernel(a, b, c, d, beside, out):
+    total = (a[...] + b[...].astype(F32)) + (c[...].astype(F32) + d[...].astype(F32))
+    out[:, :256] = total.astype(out.dtype)
+    out[:, 256:] = beside[...]
+
+
+def sum_join(a, b, c, d, beside):
+    return pl.pallas_call(
+        join_kernel,
+        in_specs=[WHOLE] * 5,
+        out_specs=WHOLE,
+        out_shape=jax.ShapeDtypeStruct((256, 512), BF),
+        compiler_params=PARAMS,
+        cost_estimate=cost(4 * a.size, 12 * a.size),
+        name="sum_join",
+    )(a, b, c, d, beside)
+
+
 def sum_four(a, b, c, d):
     return pl.pallas_call(
         sum_kernel,
@@ -398,7 +416,7 @@
     )(a, b, c, d)
 
 
-def pack_kernel(dq, middle_other, dkv, dkv_other, *outs):
+def pack_kernel(dq, joined, joined_other, *outs):
     my_chip, my_core, _ = position()
     for core in range(2):
         own_part = slice(core * HD, (core + 1) * HD)
@@ -409,28 +427,28 @@
                 for d, out in enumerate(outs):
                     target = (chip + d) % CHIPS
                     if target == 3:
-                        out[:, own_part] = dkv[:, own_part]
+                        out[:, own_part] = joined[:, own_part]
                         theirs = slice((1 - core) * HD, (2 - core) * HD)
-                        out[:TILE, theirs] = dkv_other[TILE:, own_part]
-                        out[TILE:, theirs] = dkv_other[:TILE, own_part]
+                        out[:TILE, theirs] = joined_other[TILE:, own_part]
+                        out[TILE:, theirs] = joined_other[:TILE, own_part]
                     elif target == 2 - 2 * core:
-                        out[:TILE] = middle_other[TILE:]
-                        out[TILE:] = middle_other[:TILE]
+                        out[:TILE] = joined_other[TILE:, 256:]
+                        out[TILE:] = joined_other[:TILE, 256:]
                     else:
                         first = target == core
                         out[...] = dq[:, 0:256] if first else dq[:, 512:768]
 
 
-def pack(dq, middle_other, dkv, dkv_other):
+def pack(dq, joined, joined_other):
     return pl.pallas_call(
         pack_kernel,
-        in_specs=[WHOLE] * 4,
+        in_specs=[WHOLE] * 3,
         out_specs=[WHOLE] * 4,
         out_shape=[jax.ShapeDtypeStruct((256, 256), BF)] * 4,
         compiler_params=PARAMS,
         cost_estimate=cost(0, 4 << 19),
         name="pack",
-    )(dq, middle_other, dkv, dkv_other)
+    )(dq, joined, joined_other)
 
 
 def transpose_kernel(own, far2, far1, far3, out):
@@ -531,25 +549,6 @@
     )(dq, dq_other, dkv, dkv_other, w_query, w_key, w_value)
 
 
-def final_kernel(parts, out):
-    total = parts[0:48].astype(F32)
-    for z in range(1, ZS):
-        total += parts[z * 48 : (z + 1) * 48].astype(F32)
-    out[...] = total
-
-
-def final_sum(parts):
-    return pl.pallas_call(
-        final_kernel,
-        in_specs=[WHOLE],
-        out_specs=WHOLE,
-        out_shape=jax.ShapeDtypeStruct((48, 256), F32),
-        compiler_params=PARAMS,
-        cost_estimate=cost(parts.size, 2 * parts.size),
-        name="final_sum",
-    )(parts)
-
-
 def shards(tokens, grad_heads, tile_mask, segments, w_query, w_key, w_value):
     own, up = tokens[0], grad_heads[0]
     other = lax.ppermute(own, "ctx", CORE)
@@ -585,10 +584,9 @@
         [scores[d][3] for d in range(CHIPS)], [grad_scores[d] for d in range(CHIPS)]
     )
     late, back, middle = lax.optimization_barrier((late, back, middle))
-    middle_other = lax.ppermute(middle, "ctx", CORE)
-    dkv = sum_four(terms[0], *back)
+    dkv = sum_join(terms[0], *back, middle)
     dkv_other = lax.ppermute(dkv, "ctx", CORE)
-    packed = pack(dq, middle_other, dkv, dkv_other)
+    packed = pack(dq, dkv, dkv_other)
 
     far, dkv = lax.optimization_barrier((far, dkv))
     tokens_t = transpose([own, late, far[1], far[3]])
@@ -605,7 +603,7 @@
     y_parts, grad_tokens = lax.optimization_barrier((y_parts, grad_tokens))
     y_sum = sum_four(*y_parts)
     z_parts = lax.all_to_all(y_sum, "dp", 0, 0, tiled=True, axis_index_groups=Z_GROUPS)
-    grad_projection = final_sum(z_parts)
+    grad_projection = jnp.sum(z_parts.reshape(ZS, 48, 256).astype(F32), axis=0)
     return grad_tokens[None], grad_projection
 
 

time: 79.6 us -> 79.7 us (level)
  transfers between devices with their start and end apart: 21 -> 20, of which waited for: 12 -> 11; matrix products, arithmetic and copies ran while one was open for 0% -> 0% of each run, Pallas kernels for 23% -> 23%
where the time goes in v13:
time: 79.7 us; the launch traced here: 79.5 us
  starting transfers between devices  21.6 us (27%)
  waiting for transfers between devices  18.8 us (24%)
  blocking collectives  18.8 us (24%)
  Pallas kernels  18.7 us (23%)
  between operations  0.87 us (1%)
    all_to_all x1, blocking collectives, shards(): lax.all_to_all(y_sum, 'dp', 0, 0, tiled=True, axis_index_groups=Z_GROUPS)  18.8 us
    ppermute x3, waiting for transfers between devices, shards(): lax.ppermute(packed[d], 'ctx', chip_shift(d))  6.24 us
    ppermute x3, starting transfers between devices, shards(): lax.ppermute(terms[d], 'ctx', chip_shift(CHIPS - d))  5.96 us
    pallas_call x1, Pallas kernels, input_grad(): pl.pallas_call(input_kernel, in_specs=[WHOLE] * 4 + [STAY] * 3, out_specs...  4.82 us
    ppermute x3, starting transfers between devices, shards(): lax.ppermute(terms[d], 'dp', y_shift(d))  4.56 us
    ppermute x3, starting transfers between devices, shards(): lax.ppermute(packed[d], 'ctx', chip_shift(d))  3.87 us
    ppermute x2, waiting for transfers between devices, shards(): far = {d: lax.ppermute(own, 'ctx', chip_shift(d)) for d in (1, 3)}  3.64 us
    ppermute x3, waiting for transfers between devices, shards(): lax.ppermute(terms[d], 'ctx', chip_shift(CHIPS - d))  3.37 us
  transfers between devices with their start and end apart: 20, of which 11 were waited for; matrix products, arithmetic and copies ran while one was open for 0% of the time, Pallas kernels for 23%

profile of v13, /device:TPU:8, one launch (start us, length us, event | category | flops | bytes accessed | tf_op | source)
XLA Modules:
  0.0 79.5 jit_solution(9728785621707496961)
XLA Ops:
  0.6 0.1 collective-permute-start.2
  0.7 0.5 collective-permute-start.4
  1.2 1.5 %collective-permute-start = (bf16[128,1536]{1,0:T(8,128)(2,1)}, bf16[128,1536]{1,0:T(8,128)(2,1)S(1)}, u32[]{:S(2)}, u32[]{:S(2)}) collective-permute-start(bf16[128,1536]{1,0:T(8,128)(2,1)} %bitcast.6), channel_id=1, source_target_pairs={{0,64},{32,96},{64,128},{96,160},{128,192},{160,224},{192,0},{224,... | collective-permute-start | bytes 1179656 | tf_op jit(solution)/shard_map/ppermute | solution.py:563
  2.7 1.7 %collective-permute-start.1 = (bf16[128,1536]{1,0:T(8,128)(2,1)}, bf16[128,1536]{1,0:T(8,128)(2,1)S(1)}, u32[]{:S(2)}, u32[]{:S(2)}) collective-permute-start(bf16[128,1536]{1,0:T(8,128)(2,1)} %bitcast.7), channel_id=1, source_target_pairs={{0,192},{32,224},{64,0},{96,32},{128,64},{160,96},{192,128},{224,1... | collective-permute-start | bytes 1179656 | tf_op jit(solution)/shard_map/ppermute | solution.py:563
  4.5 0.0 collective-permute-start.3
  4.5 1.6 %project_kv_own.1 = (bf16[1536,256]{1,0:T(8,128)(2,1)S(1)}, bf16[128,256]{1,0:T(8,128)(2,1)S(1)}) custom-call(bf16[128,1536]{1,0:T(8,128)(2,1)} %bitcast.8, bf16[1536,256]{1,0:T(8,128)(2,1)} %w_key.5, bf16[1536,256]{1,0:T(8,128)(2,1)} %w_value.5), custom_call_target="tpu_custom_call" | custom-call | flops 1 | bytes 1 | tf_op jit(solution)/shard_map/project_kv_own/pallas_call | solution.py:100
  6.1 0.0 copy-start
  6.1 0.0 collective-permute-done.3.mask_other
  6.1 0.0 collective-permute-done.2.other
  6.1 0.0 collective-permute-done.4.up_other
  6.1 0.3 project_kv.1.refs_0_
  6.4 1.9 %collective-permute-start.5 = (bf16[256,256]{1,0:T(8,128)(2,1)S(1)}, bf16[256,256]{1,0:T(8,128)(2,1)S(1)}, u32[]{:S(2)}, u32[]{:S(2)}) collective-permute-start(bf16[256,256]{1,0:T(8,128)(2,1)S(1)} %project_kv.1.refs_0_), channel_id=1, source_target_pairs={{0,128},{32,160},{64,192},{96,224},{128,0},{160,32},{192,64},{224,... | collective-permute-start | bytes 393224 | tf_op jit(solution)/shard_map/ppermute | solution.py:562
  8.3 0.1 stack_up.1.up
  8.4 3.2 %project_query.1 = (bf16[1536,128]{1,0:T(8,128)(2,1)S(1)}, s32[16,256]{1,0:T(8,128)S(1)}, bf16[1536,256]{1,0:T(8,128)(2,1)S(1)}) custom-call(bf16[128,1536]{1,0:T(8,128)(2,1)S(1)} %bitcast.9, bf16[128,1536]{1,0:T(8,128)(2,1)S(1)} %collective-permute-done.2.other, bf16[1536,1536]{1,0:T(8,128)(2,1)} %w_query.3, bf16[1536,256]{1,0:T(8,128)(2,1)} %w_key.5, ...), custom_call_target="tpu_custom_call" | custom-call | flops 1 | bytes 1 | tf_op jit(solution)/shard_map/project_query/pallas_call | solution.py:221
  11.6 0.7 chip_scores_0.1
  12.3 1.4 %collective-permute-done.far1 = bf16[128,1536]{1,0:T(8,128)(2,1)S(1)} collective-permute-done((bf16[128,1536]{1,0:T(8,128)(2,1)}, bf16[128,1536]{1,0:T(8,128)(2,1)S(1)}, u32[]{:S(2)}, u32[]{:S(2)}) %collective-permute-start) | collective-permute-done | bytes 393248 | tf_op jit(solution)/shard_map/ppermute | solution.py:563
  13.8 2.2 %collective-permute-done.1.far3 = bf16[128,1536]{1,0:T(8,128)(2,1)S(1)} collective-permute-done((bf16[128,1536]{1,0:T(8,128)(2,1)}, bf16[128,1536]{1,0:T(8,128)(2,1)S(1)}, u32[]{:S(2)}, u32[]{:S(2)}) %collective-permute-start.1) | collective-permute-done | bytes 393248 | tf_op jit(solution)/shard_map/ppermute | solution.py:563
  16.0 1.6 %collective-permute-done.5.refs_0_ = bf16[256,256]{1,0:T(8,128)(2,1)S(1)} collective-permute-done((bf16[256,256]{1,0:T(8,128)(2,1)S(1)}, bf16[256,256]{1,0:T(8,128)(2,1)S(1)}, u32[]{:S(2)}, u32[]{:S(2)}) %collective-permute-start.5) | collective-permute-done | bytes 131104 | tf_op jit(solution)/shard_map/ppermute | solution.py:562
  17.6 1.1 %collective-permute-start.6 = (bf16[128,1536]{1,0:T(8,128)(2,1)S(1)}, bf16[128,1536]{1,0:T(8,128)(2,1)S(1)}, u32[]{:S(2)}, u32[]{:S(2)}) collective-permute-start(bf16[128,1536]{1,0:T(8,128)(2,1)S(1)} %collective-permute-done.far1), channel_id=1, source_target_pairs={{0,64},{32,96},{64,128},{96,160},{128,192},{160,224},{192,0},{224,... | collective-permute-start | bytes 1179656 | tf_op jit(solution)/shard_map/ppermute | solution.py:571
  18.7 0.6 project_kv_far.1
  19.3 0.1 collective-permute-start.7
  19.4 0.7 chip_scores_2.1
  20.1 0.6 collective-permute-done.7.refs_1_
  20.7 0.7 chip_scores_3.1
  21.5 0.7 chip_scores_1.1
  22.2 0.6 chip_terms_2.1
  22.8 2.4 %collective-permute-start.10 = (bf16[256,256]{1,0:T(8,128)(2,1)S(1)}, bf16[256,256]{1,0:T(8,128)(2,1)S(1)}, u32[]{:S(2)}, u32[]{:S(2)}) collective-permute-start(bf16[256,256]{1,0:T(8,128)(2,1)S(1)} %get-tuple-element.98), channel_id=1, source_target_pairs={{0,128},{32,160},{64,192},{96,224},{128,0},{160,32},{192,64},{224,... | collective-permute-start | bytes 393224 | tf_op jit(solution)/shard_map/ppermute | solution.py:581
  25.2 0.6 chip_terms_3.1
  25.8 0.9 %collective-permute-start.9 = (bf16[256,256]{1,0:T(8,128)(2,1)S(1)}, bf16[256,256]{1,0:T(8,128)(2,1)S(1)}, u32[]{:S(2)}, u32[]{:S(2)}) collective-permute-start(bf16[256,256]{1,0:T(8,128)(2,1)S(1)} %get-tuple-element.95), channel_id=1, source_target_pairs={{0,64},{32,96},{64,128},{96,160},{128,192},{160,224},{192,0},{224,... | collective-permute-start | bytes 393224 | tf_op jit(solution)/shard_map/ppermute | solution.py:581
  26.8 0.6 chip_terms_1.1
  27.4 2.7 %collective-permute-start.8 = (bf16[256,256]{1,0:T(8,128)(2,1)S(1)}, bf16[256,256]{1,0:T(8,128)(2,1)S(1)}, u32[]{:S(2)}, u32[]{:S(2)}) collective-permute-start(bf16[256,256]{1,0:T(8,128)(2,1)S(1)} %get-tuple-element.92), channel_id=1, source_target_pairs={{0,192},{32,224},{64,0},{96,32},{128,64},{160,96},{192,128},{224,1... | collective-permute-start | bytes 393224 | tf_op jit(solution)/shard_map/ppermute | solution.py:581
  30.0 0.6 chip_terms_0.1
  30.6 0.7 query_grad.1
  31.3 1.7 %collective-permute-done.10.d = bf16[256,256]{1,0:T(8,128)(2,1)S(1)} collective-permute-done((bf16[256,256]{1,0:T(8,128)(2,1)S(1)}, bf16[256,256]{1,0:T(8,128)(2,1)S(1)}, u32[]{:S(2)}, u32[]{:S(2)}) %collective-permute-start.10) | collective-permute-done | bytes 131104 | tf_op jit(solution)/shard_map/ppermute | solution.py:581
  33.0 1.7 %collective-permute-done.9.c = bf16[256,256]{1,0:T(8,128)(2,1)S(1)} collective-permute-done((bf16[256,256]{1,0:T(8,128)(2,1)S(1)}, bf16[256,256]{1,0:T(8,128)(2,1)S(1)}, u32[]{:S(2)}, u32[]{:S(2)}) %collective-permute-start.9) | collective-permute-done | bytes 131104 | tf_op jit(solution)/shard_map/ppermute | solution.py:581
  34.7 0.0 collective-permute-done.8.b
  34.7 0.0 collective-permute-done.6.far2
  34.7 0.1 sum_join.1.joined.dkv
  34.8 0.1 collective-permute-start.11
  34.9 0.5 transpose_tokens.1.tokens_t
  35.3 1.1 %collective-permute-done.11.joined_other.dkv_other = bf16[256,512]{1,0:T(8,128)(2,1)S(1)} collective-permute-done((bf16[256,512]{1,0:T(8,128)(2,1)S(1)}, bf16[256,512]{1,0:T(8,128)(2,1)S(1)}, u32[]{:S(2)}, u32[]{:S(2)}) %collective-permute-start.11) | collective-permute-done | bytes 262176 | tf_op jit(solution)/shard_map/ppermute | solution.py:588
  36.4 0.1 pack.1
  36.5 0.2 collective-permute-start.12
  36.7 0.6 collective-permute-start.13
  37.3 1.8 %collective-permute-start.14 = (bf16[256,256]{1,0:T(8,128)(2,1)S(1)}, bf16[256,256]{1,0:T(8,128)(2,1)S(1)}, u32[]{:S(2)}, u32[]{:S(2)}) collective-permute-start(bf16[256,256]{1,0:T(8,128)(2,1)S(1)} %get-tuple-element.127), channel_id=1, source_target_pairs={{0,64},{32,96},{64,128},{96,160},{128,192},{160,224},{192,0},{224,... | collective-permute-start | bytes 393224 | tf_op jit(solution)/shard_map/ppermute | solution.py:596
  39.1 1.4 %collective-permute-start.15 = (bf16[256,256]{1,0:T(8,128)(2,1)S(1)}, bf16[256,256]{1,0:T(8,128)(2,1)S(1)}, u32[]{:S(2)}, u32[]{:S(2)}) collective-permute-start(bf16[256,256]{1,0:T(8,128)(2,1)S(1)} %get-tuple-element.128), channel_id=1, source_target_pairs={{0,192},{32,224},{64,0},{96,32},{128,64},{160,96},{192,128},{224,1... | collective-permute-start | bytes 393224 | tf_op jit(solution)/shard_map/ppermute | solution.py:596
  40.5 0.0 collective-permute-start.19
  40.5 4.0 %collective-permute-done.13.b = bf16[256,256]{1,0:T(8,128)(2,1)S(1)} collective-permute-done((bf16[256,256]{1,0:T(8,128)(2,1)S(1)}, bf16[256,256]{1,0:T(8,128)(2,1)S(1)}, u32[]{:S(2)}, u32[]{:S(2)}) %collective-permute-start.13) | collective-permute-done | bytes 131104 | tf_op jit(solution)/shard_map/ppermute | solution.py:596
  44.6 2.2 %collective-permute-done.14.c = bf16[256,256]{1,0:T(8,128)(2,1)S(1)} collective-permute-done((bf16[256,256]{1,0:T(8,128)(2,1)S(1)}, bf16[256,256]{1,0:T(8,128)(2,1)S(1)}, u32[]{:S(2)}, u32[]{:S(2)}) %collective-permute-start.14) | collective-permute-done | bytes 131104 | tf_op jit(solution)/shard_map/ppermute | solution.py:596
  46.8 0.0 collective-permute-done.15.d
  46.8 0.4 weight_grad_2.1
  47.2 2.4 %collective-permute-start.18 = (bf16[384,256]{1,0:T(8,128)(2,1)S(1)}, bf16[384,256]{1,0:T(8,128)(2,1)S(1)}, u32[]{:S(2)}, u32[]{:S(2)}) collective-permute-start(bf16[384,256]{1,0:T(8,128)(2,1)S(1)} %weight_grad_2.1), channel_id=1, source_target_pairs={{0,16},{1,17},{2,18},{3,19},{4,20},{5,21},{6,22},{7,23},{8,24},{9,... | collective-permute-start | bytes 589832 | tf_op jit(solution)/shard_map/ppermute | solution.py:599
  49.5 0.4 weight_grad_3.1
  49.9 1.4 %collective-permute-start.17 = (bf16[384,256]{1,0:T(8,128)(2,1)S(1)}, bf16[384,256]{1,0:T(8,128)(2,1)S(1)}, u32[]{:S(2)}, u32[]{:S(2)}) collective-permute-start(bf16[384,256]{1,0:T(8,128)(2,1)S(1)} %weight_grad_3.1), channel_id=1, source_target_pairs={{0,24},{1,25},{2,26},{3,27},{4,28},{5,29},{6,30},{7,31},{8,0},{9,1... | collective-permute-start | bytes 589832 | tf_op jit(solution)/shard_map/ppermute | solution.py:599
  51.3 0.4 weight_grad_1.1
  51.7 0.8 collective-permute-start.16
  52.5 0.0 collective-permute-done.19.dq_other
  52.5 4.8 %input_grad.1 = bf16[128,1536]{1,0:T(8,128)(2,1)} custom-call(bf16[256,768]{1,0:T(8,128)(2,1)S(1)} %get-tuple-element.118.dq, bf16[128,768]{1,0:T(8,128)(2,1)S(1)} %collective-permute-done.19.dq_other, bf16[256,512]{1,0:T(8,128)(2,1)S(1)} %sum_join.1.joined.dkv, bf16[256,512]{1,0:T(8,128)(2,1)S(1)} %collective-permute-done.11.joined_other.dkv_other, ...), custom_call_target="tpu_custom_call" | custom-call | flops 1 | bytes 1 | tf_op jit(solution)/shard_map/input_grad/pallas_call | solution.py:536
  57.3 0.4 weight_grad_0.1.a
  57.7 2.1 %collective-permute-done.17.c = bf16[384,256]{1,0:T(8,128)(2,1)S(1)} collective-permute-done((bf16[384,256]{1,0:T(8,128)(2,1)S(1)}, bf16[384,256]{1,0:T(8,128)(2,1)S(1)}, u32[]{:S(2)}, u32[]{:S(2)}) %collective-permute-start.17) | collective-permute-done | bytes 196640 | tf_op jit(solution)/shard_map/ppermute | solution.py:599
  59.8 0.1 collective-permute-done.16.b
  59.9 0.1 sum_four.1
  60.0 18.8 %all_to_all.9 = bf16[8,48,256]{2,1,0:T(8,128)(2,1)S(1)} all-to-all(bf16[8,48,256]{2,1,0:T(8,128)(2,1)S(1)} %bitcast.11), channel_id=1, replica_groups={{0,1,2,3,4,5,6,7},{8,9,10,11,12,13,14,15},{16,17,18,19,20,21,22,23},{24..., dimensions={0} | all-to-all | bytes 393216 | tf_op jit(solution)/shard_map/all_to_all | solution.py:605
  78.8 0.6 convert_reduce_fusion
  (6 shorter events, 0.0 us)
Async XLA Ops:
  0.6 5.5 %collective-permute-start.2 = (bf16[128,1536]{1,0:T(8,128)(2,1)}, bf16[128,1536]{1,0:T(8,128)(2,1)S(1)}, u32[]{:S(2)}, u32[]{:S(2)}) collective-permute-start(bf16[128,1536]{1,0:T(8,128)(2,1)} %bitcast.5), channel_id=1, source_target_pairs={{0,32},{32,0},{64,96},{96,64},{128,160},{160,128},{192,224},{224,1... | collective-permute-start | bytes 1179656 | tf_op jit(solution)/shard_map/ppermute | solution.py:554
  0.7 5.4 %collective-permute-start.4 = (bf16[128,1536]{1,0:T(8,128)(2,1)}, bf16[128,1536]{1,0:T(8,128)(2,1)S(1)}, u32[]{:S(2)}, u32[]{:S(2)}) collective-permute-start(bf16[128,1536]{1,0:T(8,128)(2,1)} %bitcast.12), channel_id=1, source_target_pairs={{0,32},{32,0},{64,96},{96,64},{128,160},{160,128},{192,224},{224,1... | collective-permute-start | bytes 1179656 | tf_op jit(solution)/shard_map/ppermute | solution.py:555
  1.2 12.5 %collective-permute-start = (bf16[128,1536]{1,0:T(8,128)(2,1)}, bf16[128,1536]{1,0:T(8,128)(2,1)S(1)}, u32[]{:S(2)}, u32[]{:S(2)}) collective-permute-start(bf16[128,1536]{1,0:T(8,128)(2,1)} %bitcast.6), channel_id=1, source_target_pairs={{0,64},{32,96},{64,128},{96,160},{128,192},{160,224},{192,0},{224,... | collective-permute-start | bytes 1179656 | tf_op jit(solution)/shard_map/ppermute | solution.py:563
  2.7 13.3 %collective-permute-start.1 = (bf16[128,1536]{1,0:T(8,128)(2,1)}, bf16[128,1536]{1,0:T(8,128)(2,1)S(1)}, u32[]{:S(2)}, u32[]{:S(2)}) collective-permute-start(bf16[128,1536]{1,0:T(8,128)(2,1)} %bitcast.7), channel_id=1, source_target_pairs={{0,192},{32,224},{64,0},{96,32},{128,64},{160,96},{192,128},{224,1... | collective-permute-start | bytes 1179656 | tf_op jit(solution)/shard_map/ppermute | solution.py:563
  4.5 3.8 %copy-start.1 = (bf16[1,128,1536]{2,1,0:T(8,128)(2,1)S(1)}, bf16[1,128,1536]{2,1,0:T(8,128)(2,1)}, u32[]{:S(2)}) copy-start(bf16[1,128,1536]{2,1,0:T(8,128)(2,1)} %param.8) | copy-start | bytes 1179652
  4.5 1.6 %collective-permute-start.3 = (s32[1,8]{1,0:T(1,128)}, s32[1,8]{1,0:T(1,128)S(1)}, u32[]{:S(2)}, u32[]{:S(2)}) collective-permute-start(s32[1,8]{1,0:T(1,128)} %bitcast.15), channel_id=1, source_target_pairs={{0,32},{32,0},{64,96},{96,64},{128,160},{160,128},{192,224},{224,1... | collective-permute-start | bytes 104 | tf_op jit(solution)/shard_map/ppermute | solution.py:556
  6.1 2.3 %copy-start = (bf16[1,128,1536]{2,1,0:T(8,128)(2,1)S(1)}, bf16[1,128,1536]{2,1,0:T(8,128)(2,1)}, u32[]{:S(2)}) copy-start(bf16[1,128,1536]{2,1,0:T(8,128)(2,1)} %param.7) | copy-start | bytes 1179652
  6.4 11.2 %collective-permute-start.5 = (bf16[256,256]{1,0:T(8,128)(2,1)S(1)}, bf16[256,256]{1,0:T(8,128)(2,1)S(1)}, u32[]{:S(2)}, u32[]{:S(2)}) collective-permute-start(bf16[256,256]{1,0:T(8,128)(2,1)S(1)} %project_kv.1.refs_0_), channel_id=1, source_target_pairs={{0,128},{32,160},{64,192},{96,224},{128,0},{160,32},{192,64},{224,... | collective-permute-start | bytes 393224 | tf_op jit(solution)/shard_map/ppermute | solution.py:562
  17.6 17.1 %collective-permute-start.6 = (bf16[128,1536]{1,0:T(8,128)(2,1)S(1)}, bf16[128,1536]{1,0:T(8,128)(2,1)S(1)}, u32[]{:S(2)}, u32[]{:S(2)}) collective-permute-start(bf16[128,1536]{1,0:T(8,128)(2,1)S(1)} %collective-permute-done.far1), channel_id=1, source_target_pairs={{0,64},{32,96},{64,128},{96,160},{128,192},{160,224},{192,0},{224,... | collective-permute-start | bytes 1179656 | tf_op jit(solution)/shard_map/ppermute | solution.py:571
  19.3 1.4 %collective-permute-start.7 = (bf16[256,256]{1,0:T(8,128)(2,1)S(1)}, bf16[256,256]{1,0:T(8,128)(2,1)S(1)}, u32[]{:S(2)}, u32[]{:S(2)}) collective-permute-start(bf16[256,256]{1,0:T(8,128)(2,1)S(1)} %get-tuple-element.84), channel_id=1, source_target_pairs={{0,32},{32,0},{64,96},{96,64},{128,160},{160,128},{192,224},{224,1... | collective-permute-start | bytes 393224 | tf_op jit(solution)/shard_map/ppermute | solution.py:573
  22.8 10.1 %collective-permute-start.10 = (bf16[256,256]{1,0:T(8,128)(2,1)S(1)}, bf16[256,256]{1,0:T(8,128)(2,1)S(1)}, u32[]{:S(2)}, u32[]{:S(2)}) collective-permute-start(bf16[256,256]{1,0:T(8,128)(2,1)S(1)} %get-tuple-element.98), channel_id=1, source_target_pairs={{0,128},{32,160},{64,192},{96,224},{128,0},{160,32},{192,64},{224,... | collective-permute-start | bytes 393224 | tf_op jit(solution)/shard_map/ppermute | solution.py:581
  25.8 8.8 %collective-permute-start.9 = (bf16[256,256]{1,0:T(8,128)(2,1)S(1)}, bf16[256,256]{1,0:T(8,128)(2,1)S(1)}, u32[]{:S(2)}, u32[]{:S(2)}) collective-permute-start(bf16[256,256]{1,0:T(8,128)(2,1)S(1)} %get-tuple-element.95), channel_id=1, source_target_pairs={{0,64},{32,96},{64,128},{96,160},{128,192},{160,224},{192,0},{224,... | collective-permute-start | bytes 393224 | tf_op jit(solution)/shard_map/ppermute | solution.py:581
  27.4 7.3 %collective-permute-start.8 = (bf16[256,256]{1,0:T(8,128)(2,1)S(1)}, bf16[256,256]{1,0:T(8,128)(2,1)S(1)}, u32[]{:S(2)}, u32[]{:S(2)}) collective-permute-start(bf16[256,256]{1,0:T(8,128)(2,1)S(1)} %get-tuple-element.92), channel_id=1, source_target_pairs={{0,192},{32,224},{64,0},{96,32},{128,64},{160,96},{192,128},{224,1... | collective-permute-start | bytes 393224 | tf_op jit(solution)/shard_map/ppermute | solution.py:581
  34.8 1.6 %collective-permute-start.11 = (bf16[256,512]{1,0:T(8,128)(2,1)S(1)}, bf16[256,512]{1,0:T(8,128)(2,1)S(1)}, u32[]{:S(2)}, u32[]{:S(2)}) collective-permute-start(bf16[256,512]{1,0:T(8,128)(2,1)S(1)} %sum_join.1.joined.dkv), channel_id=1, source_target_pairs={{0,32},{32,0},{64,96},{96,64},{128,160},{160,128},{192,224},{224,1... | collective-permute-start | bytes 786440 | tf_op jit(solution)/shard_map/ppermute | solution.py:588
  36.5 10.3 %collective-permute-start.12 = (bf16[1536,512]{1,0:T(8,128)(2,1)S(1)}, bf16[1536,512]{1,0:T(8,128)(2,1)S(1)}, u32[]{:S(2)}, u32[]{:S(2)}) collective-permute-start(bf16[1536,512]{1,0:T(8,128)(2,1)S(1)} %transpose_tokens.1.tokens_t), channel_id=1, source_target_pairs={{0,32},{32,0},{64,96},{96,64},{128,160},{160,128},{192,224},{224,1... | collective-permute-start | bytes 4718600 | tf_op jit(solution)/shard_map/ppermute | solution.py:595
  36.7 7.9 %collective-permute-start.13 = (bf16[256,256]{1,0:T(8,128)(2,1)S(1)}, bf16[256,256]{1,0:T(8,128)(2,1)S(1)}, u32[]{:S(2)}, u32[]{:S(2)}) collective-permute-start(bf16[256,256]{1,0:T(8,128)(2,1)S(1)} %get-tuple-element.126), channel_id=1, source_target_pairs={{0,128},{32,160},{64,192},{96,224},{128,0},{160,32},{192,64},{224,... | collective-permute-start | bytes 393224 | tf_op jit(solution)/shard_map/ppermute | solution.py:596
  37.3 9.5 %collective-permute-start.14 = (bf16[256,256]{1,0:T(8,128)(2,1)S(1)}, bf16[256,256]{1,0:T(8,128)(2,1)S(1)}, u32[]{:S(2)}, u32[]{:S(2)}) collective-permute-start(bf16[256,256]{1,0:T(8,128)(2,1)S(1)} %get-tuple-element.127), channel_id=1, source_target_pairs={{0,64},{32,96},{64,128},{96,160},{128,192},{160,224},{192,0},{224,... | collective-permute-start | bytes 393224 | tf_op jit(solution)/shard_map/ppermute | solution.py:596
  39.1 7.7 %collective-permute-start.15 = (bf16[256,256]{1,0:T(8,128)(2,1)S(1)}, bf16[256,256]{1,0:T(8,128)(2,1)S(1)}, u32[]{:S(2)}, u32[]{:S(2)}) collective-permute-start(bf16[256,256]{1,0:T(8,128)(2,1)S(1)} %get-tuple-element.128), channel_id=1, source_target_pairs={{0,192},{32,224},{64,0},{96,32},{128,64},{160,96},{192,128},{224,1... | collective-permute-start | bytes 393224 | tf_op jit(solution)/shard_map/ppermute | solution.py:596
  40.5 11.9 %collective-permute-start.19 = (bf16[128,768]{1,0:T(8,128)(2,1)S(1)}, bf16[128,768]{1,0:T(8,128)(2,1)S(1)}, u32[]{:S(2)}, u32[]{:S(2)}) collective-permute-start(bf16[128,768]{1,0:T(8,128)(2,1)S(1)} %get-tuple-element.129), channel_id=1, source_target_pairs={{0,32},{32,0},{64,96},{96,64},{128,160},{160,128},{192,224},{224,1... | collective-permute-start | bytes 589832 | tf_op jit(solution)/shard_map/ppermute | solution.py:594
  47.2 10.5 %collective-permute-start.18 = (bf16[384,256]{1,0:T(8,128)(2,1)S(1)}, bf16[384,256]{1,0:T(8,128)(2,1)S(1)}, u32[]{:S(2)}, u32[]{:S(2)}) collective-permute-start(bf16[384,256]{1,0:T(8,128)(2,1)S(1)} %weight_grad_2.1), channel_id=1, source_target_pairs={{0,16},{1,17},{2,18},{3,19},{4,20},{5,21},{6,22},{7,23},{8,24},{9,... | collective-permute-start | bytes 589832 | tf_op jit(solution)/shard_map/ppermute | solution.py:599
  49.9 9.9 %collective-permute-start.17 = (bf16[384,256]{1,0:T(8,128)(2,1)S(1)}, bf16[384,256]{1,0:T(8,128)(2,1)S(1)}, u32[]{:S(2)}, u32[]{:S(2)}) collective-permute-start(bf16[384,256]{1,0:T(8,128)(2,1)S(1)} %weight_grad_3.1), channel_id=1, source_target_pairs={{0,24},{1,25},{2,26},{3,27},{4,28},{5,29},{6,30},{7,31},{8,0},{9,1... | collective-permute-start | bytes 589832 | tf_op jit(solution)/shard_map/ppermute | solution.py:599
  51.7 8.2 %collective-permute-start.16 = (bf16[384,256]{1,0:T(8,128)(2,1)S(1)}, bf16[384,256]{1,0:T(8,128)(2,1)S(1)}, u32[]{:S(2)}, u32[]{:S(2)}) collective-permute-start(bf16[384,256]{1,0:T(8,128)(2,1)S(1)} %weight_grad_1.1), channel_id=1, source_target_pairs={{0,8},{1,9},{2,10},{3,11},{4,12},{5,13},{6,14},{7,15},{8,16},{9,17... | collective-permute-start | bytes 589832 | tf_op jit(solution)/shard_map/ppermute | solution.py:599

commit v14 on v13

--- a/solution.py
+++ b/solution.py
@@ -33,12 +33,12 @@
 NT = (((1,), (1,)), ((), ()))
 
 
-def chip_shift(d):
-    return [(i, ((i // 2 + d) % CHIPS) * 2 + i % 2) for i in range(8)]
-
-
-def y_shift(d):
-    return [(i, ((i // ZS + d) % YS) * ZS + i % ZS) for i in range(32)]
+def chip_pair(d):
+    return [(i, ((i // 2) ^ d) * 2 + i % 2) for i in range(8)]
+
+
+def y_pair(d):
+    return [(i, ((i // ZS) ^ d) * ZS + i % ZS) for i in range(32)]
 
 
 Z_GROUPS = [[y * ZS + z for z in range(ZS)] for y in range(YS)]
@@ -194,7 +194,7 @@
         )
         for d in range(CHIPS):
             for key_slot in range(2):
-                key_tile = 2 * lax.rem(chip + CHIPS - d, CHIPS) + (
+                key_tile = 2 * lax.bitwise_xor(chip, jnp.int32(d)) + (
                     core if key_slot == 0 else 1 - core
                 )
                 seen = masks[0, key_tile] == 1
@@ -425,7 +425,7 @@
             @pl.when((my_core == core) & (my_chip == chip))
             def _(core=core, own_part=own_part, chip=chip):
                 for d, out in enumerate(outs):
-                    target = (chip + d) % CHIPS
+                    target = chip ^ d
                     if target == 3:
                         out[:, own_part] = joined[:, own_part]
                         theirs = slice((1 - core) * HD, (2 - core) * HD)
@@ -473,7 +473,7 @@
     right = jnp.concatenate([part[:TILE] for part in parts], axis=0)
     right_other = jnp.concatenate([part[TILE:] for part in parts], axis=0)
     _, _, chip = position()
-    row = pl.multiple_of(lax.rem(chip + shift, YS) * (D // YS), 128)
+    row = pl.multiple_of(lax.bitwise_xor(chip, jnp.int32(shift)) * (D // YS), 128)
     rows = pl.ds(row, D // YS)
     total = dot(tokens_t[rows], right) + dot(other_t[rows], right_other)
     out[...] = total.astype(out.dtype)
@@ -559,8 +559,8 @@
     w_query, w_key, w_value = (in_hbm(w) for w in (w_query, w_key, w_value))
     weights, kv_own = project_kv_own(in_hbm(own), w_key, w_value)
     kv = project_kv(other, weights, kv_own)
-    kv2 = lax.ppermute(kv, "ctx", chip_shift(2))
-    far = {d: lax.ppermute(own, "ctx", chip_shift(d)) for d in (1, 3)}
+    kv2 = lax.ppermute(kv, "ctx", chip_pair(2))
+    far = {d: lax.ppermute(own, "ctx", chip_pair(d)) for d in (1, 3)}
     query, limits, weights_other = project_query(
         own, other, w_query, w_key, w_value,
         in_hbm(segments), in_hbm(tile_mask[0]), mask_other,
@@ -568,7 +568,7 @@
     up = stack_up(up, up_other)
     scores = {0: chip_scores(0, limits, query, up, kv)}
     far, kv2, scores[0] = lax.optimization_barrier((far, kv2, scores[0]))
-    late = lax.ppermute(far[1], "ctx", chip_shift(1))
+    late = lax.ppermute(far[3], "ctx", chip_pair(1))
     mine, theirs = project_kv_far(far[1], far[3], weights, weights_other)
     theirs = lax.ppermute(theirs, "ctx", CORE)
     for i, d in enumerate((1, 3)):
@@ -578,7 +578,7 @@
     terms, grad_scores = {}, {}
     for d in (3, 1, 2):
         terms[d], grad_scores[d] = chip_terms(d, *scores[d][:2], factors, query, up)
-    back = [lax.ppermute(terms[d], "ctx", chip_shift(CHIPS - d)) for d in (1, 3, 2)]
+    back = [lax.ppermute(terms[d], "ctx", chip_pair(d)) for d in (1, 3, 2)]
     terms[0], grad_scores[0] = chip_terms(0, *scores[0][:2], factors, query, up)
     dq, middle, theirs = query_grad(
         [scores[d][3] for d in range(CHIPS)], [grad_scores[d] for d in range(CHIPS)]
@@ -593,10 +593,10 @@
     tokens_t, packed, theirs = lax.optimization_barrier((tokens_t, packed, theirs))
     dq_other = lax.ppermute(theirs, "ctx", CORE)
     other_t = lax.ppermute(tokens_t, "ctx", CORE)
-    columns = {d: lax.ppermute(packed[d], "ctx", chip_shift(d)) for d in (2, 1, 3)}
+    columns = {d: lax.ppermute(packed[d], "ctx", chip_pair(d)) for d in (2, 1, 3)}
     columns = [packed[0]] + [columns[d] for d in (2, 1, 3)]
     terms = [weight_grad(d, tokens_t, other_t, columns) for d in range(YS)]
-    y_parts = [terms[0]] + [lax.ppermute(terms[d], "dp", y_shift(d)) for d in (1, 3, 2)]
+    y_parts = [terms[0]] + [lax.ppermute(terms[d], "dp", y_pair(d)) for d in (1, 3, 2)]
     grad_tokens = input_grad(
         dq, dq_other, dkv, dkv_other, w_query, w_key, w_value
     )

time: 79.7 us -> 79.1 us (level)
  starting transfers between devices: 21.6 us -> 19.5 us
  waiting for transfers between devices: 18.8 us -> 20.4 us
    ppermute x13, starting transfers between devices: 20.7 us -> 18.5 us  [the longest x3 5.14 us: shards(): back = [lax.ppermute(terms[d], 'ctx', chip_pair(d)) for d in (1, 3, 2)]]
    ppermute x13, waiting for transfers between devices: 17.1 us -> 18.7 us  [the longest x2 6.27 us: shards(): far = {d: lax.ppermute(own, 'ctx', chip_pair(d)) for d in (1, 3)}]
where the time goes in v14:
time: 79.1 us; the launch traced here: 79 us
  waiting for transfers between devices  20.4 us (26%)
  starting transfers between devices  19.5 us (25%)
  Pallas kernels  18.8 us (24%)
  blocking collectives  18.8 us (24%)
  between operations  0.88 us (1%)
    all_to_all x1, blocking collectives, shards(): lax.all_to_all(y_sum, 'dp', 0, 0, tiled=True, axis_index_groups=Z_GROUPS)  18.8 us
    ppermute x2, waiting for transfers between devices, shards(): far = {d: lax.ppermute(own, 'ctx', chip_pair(d)) for d in (1, 3)}  6.27 us
    ppermute x3, waiting for transfers between devices, shards(): lax.ppermute(packed[d], 'ctx', chip_pair(d))  5.98 us
    ppermute x3, starting transfers between devices, shards(): back = [lax.ppermute(terms[d], 'ctx', chip_pair(d)) for d in (1, 3, 2)]  5.14 us
    ppermute x3, starting transfers between devices, shards(): lax.ppermute(terms[d], 'dp', y_pair(d))  4.95 us
    pallas_call x1, Pallas kernels, input_grad(): pl.pallas_call(input_kernel, in_specs=[WHOLE] * 4 + [STAY] * 3, out_specs...  4.83 us
    ppermute x3, waiting for transfers between devices, shards(): back = [lax.ppermute(terms[d], 'ctx', chip_pair(d)) for d in (1, 3, 2)]  4.6 us
    ppermute x3, starting transfers between devices, shards(): lax.ppermute(packed[d], 'ctx', chip_pair(d))  4.13 us
  transfers between devices with their start and end apart: 20, of which 11 were waited for; matrix products, arithmetic and copies ran while one was open for 0% of the time, Pallas kernels for 23%

profile of v14, /device:TPU:8, one launch (start us, length us, event | category | flops | bytes accessed | tf_op | source)
XLA Modules:
  0.0 79.0 jit_solution(383703593121985696)
XLA Ops:
  0.6 0.1 collective-permute-start.2
  0.7 0.5 collective-permute-start.4
  1.2 1.5 %collective-permute-start = (bf16[128,1536]{1,0:T(8,128)(2,1)}, bf16[128,1536]{1,0:T(8,128)(2,1)S(1)}, u32[]{:S(2)}, u32[]{:S(2)}) collective-permute-start(bf16[128,1536]{1,0:T(8,128)(2,1)} %bitcast.6), channel_id=1, source_target_pairs={{0,64},{32,96},{64,0},{96,32},{128,192},{160,224},{192,128},{224,1... | collective-permute-start | bytes 1179656 | tf_op jit(solution)/shard_map/ppermute | solution.py:563
  2.7 2.1 %collective-permute-start.1 = (bf16[128,1536]{1,0:T(8,128)(2,1)}, bf16[128,1536]{1,0:T(8,128)(2,1)S(1)}, u32[]{:S(2)}, u32[]{:S(2)}) collective-permute-start(bf16[128,1536]{1,0:T(8,128)(2,1)} %bitcast.7), channel_id=1, source_target_pairs={{0,192},{32,224},{64,128},{96,160},{128,64},{160,96},{192,0},{224,... | collective-permute-start | bytes 1179656 | tf_op jit(solution)/shard_map/ppermute | solution.py:563
  4.8 0.0 collective-permute-start.3
  4.8 1.6 %project_kv_own.1 = (bf16[1536,256]{1,0:T(8,128)(2,1)S(1)}, bf16[128,256]{1,0:T(8,128)(2,1)S(1)}) custom-call(bf16[128,1536]{1,0:T(8,128)(2,1)} %bitcast.8, bf16[1536,256]{1,0:T(8,128)(2,1)} %w_key.5, bf16[1536,256]{1,0:T(8,128)(2,1)} %w_value.5), custom_call_target="tpu_custom_call" | custom-call | flops 1 | bytes 1 | tf_op jit(solution)/shard_map/project_kv_own/pallas_call | solution.py:100
  6.4 0.0 copy-start
  6.4 0.0 collective-permute-done.3.mask_other
  6.4 0.0 collective-permute-done.2.other
  6.4 0.0 collective-permute-done.4.up_other
  6.5 0.3 project_kv.1.refs_0_
  6.7 0.7 collective-permute-start.5
  7.5 0.1 stack_up.1.up
  7.6 3.2 %project_query.1 = (bf16[1536,128]{1,0:T(8,128)(2,1)S(1)}, s32[16,256]{1,0:T(8,128)S(1)}, bf16[1536,256]{1,0:T(8,128)(2,1)S(1)}) custom-call(bf16[128,1536]{1,0:T(8,128)(2,1)S(1)} %bitcast.9, bf16[128,1536]{1,0:T(8,128)(2,1)S(1)} %collective-permute-done.2.other, bf16[1536,1536]{1,0:T(8,128)(2,1)} %w_query.3, bf16[1536,256]{1,0:T(8,128)(2,1)} %w_key.5, ...), custom_call_target="tpu_custom_call" | custom-call | flops 1 | bytes 1 | tf_op jit(solution)/shard_map/project_query/pallas_call | solution.py:221
  10.8 0.7 chip_scores_0.1
  11.5 1.9 %collective-permute-done.far1 = bf16[128,1536]{1,0:T(8,128)(2,1)S(1)} collective-permute-done((bf16[128,1536]{1,0:T(8,128)(2,1)}, bf16[128,1536]{1,0:T(8,128)(2,1)S(1)}, u32[]{:S(2)}, u32[]{:S(2)}) %collective-permute-start) | collective-permute-done | bytes 393248 | tf_op jit(solution)/shard_map/ppermute | solution.py:563
  13.4 4.4 %collective-permute-done.1.far3 = bf16[128,1536]{1,0:T(8,128)(2,1)S(1)} collective-permute-done((bf16[128,1536]{1,0:T(8,128)(2,1)}, bf16[128,1536]{1,0:T(8,128)(2,1)S(1)}, u32[]{:S(2)}, u32[]{:S(2)}) %collective-permute-start.1) | collective-permute-done | bytes 393248 | tf_op jit(solution)/shard_map/ppermute | solution.py:563
  17.8 0.0 collective-permute-done.5.refs_0_
  17.8 0.0 collective-permute-start.6
  17.8 0.6 project_kv_far.1
  18.4 0.1 collective-permute-start.7
  18.5 0.7 chip_scores_2.1
  19.2 0.6 collective-permute-done.7.refs_1_
  19.8 0.7 chip_scores_3.1
  20.6 0.7 chip_scores_1.1
  21.3 0.6 chip_terms_2.1
  21.9 3.6 %collective-permute-start.10 = (bf16[256,256]{1,0:T(8,128)(2,1)S(1)}, bf16[256,256]{1,0:T(8,128)(2,1)S(1)}, u32[]{:S(2)}, u32[]{:S(2)}) collective-permute-start(bf16[256,256]{1,0:T(8,128)(2,1)S(1)} %get-tuple-element.98), channel_id=1, source_target_pairs={{0,128},{32,160},{64,192},{96,224},{128,0},{160,32},{192,64},{224,... | collective-permute-start | bytes 393224 | tf_op jit(solution)/shard_map/ppermute | solution.py:581
  25.6 0.6 chip_terms_3.1
  26.2 1.2 %collective-permute-start.9 = (bf16[256,256]{1,0:T(8,128)(2,1)S(1)}, bf16[256,256]{1,0:T(8,128)(2,1)S(1)}, u32[]{:S(2)}, u32[]{:S(2)}) collective-permute-start(bf16[256,256]{1,0:T(8,128)(2,1)S(1)} %get-tuple-element.95), channel_id=1, source_target_pairs={{0,192},{32,224},{64,128},{96,160},{128,64},{160,96},{192,0},{224,... | collective-permute-start | bytes 393224 | tf_op jit(solution)/shard_map/ppermute | solution.py:581
  27.4 0.6 chip_terms_1.1
  28.0 0.3 collective-permute-start.8
  28.3 0.6 chip_terms_0.1
  28.9 0.7 query_grad.1
  29.6 2.6 %collective-permute-done.10.d = bf16[256,256]{1,0:T(8,128)(2,1)S(1)} collective-permute-done((bf16[256,256]{1,0:T(8,128)(2,1)S(1)}, bf16[256,256]{1,0:T(8,128)(2,1)S(1)}, u32[]{:S(2)}, u32[]{:S(2)}) %collective-permute-start.10) | collective-permute-done | bytes 131104 | tf_op jit(solution)/shard_map/ppermute | solution.py:581
  32.2 2.0 %collective-permute-done.9.c = bf16[256,256]{1,0:T(8,128)(2,1)S(1)} collective-permute-done((bf16[256,256]{1,0:T(8,128)(2,1)S(1)}, bf16[256,256]{1,0:T(8,128)(2,1)S(1)}, u32[]{:S(2)}, u32[]{:S(2)}) %collective-permute-start.9) | collective-permute-done | bytes 131104 | tf_op jit(solution)/shard_map/ppermute | solution.py:581
  34.2 0.0 collective-permute-done.8.b
  34.2 0.0 collective-permute-done.6.far2
  34.2 0.1 sum_join.1.joined.dkv
  34.3 0.1 collective-permute-start.11
  34.4 0.5 transpose_tokens.1.tokens_t
  34.8 1.1 %collective-permute-done.11.joined_other.dkv_other = bf16[256,512]{1,0:T(8,128)(2,1)S(1)} collective-permute-done((bf16[256,512]{1,0:T(8,128)(2,1)S(1)}, bf16[256,512]{1,0:T(8,128)(2,1)S(1)}, u32[]{:S(2)}, u32[]{:S(2)}) %collective-permute-start.11) | collective-permute-done | bytes 262176 | tf_op jit(solution)/shard_map/ppermute | solution.py:588
  35.9 0.1 pack.1
  36.0 0.2 collective-permute-start.12
  36.2 1.1 %collective-permute-start.13 = (bf16[256,256]{1,0:T(8,128)(2,1)S(1)}, bf16[256,256]{1,0:T(8,128)(2,1)S(1)}, u32[]{:S(2)}, u32[]{:S(2)}) collective-permute-start(bf16[256,256]{1,0:T(8,128)(2,1)S(1)} %get-tuple-element.126), channel_id=1, source_target_pairs={{0,128},{32,160},{64,192},{96,224},{128,0},{160,32},{192,64},{224,... | collective-permute-start | bytes 393224 | tf_op jit(solution)/shard_map/ppermute | solution.py:596
  37.2 1.1 %collective-permute-start.14 = (bf16[256,256]{1,0:T(8,128)(2,1)S(1)}, bf16[256,256]{1,0:T(8,128)(2,1)S(1)}, u32[]{:S(2)}, u32[]{:S(2)}) collective-permute-start(bf16[256,256]{1,0:T(8,128)(2,1)S(1)} %get-tuple-element.127), channel_id=1, source_target_pairs={{0,64},{32,96},{64,0},{96,32},{128,192},{160,224},{192,128},{224,1... | collective-permute-start | bytes 393224 | tf_op jit(solution)/shard_map/ppermute | solution.py:596
  38.4 1.9 %collective-permute-start.15 = (bf16[256,256]{1,0:T(8,128)(2,1)S(1)}, bf16[256,256]{1,0:T(8,128)(2,1)S(1)}, u32[]{:S(2)}, u32[]{:S(2)}) collective-permute-start(bf16[256,256]{1,0:T(8,128)(2,1)S(1)} %get-tuple-element.128), channel_id=1, source_target_pairs={{0,192},{32,224},{64,128},{96,160},{128,64},{160,96},{192,0},{224,... | collective-permute-start | bytes 393224 | tf_op jit(solution)/shard_map/ppermute | solution.py:596
  40.3 0.0 collective-permute-start.19
  40.3 3.7 %collective-permute-done.13.b = bf16[256,256]{1,0:T(8,128)(2,1)S(1)} collective-permute-done((bf16[256,256]{1,0:T(8,128)(2,1)S(1)}, bf16[256,256]{1,0:T(8,128)(2,1)S(1)}, u32[]{:S(2)}, u32[]{:S(2)}) %collective-permute-start.13) | collective-permute-done | bytes 131104 | tf_op jit(solution)/shard_map/ppermute | solution.py:596
  44.0 0.9 %collective-permute-done.14.c = bf16[256,256]{1,0:T(8,128)(2,1)S(1)} collective-permute-done((bf16[256,256]{1,0:T(8,128)(2,1)S(1)}, bf16[256,256]{1,0:T(8,128)(2,1)S(1)}, u32[]{:S(2)}, u32[]{:S(2)}) %collective-permute-start.14) | collective-permute-done | bytes 131104 | tf_op jit(solution)/shard_map/ppermute | solution.py:596
  44.9 1.4 %collective-permute-done.15.d = bf16[256,256]{1,0:T(8,128)(2,1)S(1)} collective-permute-done((bf16[256,256]{1,0:T(8,128)(2,1)S(1)}, bf16[256,256]{1,0:T(8,128)(2,1)S(1)}, u32[]{:S(2)}, u32[]{:S(2)}) %collective-permute-start.15) | collective-permute-done | bytes 131104 | tf_op jit(solution)/shard_map/ppermute | solution.py:596
  46.3 0.4 weight_grad_2.1
  46.7 2.4 %collective-permute-start.18 = (bf16[384,256]{1,0:T(8,128)(2,1)S(1)}, bf16[384,256]{1,0:T(8,128)(2,1)S(1)}, u32[]{:S(2)}, u32[]{:S(2)}) collective-permute-start(bf16[384,256]{1,0:T(8,128)(2,1)S(1)} %weight_grad_2.1), channel_id=1, source_target_pairs={{0,16},{1,17},{2,18},{3,19},{4,20},{5,21},{6,22},{7,23},{8,24},{9,... | collective-permute-start | bytes 589832 | tf_op jit(solution)/shard_map/ppermute | solution.py:599
  49.1 0.4 weight_grad_3.1
  49.4 0.1 collective-permute-start.17
  49.5 0.4 weight_grad_1.1
  49.9 2.5 %collective-permute-start.16 = (bf16[384,256]{1,0:T(8,128)(2,1)S(1)}, bf16[384,256]{1,0:T(8,128)(2,1)S(1)}, u32[]{:S(2)}, u32[]{:S(2)}) collective-permute-start(bf16[384,256]{1,0:T(8,128)(2,1)S(1)} %weight_grad_1.1), channel_id=1, source_target_pairs={{0,8},{1,9},{2,10},{3,11},{4,12},{5,13},{6,14},{7,15},{8,0},{9,1},... | collective-permute-start | bytes 589832 | tf_op jit(solution)/shard_map/ppermute | solution.py:599
  52.4 0.0 collective-permute-done.19.dq_other
  52.4 4.8 %input_grad.1 = bf16[128,1536]{1,0:T(8,128)(2,1)} custom-call(bf16[256,768]{1,0:T(8,128)(2,1)S(1)} %get-tuple-element.118.dq, bf16[128,768]{1,0:T(8,128)(2,1)S(1)} %collective-permute-done.19.dq_other, bf16[256,512]{1,0:T(8,128)(2,1)S(1)} %sum_join.1.joined.dkv, bf16[256,512]{1,0:T(8,128)(2,1)S(1)} %collective-permute-done.11.joined_other.dkv_other, ...), custom_call_target="tpu_custom_call" | custom-call | flops 1 | bytes 1 | tf_op jit(solution)/shard_map/input_grad/pallas_call | solution.py:536
  57.2 0.4 weight_grad_0.1.a
  57.6 1.7 %collective-permute-done.17.c = bf16[384,256]{1,0:T(8,128)(2,1)S(1)} collective-permute-done((bf16[384,256]{1,0:T(8,128)(2,1)S(1)}, bf16[384,256]{1,0:T(8,128)(2,1)S(1)}, u32[]{:S(2)}, u32[]{:S(2)}) %collective-permute-start.17) | collective-permute-done | bytes 196640 | tf_op jit(solution)/shard_map/ppermute | solution.py:599
  59.3 0.2 collective-permute-done.16.b
  59.4 0.1 sum_four.1
  59.5 18.8 %all_to_all.9 = bf16[8,48,256]{2,1,0:T(8,128)(2,1)S(1)} all-to-all(bf16[8,48,256]{2,1,0:T(8,128)(2,1)S(1)} %bitcast.11), channel_id=1, replica_groups={{0,1,2,3,4,5,6,7},{8,9,10,11,12,13,14,15},{16,17,18,19,20,21,22,23},{24..., dimensions={0} | all-to-all | bytes 393216 | tf_op jit(solution)/shard_map/all_to_all | solution.py:605
  78.3 0.6 convert_reduce_fusion
  (6 shorter events, 0.0 us)
Async XLA Ops:
  0.6 5.8 %collective-permute-start.2 = (bf16[128,1536]{1,0:T(8,128)(2,1)}, bf16[128,1536]{1,0:T(8,128)(2,1)S(1)}, u32[]{:S(2)}, u32[]{:S(2)}) collective-permute-start(bf16[128,1536]{1,0:T(8,128)(2,1)} %bitcast.5), channel_id=1, source_target_pairs={{0,32},{32,0},{64,96},{96,64},{128,160},{160,128},{192,224},{224,1... | collective-permute-start | bytes 1179656 | tf_op jit(solution)/shard_map/ppermute | solution.py:554
  0.7 5.7 %collective-permute-start.4 = (bf16[128,1536]{1,0:T(8,128)(2,1)}, bf16[128,1536]{1,0:T(8,128)(2,1)S(1)}, u32[]{:S(2)}, u32[]{:S(2)}) collective-permute-start(bf16[128,1536]{1,0:T(8,128)(2,1)} %bitcast.12), channel_id=1, source_target_pairs={{0,32},{32,0},{64,96},{96,64},{128,160},{160,128},{192,224},{224,1... | collective-permute-start | bytes 1179656 | tf_op jit(solution)/shard_map/ppermute | solution.py:555
  1.2 12.2 %collective-permute-start = (bf16[128,1536]{1,0:T(8,128)(2,1)}, bf16[128,1536]{1,0:T(8,128)(2,1)S(1)}, u32[]{:S(2)}, u32[]{:S(2)}) collective-permute-start(bf16[128,1536]{1,0:T(8,128)(2,1)} %bitcast.6), channel_id=1, source_target_pairs={{0,64},{32,96},{64,0},{96,32},{128,192},{160,224},{192,128},{224,1... | collective-permute-start | bytes 1179656 | tf_op jit(solution)/shard_map/ppermute | solution.py:563
  2.7 15.1 %collective-permute-start.1 = (bf16[128,1536]{1,0:T(8,128)(2,1)}, bf16[128,1536]{1,0:T(8,128)(2,1)S(1)}, u32[]{:S(2)}, u32[]{:S(2)}) collective-permute-start(bf16[128,1536]{1,0:T(8,128)(2,1)} %bitcast.7), channel_id=1, source_target_pairs={{0,192},{32,224},{64,128},{96,160},{128,64},{160,96},{192,0},{224,... | collective-permute-start | bytes 1179656 | tf_op jit(solution)/shard_map/ppermute | solution.py:563
  4.8 2.7 %copy-start.1 = (bf16[1,128,1536]{2,1,0:T(8,128)(2,1)S(1)}, bf16[1,128,1536]{2,1,0:T(8,128)(2,1)}, u32[]{:S(2)}) copy-start(bf16[1,128,1536]{2,1,0:T(8,128)(2,1)} %param.8) | copy-start | bytes 1179652
  4.8 1.6 %collective-permute-start.3 = (s32[1,8]{1,0:T(1,128)}, s32[1,8]{1,0:T(1,128)S(1)}, u32[]{:S(2)}, u32[]{:S(2)}) collective-permute-start(s32[1,8]{1,0:T(1,128)} %bitcast.15), channel_id=1, source_target_pairs={{0,32},{32,0},{64,96},{96,64},{128,160},{160,128},{192,224},{224,1... | collective-permute-start | bytes 104 | tf_op jit(solution)/shard_map/ppermute | solution.py:556
  6.4 1.1 %copy-start = (bf16[1,128,1536]{2,1,0:T(8,128)(2,1)S(1)}, bf16[1,128,1536]{2,1,0:T(8,128)(2,1)}, u32[]{:S(2)}) copy-start(bf16[1,128,1536]{2,1,0:T(8,128)(2,1)} %param.7) | copy-start | bytes 1179652
  6.7 11.1 %collective-permute-start.5 = (bf16[256,256]{1,0:T(8,128)(2,1)S(1)}, bf16[256,256]{1,0:T(8,128)(2,1)S(1)}, u32[]{:S(2)}, u32[]{:S(2)}) collective-permute-start(bf16[256,256]{1,0:T(8,128)(2,1)S(1)} %project_kv.1.refs_0_), channel_id=1, source_target_pairs={{0,128},{32,160},{64,192},{96,224},{128,0},{160,32},{192,64},{224,... | collective-permute-start | bytes 393224 | tf_op jit(solution)/shard_map/ppermute | solution.py:562
  17.8 16.4 %collective-permute-start.6 = (bf16[128,1536]{1,0:T(8,128)(2,1)S(1)}, bf16[128,1536]{1,0:T(8,128)(2,1)S(1)}, u32[]{:S(2)}, u32[]{:S(2)}) collective-permute-start(bf16[128,1536]{1,0:T(8,128)(2,1)S(1)} %collective-permute-done.1.far3), channel_id=1, source_target_pairs={{0,64},{32,96},{64,0},{96,32},{128,192},{160,224},{192,128},{224,1... | collective-permute-start | bytes 1179656 | tf_op jit(solution)/shard_map/ppermute | solution.py:571
  18.4 1.4 %collective-permute-start.7 = (bf16[256,256]{1,0:T(8,128)(2,1)S(1)}, bf16[256,256]{1,0:T(8,128)(2,1)S(1)}, u32[]{:S(2)}, u32[]{:S(2)}) collective-permute-start(bf16[256,256]{1,0:T(8,128)(2,1)S(1)} %get-tuple-element.84), channel_id=1, source_target_pairs={{0,32},{32,0},{64,96},{96,64},{128,160},{160,128},{192,224},{224,1... | collective-permute-start | bytes 393224 | tf_op jit(solution)/shard_map/ppermute | solution.py:573
  21.9 10.3 %collective-permute-start.10 = (bf16[256,256]{1,0:T(8,128)(2,1)S(1)}, bf16[256,256]{1,0:T(8,128)(2,1)S(1)}, u32[]{:S(2)}, u32[]{:S(2)}) collective-permute-start(bf16[256,256]{1,0:T(8,128)(2,1)S(1)} %get-tuple-element.98), channel_id=1, source_target_pairs={{0,128},{32,160},{64,192},{96,224},{128,0},{160,32},{192,64},{224,... | collective-permute-start | bytes 393224 | tf_op jit(solution)/shard_map/ppermute | solution.py:581
  26.2 8.0 %collective-permute-start.9 = (bf16[256,256]{1,0:T(8,128)(2,1)S(1)}, bf16[256,256]{1,0:T(8,128)(2,1)S(1)}, u32[]{:S(2)}, u32[]{:S(2)}) collective-permute-start(bf16[256,256]{1,0:T(8,128)(2,1)S(1)} %get-tuple-element.95), channel_id=1, source_target_pairs={{0,192},{32,224},{64,128},{96,160},{128,64},{160,96},{192,0},{224,... | collective-permute-start | bytes 393224 | tf_op jit(solution)/shard_map/ppermute | solution.py:581
  28.0 6.2 %collective-permute-start.8 = (bf16[256,256]{1,0:T(8,128)(2,1)S(1)}, bf16[256,256]{1,0:T(8,128)(2,1)S(1)}, u32[]{:S(2)}, u32[]{:S(2)}) collective-permute-start(bf16[256,256]{1,0:T(8,128)(2,1)S(1)} %get-tuple-element.92), channel_id=1, source_target_pairs={{0,64},{32,96},{64,0},{96,32},{128,192},{160,224},{192,128},{224,1... | collective-permute-start | bytes 393224 | tf_op jit(solution)/shard_map/ppermute | solution.py:581
  34.3 1.6 %collective-permute-start.11 = (bf16[256,512]{1,0:T(8,128)(2,1)S(1)}, bf16[256,512]{1,0:T(8,128)(2,1)S(1)}, u32[]{:S(2)}, u32[]{:S(2)}) collective-permute-start(bf16[256,512]{1,0:T(8,128)(2,1)S(1)} %sum_join.1.joined.dkv), channel_id=1, source_target_pairs={{0,32},{32,0},{64,96},{96,64},{128,160},{160,128},{192,224},{224,1... | collective-permute-start | bytes 786440 | tf_op jit(solution)/shard_map/ppermute | solution.py:588
  36.0 10.3 %collective-permute-start.12 = (bf16[1536,512]{1,0:T(8,128)(2,1)S(1)}, bf16[1536,512]{1,0:T(8,128)(2,1)S(1)}, u32[]{:S(2)}, u32[]{:S(2)}) collective-permute-start(bf16[1536,512]{1,0:T(8,128)(2,1)S(1)} %transpose_tokens.1.tokens_t), channel_id=1, source_target_pairs={{0,32},{32,0},{64,96},{96,64},{128,160},{160,128},{192,224},{224,1... | collective-permute-start | bytes 4718600 | tf_op jit(solution)/shard_map/ppermute | solution.py:595
  36.2 7.8 %collective-permute-start.13 = (bf16[256,256]{1,0:T(8,128)(2,1)S(1)}, bf16[256,256]{1,0:T(8,128)(2,1)S(1)}, u32[]{:S(2)}, u32[]{:S(2)}) collective-permute-start(bf16[256,256]{1,0:T(8,128)(2,1)S(1)} %get-tuple-element.126), channel_id=1, source_target_pairs={{0,128},{32,160},{64,192},{96,224},{128,0},{160,32},{192,64},{224,... | collective-permute-start | bytes 393224 | tf_op jit(solution)/shard_map/ppermute | solution.py:596
  37.2 7.7 %collective-permute-start.14 = (bf16[256,256]{1,0:T(8,128)(2,1)S(1)}, bf16[256,256]{1,0:T(8,128)(2,1)S(1)}, u32[]{:S(2)}, u32[]{:S(2)}) collective-permute-start(bf16[256,256]{1,0:T(8,128)(2,1)S(1)} %get-tuple-element.127), channel_id=1, source_target_pairs={{0,64},{32,96},{64,0},{96,32},{128,192},{160,224},{192,128},{224,1... | collective-permute-start | bytes 393224 | tf_op jit(solution)/shard_map/ppermute | solution.py:596
  38.4 7.9 %collective-permute-start.15 = (bf16[256,256]{1,0:T(8,128)(2,1)S(1)}, bf16[256,256]{1,0:T(8,128)(2,1)S(1)}, u32[]{:S(2)}, u32[]{:S(2)}) collective-permute-start(bf16[256,256]{1,0:T(8,128)(2,1)S(1)} %get-tuple-element.128), channel_id=1, source_target_pairs={{0,192},{32,224},{64,128},{96,160},{128,64},{160,96},{192,0},{224,... | collective-permute-start | bytes 393224 | tf_op jit(solution)/shard_map/ppermute | solution.py:596
  40.3 12.1 %collective-permute-start.19 = (bf16[128,768]{1,0:T(8,128)(2,1)S(1)}, bf16[128,768]{1,0:T(8,128)(2,1)S(1)}, u32[]{:S(2)}, u32[]{:S(2)}) collective-permute-start(bf16[128,768]{1,0:T(8,128)(2,1)S(1)} %get-tuple-element.129), channel_id=1, source_target_pairs={{0,32},{32,0},{64,96},{96,64},{128,160},{160,128},{192,224},{224,1... | collective-permute-start | bytes 589832 | tf_op jit(solution)/shard_map/ppermute | solution.py:594
  46.7 10.9 %collective-permute-start.18 = (bf16[384,256]{1,0:T(8,128)(2,1)S(1)}, bf16[384,256]{1,0:T(8,128)(2,1)S(1)}, u32[]{:S(2)}, u32[]{:S(2)}) collective-permute-start(bf16[384,256]{1,0:T(8,128)(2,1)S(1)} %weight_grad_2.1), channel_id=1, source_target_pairs={{0,16},{1,17},{2,18},{3,19},{4,20},{5,21},{6,22},{7,23},{8,24},{9,... | collective-permute-start | bytes 589832 | tf_op jit(solution)/shard_map/ppermute | solution.py:599
  49.4 9.9 %collective-permute-start.17 = (bf16[384,256]{1,0:T(8,128)(2,1)S(1)}, bf16[384,256]{1,0:T(8,128)(2,1)S(1)}, u32[]{:S(2)}, u32[]{:S(2)}) collective-permute-start(bf16[384,256]{1,0:T(8,128)(2,1)S(1)} %weight_grad_3.1), channel_id=1, source_target_pairs={{0,24},{1,25},{2,26},{3,27},{4,28},{5,29},{6,30},{7,31},{8,16},{9,... | collective-permute-start | bytes 589832 | tf_op jit(solution)/shard_map/ppermute | solution.py:599
  49.9 9.5 %collective-permute-start.16 = (bf16[384,256]{1,0:T(8,128)(2,1)S(1)}, bf16[384,256]{1,0:T(8,128)(2,1)S(1)}, u32[]{:S(2)}, u32[]{:S(2)}) collective-permute-start(bf16[384,256]{1,0:T(8,128)(2,1)S(1)} %weight_grad_1.1), channel_id=1, source_target_pairs={{0,8},{1,9},{2,10},{3,11},{4,12},{5,13},{6,14},{7,15},{8,0},{9,1},... | collective-permute-start | bytes 589832 | tf_op jit(solution)/shard_map/ppermute | solution.py:599

commit v15 on v14

--- a/solution.py
+++ b/solution.py
@@ -567,8 +567,8 @@
     )
     up = stack_up(up, up_other)
     scores = {0: chip_scores(0, limits, query, up, kv)}
-    far, kv2, scores[0] = lax.optimization_barrier((far, kv2, scores[0]))
-    late = lax.ppermute(far[3], "ctx", chip_pair(1))
+    far[1], kv2, scores[0] = lax.optimization_barrier((far[1], kv2, scores[0]))
+    late = lax.ppermute(far[1], "ctx", chip_pair(3))
     mine, theirs = project_kv_far(far[1], far[3], weights, weights_other)
     theirs = lax.ppermute(theirs, "ctx", CORE)
     for i, d in enumerate((1, 3)):
@@ -578,7 +578,7 @@
     terms, grad_scores = {}, {}
     for d in (3, 1, 2):
         terms[d], grad_scores[d] = chip_terms(d, *scores[d][:2], factors, query, up)
-    back = [lax.ppermute(terms[d], "ctx", chip_pair(d)) for d in (1, 3, 2)]
+    back = [lax.ppermute(terms[d], "ctx", chip_pair(d)) for d in (3, 1, 2)]
     terms[0], grad_scores[0] = chip_terms(0, *scores[0][:2], factors, query, up)
     dq, middle, theirs = query_grad(
         [scores[d][3] for d in range(CHIPS)], [grad_scores[d] for d in range(CHIPS)]

time: 79.1 us -> 79.7 us (level)
    ppermute x2, waiting for transfers between devices: 6.27 us -> 1.89 us  [shards(): far = {d: lax.ppermute(own, 'ctx', chip_pair(d)) for d in (1, 3)}]
    ppermute x1, waiting for transfers between devices: 0.01 us -> 4.26 us  [shards(): kv2 = lax.ppermute(kv, 'ctx', chip_pair(2))]
where the time goes in v15:
time: 79.7 us; the launch traced here: 79.5 us
  waiting for transfers between devices  21.1 us (26%)
  starting transfers between devices  19.4 us (24%)
  blocking collectives  18.8 us (24%)
  Pallas kernels  18.7 us (23%)
  between operations  0.87 us (1%)
    all_to_all x1, blocking collectives, shards(): lax.all_to_all(y_sum, 'dp', 0, 0, tiled=True, axis_index_groups=Z_GROUPS)  18.8 us
    ppermute x3, waiting for transfers between devices, shards(): lax.ppermute(packed[d], 'ctx', chip_pair(d))  5.98 us
    ppermute x3, waiting for transfers between devices, shards(): back = [lax.ppermute(terms[d], 'ctx', chip_pair(d)) for d in (3, 1, 2)]  5.39 us
    ppermute x3, starting transfers between devices, shards(): lax.ppermute(terms[d], 'dp', y_pair(d))  4.95 us
    pallas_call x1, Pallas kernels, input_grad(): pl.pallas_call(input_kernel, in_specs=[WHOLE] * 4 + [STAY] * 3, out_specs...  4.82 us
    ppermute x3, starting transfers between devices, shards(): back = [lax.ppermute(terms[d], 'ctx', chip_pair(d)) for d in (3, 1, 2)]  4.54 us
    ppermute x1, waiting for transfers between devices, shards(): kv2 = lax.ppermute(kv, 'ctx', chip_pair(2))  4.26 us
    ppermute x3, starting transfers between devices, shards(): lax.ppermute(packed[d], 'ctx', chip_pair(d))  4.13 us
  transfers between devices with their start and end apart: 20, of which 11 were waited for; matrix products, arithmetic and copies ran while one was open for 0% of the time, Pallas kernels for 23%

profile of v15, /device:TPU:8, one launch (start us, length us, event | category | flops | bytes accessed | tf_op | source)
XLA Modules:
  0.0 79.5 jit_solution(11122007962794419717)
XLA Ops:
  0.6 0.1 collective-permute-start.1
  0.7 0.5 collective-permute-start.3
  1.2 1.5 %collective-permute-start = (bf16[128,1536]{1,0:T(8,128)(2,1)}, bf16[128,1536]{1,0:T(8,128)(2,1)S(1)}, u32[]{:S(2)}, u32[]{:S(2)}) collective-permute-start(bf16[128,1536]{1,0:T(8,128)(2,1)} %bitcast.6), channel_id=1, source_target_pairs={{0,64},{32,96},{64,0},{96,32},{128,192},{160,224},{192,128},{224,1... | collective-permute-start | bytes 1179656 | tf_op jit(solution)/shard_map/ppermute | solution.py:563
  2.7 2.1 %collective-permute-start.6 = (bf16[128,1536]{1,0:T(8,128)(2,1)}, bf16[128,1536]{1,0:T(8,128)(2,1)S(1)}, u32[]{:S(2)}, u32[]{:S(2)}) collective-permute-start(bf16[128,1536]{1,0:T(8,128)(2,1)} %bitcast.7), channel_id=1, source_target_pairs={{0,192},{32,224},{64,128},{96,160},{128,64},{160,96},{192,0},{224,... | collective-permute-start | bytes 1179656 | tf_op jit(solution)/shard_map/ppermute | solution.py:563
  4.8 0.0 collective-permute-start.2
  4.8 1.6 %project_kv_own.1 = (bf16[1536,256]{1,0:T(8,128)(2,1)S(1)}, bf16[128,256]{1,0:T(8,128)(2,1)S(1)}) custom-call(bf16[128,1536]{1,0:T(8,128)(2,1)} %bitcast.8, bf16[1536,256]{1,0:T(8,128)(2,1)} %w_key.5, bf16[1536,256]{1,0:T(8,128)(2,1)} %w_value.5), custom_call_target="tpu_custom_call" | custom-call | flops 1 | bytes 1 | tf_op jit(solution)/shard_map/project_kv_own/pallas_call | solution.py:100
  6.4 0.0 copy-start
  6.4 0.0 collective-permute-done.2.mask_other
  6.4 0.0 collective-permute-done.1.other
  6.4 0.0 collective-permute-done.3.up_other
  6.5 0.3 project_kv.1.refs_0_
  6.7 0.7 collective-permute-start.4
  7.5 0.1 stack_up.1.up
  7.6 3.2 %project_query.1 = (bf16[1536,128]{1,0:T(8,128)(2,1)S(1)}, s32[16,256]{1,0:T(8,128)S(1)}, bf16[1536,256]{1,0:T(8,128)(2,1)S(1)}) custom-call(bf16[128,1536]{1,0:T(8,128)(2,1)S(1)} %bitcast.9, bf16[128,1536]{1,0:T(8,128)(2,1)S(1)} %collective-permute-done.1.other, bf16[1536,1536]{1,0:T(8,128)(2,1)} %w_query.3, bf16[1536,256]{1,0:T(8,128)(2,1)} %w_key.5, ...), custom_call_target="tpu_custom_call" | custom-call | flops 1 | bytes 1 | tf_op jit(solution)/shard_map/project_query/pallas_call | solution.py:221
  10.8 0.7 chip_scores_0.1
  11.5 1.9 %collective-permute-done.far1 = bf16[128,1536]{1,0:T(8,128)(2,1)S(1)} collective-permute-done((bf16[128,1536]{1,0:T(8,128)(2,1)}, bf16[128,1536]{1,0:T(8,128)(2,1)S(1)}, u32[]{:S(2)}, u32[]{:S(2)}) %collective-permute-start) | collective-permute-done | bytes 393248 | tf_op jit(solution)/shard_map/ppermute | solution.py:563
  13.4 4.3 %collective-permute-done.4.refs_0_ = bf16[256,256]{1,0:T(8,128)(2,1)S(1)} collective-permute-done((bf16[256,256]{1,0:T(8,128)(2,1)S(1)}, bf16[256,256]{1,0:T(8,128)(2,1)S(1)}, u32[]{:S(2)}, u32[]{:S(2)}) %collective-permute-start.4) | collective-permute-done | bytes 131104 | tf_op jit(solution)/shard_map/ppermute | solution.py:562
  17.7 0.5 collective-permute-start.5
  18.2 0.6 project_kv_far.1
  18.7 0.1 collective-permute-start.7
  18.8 0.7 chip_scores_2.1
  19.6 0.6 collective-permute-done.7.refs_1_
  20.2 0.7 chip_scores_1.1
  20.9 0.7 chip_scores_3.1
  21.7 0.6 chip_terms_2.1
  22.3 1.8 %collective-permute-start.10 = (bf16[256,256]{1,0:T(8,128)(2,1)S(1)}, bf16[256,256]{1,0:T(8,128)(2,1)S(1)}, u32[]{:S(2)}, u32[]{:S(2)}) collective-permute-start(bf16[256,256]{1,0:T(8,128)(2,1)S(1)} %get-tuple-element.96), channel_id=1, source_target_pairs={{0,128},{32,160},{64,192},{96,224},{128,0},{160,32},{192,64},{224,... | collective-permute-start | bytes 393224 | tf_op jit(solution)/shard_map/ppermute | solution.py:581
  24.1 0.6 chip_terms_1.1
  24.7 2.0 %collective-permute-start.9 = (bf16[256,256]{1,0:T(8,128)(2,1)S(1)}, bf16[256,256]{1,0:T(8,128)(2,1)S(1)}, u32[]{:S(2)}, u32[]{:S(2)}) collective-permute-start(bf16[256,256]{1,0:T(8,128)(2,1)S(1)} %get-tuple-element.93), channel_id=1, source_target_pairs={{0,64},{32,96},{64,0},{96,32},{128,192},{160,224},{192,128},{224,1... | collective-permute-start | bytes 393224 | tf_op jit(solution)/shard_map/ppermute | solution.py:581
  26.7 0.6 chip_terms_3.1
  27.3 0.7 collective-permute-start.8
  28.1 0.6 chip_terms_0.1
  28.7 0.7 query_grad.1
  29.3 0.9 %collective-permute-done.10.d = bf16[256,256]{1,0:T(8,128)(2,1)S(1)} collective-permute-done((bf16[256,256]{1,0:T(8,128)(2,1)S(1)}, bf16[256,256]{1,0:T(8,128)(2,1)S(1)}, u32[]{:S(2)}, u32[]{:S(2)}) %collective-permute-start.10) | collective-permute-done | bytes 131104 | tf_op jit(solution)/shard_map/ppermute | solution.py:581
  30.3 2.1 %collective-permute-done.9.c = bf16[256,256]{1,0:T(8,128)(2,1)S(1)} collective-permute-done((bf16[256,256]{1,0:T(8,128)(2,1)S(1)}, bf16[256,256]{1,0:T(8,128)(2,1)S(1)}, u32[]{:S(2)}, u32[]{:S(2)}) %collective-permute-start.9) | collective-permute-done | bytes 131104 | tf_op jit(solution)/shard_map/ppermute | solution.py:581
  32.4 2.4 %collective-permute-done.8.b = bf16[256,256]{1,0:T(8,128)(2,1)S(1)} collective-permute-done((bf16[256,256]{1,0:T(8,128)(2,1)S(1)}, bf16[256,256]{1,0:T(8,128)(2,1)S(1)}, u32[]{:S(2)}, u32[]{:S(2)}) %collective-permute-start.8) | collective-permute-done | bytes 131104 | tf_op jit(solution)/shard_map/ppermute | solution.py:581
  34.7 0.0 collective-permute-done.5.far2
  34.7 0.1 sum_join.1.joined.dkv
  34.8 0.1 collective-permute-start.11
  34.9 0.5 transpose_tokens.1.tokens_t
  35.4 1.1 %collective-permute-done.11.joined_other.dkv_other = bf16[256,512]{1,0:T(8,128)(2,1)S(1)} collective-permute-done((bf16[256,512]{1,0:T(8,128)(2,1)S(1)}, bf16[256,512]{1,0:T(8,128)(2,1)S(1)}, u32[]{:S(2)}, u32[]{:S(2)}) %collective-permute-start.11) | collective-permute-done | bytes 262176 | tf_op jit(solution)/shard_map/ppermute | solution.py:588
  36.4 0.1 pack.1
  36.5 0.2 collective-permute-start.12
  36.7 1.4 %collective-permute-start.14 = (bf16[256,256]{1,0:T(8,128)(2,1)S(1)}, bf16[256,256]{1,0:T(8,128)(2,1)S(1)}, u32[]{:S(2)}, u32[]{:S(2)}) collective-permute-start(bf16[256,256]{1,0:T(8,128)(2,1)S(1)} %get-tuple-element.125), channel_id=1, source_target_pairs={{0,64},{32,96},{64,0},{96,32},{128,192},{160,224},{192,128},{224,1... | collective-permute-start | bytes 393224 | tf_op jit(solution)/shard_map/ppermute | solution.py:596
  38.1 2.8 %collective-permute-start.15 = (bf16[256,256]{1,0:T(8,128)(2,1)S(1)}, bf16[256,256]{1,0:T(8,128)(2,1)S(1)}, u32[]{:S(2)}, u32[]{:S(2)}) collective-permute-start(bf16[256,256]{1,0:T(8,128)(2,1)S(1)} %get-tuple-element.126), channel_id=1, source_target_pairs={{0,192},{32,224},{64,128},{96,160},{128,64},{160,96},{192,0},{224,... | collective-permute-start | bytes 393224 | tf_op jit(solution)/shard_map/ppermute | solution.py:596
  40.8 0.0 collective-permute-start.19
  40.8 3.8 %collective-permute-done.13.b = bf16[256,256]{1,0:T(8,128)(2,1)S(1)} collective-permute-done((bf16[256,256]{1,0:T(8,128)(2,1)S(1)}, bf16[256,256]{1,0:T(8,128)(2,1)S(1)}, u32[]{:S(2)}, u32[]{:S(2)}) %collective-permute-start.13) | collective-permute-done | bytes 131104 | tf_op jit(solution)/shard_map/ppermute | solution.py:596
  44.6 0.0 collective-permute-done.14.c
  44.6 2.2 %collective-permute-done.15.d = bf16[256,256]{1,0:T(8,128)(2,1)S(1)} collective-permute-done((bf16[256,256]{1,0:T(8,128)(2,1)S(1)}, bf16[256,256]{1,0:T(8,128)(2,1)S(1)}, u32[]{:S(2)}, u32[]{:S(2)}) %collective-permute-start.15) | collective-permute-done | bytes 131104 | tf_op jit(solution)/shard_map/ppermute | solution.py:596
  46.8 0.0 collective-permute-done.12.other_t
  46.8 0.4 weight_grad_2.1
  47.2 2.4 %collective-permute-start.18 = (bf16[384,256]{1,0:T(8,128)(2,1)S(1)}, bf16[384,256]{1,0:T(8,128)(2,1)S(1)}, u32[]{:S(2)}, u32[]{:S(2)}) collective-permute-start(bf16[384,256]{1,0:T(8,128)(2,1)S(1)} %weight_grad_2.1), channel_id=1, source_target_pairs={{0,16},{1,17},{2,18},{3,19},{4,20},{5,21},{6,22},{7,23},{8,24},{9,... | collective-permute-start | bytes 589832 | tf_op jit(solution)/shard_map/ppermute | solution.py:599
  49.6 0.4 weight_grad_3.1
  50.0 0.1 collective-permute-start.17
  50.1 0.4 weight_grad_1.1
  50.4 2.5 %collective-permute-start.16 = (bf16[384,256]{1,0:T(8,128)(2,1)S(1)}, bf16[384,256]{1,0:T(8,128)(2,1)S(1)}, u32[]{:S(2)}, u32[]{:S(2)}) collective-permute-start(bf16[384,256]{1,0:T(8,128)(2,1)S(1)} %weight_grad_1.1), channel_id=1, source_target_pairs={{0,8},{1,9},{2,10},{3,11},{4,12},{5,13},{6,14},{7,15},{8,0},{9,1},... | collective-permute-start | bytes 589832 | tf_op jit(solution)/shard_map/ppermute | solution.py:599
  52.9 0.0 collective-permute-done.19.dq_other
  52.9 4.8 %input_grad.1 = bf16[128,1536]{1,0:T(8,128)(2,1)} custom-call(bf16[256,768]{1,0:T(8,128)(2,1)S(1)} %get-tuple-element.116.dq, bf16[128,768]{1,0:T(8,128)(2,1)S(1)} %collective-permute-done.19.dq_other, bf16[256,512]{1,0:T(8,128)(2,1)S(1)} %sum_join.1.joined.dkv, bf16[256,512]{1,0:T(8,128)(2,1)S(1)} %collective-permute-done.11.joined_other.dkv_other, ...), custom_call_target="tpu_custom_call" | custom-call | flops 1 | bytes 1 | tf_op jit(solution)/shard_map/input_grad/pallas_call | solution.py:536
  57.7 0.4 weight_grad_0.1.a
  58.1 0.0 collective-permute-done.18.d
  58.1 1.7 %collective-permute-done.17.c = bf16[384,256]{1,0:T(8,128)(2,1)S(1)} collective-permute-done((bf16[384,256]{1,0:T(8,128)(2,1)S(1)}, bf16[384,256]{1,0:T(8,128)(2,1)S(1)}, u32[]{:S(2)}, u32[]{:S(2)}) %collective-permute-start.17) | collective-permute-done | bytes 196640 | tf_op jit(solution)/shard_map/ppermute | solution.py:599
  59.8 0.2 collective-permute-done.16.b
  60.0 0.1 sum_four.1
  60.1 18.8 %all_to_all.9 = bf16[8,48,256]{2,1,0:T(8,128)(2,1)S(1)} all-to-all(bf16[8,48,256]{2,1,0:T(8,128)(2,1)S(1)} %bitcast.11), channel_id=1, replica_groups={{0,1,2,3,4,5,6,7},{8,9,10,11,12,13,14,15},{16,17,18,19,20,21,22,23},{24..., dimensions={0} | all-to-all | bytes 393216 | tf_op jit(solution)/shard_map/all_to_all | solution.py:605
  78.8 0.6 convert_reduce_fusion
  (6 shorter events, 0.0 us)
Async XLA Ops:
  0.6 5.8 %collective-permute-start.1 = (bf16[128,1536]{1,0:T(8,128)(2,1)}, bf16[128,1536]{1,0:T(8,128)(2,1)S(1)}, u32[]{:S(2)}, u32[]{:S(2)}) collective-permute-start(bf16[128,1536]{1,0:T(8,128)(2,1)} %bitcast.5), channel_id=1, source_target_pairs={{0,32},{32,0},{64,96},{96,64},{128,160},{160,128},{192,224},{224,1... | collective-permute-start | bytes 1179656 | tf_op jit(solution)/shard_map/ppermute | solution.py:554
  0.7 5.7 %collective-permute-start.3 = (bf16[128,1536]{1,0:T(8,128)(2,1)}, bf16[128,1536]{1,0:T(8,128)(2,1)S(1)}, u32[]{:S(2)}, u32[]{:S(2)}) collective-permute-start(bf16[128,1536]{1,0:T(8,128)(2,1)} %bitcast.12), channel_id=1, source_target_pairs={{0,32},{32,0},{64,96},{96,64},{128,160},{160,128},{192,224},{224,1... | collective-permute-start | bytes 1179656 | tf_op jit(solution)/shard_map/ppermute | solution.py:555
  1.2 12.2 %collective-permute-start = (bf16[128,1536]{1,0:T(8,128)(2,1)}, bf16[128,1536]{1,0:T(8,128)(2,1)S(1)}, u32[]{:S(2)}, u32[]{:S(2)}) collective-permute-start(bf16[128,1536]{1,0:T(8,128)(2,1)} %bitcast.6), channel_id=1, source_target_pairs={{0,64},{32,96},{64,0},{96,32},{128,192},{160,224},{192,128},{224,1... | collective-permute-start | bytes 1179656 | tf_op jit(solution)/shard_map/ppermute | solution.py:563
  2.7 15.4 %collective-permute-start.6 = (bf16[128,1536]{1,0:T(8,128)(2,1)}, bf16[128,1536]{1,0:T(8,128)(2,1)S(1)}, u32[]{:S(2)}, u32[]{:S(2)}) collective-permute-start(bf16[128,1536]{1,0:T(8,128)(2,1)} %bitcast.7), channel_id=1, source_target_pairs={{0,192},{32,224},{64,128},{96,160},{128,64},{160,96},{192,0},{224,... | collective-permute-start | bytes 1179656 | tf_op jit(solution)/shard_map/ppermute | solution.py:563
  4.8 2.7 %copy-start.1 = (bf16[1,128,1536]{2,1,0:T(8,128)(2,1)S(1)}, bf16[1,128,1536]{2,1,0:T(8,128)(2,1)}, u32[]{:S(2)}) copy-start(bf16[1,128,1536]{2,1,0:T(8,128)(2,1)} %param.8) | copy-start | bytes 1179652
  4.8 1.6 %collective-permute-start.2 = (s32[1,8]{1,0:T(1,128)}, s32[1,8]{1,0:T(1,128)S(1)}, u32[]{:S(2)}, u32[]{:S(2)}) collective-permute-start(s32[1,8]{1,0:T(1,128)} %bitcast.15), channel_id=1, source_target_pairs={{0,32},{32,0},{64,96},{96,64},{128,160},{160,128},{192,224},{224,1... | collective-permute-start | bytes 104 | tf_op jit(solution)/shard_map/ppermute | solution.py:556
  6.4 1.1 %copy-start = (bf16[1,128,1536]{2,1,0:T(8,128)(2,1)S(1)}, bf16[1,128,1536]{2,1,0:T(8,128)(2,1)}, u32[]{:S(2)}) copy-start(bf16[1,128,1536]{2,1,0:T(8,128)(2,1)} %param.7) | copy-start | bytes 1179652
  6.7 10.9 %collective-permute-start.4 = (bf16[256,256]{1,0:T(8,128)(2,1)S(1)}, bf16[256,256]{1,0:T(8,128)(2,1)S(1)}, u32[]{:S(2)}, u32[]{:S(2)}) collective-permute-start(bf16[256,256]{1,0:T(8,128)(2,1)S(1)} %project_kv.1.refs_0_), channel_id=1, source_target_pairs={{0,128},{32,160},{64,192},{96,224},{128,0},{160,32},{192,64},{224,... | collective-permute-start | bytes 393224 | tf_op jit(solution)/shard_map/ppermute | solution.py:562
  17.7 17.1 %collective-permute-start.5 = (bf16[128,1536]{1,0:T(8,128)(2,1)S(1)}, bf16[128,1536]{1,0:T(8,128)(2,1)S(1)}, u32[]{:S(2)}, u32[]{:S(2)}) collective-permute-start(bf16[128,1536]{1,0:T(8,128)(2,1)S(1)} %collective-permute-done.far1), channel_id=1, source_target_pairs={{0,192},{32,224},{64,128},{96,160},{128,64},{160,96},{192,0},{224,... | collective-permute-start | bytes 1179656 | tf_op jit(solution)/shard_map/ppermute | solution.py:571
  18.7 1.4 %collective-permute-start.7 = (bf16[256,256]{1,0:T(8,128)(2,1)S(1)}, bf16[256,256]{1,0:T(8,128)(2,1)S(1)}, u32[]{:S(2)}, u32[]{:S(2)}) collective-permute-start(bf16[256,256]{1,0:T(8,128)(2,1)S(1)} %get-tuple-element.82), channel_id=1, source_target_pairs={{0,32},{32,0},{64,96},{96,64},{128,160},{160,128},{192,224},{224,1... | collective-permute-start | bytes 393224 | tf_op jit(solution)/shard_map/ppermute | solution.py:573
  22.3 8.0 %collective-permute-start.10 = (bf16[256,256]{1,0:T(8,128)(2,1)S(1)}, bf16[256,256]{1,0:T(8,128)(2,1)S(1)}, u32[]{:S(2)}, u32[]{:S(2)}) collective-permute-start(bf16[256,256]{1,0:T(8,128)(2,1)S(1)} %get-tuple-element.96), channel_id=1, source_target_pairs={{0,128},{32,160},{64,192},{96,224},{128,0},{160,32},{192,64},{224,... | collective-permute-start | bytes 393224 | tf_op jit(solution)/shard_map/ppermute | solution.py:581
  24.7 7.7 %collective-permute-start.9 = (bf16[256,256]{1,0:T(8,128)(2,1)S(1)}, bf16[256,256]{1,0:T(8,128)(2,1)S(1)}, u32[]{:S(2)}, u32[]{:S(2)}) collective-permute-start(bf16[256,256]{1,0:T(8,128)(2,1)S(1)} %get-tuple-element.93), channel_id=1, source_target_pairs={{0,64},{32,96},{64,0},{96,32},{128,192},{160,224},{192,128},{224,1... | collective-permute-start | bytes 393224 | tf_op jit(solution)/shard_map/ppermute | solution.py:581
  27.3 7.4 %collective-permute-start.8 = (bf16[256,256]{1,0:T(8,128)(2,1)S(1)}, bf16[256,256]{1,0:T(8,128)(2,1)S(1)}, u32[]{:S(2)}, u32[]{:S(2)}) collective-permute-start(bf16[256,256]{1,0:T(8,128)(2,1)S(1)} %get-tuple-element.90), channel_id=1, source_target_pairs={{0,192},{32,224},{64,128},{96,160},{128,64},{160,96},{192,0},{224,... | collective-permute-start | bytes 393224 | tf_op jit(solution)/shard_map/ppermute | solution.py:581
  34.8 1.6 %collective-permute-start.11 = (bf16[256,512]{1,0:T(8,128)(2,1)S(1)}, bf16[256,512]{1,0:T(8,128)(2,1)S(1)}, u32[]{:S(2)}, u32[]{:S(2)}) collective-permute-start(bf16[256,512]{1,0:T(8,128)(2,1)S(1)} %sum_join.1.joined.dkv), channel_id=1, source_target_pairs={{0,32},{32,0},{64,96},{96,64},{128,160},{160,128},{192,224},{224,1... | collective-permute-start | bytes 786440 | tf_op jit(solution)/shard_map/ppermute | solution.py:588
  36.5 10.3 %collective-permute-start.12 = (bf16[1536,512]{1,0:T(8,128)(2,1)S(1)}, bf16[1536,512]{1,0:T(8,128)(2,1)S(1)}, u32[]{:S(2)}, u32[]{:S(2)}) collective-permute-start(bf16[1536,512]{1,0:T(8,128)(2,1)S(1)} %transpose_tokens.1.tokens_t), channel_id=1, source_target_pairs={{0,32},{32,0},{64,96},{96,64},{128,160},{160,128},{192,224},{224,1... | collective-permute-start | bytes 4718600 | tf_op jit(solution)/shard_map/ppermute | solution.py:595
  36.7 7.9 %collective-permute-start.13 = (bf16[256,256]{1,0:T(8,128)(2,1)S(1)}, bf16[256,256]{1,0:T(8,128)(2,1)S(1)}, u32[]{:S(2)}, u32[]{:S(2)}) collective-permute-start(bf16[256,256]{1,0:T(8,128)(2,1)S(1)} %get-tuple-element.124), channel_id=1, source_target_pairs={{0,128},{32,160},{64,192},{96,224},{128,0},{160,32},{192,64},{224,... | collective-permute-start | bytes 393224 | tf_op jit(solution)/shard_map/ppermute | solution.py:596
  36.7 7.9 %collective-permute-start.14 = (bf16[256,256]{1,0:T(8,128)(2,1)S(1)}, bf16[256,256]{1,0:T(8,128)(2,1)S(1)}, u32[]{:S(2)}, u32[]{:S(2)}) collective-permute-start(bf16[256,256]{1,0:T(8,128)(2,1)S(1)} %get-tuple-element.125), channel_id=1, source_target_pairs={{0,64},{32,96},{64,0},{96,32},{128,192},{160,224},{192,128},{224,1... | collective-permute-start | bytes 393224 | tf_op jit(solution)/shard_map/ppermute | solution.py:596
  38.1 8.8 %collective-permute-start.15 = (bf16[256,256]{1,0:T(8,128)(2,1)S(1)}, bf16[256,256]{1,0:T(8,128)(2,1)S(1)}, u32[]{:S(2)}, u32[]{:S(2)}) collective-permute-start(bf16[256,256]{1,0:T(8,128)(2,1)S(1)} %get-tuple-element.126), channel_id=1, source_target_pairs={{0,192},{32,224},{64,128},{96,160},{128,64},{160,96},{192,0},{224,... | collective-permute-start | bytes 393224 | tf_op jit(solution)/shard_map/ppermute | solution.py:596
  40.8 12.1 %collective-permute-start.19 = (bf16[128,768]{1,0:T(8,128)(2,1)S(1)}, bf16[128,768]{1,0:T(8,128)(2,1)S(1)}, u32[]{:S(2)}, u32[]{:S(2)}) collective-permute-start(bf16[128,768]{1,0:T(8,128)(2,1)S(1)} %get-tuple-element.127), channel_id=1, source_target_pairs={{0,32},{32,0},{64,96},{96,64},{128,160},{160,128},{192,224},{224,1... | collective-permute-start | bytes 589832 | tf_op jit(solution)/shard_map/ppermute | solution.py:594
  47.2 10.9 %collective-permute-start.18 = (bf16[384,256]{1,0:T(8,128)(2,1)S(1)}, bf16[384,256]{1,0:T(8,128)(2,1)S(1)}, u32[]{:S(2)}, u32[]{:S(2)}) collective-permute-start(bf16[384,256]{1,0:T(8,128)(2,1)S(1)} %weight_grad_2.1), channel_id=1, source_target_pairs={{0,16},{1,17},{2,18},{3,19},{4,20},{5,21},{6,22},{7,23},{8,24},{9,... | collective-permute-start | bytes 589832 | tf_op jit(solution)/shard_map/ppermute | solution.py:599
  50.0 9.9 %collective-permute-start.17 = (bf16[384,256]{1,0:T(8,128)(2,1)S(1)}, bf16[384,256]{1,0:T(8,128)(2,1)S(1)}, u32[]{:S(2)}, u32[]{:S(2)}) collective-permute-start(bf16[384,256]{1,0:T(8,128)(2,1)S(1)} %weight_grad_3.1), channel_id=1, source_target_pairs={{0,24},{1,25},{2,26},{3,27},{4,28},{5,29},{6,30},{7,31},{8,16},{9,... | collective-permute-start | bytes 589832 | tf_op jit(solution)/shard_map/ppermute | solution.py:599
  50.4 9.5 %collective-permute-start.16 = (bf16[384,256]{1,0:T(8,128)(2,1)S(1)}, bf16[384,256]{1,0:T(8,128)(2,1)S(1)}, u32[]{:S(2)}, u32[]{:S(2)}) collective-permute-start(bf16[384,256]{1,0:T(8,128)(2,1)S(1)} %weight_grad_1.1), channel_id=1, source_target_pairs={{0,8},{1,9},{2,10},{3,11},{4,12},{5,13},{6,14},{7,15},{8,0},{9,1},... | collective-permute-start | bytes 589832 | tf_op jit(solution)/shard_map/ppermute | solution.py:599

commit v16 on v15

--- a/solution.py
+++ b/solution.py
@@ -578,7 +578,7 @@
     terms, grad_scores = {}, {}
     for d in (3, 1, 2):
         terms[d], grad_scores[d] = chip_terms(d, *scores[d][:2], factors, query, up)
-    back = [lax.ppermute(terms[d], "ctx", chip_pair(d)) for d in (3, 1, 2)]
+    back = [lax.ppermute(terms[d], "ctx", chip_pair(d)) for d in (1, 3, 2)]
     terms[0], grad_scores[0] = chip_terms(0, *scores[0][:2], factors, query, up)
     dq, middle, theirs = query_grad(
         [scores[d][3] for d in range(CHIPS)], [grad_scores[d] for d in range(CHIPS)]

time: 79.7 us -> 79.7 us (level)
  transfers between devices with their start and end apart: 20 -> 20, of which waited for: 11 -> 10; matrix products, arithmetic and copies ran while one was open for 0% -> 0% of each run, Pallas kernels for 23% -> 23%
where the time goes in v16:
time: 79.7 us; the launch traced here: 79.5 us
  waiting for transfers between devices  21.5 us (27%)
  starting transfers between devices  18.9 us (24%)
  blocking collectives  18.8 us (24%)
  Pallas kernels  18.7 us (23%)
  between operations  0.87 us (1%)
    all_to_all x1, blocking collectives, shards(): lax.all_to_all(y_sum, 'dp', 0, 0, tiled=True, axis_index_groups=Z_GROUPS)  18.8 us
    ppermute x3, waiting for transfers between devices, shards(): lax.ppermute(packed[d], 'ctx', chip_pair(d))  5.98 us
    ppermute x3, waiting for transfers between devices, shards(): back = [lax.ppermute(terms[d], 'ctx', chip_pair(d)) for d in (1, 3, 2)]  5.85 us
    ppermute x3, starting transfers between devices, shards(): lax.ppermute(terms[d], 'dp', y_pair(d))  4.95 us
    pallas_call x1, Pallas kernels, input_grad(): pl.pallas_call(input_kernel, in_specs=[WHOLE] * 4 + [STAY] * 3, out_specs...  4.82 us
    ppermute x1, waiting for transfers between devices, shards(): kv2 = lax.ppermute(kv, 'ctx', chip_pair(2))  4.26 us
    ppermute x3, starting transfers between devices, shards(): lax.ppermute(packed[d], 'ctx', chip_pair(d))  4.13 us
    ppermute x3, starting transfers between devices, shards(): back = [lax.ppermute(terms[d], 'ctx', chip_pair(d)) for d in (1, 3, 2)]  4.08 us
  transfers between devices with their start and end apart: 20, of which 10 were waited for; matrix products, arithmetic and copies ran while one was open for 0% of the time, Pallas kernels for 23%

profile of v16, /device:TPU:8, one launch (start us, length us, event | category | flops | bytes accessed | tf_op | source)
XLA Modules:
  0.0 79.5 jit_solution(2626149494116110622)
XLA Ops:
  0.6 0.1 collective-permute-start.1
  0.7 0.5 collective-permute-start.3
  1.2 1.5 %collective-permute-start = (bf16[128,1536]{1,0:T(8,128)(2,1)}, bf16[128,1536]{1,0:T(8,128)(2,1)S(1)}, u32[]{:S(2)}, u32[]{:S(2)}) collective-permute-start(bf16[128,1536]{1,0:T(8,128)(2,1)} %bitcast.6), channel_id=1, source_target_pairs={{0,64},{32,96},{64,0},{96,32},{128,192},{160,224},{192,128},{224,1... | collective-permute-start | bytes 1179656 | tf_op jit(solution)/shard_map/ppermute | solution.py:563
  2.7 2.1 %collective-permute-start.6 = (bf16[128,1536]{1,0:T(8,128)(2,1)}, bf16[128,1536]{1,0:T(8,128)(2,1)S(1)}, u32[]{:S(2)}, u32[]{:S(2)}) collective-permute-start(bf16[128,1536]{1,0:T(8,128)(2,1)} %bitcast.7), channel_id=1, source_target_pairs={{0,192},{32,224},{64,128},{96,160},{128,64},{160,96},{192,0},{224,... | collective-permute-start | bytes 1179656 | tf_op jit(solution)/shard_map/ppermute | solution.py:563
  4.8 0.0 collective-permute-start.2
  4.8 1.6 %project_kv_own.1 = (bf16[1536,256]{1,0:T(8,128)(2,1)S(1)}, bf16[128,256]{1,0:T(8,128)(2,1)S(1)}) custom-call(bf16[128,1536]{1,0:T(8,128)(2,1)} %bitcast.8, bf16[1536,256]{1,0:T(8,128)(2,1)} %w_key.5, bf16[1536,256]{1,0:T(8,128)(2,1)} %w_value.5), custom_call_target="tpu_custom_call" | custom-call | flops 1 | bytes 1 | tf_op jit(solution)/shard_map/project_kv_own/pallas_call | solution.py:100
  6.4 0.0 copy-start
  6.4 0.0 collective-permute-done.2.mask_other
  6.4 0.0 collective-permute-done.1.other
  6.4 0.0 collective-permute-done.3.up_other
  6.5 0.3 project_kv.1.refs_0_
  6.7 0.7 collective-permute-start.4
  7.5 0.1 stack_up.1.up
  7.6 3.2 %project_query.1 = (bf16[1536,128]{1,0:T(8,128)(2,1)S(1)}, s32[16,256]{1,0:T(8,128)S(1)}, bf16[1536,256]{1,0:T(8,128)(2,1)S(1)}) custom-call(bf16[128,1536]{1,0:T(8,128)(2,1)S(1)} %bitcast.9, bf16[128,1536]{1,0:T(8,128)(2,1)S(1)} %collective-permute-done.1.other, bf16[1536,1536]{1,0:T(8,128)(2,1)} %w_query.3, bf16[1536,256]{1,0:T(8,128)(2,1)} %w_key.5, ...), custom_call_target="tpu_custom_call" | custom-call | flops 1 | bytes 1 | tf_op jit(solution)/shard_map/project_query/pallas_call | solution.py:221
  10.8 0.7 chip_scores_0.1
  11.5 1.9 %collective-permute-done.far1 = bf16[128,1536]{1,0:T(8,128)(2,1)S(1)} collective-permute-done((bf16[128,1536]{1,0:T(8,128)(2,1)}, bf16[128,1536]{1,0:T(8,128)(2,1)S(1)}, u32[]{:S(2)}, u32[]{:S(2)}) %collective-permute-start) | collective-permute-done | bytes 393248 | tf_op jit(solution)/shard_map/ppermute | solution.py:563
  13.4 4.3 %collective-permute-done.4.refs_0_ = bf16[256,256]{1,0:T(8,128)(2,1)S(1)} collective-permute-done((bf16[256,256]{1,0:T(8,128)(2,1)S(1)}, bf16[256,256]{1,0:T(8,128)(2,1)S(1)}, u32[]{:S(2)}, u32[]{:S(2)}) %collective-permute-start.4) | collective-permute-done | bytes 131104 | tf_op jit(solution)/shard_map/ppermute | solution.py:562
  17.7 0.5 collective-permute-start.5
  18.1 0.0 collective-permute-done.6.far3
  18.2 0.6 project_kv_far.1
  18.7 0.1 collective-permute-start.7
  18.8 0.7 chip_scores_2.1
  19.6 0.6 collective-permute-done.7.refs_1_
  20.2 0.7 chip_scores_3.1
  20.9 0.7 chip_scores_1.1
  21.7 0.6 chip_terms_2.1
  22.3 1.8 %collective-permute-start.10 = (bf16[256,256]{1,0:T(8,128)(2,1)S(1)}, bf16[256,256]{1,0:T(8,128)(2,1)S(1)}, u32[]{:S(2)}, u32[]{:S(2)}) collective-permute-start(bf16[256,256]{1,0:T(8,128)(2,1)S(1)} %get-tuple-element.96), channel_id=1, source_target_pairs={{0,128},{32,160},{64,192},{96,224},{128,0},{160,32},{192,64},{224,... | collective-permute-start | bytes 393224 | tf_op jit(solution)/shard_map/ppermute | solution.py:581
  24.1 0.6 chip_terms_3.1
  24.7 1.3 %collective-permute-start.9 = (bf16[256,256]{1,0:T(8,128)(2,1)S(1)}, bf16[256,256]{1,0:T(8,128)(2,1)S(1)}, u32[]{:S(2)}, u32[]{:S(2)}) collective-permute-start(bf16[256,256]{1,0:T(8,128)(2,1)S(1)} %get-tuple-element.93), channel_id=1, source_target_pairs={{0,192},{32,224},{64,128},{96,160},{128,64},{160,96},{192,0},{224,... | collective-permute-start | bytes 393224 | tf_op jit(solution)/shard_map/ppermute | solution.py:581
  26.0 0.6 chip_terms_1.1
  26.6 0.9 %collective-permute-start.8 = (bf16[256,256]{1,0:T(8,128)(2,1)S(1)}, bf16[256,256]{1,0:T(8,128)(2,1)S(1)}, u32[]{:S(2)}, u32[]{:S(2)}) collective-permute-start(bf16[256,256]{1,0:T(8,128)(2,1)S(1)} %get-tuple-element.90), channel_id=1, source_target_pairs={{0,64},{32,96},{64,0},{96,32},{128,192},{160,224},{192,128},{224,1... | collective-permute-start | bytes 393224 | tf_op jit(solution)/shard_map/ppermute | solution.py:581
  27.6 0.6 chip_terms_0.1
  28.2 0.7 query_grad.1
  28.9 0.7 collective-permute-done.10.d
  29.5 5.2 %collective-permute-done.9.c = bf16[256,256]{1,0:T(8,128)(2,1)S(1)} collective-permute-done((bf16[256,256]{1,0:T(8,128)(2,1)S(1)}, bf16[256,256]{1,0:T(8,128)(2,1)S(1)}, u32[]{:S(2)}, u32[]{:S(2)}) %collective-permute-start.9) | collective-permute-done | bytes 131104 | tf_op jit(solution)/shard_map/ppermute | solution.py:581
  34.7 0.0 collective-permute-done.8.b
  34.7 0.0 collective-permute-done.5.far2
  34.7 0.1 sum_join.1.joined.dkv
  34.8 0.1 collective-permute-start.11
  34.9 0.5 transpose_tokens.1.tokens_t
  35.4 1.1 %collective-permute-done.11.joined_other.dkv_other = bf16[256,512]{1,0:T(8,128)(2,1)S(1)} collective-permute-done((bf16[256,512]{1,0:T(8,128)(2,1)S(1)}, bf16[256,512]{1,0:T(8,128)(2,1)S(1)}, u32[]{:S(2)}, u32[]{:S(2)}) %collective-permute-start.11) | collective-permute-done | bytes 262176 | tf_op jit(solution)/shard_map/ppermute | solution.py:588
  36.4 0.1 pack.1
  36.5 0.2 collective-permute-start.12
  36.7 0.0 collective-permute-start.13
  36.7 1.4 %collective-permute-start.14 = (bf16[256,256]{1,0:T(8,128)(2,1)S(1)}, bf16[256,256]{1,0:T(8,128)(2,1)S(1)}, u32[]{:S(2)}, u32[]{:S(2)}) collective-permute-start(bf16[256,256]{1,0:T(8,128)(2,1)S(1)} %get-tuple-element.125), channel_id=1, source_target_pairs={{0,64},{32,96},{64,0},{96,32},{128,192},{160,224},{192,128},{224,1... | collective-permute-start | bytes 393224 | tf_op jit(solution)/shard_map/ppermute | solution.py:596
  38.1 2.8 %collective-permute-start.15 = (bf16[256,256]{1,0:T(8,128)(2,1)S(1)}, bf16[256,256]{1,0:T(8,128)(2,1)S(1)}, u32[]{:S(2)}, u32[]{:S(2)}) collective-permute-start(bf16[256,256]{1,0:T(8,128)(2,1)S(1)} %get-tuple-element.126), channel_id=1, source_target_pairs={{0,192},{32,224},{64,128},{96,160},{128,64},{160,96},{192,0},{224,... | collective-permute-start | bytes 393224 | tf_op jit(solution)/shard_map/ppermute | solution.py:596
  40.8 0.0 collective-permute-start.19
  40.8 3.8 %collective-permute-done.13.b = bf16[256,256]{1,0:T(8,128)(2,1)S(1)} collective-permute-done((bf16[256,256]{1,0:T(8,128)(2,1)S(1)}, bf16[256,256]{1,0:T(8,128)(2,1)S(1)}, u32[]{:S(2)}, u32[]{:S(2)}) %collective-permute-start.13) | collective-permute-done | bytes 131104 | tf_op jit(solution)/shard_map/ppermute | solution.py:596
  44.6 0.0 collective-permute-done.14.c
  44.6 2.2 %collective-permute-done.15.d = bf16[256,256]{1,0:T(8,128)(2,1)S(1)} collective-permute-done((bf16[256,256]{1,0:T(8,128)(2,1)S(1)}, bf16[256,256]{1,0:T(8,128)(2,1)S(1)}, u32[]{:S(2)}, u32[]{:S(2)}) %collective-permute-start.15) | collective-permute-done | bytes 131104 | tf_op jit(solution)/shard_map/ppermute | solution.py:596
  46.8 0.4 weight_grad_2.1
  47.2 2.4 %collective-permute-start.18 = (bf16[384,256]{1,0:T(8,128)(2,1)S(1)}, bf16[384,256]{1,0:T(8,128)(2,1)S(1)}, u32[]{:S(2)}, u32[]{:S(2)}) collective-permute-start(bf16[384,256]{1,0:T(8,128)(2,1)S(1)} %weight_grad_2.1), channel_id=1, source_target_pairs={{0,16},{1,17},{2,18},{3,19},{4,20},{5,21},{6,22},{7,23},{8,24},{9,... | collective-permute-start | bytes 589832 | tf_op jit(solution)/shard_map/ppermute | solution.py:599
  49.6 0.4 weight_grad_3.1
  50.0 0.1 collective-permute-start.17
  50.1 0.4 weight_grad_1.1
  50.4 2.5 %collective-permute-start.16 = (bf16[384,256]{1,0:T(8,128)(2,1)S(1)}, bf16[384,256]{1,0:T(8,128)(2,1)S(1)}, u32[]{:S(2)}, u32[]{:S(2)}) collective-permute-start(bf16[384,256]{1,0:T(8,128)(2,1)S(1)} %weight_grad_1.1), channel_id=1, source_target_pairs={{0,8},{1,9},{2,10},{3,11},{4,12},{5,13},{6,14},{7,15},{8,0},{9,1},... | collective-permute-start | bytes 589832 | tf_op jit(solution)/shard_map/ppermute | solution.py:599
  52.9 0.0 collective-permute-done.19.dq_other
  52.9 4.8 %input_grad.1 = bf16[128,1536]{1,0:T(8,128)(2,1)} custom-call(bf16[256,768]{1,0:T(8,128)(2,1)S(1)} %get-tuple-element.116.dq, bf16[128,768]{1,0:T(8,128)(2,1)S(1)} %collective-permute-done.19.dq_other, bf16[256,512]{1,0:T(8,128)(2,1)S(1)} %sum_join.1.joined.dkv, bf16[256,512]{1,0:T(8,128)(2,1)S(1)} %collective-permute-done.11.joined_other.dkv_other, ...), custom_call_target="tpu_custom_call" | custom-call | flops 1 | bytes 1 | tf_op jit(solution)/shard_map/input_grad/pallas_call | solution.py:536
  57.7 0.4 weight_grad_0.1.a
  58.1 1.7 %collective-permute-done.17.c = bf16[384,256]{1,0:T(8,128)(2,1)S(1)} collective-permute-done((bf16[384,256]{1,0:T(8,128)(2,1)S(1)}, bf16[384,256]{1,0:T(8,128)(2,1)S(1)}, u32[]{:S(2)}, u32[]{:S(2)}) %collective-permute-start.17) | collective-permute-done | bytes 196640 | tf_op jit(solution)/shard_map/ppermute | solution.py:599
  59.8 0.2 collective-permute-done.16.b
  60.0 0.1 sum_four.1
  60.1 18.8 %all_to_all.9 = bf16[8,48,256]{2,1,0:T(8,128)(2,1)S(1)} all-to-all(bf16[8,48,256]{2,1,0:T(8,128)(2,1)S(1)} %bitcast.11), channel_id=1, replica_groups={{0,1,2,3,4,5,6,7},{8,9,10,11,12,13,14,15},{16,17,18,19,20,21,22,23},{24..., dimensions={0} | all-to-all | bytes 393216 | tf_op jit(solution)/shard_map/all_to_all | solution.py:605
  78.8 0.6 convert_reduce_fusion
  (6 shorter events, 0.0 us)
Async XLA Ops:
  0.6 5.8 %collective-permute-start.1 = (bf16[128,1536]{1,0:T(8,128)(2,1)}, bf16[128,1536]{1,0:T(8,128)(2,1)S(1)}, u32[]{:S(2)}, u32[]{:S(2)}) collective-permute-start(bf16[128,1536]{1,0:T(8,128)(2,1)} %bitcast.5), channel_id=1, source_target_pairs={{0,32},{32,0},{64,96},{96,64},{128,160},{160,128},{192,224},{224,1... | collective-permute-start | bytes 1179656 | tf_op jit(solution)/shard_map/ppermute | solution.py:554
  0.7 5.7 %collective-permute-start.3 = (bf16[128,1536]{1,0:T(8,128)(2,1)}, bf16[128,1536]{1,0:T(8,128)(2,1)S(1)}, u32[]{:S(2)}, u32[]{:S(2)}) collective-permute-start(bf16[128,1536]{1,0:T(8,128)(2,1)} %bitcast.12), channel_id=1, source_target_pairs={{0,32},{32,0},{64,96},{96,64},{128,160},{160,128},{192,224},{224,1... | collective-permute-start | bytes 1179656 | tf_op jit(solution)/shard_map/ppermute | solution.py:555
  1.2 12.2 %collective-permute-start = (bf16[128,1536]{1,0:T(8,128)(2,1)}, bf16[128,1536]{1,0:T(8,128)(2,1)S(1)}, u32[]{:S(2)}, u32[]{:S(2)}) collective-permute-start(bf16[128,1536]{1,0:T(8,128)(2,1)} %bitcast.6), channel_id=1, source_target_pairs={{0,64},{32,96},{64,0},{96,32},{128,192},{160,224},{192,128},{224,1... | collective-permute-start | bytes 1179656 | tf_op jit(solution)/shard_map/ppermute | solution.py:563
  2.7 15.4 %collective-permute-start.6 = (bf16[128,1536]{1,0:T(8,128)(2,1)}, bf16[128,1536]{1,0:T(8,128)(2,1)S(1)}, u32[]{:S(2)}, u32[]{:S(2)}) collective-permute-start(bf16[128,1536]{1,0:T(8,128)(2,1)} %bitcast.7), channel_id=1, source_target_pairs={{0,192},{32,224},{64,128},{96,160},{128,64},{160,96},{192,0},{224,... | collective-permute-start | bytes 1179656 | tf_op jit(solution)/shard_map/ppermute | solution.py:563
  4.8 2.7 %copy-start.1 = (bf16[1,128,1536]{2,1,0:T(8,128)(2,1)S(1)}, bf16[1,128,1536]{2,1,0:T(8,128)(2,1)}, u32[]{:S(2)}) copy-start(bf16[1,128,1536]{2,1,0:T(8,128)(2,1)} %param.8) | copy-start | bytes 1179652
  4.8 1.6 %collective-permute-start.2 = (s32[1,8]{1,0:T(1,128)}, s32[1,8]{1,0:T(1,128)S(1)}, u32[]{:S(2)}, u32[]{:S(2)}) collective-permute-start(s32[1,8]{1,0:T(1,128)} %bitcast.15), channel_id=1, source_target_pairs={{0,32},{32,0},{64,96},{96,64},{128,160},{160,128},{192,224},{224,1... | collective-permute-start | bytes 104 | tf_op jit(solution)/shard_map/ppermute | solution.py:556
  6.4 1.1 %copy-start = (bf16[1,128,1536]{2,1,0:T(8,128)(2,1)S(1)}, bf16[1,128,1536]{2,1,0:T(8,128)(2,1)}, u32[]{:S(2)}) copy-start(bf16[1,128,1536]{2,1,0:T(8,128)(2,1)} %param.7) | copy-start | bytes 1179652
  6.7 10.9 %collective-permute-start.4 = (bf16[256,256]{1,0:T(8,128)(2,1)S(1)}, bf16[256,256]{1,0:T(8,128)(2,1)S(1)}, u32[]{:S(2)}, u32[]{:S(2)}) collective-permute-start(bf16[256,256]{1,0:T(8,128)(2,1)S(1)} %project_kv.1.refs_0_), channel_id=1, source_target_pairs={{0,128},{32,160},{64,192},{96,224},{128,0},{160,32},{192,64},{224,... | collective-permute-start | bytes 393224 | tf_op jit(solution)/shard_map/ppermute | solution.py:562
  17.7 17.1 %collective-permute-start.5 = (bf16[128,1536]{1,0:T(8,128)(2,1)S(1)}, bf16[128,1536]{1,0:T(8,128)(2,1)S(1)}, u32[]{:S(2)}, u32[]{:S(2)}) collective-permute-start(bf16[128,1536]{1,0:T(8,128)(2,1)S(1)} %collective-permute-done.far1), channel_id=1, source_target_pairs={{0,192},{32,224},{64,128},{96,160},{128,64},{160,96},{192,0},{224,... | collective-permute-start | bytes 1179656 | tf_op jit(solution)/shard_map/ppermute | solution.py:571
  18.7 1.4 %collective-permute-start.7 = (bf16[256,256]{1,0:T(8,128)(2,1)S(1)}, bf16[256,256]{1,0:T(8,128)(2,1)S(1)}, u32[]{:S(2)}, u32[]{:S(2)}) collective-permute-start(bf16[256,256]{1,0:T(8,128)(2,1)S(1)} %get-tuple-element.82), channel_id=1, source_target_pairs={{0,32},{32,0},{64,96},{96,64},{128,160},{160,128},{192,224},{224,1... | collective-permute-start | bytes 393224 | tf_op jit(solution)/shard_map/ppermute | solution.py:573
  22.3 7.2 %collective-permute-start.10 = (bf16[256,256]{1,0:T(8,128)(2,1)S(1)}, bf16[256,256]{1,0:T(8,128)(2,1)S(1)}, u32[]{:S(2)}, u32[]{:S(2)}) collective-permute-start(bf16[256,256]{1,0:T(8,128)(2,1)S(1)} %get-tuple-element.96), channel_id=1, source_target_pairs={{0,128},{32,160},{64,192},{96,224},{128,0},{160,32},{192,64},{224,... | collective-permute-start | bytes 393224 | tf_op jit(solution)/shard_map/ppermute | solution.py:581
  24.7 10.0 %collective-permute-start.9 = (bf16[256,256]{1,0:T(8,128)(2,1)S(1)}, bf16[256,256]{1,0:T(8,128)(2,1)S(1)}, u32[]{:S(2)}, u32[]{:S(2)}) collective-permute-start(bf16[256,256]{1,0:T(8,128)(2,1)S(1)} %get-tuple-element.93), channel_id=1, source_target_pairs={{0,192},{32,224},{64,128},{96,160},{128,64},{160,96},{192,0},{224,... | collective-permute-start | bytes 393224 | tf_op jit(solution)/shard_map/ppermute | solution.py:581
  26.6 8.1 %collective-permute-start.8 = (bf16[256,256]{1,0:T(8,128)(2,1)S(1)}, bf16[256,256]{1,0:T(8,128)(2,1)S(1)}, u32[]{:S(2)}, u32[]{:S(2)}) collective-permute-start(bf16[256,256]{1,0:T(8,128)(2,1)S(1)} %get-tuple-element.90), channel_id=1, source_target_pairs={{0,64},{32,96},{64,0},{96,32},{128,192},{160,224},{192,128},{224,1... | collective-permute-start | bytes 393224 | tf_op jit(solution)/shard_map/ppermute | solution.py:581
  34.8 1.6 %collective-permute-start.11 = (bf16[256,512]{1,0:T(8,128)(2,1)S(1)}, bf16[256,512]{1,0:T(8,128)(2,1)S(1)}, u32[]{:S(2)}, u32[]{:S(2)}) collective-permute-start(bf16[256,512]{1,0:T(8,128)(2,1)S(1)} %sum_join.1.joined.dkv), channel_id=1, source_target_pairs={{0,32},{32,0},{64,96},{96,64},{128,160},{160,128},{192,224},{224,1... | collective-permute-start | bytes 786440 | tf_op jit(solution)/shard_map/ppermute | solution.py:588
  36.5 10.3 %collective-permute-start.12 = (bf16[1536,512]{1,0:T(8,128)(2,1)S(1)}, bf16[1536,512]{1,0:T(8,128)(2,1)S(1)}, u32[]{:S(2)}, u32[]{:S(2)}) collective-permute-start(bf16[1536,512]{1,0:T(8,128)(2,1)S(1)} %transpose_tokens.1.tokens_t), channel_id=1, source_target_pairs={{0,32},{32,0},{64,96},{96,64},{128,160},{160,128},{192,224},{224,1... | collective-permute-start | bytes 4718600 | tf_op jit(solution)/shard_map/ppermute | solution.py:595
  36.7 7.9 %collective-permute-start.13 = (bf16[256,256]{1,0:T(8,128)(2,1)S(1)}, bf16[256,256]{1,0:T(8,128)(2,1)S(1)}, u32[]{:S(2)}, u32[]{:S(2)}) collective-permute-start(bf16[256,256]{1,0:T(8,128)(2,1)S(1)} %get-tuple-element.124), channel_id=1, source_target_pairs={{0,128},{32,160},{64,192},{96,224},{128,0},{160,32},{192,64},{224,... | collective-permute-start | bytes 393224 | tf_op jit(solution)/shard_map/ppermute | solution.py:596
  36.7 7.9 %collective-permute-start.14 = (bf16[256,256]{1,0:T(8,128)(2,1)S(1)}, bf16[256,256]{1,0:T(8,128)(2,1)S(1)}, u32[]{:S(2)}, u32[]{:S(2)}) collective-permute-start(bf16[256,256]{1,0:T(8,128)(2,1)S(1)} %get-tuple-element.125), channel_id=1, source_target_pairs={{0,64},{32,96},{64,0},{96,32},{128,192},{160,224},{192,128},{224,1... | collective-permute-start | bytes 393224 | tf_op jit(solution)/shard_map/ppermute | solution.py:596
  38.1 8.8 %collective-permute-start.15 = (bf16[256,256]{1,0:T(8,128)(2,1)S(1)}, bf16[256,256]{1,0:T(8,128)(2,1)S(1)}, u32[]{:S(2)}, u32[]{:S(2)}) collective-permute-start(bf16[256,256]{1,0:T(8,128)(2,1)S(1)} %get-tuple-element.126), channel_id=1, source_target_pairs={{0,192},{32,224},{64,128},{96,160},{128,64},{160,96},{192,0},{224,... | collective-permute-start | bytes 393224 | tf_op jit(solution)/shard_map/ppermute | solution.py:596
  40.8 12.1 %collective-permute-start.19 = (bf16[128,768]{1,0:T(8,128)(2,1)S(1)}, bf16[128,768]{1,0:T(8,128)(2,1)S(1)}, u32[]{:S(2)}, u32[]{:S(2)}) collective-permute-start(bf16[128,768]{1,0:T(8,128)(2,1)S(1)} %get-tuple-element.127), channel_id=1, source_target_pairs={{0,32},{32,0},{64,96},{96,64},{128,160},{160,128},{192,224},{224,1... | collective-permute-start | bytes 589832 | tf_op jit(solution)/shard_map/ppermute | solution.py:594
  47.2 10.9 %collective-permute-start.18 = (bf16[384,256]{1,0:T(8,128)(2,1)S(1)}, bf16[384,256]{1,0:T(8,128)(2,1)S(1)}, u32[]{:S(2)}, u32[]{:S(2)}) collective-permute-start(bf16[384,256]{1,0:T(8,128)(2,1)S(1)} %weight_grad_2.1), channel_id=1, source_target_pairs={{0,16},{1,17},{2,18},{3,19},{4,20},{5,21},{6,22},{7,23},{8,24},{9,... | collective-permute-start | bytes 589832 | tf_op jit(solution)/shard_map/ppermute | solution.py:599
  50.0 9.9 %collective-permute-start.17 = (bf16[384,256]{1,0:T(8,128)(2,1)S(1)}, bf16[384,256]{1,0:T(8,128)(2,1)S(1)}, u32[]{:S(2)}, u32[]{:S(2)}) collective-permute-start(bf16[384,256]{1,0:T(8,128)(2,1)S(1)} %weight_grad_3.1), channel_id=1, source_target_pairs={{0,24},{1,25},{2,26},{3,27},{4,28},{5,29},{6,30},{7,31},{8,16},{9,... | collective-permute-start | bytes 589832 | tf_op jit(solution)/shard_map/ppermute | solution.py:599
  50.4 9.5 %collective-permute-start.16 = (bf16[384,256]{1,0:T(8,128)(2,1)S(1)}, bf16[384,256]{1,0:T(8,128)(2,1)S(1)}, u32[]{:S(2)}, u32[]{:S(2)}) collective-permute-start(bf16[384,256]{1,0:T(8,128)(2,1)S(1)} %weight_grad_1.1), channel_id=1, source_target_pairs={{0,8},{1,9},{2,10},{3,11},{4,12},{5,13},{6,14},{7,15},{8,0},{9,1},... | collective-permute-start | bytes 589832 | tf_op jit(solution)/shard_map/ppermute | solution.py:599

commit v17 on v14

--- a/solution.py
+++ b/solution.py
@@ -112,23 +112,21 @@
     )(own, w_key, w_value)
 
 
-def kv_far_kernel(far1, far3, weights, weights_other, mine, theirs):
-    for i, rows in enumerate((far1, far3)):
-        part = slice(i * TILE, (i + 1) * TILE)
-        theirs[part] = dot(rows[...], weights_other[...]).astype(BF)
-        mine[part] = dot(rows[...], weights[...]).astype(BF)
-
-
-def project_kv_far(far1, far3, weights, weights_other):
+def kv_far_kernel(far1, far3, weights, out):
+    out[:TILE] = dot(far1[...], weights[...]).astype(BF)
+    out[TILE:] = dot(far3[...], weights[...]).astype(BF)
+
+
+def project_kv_far(far1, far3, weights):
     return pl.pallas_call(
         kv_far_kernel,
-        in_specs=[WHOLE] * 4,
-        out_specs=[WHOLE] * 2,
-        out_shape=[jax.ShapeDtypeStruct((2 * TILE, 2 * HD), BF)] * 2,
-        compiler_params=PARAMS,
-        cost_estimate=cost(8 * TILE * D * 256, 4 * (TILE * D + D * 256)),
+        in_specs=[WHOLE] * 3,
+        out_specs=WHOLE,
+        out_shape=jax.ShapeDtypeStruct((2 * TILE, 2 * HD), BF),
+        compiler_params=PARAMS,
+        cost_estimate=cost(4 * TILE * D * 256, 2 * (2 * TILE * D + D * 256)),
         name="project_kv_far",
-    )(far1, far3, weights, weights_other)
+    )(far1, far3, weights)
 
 
 def kv_kernel(other, weights, kv_own, out):
@@ -569,8 +567,9 @@
     scores = {0: chip_scores(0, limits, query, up, kv)}
     far, kv2, scores[0] = lax.optimization_barrier((far, kv2, scores[0]))
     late = lax.ppermute(far[3], "ctx", chip_pair(1))
-    mine, theirs = project_kv_far(far[1], far[3], weights, weights_other)
+    theirs = project_kv_far(far[1], far[3], weights_other)
     theirs = lax.ppermute(theirs, "ctx", CORE)
+    mine = project_kv_far(far[1], far[3], weights)
     for i, d in enumerate((1, 3)):
         scores[d] = chip_scores(d, limits, query, up, mine, theirs, part=i)
     scores[2] = chip_scores(2, limits, query, up, kv2)

time: 79.1 us -> 79.1 us (level)
  transfers between devices with their start and end apart: 20 -> 20, of which waited for: 11 -> 11; matrix products, arithmetic and copies ran while one was open for 0% -> 0% of each run, Pallas kernels for 23% -> 24%
where the time goes in v17:
time: 79.1 us; the launch traced here: 78.9 us
  waiting for transfers between devices  20.2 us (26%)
  starting transfers between devices  19.5 us (25%)
  Pallas kernels  18.9 us (24%)
  blocking collectives  18.7 us (24%)
  between operations  0.89 us (1%)
    all_to_all x1, blocking collectives, shards(): lax.all_to_all(y_sum, 'dp', 0, 0, tiled=True, axis_index_groups=Z_GROUPS)  18.7 us
    ppermute x2, waiting for transfers between devices, shards(): far = {d: lax.ppermute(own, 'ctx', chip_pair(d)) for d in (1, 3)}  6.27 us
    ppermute x3, waiting for transfers between devices, shards(): lax.ppermute(packed[d], 'ctx', chip_pair(d))  5.98 us
    ppermute x3, starting transfers between devices, shards(): back = [lax.ppermute(terms[d], 'ctx', chip_pair(d)) for d in (1, 3, 2)]  5.15 us
    ppermute x3, starting transfers between devices, shards(): lax.ppermute(terms[d], 'dp', y_pair(d))  4.95 us
    pallas_call x1, Pallas kernels, input_grad(): pl.pallas_call(input_kernel, in_specs=[WHOLE] * 4 + [STAY] * 3, out_specs...  4.83 us
    ppermute x3, waiting for transfers between devices, shards(): back = [lax.ppermute(terms[d], 'ctx', chip_pair(d)) for d in (1, 3, 2)]  4.79 us
    ppermute x3, starting transfers between devices, shards(): lax.ppermute(packed[d], 'ctx', chip_pair(d))  4.13 us
  transfers between devices with their start and end apart: 20, of which 11 were waited for; matrix products, arithmetic and copies ran while one was open for 0% of the time, Pallas kernels for 24%

profile of v17, /device:TPU:8, one launch (start us, length us, event | category | flops | bytes accessed | tf_op | source)
XLA Modules:
  0.0 78.9 jit_solution(1146081898506021899)
XLA Ops:
  0.6 0.1 collective-permute-start.2
  0.7 0.5 collective-permute-start.4
  1.2 1.5 %collective-permute-start = (bf16[128,1536]{1,0:T(8,128)(2,1)}, bf16[128,1536]{1,0:T(8,128)(2,1)S(1)}, u32[]{:S(2)}, u32[]{:S(2)}) collective-permute-start(bf16[128,1536]{1,0:T(8,128)(2,1)} %bitcast.6), channel_id=1, source_target_pairs={{0,64},{32,96},{64,0},{96,32},{128,192},{160,224},{192,128},{224,1... | collective-permute-start | bytes 1179656 | tf_op jit(solution)/shard_map/ppermute | solution.py:561
  2.7 2.1 %collective-permute-start.1 = (bf16[128,1536]{1,0:T(8,128)(2,1)}, bf16[128,1536]{1,0:T(8,128)(2,1)S(1)}, u32[]{:S(2)}, u32[]{:S(2)}) collective-permute-start(bf16[128,1536]{1,0:T(8,128)(2,1)} %bitcast.7), channel_id=1, source_target_pairs={{0,192},{32,224},{64,128},{96,160},{128,64},{160,96},{192,0},{224,... | collective-permute-start | bytes 1179656 | tf_op jit(solution)/shard_map/ppermute | solution.py:561
  4.8 0.0 collective-permute-start.3
  4.8 1.6 %project_kv_own.1 = (bf16[1536,256]{1,0:T(8,128)(2,1)S(1)}, bf16[128,256]{1,0:T(8,128)(2,1)S(1)}) custom-call(bf16[128,1536]{1,0:T(8,128)(2,1)} %bitcast.8, bf16[1536,256]{1,0:T(8,128)(2,1)} %w_key.5, bf16[1536,256]{1,0:T(8,128)(2,1)} %w_value.5), custom_call_target="tpu_custom_call" | custom-call | flops 1 | bytes 1 | tf_op jit(solution)/shard_map/project_kv_own/pallas_call | solution.py:100
  6.4 0.0 copy-start
  6.4 0.0 collective-permute-done.3.mask_other
  6.4 0.0 collective-permute-done.2.other
  6.4 0.0 collective-permute-done.4.up_other
  6.5 0.3 project_kv.1.refs_0_
  6.7 0.7 collective-permute-start.5
  7.5 0.1 stack_up.1.up
  7.6 3.2 %project_query.1 = (bf16[1536,128]{1,0:T(8,128)(2,1)S(1)}, s32[16,256]{1,0:T(8,128)S(1)}, bf16[1536,256]{1,0:T(8,128)(2,1)S(1)}) custom-call(bf16[128,1536]{1,0:T(8,128)(2,1)S(1)} %bitcast.9, bf16[128,1536]{1,0:T(8,128)(2,1)S(1)} %collective-permute-done.2.other, bf16[1536,1536]{1,0:T(8,128)(2,1)} %w_query.3, bf16[1536,256]{1,0:T(8,128)(2,1)} %w_key.5, ...), custom_call_target="tpu_custom_call" | custom-call | flops 1 | bytes 1 | tf_op jit(solution)/shard_map/project_query/pallas_call | solution.py:219
  10.8 0.7 chip_scores_0.1
  11.5 1.9 %collective-permute-done.far1 = bf16[128,1536]{1,0:T(8,128)(2,1)S(1)} collective-permute-done((bf16[128,1536]{1,0:T(8,128)(2,1)}, bf16[128,1536]{1,0:T(8,128)(2,1)S(1)}, u32[]{:S(2)}, u32[]{:S(2)}) %collective-permute-start) | collective-permute-done | bytes 393248 | tf_op jit(solution)/shard_map/ppermute | solution.py:561
  13.4 4.4 %collective-permute-done.1.far3 = bf16[128,1536]{1,0:T(8,128)(2,1)S(1)} collective-permute-done((bf16[128,1536]{1,0:T(8,128)(2,1)}, bf16[128,1536]{1,0:T(8,128)(2,1)S(1)}, u32[]{:S(2)}, u32[]{:S(2)}) %collective-permute-start.1) | collective-permute-done | bytes 393248 | tf_op jit(solution)/shard_map/ppermute | solution.py:561
  17.8 0.0 collective-permute-done.5.refs_0_
  17.8 0.0 collective-permute-start.6
  17.8 0.4 project_kv_far.3
  18.2 0.1 collective-permute-start.7
  18.3 0.4 project_kv_far.2.refs_0_
  18.7 0.7 chip_scores_2.1
  19.4 0.2 collective-permute-done.7.refs_1_
  19.6 0.7 chip_scores_3.1
  20.3 0.7 chip_scores_1.1
  21.1 0.6 chip_terms_2.1
  21.7 3.7 %collective-permute-start.10 = (bf16[256,256]{1,0:T(8,128)(2,1)S(1)}, bf16[256,256]{1,0:T(8,128)(2,1)S(1)}, u32[]{:S(2)}, u32[]{:S(2)}) collective-permute-start(bf16[256,256]{1,0:T(8,128)(2,1)S(1)} %get-tuple-element.94), channel_id=1, source_target_pairs={{0,128},{32,160},{64,192},{96,224},{128,0},{160,32},{192,64},{224,... | collective-permute-start | bytes 393224 | tf_op jit(solution)/shard_map/ppermute | solution.py:580
  25.4 0.6 chip_terms_3.1
  26.0 1.2 %collective-permute-start.9 = (bf16[256,256]{1,0:T(8,128)(2,1)S(1)}, bf16[256,256]{1,0:T(8,128)(2,1)S(1)}, u32[]{:S(2)}, u32[]{:S(2)}) collective-permute-start(bf16[256,256]{1,0:T(8,128)(2,1)S(1)} %get-tuple-element.91), channel_id=1, source_target_pairs={{0,192},{32,224},{64,128},{96,160},{128,64},{160,96},{192,0},{224,... | collective-permute-start | bytes 393224 | tf_op jit(solution)/shard_map/ppermute | solution.py:580
  27.2 0.6 chip_terms_1.1
  27.8 0.3 collective-permute-start.8
  28.1 0.6 chip_terms_0.1
  28.7 0.7 query_grad.1
  29.4 2.9 %collective-permute-done.10.d = bf16[256,256]{1,0:T(8,128)(2,1)S(1)} collective-permute-done((bf16[256,256]{1,0:T(8,128)(2,1)S(1)}, bf16[256,256]{1,0:T(8,128)(2,1)S(1)}, u32[]{:S(2)}, u32[]{:S(2)}) %collective-permute-start.10) | collective-permute-done | bytes 131104 | tf_op jit(solution)/shard_map/ppermute | solution.py:580
  32.3 1.9 %collective-permute-done.9.c = bf16[256,256]{1,0:T(8,128)(2,1)S(1)} collective-permute-done((bf16[256,256]{1,0:T(8,128)(2,1)S(1)}, bf16[256,256]{1,0:T(8,128)(2,1)S(1)}, u32[]{:S(2)}, u32[]{:S(2)}) %collective-permute-start.9) | collective-permute-done | bytes 131104 | tf_op jit(solution)/shard_map/ppermute | solution.py:580
  34.2 0.0 collective-permute-done.8.b
  34.2 0.0 collective-permute-done.6.far2
  34.2 0.1 sum_join.1.joined.dkv
  34.2 0.1 collective-permute-start.11
  34.3 0.5 transpose_tokens.1.tokens_t
  34.8 1.1 %collective-permute-done.11.joined_other.dkv_other = bf16[256,512]{1,0:T(8,128)(2,1)S(1)} collective-permute-done((bf16[256,512]{1,0:T(8,128)(2,1)S(1)}, bf16[256,512]{1,0:T(8,128)(2,1)S(1)}, u32[]{:S(2)}, u32[]{:S(2)}) %collective-permute-start.11) | collective-permute-done | bytes 262176 | tf_op jit(solution)/shard_map/ppermute | solution.py:587
  35.9 0.1 pack.1
  36.0 0.2 collective-permute-start.12
  36.2 1.1 %collective-permute-start.13 = (bf16[256,256]{1,0:T(8,128)(2,1)S(1)}, bf16[256,256]{1,0:T(8,128)(2,1)S(1)}, u32[]{:S(2)}, u32[]{:S(2)}) collective-permute-start(bf16[256,256]{1,0:T(8,128)(2,1)S(1)} %get-tuple-element.122), channel_id=1, source_target_pairs={{0,128},{32,160},{64,192},{96,224},{128,0},{160,32},{192,64},{224,... | collective-permute-start | bytes 393224 | tf_op jit(solution)/shard_map/ppermute | solution.py:595
  37.2 1.1 %collective-permute-start.14 = (bf16[256,256]{1,0:T(8,128)(2,1)S(1)}, bf16[256,256]{1,0:T(8,128)(2,1)S(1)}, u32[]{:S(2)}, u32[]{:S(2)}) collective-permute-start(bf16[256,256]{1,0:T(8,128)(2,1)S(1)} %get-tuple-element.123), channel_id=1, source_target_pairs={{0,64},{32,96},{64,0},{96,32},{128,192},{160,224},{192,128},{224,1... | collective-permute-start | bytes 393224 | tf_op jit(solution)/shard_map/ppermute | solution.py:595
  38.4 1.9 %collective-permute-start.15 = (bf16[256,256]{1,0:T(8,128)(2,1)S(1)}, bf16[256,256]{1,0:T(8,128)(2,1)S(1)}, u32[]{:S(2)}, u32[]{:S(2)}) collective-permute-start(bf16[256,256]{1,0:T(8,128)(2,1)S(1)} %get-tuple-element.124), channel_id=1, source_target_pairs={{0,192},{32,224},{64,128},{96,160},{128,64},{160,96},{192,0},{224,... | collective-permute-start | bytes 393224 | tf_op jit(solution)/shard_map/ppermute | solution.py:595
  40.3 0.0 collective-permute-start.19
  40.3 3.7 %collective-permute-done.13.b = bf16[256,256]{1,0:T(8,128)(2,1)S(1)} collective-permute-done((bf16[256,256]{1,0:T(8,128)(2,1)S(1)}, bf16[256,256]{1,0:T(8,128)(2,1)S(1)}, u32[]{:S(2)}, u32[]{:S(2)}) %collective-permute-start.13) | collective-permute-done | bytes 131104 | tf_op jit(solution)/shard_map/ppermute | solution.py:595
  44.0 0.9 %collective-permute-done.14.c = bf16[256,256]{1,0:T(8,128)(2,1)S(1)} collective-permute-done((bf16[256,256]{1,0:T(8,128)(2,1)S(1)}, bf16[256,256]{1,0:T(8,128)(2,1)S(1)}, u32[]{:S(2)}, u32[]{:S(2)}) %collective-permute-start.14) | collective-permute-done | bytes 131104 | tf_op jit(solution)/shard_map/ppermute | solution.py:595
  44.9 1.3 %collective-permute-done.15.d = bf16[256,256]{1,0:T(8,128)(2,1)S(1)} collective-permute-done((bf16[256,256]{1,0:T(8,128)(2,1)S(1)}, bf16[256,256]{1,0:T(8,128)(2,1)S(1)}, u32[]{:S(2)}, u32[]{:S(2)}) %collective-permute-start.15) | collective-permute-done | bytes 131104 | tf_op jit(solution)/shard_map/ppermute | solution.py:595
  46.3 0.4 weight_grad_2.1
  46.6 2.4 %collective-permute-start.18 = (bf16[384,256]{1,0:T(8,128)(2,1)S(1)}, bf16[384,256]{1,0:T(8,128)(2,1)S(1)}, u32[]{:S(2)}, u32[]{:S(2)}) collective-permute-start(bf16[384,256]{1,0:T(8,128)(2,1)S(1)} %weight_grad_2.1), channel_id=1, source_target_pairs={{0,16},{1,17},{2,18},{3,19},{4,20},{5,21},{6,22},{7,23},{8,24},{9,... | collective-permute-start | bytes 589832 | tf_op jit(solution)/shard_map/ppermute | solution.py:598
  49.0 0.4 weight_grad_3.1
  49.4 0.1 collective-permute-start.17
  49.5 0.4 weight_grad_1.1
  49.9 2.5 %collective-permute-start.16 = (bf16[384,256]{1,0:T(8,128)(2,1)S(1)}, bf16[384,256]{1,0:T(8,128)(2,1)S(1)}, u32[]{:S(2)}, u32[]{:S(2)}) collective-permute-start(bf16[384,256]{1,0:T(8,128)(2,1)S(1)} %weight_grad_1.1), channel_id=1, source_target_pairs={{0,8},{1,9},{2,10},{3,11},{4,12},{5,13},{6,14},{7,15},{8,0},{9,1},... | collective-permute-start | bytes 589832 | tf_op jit(solution)/shard_map/ppermute | solution.py:598
  52.4 4.8 %input_grad.1 = bf16[128,1536]{1,0:T(8,128)(2,1)} custom-call(bf16[256,768]{1,0:T(8,128)(2,1)S(1)} %get-tuple-element.114.dq, bf16[128,768]{1,0:T(8,128)(2,1)S(1)} %collective-permute-done.19.dq_other, bf16[256,512]{1,0:T(8,128)(2,1)S(1)} %sum_join.1.joined.dkv, bf16[256,512]{1,0:T(8,128)(2,1)S(1)} %collective-permute-done.11.joined_other.dkv_other, ...), custom_call_target="tpu_custom_call" | custom-call | flops 1 | bytes 1 | tf_op jit(solution)/shard_map/input_grad/pallas_call | solution.py:534
  57.2 0.4 weight_grad_0.1.a
  57.6 1.7 %collective-permute-done.17.c = bf16[384,256]{1,0:T(8,128)(2,1)S(1)} collective-permute-done((bf16[384,256]{1,0:T(8,128)(2,1)S(1)}, bf16[384,256]{1,0:T(8,128)(2,1)S(1)}, u32[]{:S(2)}, u32[]{:S(2)}) %collective-permute-start.17) | collective-permute-done | bytes 196640 | tf_op jit(solution)/shard_map/ppermute | solution.py:598
  59.3 0.1 collective-permute-done.16.b
  59.4 0.1 sum_four.1
  59.5 18.7 %all_to_all.9 = bf16[8,48,256]{2,1,0:T(8,128)(2,1)S(1)} all-to-all(bf16[8,48,256]{2,1,0:T(8,128)(2,1)S(1)} %bitcast.11), channel_id=1, replica_groups={{0,1,2,3,4,5,6,7},{8,9,10,11,12,13,14,15},{16,17,18,19,20,21,22,23},{24..., dimensions={0} | all-to-all | bytes 393216 | tf_op jit(solution)/shard_map/all_to_all | solution.py:604
  78.2 0.6 convert_reduce_fusion
  (7 shorter events, 0.0 us)
Async XLA Ops:
  0.6 5.8 %collective-permute-start.2 = (bf16[128,1536]{1,0:T(8,128)(2,1)}, bf16[128,1536]{1,0:T(8,128)(2,1)S(1)}, u32[]{:S(2)}, u32[]{:S(2)}) collective-permute-start(bf16[128,1536]{1,0:T(8,128)(2,1)} %bitcast.5), channel_id=1, source_target_pairs={{0,32},{32,0},{64,96},{96,64},{128,160},{160,128},{192,224},{224,1... | collective-permute-start | bytes 1179656 | tf_op jit(solution)/shard_map/ppermute | solution.py:552
  0.7 5.7 %collective-permute-start.4 = (bf16[128,1536]{1,0:T(8,128)(2,1)}, bf16[128,1536]{1,0:T(8,128)(2,1)S(1)}, u32[]{:S(2)}, u32[]{:S(2)}) collective-permute-start(bf16[128,1536]{1,0:T(8,128)(2,1)} %bitcast.12), channel_id=1, source_target_pairs={{0,32},{32,0},{64,96},{96,64},{128,160},{160,128},{192,224},{224,1... | collective-permute-start | bytes 1179656 | tf_op jit(solution)/shard_map/ppermute | solution.py:553
  1.2 12.2 %collective-permute-start = (bf16[128,1536]{1,0:T(8,128)(2,1)}, bf16[128,1536]{1,0:T(8,128)(2,1)S(1)}, u32[]{:S(2)}, u32[]{:S(2)}) collective-permute-start(bf16[128,1536]{1,0:T(8,128)(2,1)} %bitcast.6), channel_id=1, source_target_pairs={{0,64},{32,96},{64,0},{96,32},{128,192},{160,224},{192,128},{224,1... | collective-permute-start | bytes 1179656 | tf_op jit(solution)/shard_map/ppermute | solution.py:561
  2.7 15.1 %collective-permute-start.1 = (bf16[128,1536]{1,0:T(8,128)(2,1)}, bf16[128,1536]{1,0:T(8,128)(2,1)S(1)}, u32[]{:S(2)}, u32[]{:S(2)}) collective-permute-start(bf16[128,1536]{1,0:T(8,128)(2,1)} %bitcast.7), channel_id=1, source_target_pairs={{0,192},{32,224},{64,128},{96,160},{128,64},{160,96},{192,0},{224,... | collective-permute-start | bytes 1179656 | tf_op jit(solution)/shard_map/ppermute | solution.py:561
  4.8 2.7 %copy-start.1 = (bf16[1,128,1536]{2,1,0:T(8,128)(2,1)S(1)}, bf16[1,128,1536]{2,1,0:T(8,128)(2,1)}, u32[]{:S(2)}) copy-start(bf16[1,128,1536]{2,1,0:T(8,128)(2,1)} %param.8) | copy-start | bytes 1179652
  4.8 1.6 %collective-permute-start.3 = (s32[1,8]{1,0:T(1,128)}, s32[1,8]{1,0:T(1,128)S(1)}, u32[]{:S(2)}, u32[]{:S(2)}) collective-permute-start(s32[1,8]{1,0:T(1,128)} %bitcast.15), channel_id=1, source_target_pairs={{0,32},{32,0},{64,96},{96,64},{128,160},{160,128},{192,224},{224,1... | collective-permute-start | bytes 104 | tf_op jit(solution)/shard_map/ppermute | solution.py:554
  6.4 1.1 %copy-start = (bf16[1,128,1536]{2,1,0:T(8,128)(2,1)S(1)}, bf16[1,128,1536]{2,1,0:T(8,128)(2,1)}, u32[]{:S(2)}) copy-start(bf16[1,128,1536]{2,1,0:T(8,128)(2,1)} %param.7) | copy-start | bytes 1179652
  6.7 11.1 %collective-permute-start.5 = (bf16[256,256]{1,0:T(8,128)(2,1)S(1)}, bf16[256,256]{1,0:T(8,128)(2,1)S(1)}, u32[]{:S(2)}, u32[]{:S(2)}) collective-permute-start(bf16[256,256]{1,0:T(8,128)(2,1)S(1)} %project_kv.1.refs_0_), channel_id=1, source_target_pairs={{0,128},{32,160},{64,192},{96,224},{128,0},{160,32},{192,64},{224,... | collective-permute-start | bytes 393224 | tf_op jit(solution)/shard_map/ppermute | solution.py:560
  17.8 16.4 %collective-permute-start.6 = (bf16[128,1536]{1,0:T(8,128)(2,1)S(1)}, bf16[128,1536]{1,0:T(8,128)(2,1)S(1)}, u32[]{:S(2)}, u32[]{:S(2)}) collective-permute-start(bf16[128,1536]{1,0:T(8,128)(2,1)S(1)} %collective-permute-done.1.far3), channel_id=1, source_target_pairs={{0,64},{32,96},{64,0},{96,32},{128,192},{160,224},{192,128},{224,1... | collective-permute-start | bytes 1179656 | tf_op jit(solution)/shard_map/ppermute | solution.py:569
  18.2 1.4 %collective-permute-start.7 = (bf16[256,256]{1,0:T(8,128)(2,1)S(1)}, bf16[256,256]{1,0:T(8,128)(2,1)S(1)}, u32[]{:S(2)}, u32[]{:S(2)}) collective-permute-start(bf16[256,256]{1,0:T(8,128)(2,1)S(1)} %project_kv_far.3), channel_id=1, source_target_pairs={{0,32},{32,0},{64,96},{96,64},{128,160},{160,128},{192,224},{224,1... | collective-permute-start | bytes 393224 | tf_op jit(solution)/shard_map/ppermute | solution.py:571
  21.7 10.5 %collective-permute-start.10 = (bf16[256,256]{1,0:T(8,128)(2,1)S(1)}, bf16[256,256]{1,0:T(8,128)(2,1)S(1)}, u32[]{:S(2)}, u32[]{:S(2)}) collective-permute-start(bf16[256,256]{1,0:T(8,128)(2,1)S(1)} %get-tuple-element.94), channel_id=1, source_target_pairs={{0,128},{32,160},{64,192},{96,224},{128,0},{160,32},{192,64},{224,... | collective-permute-start | bytes 393224 | tf_op jit(solution)/shard_map/ppermute | solution.py:580
  26.0 8.2 %collective-permute-start.9 = (bf16[256,256]{1,0:T(8,128)(2,1)S(1)}, bf16[256,256]{1,0:T(8,128)(2,1)S(1)}, u32[]{:S(2)}, u32[]{:S(2)}) collective-permute-start(bf16[256,256]{1,0:T(8,128)(2,1)S(1)} %get-tuple-element.91), channel_id=1, source_target_pairs={{0,192},{32,224},{64,128},{96,160},{128,64},{160,96},{192,0},{224,... | collective-permute-start | bytes 393224 | tf_op jit(solution)/shard_map/ppermute | solution.py:580
  27.8 6.3 %collective-permute-start.8 = (bf16[256,256]{1,0:T(8,128)(2,1)S(1)}, bf16[256,256]{1,0:T(8,128)(2,1)S(1)}, u32[]{:S(2)}, u32[]{:S(2)}) collective-permute-start(bf16[256,256]{1,0:T(8,128)(2,1)S(1)} %get-tuple-element.88), channel_id=1, source_target_pairs={{0,64},{32,96},{64,0},{96,32},{128,192},{160,224},{192,128},{224,1... | collective-permute-start | bytes 393224 | tf_op jit(solution)/shard_map/ppermute | solution.py:580
  34.2 1.6 %collective-permute-start.11 = (bf16[256,512]{1,0:T(8,128)(2,1)S(1)}, bf16[256,512]{1,0:T(8,128)(2,1)S(1)}, u32[]{:S(2)}, u32[]{:S(2)}) collective-permute-start(bf16[256,512]{1,0:T(8,128)(2,1)S(1)} %sum_join.1.joined.dkv), channel_id=1, source_target_pairs={{0,32},{32,0},{64,96},{96,64},{128,160},{160,128},{192,224},{224,1... | collective-permute-start | bytes 786440 | tf_op jit(solution)/shard_map/ppermute | solution.py:587
  36.0 10.3 %collective-permute-start.12 = (bf16[1536,512]{1,0:T(8,128)(2,1)S(1)}, bf16[1536,512]{1,0:T(8,128)(2,1)S(1)}, u32[]{:S(2)}, u32[]{:S(2)}) collective-permute-start(bf16[1536,512]{1,0:T(8,128)(2,1)S(1)} %transpose_tokens.1.tokens_t), channel_id=1, source_target_pairs={{0,32},{32,0},{64,96},{96,64},{128,160},{160,128},{192,224},{224,1... | collective-permute-start | bytes 4718600 | tf_op jit(solution)/shard_map/ppermute | solution.py:594
  36.2 7.8 %collective-permute-start.13 = (bf16[256,256]{1,0:T(8,128)(2,1)S(1)}, bf16[256,256]{1,0:T(8,128)(2,1)S(1)}, u32[]{:S(2)}, u32[]{:S(2)}) collective-permute-start(bf16[256,256]{1,0:T(8,128)(2,1)S(1)} %get-tuple-element.122), channel_id=1, source_target_pairs={{0,128},{32,160},{64,192},{96,224},{128,0},{160,32},{192,64},{224,... | collective-permute-start | bytes 393224 | tf_op jit(solution)/shard_map/ppermute | solution.py:595
  37.2 7.7 %collective-permute-start.14 = (bf16[256,256]{1,0:T(8,128)(2,1)S(1)}, bf16[256,256]{1,0:T(8,128)(2,1)S(1)}, u32[]{:S(2)}, u32[]{:S(2)}) collective-permute-start(bf16[256,256]{1,0:T(8,128)(2,1)S(1)} %get-tuple-element.123), channel_id=1, source_target_pairs={{0,64},{32,96},{64,0},{96,32},{128,192},{160,224},{192,128},{224,1... | collective-permute-start | bytes 393224 | tf_op jit(solution)/shard_map/ppermute | solution.py:595
  38.4 7.9 %collective-permute-start.15 = (bf16[256,256]{1,0:T(8,128)(2,1)S(1)}, bf16[256,256]{1,0:T(8,128)(2,1)S(1)}, u32[]{:S(2)}, u32[]{:S(2)}) collective-permute-start(bf16[256,256]{1,0:T(8,128)(2,1)S(1)} %get-tuple-element.124), channel_id=1, source_target_pairs={{0,192},{32,224},{64,128},{96,160},{128,64},{160,96},{192,0},{224,... | collective-permute-start | bytes 393224 | tf_op jit(solution)/shard_map/ppermute | solution.py:595
  40.3 12.1 %collective-permute-start.19 = (bf16[128,768]{1,0:T(8,128)(2,1)S(1)}, bf16[128,768]{1,0:T(8,128)(2,1)S(1)}, u32[]{:S(2)}, u32[]{:S(2)}) collective-permute-start(bf16[128,768]{1,0:T(8,128)(2,1)S(1)} %get-tuple-element.125), channel_id=1, source_target_pairs={{0,32},{32,0},{64,96},{96,64},{128,160},{160,128},{192,224},{224,1... | collective-permute-start | bytes 589832 | tf_op jit(solution)/shard_map/ppermute | solution.py:593
  46.6 10.9 %collective-permute-start.18 = (bf16[384,256]{1,0:T(8,128)(2,1)S(1)}, bf16[384,256]{1,0:T(8,128)(2,1)S(1)}, u32[]{:S(2)}, u32[]{:S(2)}) collective-permute-start(bf16[384,256]{1,0:T(8,128)(2,1)S(1)} %weight_grad_2.1), channel_id=1, source_target_pairs={{0,16},{1,17},{2,18},{3,19},{4,20},{5,21},{6,22},{7,23},{8,24},{9,... | collective-permute-start | bytes 589832 | tf_op jit(solution)/shard_map/ppermute | solution.py:598
  49.4 9.9 %collective-permute-start.17 = (bf16[384,256]{1,0:T(8,128)(2,1)S(1)}, bf16[384,256]{1,0:T(8,128)(2,1)S(1)}, u32[]{:S(2)}, u32[]{:S(2)}) collective-permute-start(bf16[384,256]{1,0:T(8,128)(2,1)S(1)} %weight_grad_3.1), channel_id=1, source_target_pairs={{0,24},{1,25},{2,26},{3,27},{4,28},{5,29},{6,30},{7,31},{8,16},{9,... | collective-permute-start | bytes 589832 | tf_op jit(solution)/shard_map/ppermute | solution.py:598
  49.9 9.5 %collective-permute-start.16 = (bf16[384,256]{1,0:T(8,128)(2,1)S(1)}, bf16[384,256]{1,0:T(8,128)(2,1)S(1)}, u32[]{:S(2)}, u32[]{:S(2)}) collective-permute-start(bf16[384,256]{1,0:T(8,128)(2,1)S(1)} %weight_grad_1.1), channel_id=1, source_target_pairs={{0,8},{1,9},{2,10},{3,11},{4,12},{5,13},{6,14},{7,15},{8,0},{9,1},... | collective-permute-start | bytes 589832 | tf_op jit(solution)/shard_map/ppermute | solution.py:598
